TPU v7x, 32 devices: a whole 2x2x4 slice. The times are simulated.
32 devices in a mesh: groups: 2 (over x), prow: 16 (over z, y, core).
Axes of the slice: x: 2, y: 2, z: 4, core: 2. Of those that a mesh axis runs over, the one named last changes fastest.
Arguments:
- green_same: bfloat16 [18432, 512], P(('groups', 'prow')), parts along dimension 0, may hold values from -6 to 6
- green_opp: bfloat16 [18432, 512], P(('groups', 'prow')), parts along dimension 0, may hold values from -6 to 6
- interaction: bfloat16 [18432, 9216], P(('groups', 'prow')), parts along dimension 0, may hold values from -0.0625 to 0.0625
- pattern: int32 [192, 96], P('groups'), parts along dimension 0, may hold values 0 or 1
- occupation: float32 [192], P('groups'), parts along dimension 0, may hold values from 0.05 to 0.95
- hopping: float32 [192, 96], P('groups'), parts along dimension 0, may hold values from -0.625 to 0.625
Outputs:
- slope_same: float32 [18432, 512], P(('groups', 'prow')), parts along dimension 0
- slope_opp: float32 [18432, 512], P(('groups', 'prow')), parts along dimension 0
- next_same: bfloat16 [18432, 512], P(('groups', 'prow')), parts along dimension 0
- next_opp: bfloat16 [18432, 512], P(('groups', 'prow')), parts along dimension 0
- collision: float32 [192, 512], P('groups'), parts along dimension 0
There are 2 independent parts, one for each index of `groups`. A program takes and returns all parts, laid end to end along the dimension named above; each array names one. Nothing has to cross between parts.
All inputs are finite; a program needn't handle non-finite values.
Results may differ from a plain program's by a relative error of at most 0.0035.
Values may be sent and summed in bfloat16 or wider, within the bound.
No kernel may reach another device: no remote copies, remote signals or barrier semaphores. Data moves between devices by JAX's collectives and lax.ppermute only.
A program may use at most 256 MiB of HBM per device.

v0:
```python
import math

import jax
import jax.numpy as jnp
from jax import lax
from jax.sharding import PartitionSpec as P


def swap_orbitals(block, orbitals):
    count = block.shape[1]
    return (
        block.reshape(orbitals, orbitals, count)
        .transpose(1, 0, 2)
        .reshape(orbitals * orbitals, count)
    )


def product(left, right):
    return jnp.dot(left, right, preferred_element_type=jnp.float32)


def per_device(green_same, green_opp, interaction, pattern, occupation, hopping):
    rows, width = green_same.shape
    orbitals = hopping.shape[0]
    pairs = orbitals * orbitals
    highest = lax.Precision.HIGHEST
    row_ids = lax.axis_index("prow") * rows + jnp.arange(rows, dtype=jnp.int32)
    orbit_ids = jnp.arange(orbitals, dtype=jnp.int32)
    first_hot = (row_ids[:, None] // orbitals == orbit_ids[None, :]).astype(jnp.float32)
    second_hot = (row_ids[:, None] % orbitals == orbit_ids[None, :]).astype(jnp.float32)
    linked = jnp.dot(first_hot, pattern.astype(jnp.float32), precision=highest)
    screened = (
        interaction.astype(jnp.float32).reshape(rows, orbitals, orbitals) * linked[:, :, None]
    )
    polar_factor = occupation[:, None] - occupation[None, :]
    ladder_factor = 1.0 - occupation[:, None] - occupation[None, :]
    polar_terms = screened * polar_factor[None]
    hop_first = jnp.dot(first_hot, hopping, precision=highest)
    hop_second = jnp.dot(second_hot, hopping, precision=highest)
    pair_hopping = (
        hop_first[:, :, None] * second_hot[:, None, :]
        + first_hot[:, :, None] * hop_second[:, None, :]
    )
    kernel_direct = (polar_terms + pair_hopping).astype(jnp.bfloat16).reshape(rows, pairs)
    kernel_polar = polar_terms.astype(jnp.bfloat16).reshape(rows, pairs)
    ladder_terms = (screened * ladder_factor[None]).astype(jnp.bfloat16)
    kernel_ladder = ladder_terms.reshape(rows, pairs)
    column_same, column_opp = (
        lax.all_to_all(green_same, "prow", split_axis=1, concat_axis=0, tiled=True),
        lax.all_to_all(green_opp, "prow", split_axis=1, concat_axis=0, tiled=True),
    )
    flipped_same = swap_orbitals(column_same, orbitals)
    flipped_opp = swap_orbitals(column_opp, orbitals)
    swapped_same, swapped_opp = (
        lax.all_to_all(flipped_same, "prow", split_axis=0, concat_axis=1, tiled=True),
        lax.all_to_all(flipped_opp, "prow", split_axis=0, concat_axis=1, tiled=True),
    )
    same_piece = lax.all_gather(green_same, "prow", axis=0, tiled=True)
    opp_piece = lax.all_gather(green_opp, "prow", axis=0, tiled=True)
    swap_same = lax.all_gather(swapped_same, "prow", axis=0, tiled=True)
    swap_opp = lax.all_gather(swapped_opp, "prow", axis=0, tiled=True)
    new_same = (
        product(kernel_direct, same_piece)
        + product(kernel_polar, opp_piece)
        + product(kernel_ladder, swap_same)
    )
    new_opp = (
        product(kernel_direct, opp_piece)
        + product(kernel_polar, same_piece)
        + product(kernel_ladder, swap_opp)
    )
    next_same = (green_same.astype(jnp.float32) + 0.5 * new_same).astype(jnp.bfloat16)
    next_opp = (green_opp.astype(jnp.float32) + 0.5 * new_opp).astype(jnp.bfloat16)
    share = jnp.dot(first_hot.T, new_same + new_opp, precision=highest) * (
        1.0 / math.sqrt(orbitals)
    )
    collision = lax.psum(share, "prow")
    return (new_same, new_opp, next_same, next_opp, collision)


def solution(mesh):
    placed = (
        P(("groups", "prow"), None),
        P(("groups", "prow"), None),
        P(("groups", "prow"), None),
        P("groups", None),
        P("groups"),
        P("groups", None),
    )
    return jax.shard_map(
        per_device,
        mesh=mesh,
        in_specs=placed,
        out_specs=(
            P(("groups", "prow"), None),
            P(("groups", "prow"), None),
            P(("groups", "prow"), None),
            P(("groups", "prow"), None),
            P("groups", None),
        ),
        check_vma=False,
    )
```

profile of v0, /device:TPU:0, one launch (start us, length us, event | category | flops | bytes accessed | tf_op | source)
XLA Modules:
  0.0 494.3 jit_solution(10400395329778583133)
XLA Ops:
  7.2 0.0 copy-start
  7.2 0.0 copy-start.4
  7.2 0.0 all-gather.7.cloned.1.call-start
  7.2 0.7 all-gather.7.cloned.1.call-update
  7.9 0.0 all-gather.5.cloned.1.call-start
  8.0 0.7 all-gather.5.cloned.1.call-update
  8.7 0.0 all-gather.11.cloned.1.call-start
  8.7 1.4 copy.29
  10.1 36.6 %all_to_all.70 = bf16[576,16,32]{0,2,1:T(8,128)(2,1)S(1)} all-to-all(bf16[576,16,32]{0,2,1:T(8,128)(2,1)S(1)} %bitcast.56), channel_id=1, replica_groups=mesh['groups'=2,'prow'=16] {'prow'}, dimensions={1} | all-to-all | bytes 1179648 | tf_op jit(solution)/shard_map/all_to_all | solution.py:50
  46.7 0.2 copy.30
  46.9 1.1 reshape.174
  48.0 0.4 copy.31
  48.3 0.0 copy-start.8
  48.3 0.6 all_to_all.62
  48.9 0.1 copy.32
  49.1 36.9 %all_to_all.71 = bf16[16,576,32]{1,2,0:T(8,128)(2,1)S(1)} all-to-all(bf16[16,576,32]{1,2,0:T(8,128)(2,1)S(1)} %copy.32), channel_id=1, replica_groups=mesh['groups'=2,'prow'=16] {'prow'}, dimensions={0} | all-to-all | bytes 1179648 | tf_op jit(solution)/shard_map/all_to_all | solution.py:56
  85.9 1.1 copy.33
  87.0 0.0 all-gather.11.cloned.1.call-update
  87.0 0.0 all-gather.9.cloned.1.call-start
  87.1 0.0 copy-done.4
  87.1 0.3 copy.24
  87.4 37.4 %all_to_all.72 = bf16[576,16,32]{0,2,1:T(8,128)(2,1)S(1)} all-to-all(bf16[576,16,32]{0,2,1:T(8,128)(2,1)S(1)} %bitcast.57), channel_id=1, replica_groups=mesh['groups'=2,'prow'=16] {'prow'}, dimensions={1} | all-to-all | bytes 1179648 | tf_op jit(solution)/shard_map/all_to_all | solution.py:49
  124.8 0.2 copy.25
  125.0 1.1 reshape.173
  126.1 0.4 copy.26
  126.5 0.6 all_to_all.55
  127.1 0.1 copy.27
  127.2 30.3 %all_to_all.73 = bf16[16,576,32]{1,2,0:T(8,128)(2,1)S(1)} all-to-all(bf16[16,576,32]{1,2,0:T(8,128)(2,1)S(1)} %copy.27), channel_id=1, replica_groups=mesh['groups'=2,'prow'=16] {'prow'}, dimensions={0} | all-to-all | bytes 1179648 | tf_op jit(solution)/shard_map/all_to_all | solution.py:55
  157.5 1.1 copy.28
  158.6 0.0 all-gather.9.cloned.1.call-update
  158.6 0.2 all-reduce.2.cloned.1.call-start
  158.8 0.0 copy-done.8
  158.8 0.3 broadcast_reduce_fusion
  159.2 0.1 sub.53
  159.3 0.1 sub.60
  159.4 0.1 sub.55
  159.5 0.0 copy-start.7
  159.5 15.8 %copy.23 = bf16[576,9216]{0,1:T(8,128)(2,1)} copy(bf16[576,9216]{1,0:T(8,128)(2,1)} %param.8) | data formatting | bytes 21233664 | tf_op args[2]
  175.3 0.0 copy-done
  175.3 0.3 fusion.11
  175.6 0.3 fusion.8
  176.0 0.3 fusion.12
  176.4 12.0 %multiply_add_fusion = f32[576,96,96]{0,2,1:T(8,128)} fusion(f32[576,96]{0,1:T(8,128)S(1)} %fusion.8, f32[576,96]{0,1:T(8,128)S(1)} %get-tuple-element.17, f32[576,96]{0,1:T(8,128)S(1)} %get-tuple-element.16, f32[576,96]{0,1:T(8,128)S(1)} %fusion.11), kind=kLoop, calls=%fused_computation.4 | loop fusion | flops 15925248 | bytes 22118400 | tf_op jit(solution)/shard_map/add | solution.py:41
  188.3 53.9 %fusion.2 = (bf16[576,9216]{0,1:T(8,128)(2,1)}, bf16[576,9216]{0,1:T(8,128)(2,1)}, bf16[576,9216]{0,1:T(8,128)(2,1)}) fusion(bf16[576,9216]{0,1:T(8,128)(2,1)} %copy.23, f32[9216]{0:T(1024)S(1)} %get-tuple-element.9, f32[576,96]{0,1:T(8,128)S(1)} %fusion.12, f32[576,96,96]{0,2,1:T(8,128)} %multiply_add_fusion, f32[9216]{0:T(1024)S(1)} %get-tuple-element.8), kind=kLoop, calls=%fused_computation.6 | loop fusion | flops 42467328 | bytes 63995904 | tf_op jit(solution)/shard_map/convert_element_type | solution.py:45
  242.2 0.0 all-gather.7.cloned.1.call-done
  242.3 12.5 %fusion.25 = f32[576,512]{1,0:T(8,128)S(1)} fusion(bf16[576,9216]{0,1:T(8,128)(2,1)} %get-tuple-element.6, bf16[9216,512]{1,0:T(8,128)(2,1)} %all-gather.7.cloned.1.call-done), kind=kOutput, calls=%fused_computation.42 | convolution fusion | flops 5435817984 | bytes 21233664 | tf_op jit(solution)/shard_map/dot_general | solution.py:19
  254.8 0.0 all-gather.5.cloned.1.call-done
  254.8 0.0 slice-start
  254.8 0.0 slice-start.1
  254.9 12.7 %fusion.24 = f32[576,512]{1,0:T(8,128)S(1)} fusion(bf16[576,9216]{0,1:T(8,128)(2,1)} %get-tuple-element.6, bf16[9216,512]{1,0:T(8,128)(2,1)} %all-gather.5.cloned.1.call-done), kind=kOutput, calls=%fused_computation.41 | convolution fusion | flops 5435817984 | bytes 21233664 | tf_op jit(solution)/shard_map/dot_general | solution.py:19
  267.6 0.0 slice-start.2
  267.6 9.7 %convolution_add_fusion.1 = f32[576,512]{1,0:T(8,128)} fusion(f32[576,512]{1,0:T(8,128)S(1)} %fusion.25, bf16[576,9216]{0,1:T(8,128)(2,1)S(1)} %copy-done.2, bf16[9216,512]{1,0:T(8,128)(2,1)} %all-gather.5.cloned.1.call-done), kind=kOutput, calls=%fused_computation.8 | convolution fusion | flops 5436112896 | bytes 22413312 | tf_op jit(solution)/shard_map/dot_general | solution.py:19
  277.3 0.0 slice-done.2
  277.3 0.0 copy-start.3
  277.3 5.7 %convolution_add_fusion.3 = f32[576,512]{1,0:T(8,128)S(1)} fusion(f32[576,512]{1,0:T(8,128)S(1)} %fusion.24, bf16[576,9216]{0,1:T(8,128)(2,1)S(1)} %copy-done.2, bf16[9216,512]{1,0:T(8,128)(2,1)S(1)} %bitcast.49), kind=kOutput, calls=%fused_computation.10 | convolution fusion | flops 5436112896 | bytes 22413312 | tf_op jit(solution)/shard_map/dot_general | solution.py:19
  283.0 17.0 %all-gather.11.cloned.1.call-done = bf16[9216,512]{1,0:T(8,128)(2,1)} async-done(((bf16[576,512]{1,0:T(8,128)(2,1)}), bf16[9216,512]{1,0:T(8,128)(2,1)}) %all-gather.11.cloned.1.call-update) | async-done | bytes 9437200 | tf_op jit(solution)/shard_map/all_gather | solution.py:61
  300.0 13.4 %add_convert_fusion = (bf16[576,512]{1,0:T(8,128)(2,1)}, f32[576,512]{1,0:T(8,128)}) fusion(bf16[576,512]{1,0:T(8,128)(2,1)S(1)} %copy-done.3, f32[576,512]{1,0:T(8,128)} %convolution_add_fusion.1, bf16[576,9216]{0,1:T(8,128)(2,1)} %get-tuple-element.7, bf16[9216,512]{1,0:T(8,128)(2,1)} %all-gather.11.cloned.1.call-done), kind=kOutput, calls=%fused_computation.13 | convolution fusion | flops 5437292544 | bytes 23592960 | tf_op jit(solution)/shard_map/dot_general | solution.py:19
  313.5 68.9 %all-gather.9.cloned.1.call-done = bf16[9216,512]{1,0:T(8,128)(2,1)} async-done(((bf16[576,512]{1,0:T(8,128)(2,1)}), bf16[9216,512]{1,0:T(8,128)(2,1)}) %all-gather.9.cloned.1.call-update) | async-done | bytes 9437200 | tf_op jit(solution)/shard_map/all_gather | solution.py:60
  382.4 13.4 %add_convert_fusion.1 = (bf16[576,512]{1,0:T(8,128)(2,1)}, f32[576,512]{1,0:T(8,128)S(1)}) fusion(bf16[576,512]{1,0:T(8,128)(2,1)S(1)} %copy-done.4, f32[576,512]{1,0:T(8,128)S(1)} %convolution_add_fusion.3, bf16[576,9216]{0,1:T(8,128)(2,1)} %get-tuple-element.7, bf16[9216,512]{1,0:T(8,128)(2,1)} %all-gather.9.cloned.1.call-done), kind=kOutput, calls=%fused_computation.14 | convolution fusion | flops 5437292544 | bytes 23592960 | tf_op jit(solution)/shard_map/dot_general | solution.py:19
  395.7 1.0 copy-done.6
  396.8 1.4 fusion.5
  398.1 0.0 all-reduce.2.cloned.1.call-update
  398.1 88.0 %all-reduce.2.cloned.1.call-done = f32[96,512]{1,0:T(8,128)} async-done(((f32[96,512]{1,0:T(8,128)}), f32[96,512]{1,0:T(8,128)}) %all-reduce.2.cloned.1.call-update) | async-done | bytes 196624 | tf_op jit(solution)/shard_map/psum | solution.py:77
  486.1 1.6 copy.35
  (18 shorter events, 0.1 us)
Async XLA Ops:
  7.2 168.1 %copy-start = (f32[96,96]{1,0:T(8,128)S(1)}, f32[96,96]{1,0:T(8,128)}, u32[]{:S(2)}) copy-start(f32[96,96]{1,0:T(8,128)} %param.11) | copy-start | bytes 110596
  7.2 79.9 %copy-start.4 = (bf16[576,512]{1,0:T(8,128)(2,1)S(1)}, bf16[576,512]{1,0:T(8,128)(2,1)}, u32[]{:S(2)}) copy-start(bf16[576,512]{1,0:T(8,128)(2,1)} %param.6) | copy-start | bytes 1769476
  7.2 235.1 %all-gather.7.cloned.1.call-start = ((), (), s32[]{:S(2)}) async-start(), calls=%async_computation.5 | async-start | bytes 10027008 | tf_op jit(solution)/shard_map/all_gather | solution.py:59
  7.9 246.9 %all-gather.5.cloned.1.call-start = ((), (), s32[]{:S(2)}) async-start(), calls=%async_computation.4 | async-start | bytes 10027008 | tf_op jit(solution)/shard_map/all_gather | solution.py:58
  8.7 291.4 %all-gather.11.cloned.1.call-start = ((), (), s32[]{:S(2)}) async-start(), calls=%async_computation.7 | async-start | bytes 10027008 | tf_op jit(solution)/shard_map/all_gather | solution.py:61
  48.3 110.5 %copy-start.8 = (f32[96]{0:T(128)S(1)}, f32[96]{0:T(128)}, u32[]{:S(2)}) copy-start(f32[96]{0:T(128)} %param.10) | copy-start | bytes 1156
  87.0 295.3 %all-gather.9.cloned.1.call-start = ((), (), s32[]{:S(2)}) async-start(), calls=%async_computation.6 | async-start | bytes 10027008 | tf_op jit(solution)/shard_map/all_gather | solution.py:60
  158.6 327.6 %all-reduce.2.cloned.1.call-start = ((), (), s32[]{:S(2)}) async-start(), calls=%async_computation.8 | async-start | bytes 393216 | tf_op jit(solution)/shard_map/psum | solution.py:77
  159.5 16.5 %copy-start.7 = (s32[96,96]{1,0:T(8,128)S(1)}, s32[96,96]{1,0:T(8,128)}, u32[]{:S(2)}) copy-start(s32[96,96]{1,0:T(8,128)} %param.9) | copy-start | bytes 110596
  254.8 12.8 %copy-start.2 = (bf16[576,9216]{0,1:T(8,128)(2,1)S(1)}, bf16[576,9216]{0,1:T(8,128)(2,1)}, u32[]{:S(2)}) copy-start(bf16[576,9216]{0,1:T(8,128)(2,1)} %get-tuple-element.5) | copy-start | bytes 31850500
  254.8 22.5 %slice-start = ((s8[9437184]{0:T(1024)(128)(4,1)}), s8[4194304]{0:T(1024)(128)(4,1)S(1)}, s32[]{:S(2)}) async-start(s8[9437184]{0:T(1024)(128)(4,1)} %bitcast.48), calls=%async_computation.9 | async-start | bytes 8388608
  254.8 22.5 %slice-start.1 = ((s8[9437184]{0:T(1024)(128)(4,1)}), s8[4194304]{0:T(1024)(128)(4,1)S(1)}, s32[]{:S(2)}) async-start(s8[9437184]{0:T(1024)(128)(4,1)} %bitcast.48), calls=%async_computation.10 | async-start | bytes 8388608
  267.6 9.7 %slice-start.2 = ((s8[9437184]{0:T(1024)(128)(4,1)}), s8[1048576]{0:T(1024)(128)(4,1)S(1)}, s32[]{:S(2)}) async-start(s8[9437184]{0:T(1024)(128)(4,1)} %bitcast.48), calls=%async_computation.11 | async-start | bytes 2097152
  277.3 22.7 %copy-start.3 = (bf16[576,512]{1,0:T(8,128)(2,1)S(1)}, bf16[576,512]{1,0:T(8,128)(2,1)}, u32[]{:S(2)}) copy-start(bf16[576,512]{1,0:T(8,128)(2,1)} %param.7) | copy-start | bytes 1769476
  300.0 187.7 %copy-start.1 = (f32[96,96]{1,0:T(8,128)S(1)}, f32[96,96]{1,0:T(8,128)}, u32[]{:S(2)}) copy-start(f32[96,96]{1,0:T(8,128)} %param.11) | copy-start | bytes 110596
  382.4 14.4 %copy-start.5 = (f32[576,512]{1,0:T(8,128)S(1)}, f32[576,512]{1,0:T(8,128)}, u32[]{:S(2)}) copy-start(f32[576,512]{1,0:T(8,128)} %get-tuple-element.19) | copy-start | bytes 3538948
  395.7 1.0 copy-start.6
Sparse Core Ops, SparseCore 0:
  10.3 116.6 all-gather.6
  129.3 88.0 all-gather.4
  220.3 79.7 all-gather.10
  302.7 79.5 all-gather.8
  398.3 87.8 all-reduce.1
where the time goes:
time: 498 us; the launch traced here: 494 us
  waiting for transfers between devices  175 us (35%)
  blocking collectives  141 us (28%)
  matrix products  69.7 us (14%)
  other arithmetic  66 us (13%)
  local copies, waits for them, and re-layouts  27.6 us (6%)
  between operations  14.1 us (3%)
    psum x1, waiting for transfers between devices, per_device(): collision = lax.psum(share, 'prow')  88 us
    all_gather x1, waiting for transfers between devices, per_device(): swap_same = lax.all_gather(swapped_same, 'prow', axis=0, tiled=True)  68.9 us
    dot_general x6, matrix products, product(): return jnp.dot(left, right, preferred_element_type=jnp.float32)  67.4 us
    convert_element_type x1, other arithmetic, per_device(): kernel_polar = polar_terms.astype(jnp.bfloat16).reshape(rows, pairs)  53.9 us
    all_to_all x1, blocking collectives, per_device(): lax.all_to_all(green_same, 'prow', split_axis=1, concat_axis=0, tiled=True)  37.4 us
    all_to_all x1, blocking collectives, per_device(): lax.all_to_all(flipped_opp, 'prow', split_axis=0, concat_axis=1, tiled=True)  36.9 us
    all_to_all x1, blocking collectives, per_device(): lax.all_to_all(green_opp, 'prow', split_axis=1, concat_axis=0, tiled=True)  36.6 us
    all_to_all x1, blocking collectives, per_device(): lax.all_to_all(flipped_same, 'prow', split_axis=0, concat_axis=1, tiled=T...  30.3 us
  transfers between devices with their start and end apart: 5, of which 3 were waited for; matrix products, arithmetic and copies ran while one was open for 29% of the time, Pallas kernels for 0%

commit v1 on v0

--- a/solution.py
+++ b/solution.py
@@ -1,9 +1,14 @@
+import functools
 import math
 
 import jax
 import jax.numpy as jnp
 from jax import lax
+from jax.experimental import pallas as pl
+from jax.experimental.pallas import tpu as pltpu
 from jax.sharding import PartitionSpec as P
+
+MIB = 1 << 20
 
 
 def swap_orbitals(block, orbitals):
@@ -19,7 +24,7 @@
     return jnp.dot(left, right, preferred_element_type=jnp.float32)
 
 
-def per_device(green_same, green_opp, interaction, pattern, occupation, hopping):
+def plain_form(green_same, green_opp, interaction, pattern, occupation, hopping):
     rows, width = green_same.shape
     orbitals = hopping.shape[0]
     pairs = orbitals * orbitals
@@ -43,31 +48,18 @@
     )
     kernel_direct = (polar_terms + pair_hopping).astype(jnp.bfloat16).reshape(rows, pairs)
     kernel_polar = polar_terms.astype(jnp.bfloat16).reshape(rows, pairs)
-    ladder_terms = (screened * ladder_factor[None]).astype(jnp.bfloat16)
-    kernel_ladder = ladder_terms.reshape(rows, pairs)
-    column_same, column_opp = (
-        lax.all_to_all(green_same, "prow", split_axis=1, concat_axis=0, tiled=True),
-        lax.all_to_all(green_opp, "prow", split_axis=1, concat_axis=0, tiled=True),
-    )
-    flipped_same = swap_orbitals(column_same, orbitals)
-    flipped_opp = swap_orbitals(column_opp, orbitals)
-    swapped_same, swapped_opp = (
-        lax.all_to_all(flipped_same, "prow", split_axis=0, concat_axis=1, tiled=True),
-        lax.all_to_all(flipped_opp, "prow", split_axis=0, concat_axis=1, tiled=True),
-    )
+    kernel_ladder = (screened * ladder_factor[None]).astype(jnp.bfloat16).reshape(rows, pairs)
     same_piece = lax.all_gather(green_same, "prow", axis=0, tiled=True)
     opp_piece = lax.all_gather(green_opp, "prow", axis=0, tiled=True)
-    swap_same = lax.all_gather(swapped_same, "prow", axis=0, tiled=True)
-    swap_opp = lax.all_gather(swapped_opp, "prow", axis=0, tiled=True)
     new_same = (
         product(kernel_direct, same_piece)
         + product(kernel_polar, opp_piece)
-        + product(kernel_ladder, swap_same)
+        + product(kernel_ladder, swap_orbitals(same_piece, orbitals))
     )
     new_opp = (
         product(kernel_direct, opp_piece)
         + product(kernel_polar, same_piece)
-        + product(kernel_ladder, swap_opp)
+        + product(kernel_ladder, swap_orbitals(opp_piece, orbitals))
     )
     next_same = (green_same.astype(jnp.float32) + 0.5 * new_same).astype(jnp.bfloat16)
     next_opp = (green_opp.astype(jnp.float32) + 0.5 * new_opp).astype(jnp.bfloat16)
@@ -76,6 +68,268 @@
     )
     collision = lax.psum(share, "prow")
     return (new_same, new_opp, next_same, next_opp, collision)
+
+
+def build_body(orbitals, firsts, span, pairs, *refs):
+    inter_ref, rows_ref, eye_ref, hop_ref = refs[:4]
+    direct_ref, polar_ref, ladder_ref, turned_ref = refs[-4:]
+    tiles = pairs // span
+    per_tile = span // orbitals
+    strips = -(-firsts * orbitals // 128)
+
+    @pl.loop(0, tiles)
+    def _(tile):
+        cols = pl.ds(pl.multiple_of(tile * span, 128), span)
+        block = inter_ref[:, cols].astype(jnp.float32)
+        for strip in range(strips):
+            piece = block[strip * 128 : (strip + 1) * 128]
+            if piece.shape[0] < 128:
+                piece = jnp.concatenate(
+                    [piece, jnp.zeros((128 - piece.shape[0], span), jnp.float32)], axis=0
+                )
+            turned_ref[pl.ds(pl.multiple_of(strip * pairs + tile * span, 128), span), :] = piece.T
+        for first in range(firsts):
+            part = slice(first * orbitals, (first + 1) * orbitals)
+            facts = rows_ref[first, :, cols]
+            polar = block[part] * facts[0:1]
+            hop = facts[2:3] * eye_ref[...] + facts[3:4] * hop_ref[...]
+            polar_ref[part, cols] = polar.astype(jnp.bfloat16)
+            direct_ref[part, cols] = (polar + hop).astype(jnp.bfloat16)
+
+    @pl.loop(0, tiles)
+    def _(tile):
+        cols = pl.ds(pl.multiple_of(tile * span, 128), span)
+        blocks = []
+        for strip in range(strips):
+            pieces = [
+                turned_ref[
+                    pl.ds(strip * pairs + tile * per_tile + inner, orbitals, stride=orbitals), :
+                ]
+                for inner in range(per_tile)
+            ]
+            blocks.append(jnp.concatenate(pieces, axis=0).T)
+        block = jnp.concatenate(blocks, axis=0)
+        for first in range(firsts):
+            part = slice(first * orbitals, (first + 1) * orbitals)
+            ladder = block[part] * rows_ref[first, 1:2, cols]
+            ladder_ref[part, cols] = ladder.astype(jnp.bfloat16)
+
+
+def build_kernels(interaction, facts, eye, hop, orbitals, firsts):
+    rows, pairs = interaction.shape
+    height = firsts * orbitals
+    span = 4 * orbitals
+    shape = jax.ShapeDtypeStruct((rows, pairs), jnp.bfloat16)
+    made = ()
+    for step in range(rows // height):
+        wide = pl.BlockSpec((height, pairs), lambda g, step=step: (step, 0))
+        made = pl.pallas_call(
+            functools.partial(build_body, orbitals, firsts, span, pairs),
+            grid=(1,),
+            in_specs=[
+                wide,
+                pl.BlockSpec((firsts, 4, pairs), lambda g, step=step: (step, 0, 0)),
+                pl.BlockSpec((orbitals, span), lambda g: (0, 0)),
+                pl.BlockSpec((orbitals, span), lambda g: (0, 0)),
+            ]
+            + [pl.BlockSpec(memory_space=pl.ANY)] * len(made),
+            out_specs=[wide] * 3,
+            out_shape=[shape] * 3,
+            scratch_shapes=[pltpu.VMEM((-(-height // 128) * pairs, 128), jnp.float32)],
+            input_output_aliases={4 + n: n for n in range(len(made))},
+            compiler_params=pltpu.CompilerParams(vmem_limit_bytes=56 * MIB),
+            cost_estimate=pl.CostEstimate(
+                flops=20 * height * pairs, bytes_accessed=8 * height * pairs, transcendentals=0
+            ),
+            name="build_kernels",
+        )(interaction, facts, eye, hop, *made)
+    return made
+
+
+def step_body(chips, opening, closing, orbitals, scale, *refs):
+    place_ref = refs[0]
+    refs = list(refs[1:])
+    mats = [[refs.pop(0) for _ in range(chips)] for _ in range(3)]
+    greens = [[[refs.pop(0) for _ in range(2)] for _ in range(2)] for _ in range(chips)]
+    sums = [] if opening else [refs.pop(0) for _ in range(2)]
+    olds = [refs.pop(0) for _ in range(2)] if closing else []
+    held = refs.pop()
+    core = place_ref[0]
+    rows = greens[0][0][0].shape[0]
+
+    @pl.when(pl.program_id(0) == 0)
+    def _():
+        for chip in range(chips):
+            for kind in range(2):
+                for which in range(2):
+                    lane = core if which == 0 else 1 - core
+                    held[2 * chip + kind, pl.ds(pl.multiple_of(lane * rows, 64), rows), :] = greens[
+                        chip
+                    ][kind][which][...]
+
+    totals = [None, None]
+    for kind in range(2):
+        total = None
+        for chip in range(chips):
+            mine = held[2 * chip + kind]
+            other = held[2 * chip + 1 - kind]
+            term = (
+                product(mats[0][chip][...], mine)
+                + product(mats[1][chip][...], other)
+                + product(mats[2][chip][...], mine)
+            )
+            total = term if total is None else total + term
+        totals[kind] = total if opening else sums[kind][...] + total
+    refs[0][...] = totals[0]
+    refs[1][...] = totals[1]
+    if closing:
+        for kind in range(2):
+            old = olds[kind][...].astype(jnp.float32)
+            refs[2 + kind][...] = (old + 0.5 * totals[kind]).astype(jnp.bfloat16)
+        both = totals[0] + totals[1]
+        count = both.shape[0] // orbitals
+        for first in range(count):
+            refs[4][0, first : first + 1, :] = (
+                jnp.sum(both[first * orbitals : (first + 1) * orbitals], axis=0, keepdims=True)
+                * scale
+            )
+
+
+def step(place, mats, greens, sums, olds, orbitals):
+    chips = len(greens)
+    opening, closing = not sums, bool(olds)
+    rows, width = greens[0][0][0].shape
+    height = 2 * orbitals
+    wide = 2 * rows
+    tall = pl.BlockSpec((height, width), lambda g, p: (g, 0))
+    mat_specs = [
+        pl.BlockSpec((height, wide), lambda g, p, chip=chip: (g, p[1 + chip]))
+        for _ in range(3)
+        for chip in range(chips)
+    ]
+    whole = pl.BlockSpec((rows, width), lambda g, p: (0, 0))
+    out_specs = [tall, tall]
+    out_shape = [jax.ShapeDtypeStruct((rows, width), jnp.float32)] * 2
+    if closing:
+        out_specs += [tall, tall, pl.BlockSpec((1, 2, width), lambda g, p: (g, 0, 0))]
+        out_shape += [jax.ShapeDtypeStruct((rows, width), jnp.bfloat16)] * 2
+        out_shape += [jax.ShapeDtypeStruct((rows // height, 2, width), jnp.float32)]
+    operands = [mats[m] for m in range(3) for _ in range(chips)]
+    operands += [greens[c][k][w] for c in range(chips) for k in range(2) for w in range(2)]
+    in_specs = mat_specs + [whole] * (4 * chips)
+    aliases = {}
+    if not opening:
+        aliases = {1 + len(operands): 0, 2 + len(operands): 1}
+        operands += list(sums)
+        in_specs += [tall, tall]
+    if closing:
+        operands += list(olds)
+        in_specs += [tall, tall]
+    return pl.pallas_call(
+        functools.partial(
+            step_body, chips, opening, closing, orbitals, 1.0 / math.sqrt(orbitals)
+        ),
+        grid_spec=pltpu.PrefetchScalarGridSpec(
+            num_scalar_prefetch=1,
+            grid=(rows // height,),
+            in_specs=in_specs,
+            out_specs=out_specs,
+            scratch_shapes=[pltpu.VMEM((2 * chips, wide, width), jnp.bfloat16)],
+        ),
+        out_shape=out_shape,
+        input_output_aliases=aliases,
+        compiler_params=pltpu.CompilerParams(vmem_limit_bytes=56 * MIB),
+        cost_estimate=pl.CostEstimate(
+            flops=12 * chips * rows * wide * width,
+            bytes_accessed=6 * chips * rows * wide + 16 * rows * width,
+            transcendentals=0,
+        ),
+        name="add_products",
+    )(place, *operands)
+
+
+def ring_form(green_same, green_opp, interaction, pattern, occupation, hopping):
+    rows, width = green_same.shape
+    orbitals = hopping.shape[0]
+    pairs = orbitals * orbitals
+    devices = pairs // rows
+    chips = devices // 2
+    me = lax.axis_index("prow")
+    core, chip = me % 2, me // 2
+    order = list(range(0, chips, 2)) + list(range(chips - 1, 0, -2))
+    spot = [order.index(c) for c in range(chips)]
+    ahead = [order[(spot[c] + 1) % chips] for c in range(chips)]
+    right = [(2 * c + k, 2 * ahead[c] + k) for c in range(chips) for k in range(2)]
+    left = [(b, a) for a, b in right]
+    across = [(d, d ^ 1) for d in range(devices)]
+    order_at = jnp.array(order, jnp.int32)
+    my_spot = jnp.array(spot, jnp.int32)[chip]
+
+    def send(block, pairs_of):
+        return lax.ppermute(block, "prow", pairs_of)
+
+    per = rows // orbitals
+    start = me * per
+    occ_row = jnp.repeat(occupation, orbitals)
+    occ_col = jnp.tile(occupation, orbitals)
+    my_pattern = lax.dynamic_slice_in_dim(pattern, start, per, 0).astype(jnp.float32)
+    my_hop = lax.dynamic_slice_in_dim(hopping, start, per, 0)
+    firsts = start + jnp.arange(per, dtype=jnp.int32)
+    second_ids = jnp.arange(pairs, dtype=jnp.int32) // orbitals
+    facts = jnp.stack(
+        [
+            jnp.repeat(my_pattern, orbitals, axis=1) * (occ_row - occ_col)[None],
+            jnp.tile(my_pattern, (1, orbitals)) * (1.0 - occ_col - occ_row)[None],
+            jnp.repeat(my_hop, orbitals, axis=1),
+            (firsts[:, None] == second_ids[None]).astype(jnp.float32),
+        ],
+        axis=1,
+    )
+    eye = jnp.tile(jnp.eye(orbitals, dtype=jnp.float32), (1, 4))
+    hop = jnp.tile(hopping, (1, 4))
+    mats = build_kernels(interaction, facts, eye, hop, orbitals, 2)
+
+    own = (green_same, green_opp)
+    partner = [send(block, across) for block in own]
+    place = jnp.stack([core, chip]).astype(jnp.int32)
+    sums = step(place, mats, [[[own[k], partner[k]] for k in range(2)]], (), (), orbitals)
+    going = [own, own]
+    half = chips // 2
+    for hop_count in range(1, half):
+        going = [
+            [send(going[0][k], right) for k in range(2)],
+            [send(going[1][k], left) for k in range(2)],
+        ]
+        shared = [[send(block, across) for block in side] for side in going]
+        greens = [
+            [[going[side][k], shared[side][k]] for k in range(2)] for side in range(2)
+        ]
+        behind = order_at[(my_spot - hop_count) % chips]
+        before = order_at[(my_spot + hop_count) % chips]
+        place = jnp.stack([core, behind, before]).astype(jnp.int32)
+        sums = step(place, mats, greens, sums, (), orbitals)
+    far = [send(going[0][0], right), send(going[1][1], left)]
+    shared = [send(block, across) for block in far]
+    place = jnp.stack([core, order_at[(my_spot + half) % chips]]).astype(jnp.int32)
+    new_same, new_opp, next_same, next_opp, share = step(
+        place,
+        mats,
+        [[[far[k], shared[k]] for k in range(2)]],
+        sums,
+        own,
+        orbitals,
+    )
+    collision = lax.all_gather(share.reshape(per, width), "prow", axis=0, tiled=True)
+    return (new_same, new_opp, next_same, next_opp, collision)
+
+
+def per_device(green_same, green_opp, interaction, pattern, occupation, hopping):
+    rows = green_same.shape[0]
+    orbitals = hopping.shape[0]
+    devices = orbitals * orbitals // rows
+    fits = rows % (2 * orbitals) == 0 and rows % 64 == 0 and devices % 4 == 0 and devices >= 8
+    form = ring_form if fits else plain_form
+    return form(green_same, green_opp, interaction, pattern, occupation, hopping)
 
 
 def solution(mesh):

time: 498 us -> 213 us (0.43)
  waiting for transfers between devices: 175 us -> 29.8 us
  blocking collectives: 141 us -> 21.3 us
  Pallas kernels: 0 us -> 115 us
  matrix products: 69.7 us -> 0 us
  other arithmetic: 66 us -> 10.5 us
  starting transfers between devices: 0.38 us -> 18.2 us
  local copies, waits for them, and re-layouts: 27.6 us -> 12.5 us
  between operations: 14.1 us -> 5.71 us
    all_to_all x4 -> x0, blocking collectives: 141 us -> none  [the longest x1 37.4 us: per_device(): lax.all_to_all(green_same, 'prow', split_axis=1, concat_axis=0, tiled=True)]
    pallas_call x0 -> x8, Pallas kernels: none -> 115 us  [the longest x5 65 us: step(): pl.pallas_call(functools.partial(step_body, chips, opening, closing, orbi...]
    psum x1 -> x0, waiting for transfers between devices: 88 us -> none  [per_device(): collision = lax.psum(share, 'prow')]
    all_gather x4 -> x0, waiting for transfers between devices: 86 us -> none  [the longest x1 68.9 us: per_device(): swap_same = lax.all_gather(swapped_same, 'prow', axis=0, tiled=True)]
    dot_general x10 -> x0, matrix products: 69.7 us -> none  [the longest x6 67.4 us: product(): return jnp.dot(left, right, preferred_element_type=jnp.float32)]
    convert_element_type x2 -> x3, other arithmetic: 53.9 us -> 0.9 us  [the longest x1 0.7 us: ring_form(): lax.dynamic_slice_in_dim(pattern, start, per, 0).astype(jnp.float32)]
    ppermute x0 -> x30, waiting for transfers between devices: none -> 29.8 us  [send(): return lax.ppermute(block, 'prow', pairs_of)]
    all_gather x0 -> x1, blocking collectives: none -> 21.3 us  [ring_form(): lax.all_gather(share.reshape(per, width), 'prow', axis=0, tiled=True)]
  transfers between devices with their start and end apart: 5 -> 30, of which waited for: 3 -> 4; matrix products, arithmetic and copies ran while one was open for 29% -> 9% of each run, Pallas kernels for 0% -> 49%
where the time goes in v1:
time: 213 us
  Pallas kernels  115 us (54%)
  waiting for transfers between devices  29.8 us (14%)
  blocking collectives  21.3 us (10%)
  starting transfers between devices  18.2 us (9%)
  local copies, waits for them, and re-layouts  12.5 us (6%)
  other arithmetic  10.5 us (5%)
  between operations  5.71 us (3%)
    pallas_call x5, Pallas kernels, step(): pl.pallas_call(functools.partial(step_body, chips, opening, closing, orbi...  65 us
    pallas_call x3, Pallas kernels, build_kernels(): pl.pallas_call(functools.partial(build_body, orbitals, firsts, span, pair...  49.8 us
    ppermute x30, waiting for transfers between devices, send(): return lax.ppermute(block, 'prow', pairs_of)  29.8 us
    all_gather x1, blocking collectives, ring_form(): lax.all_gather(share.reshape(per, width), 'prow', axis=0, tiled=True)  21.3 us
    ppermute x30, starting transfers between devices, send(): return lax.ppermute(block, 'prow', pairs_of)  18.2 us
    another operation x3, other arithmetic, ring_form(): place = jnp.stack([core, behind, before]).astype(jnp.int32)  5.6 us
  transfers between devices with their start and end apart: 30, of which 4 were waited for; matrix products, arithmetic and copies ran while one was open for 9% of the time, Pallas kernels for 49%

profile of v1, /device:TPU:0, one launch (start us, length us, event | category | flops | bytes accessed | tf_op | source)
XLA Modules:
  0.0 212.7 jit_solution(1825137609815475671)
XLA Ops:
  0.6 0.5 collective-permute-start.28
  1.1 2.6 %collective-permute-start = (bf16[576,512]{1,0:T(8,128)(2,1)}, bf16[576,512]{1,0:T(8,128)(2,1)S(1)}, u32[]{:S(2)}, u32[]{:S(2)}) collective-permute-start(bf16[576,512]{1,0:T(8,128)(2,1)} %refs_10_.1), channel_id=1, source_target_pairs={{0,4},{1,5},{2,0},{3,1},{4,8},{5,9},{6,2},{7,3},{8,12},{9,13},{10,... | collective-permute-start | bytes 1769480 | tf_op jit(solution)/shard_map/ppermute | solution.py:269
  3.8 0.2 collective-permute-start.29
  4.0 1.6 collective-permute-start.11
  5.5 0.4 collective-permute-start.15
  6.0 0.7 dynamic-slice_convert_fusion
  6.7 0.1 broadcast_in_dim.6
  6.8 0.3 reshape.189
  7.2 0.3 tile.47
  7.5 0.7 broadcast_in_dim.14
  8.3 0.7 tile.44
  9.1 0.4 broadcast_multiply_fusion
  9.5 0.3 collective-permute-start.5
  9.8 8.3 %collective-permute-done.refs_7_ = bf16[576,512]{1,0:T(8,128)(2,1)S(1)} collective-permute-done((bf16[576,512]{1,0:T(8,128)(2,1)}, bf16[576,512]{1,0:T(8,128)(2,1)S(1)}, u32[]{:S(2)}, u32[]{:S(2)}) %collective-permute-start) | collective-permute-done | bytes 589856 | tf_op jit(solution)/shard_map/ppermute | solution.py:269
  18.1 12.4 %collective-permute-done.11.refs_9_ = bf16[576,512]{1,0:T(8,128)(2,1)S(1)} collective-permute-done((bf16[576,512]{1,0:T(8,128)(2,1)}, bf16[576,512]{1,0:T(8,128)(2,1)S(1)}, u32[]{:S(2)}, u32[]{:S(2)}) %collective-permute-start.11) | collective-permute-done | bytes 589856 | tf_op jit(solution)/shard_map/ppermute | solution.py:269
  30.5 0.2 compare_convert_fusion
  30.7 0.7 constant_dynamic-slice_fusion
  31.6 0.3 stack_reshape.3
  31.9 1.9 collective-permute-start.1
  33.8 1.6 collective-permute-start.12
  35.4 0.5 collective-permute-start.16
  35.9 0.2 collective-permute-start.27
  36.0 1.7 pad_maximum_fusion.refs_1_
  37.8 1.2 dynamic_slice.30
  43.8 0.8 tile.49.refs_2_
  44.6 0.8 tile.50
  45.4 0.8 tile.51.refs_3_
  46.2 1.6 fusion.5
  47.8 16.6 %build_kernels.3 = (bf16[576,9216]{1,0:T(8,128)(2,1)}, bf16[576,9216]{1,0:T(8,128)(2,1)}, bf16[576,9216]{1,0:T(8,128)(2,1)}) custom-call(bf16[576,9216]{1,0:T(8,128)(2,1)} %refs_0_.5, f32[6,4,9216]{2,1,0:T(4,128)} %pad_maximum_fusion.refs_1_, f32[96,384]{1,0:T(8,128)} %tile.49.refs_2_, f32[96,384]{1,0:T(8,128)} %tile.51.refs_3_), custom_call_target="tpu_custom_call" | custom-call | flops 35389440 | bytes 14155776 | tf_op jit(solution)/shard_map/build_kernels/pallas_call | solution.py:126
  64.4 16.6 %build_kernels.4 = (bf16[576,9216]{1,0:T(8,128)(2,1)}, bf16[576,9216]{1,0:T(8,128)(2,1)}, bf16[576,9216]{1,0:T(8,128)(2,1)}) custom-call(bf16[576,9216]{1,0:T(8,128)(2,1)} %refs_0_.5, f32[6,4,9216]{2,1,0:T(4,128)} %pad_maximum_fusion.refs_1_, f32[96,384]{1,0:T(8,128)} %tile.49.refs_2_, ...), custom_call_target="tpu_custom_call", output_to_operand_aliasing={{0}: (4, {}), {1}: (5, {}), {2}: (6, {})} | custom-call | flops 35389440 | bytes 14155776 | tf_op jit(solution)/shard_map/build_kernels/pallas_call | solution.py:126
  81.0 16.6 %build_kernels.5 = (bf16[576,9216]{1,0:T(8,128)(2,1)}, bf16[576,9216]{1,0:T(8,128)(2,1)}, bf16[576,9216]{1,0:T(8,128)(2,1)}) custom-call(bf16[576,9216]{1,0:T(8,128)(2,1)} %refs_0_.5, f32[6,4,9216]{2,1,0:T(4,128)} %pad_maximum_fusion.refs_1_, f32[96,384]{1,0:T(8,128)} %tile.49.refs_2_, ...), custom_call_target="tpu_custom_call", output_to_operand_aliasing={{0}: (4, {}), {1}: (5, {}), {2}: (6, {})} | custom-call | flops 35389440 | bytes 14155776 | tf_op jit(solution)/shard_map/build_kernels/pallas_call | solution.py:126
  97.6 0.6 pad_add_fusion.4.refs_0_
  98.2 1.3 pad_add_fusion.refs_0_
  99.4 1.8 pad_add_fusion.3.refs_0_
  101.2 0.3 collective-permute-start.6
  101.7 1.7 collective-permute-start.2
  103.3 0.2 collective-permute-start.21
  103.5 0.3 collective-permute-start.22
  103.9 2.0 pad_add_fusion.2.refs_0_
  105.8 1.8 pad_add_fusion.1.refs_0_
  107.7 8.9 %add_products.5 = (f32[576,512]{1,0:T(8,128)}, f32[576,512]{1,0:T(8,128)}) custom-call(s32[2]{0:T(128)} %pad_add_fusion.4.refs_0_, bf16[576,9216]{1,0:T(8,128)(2,1)} %get-tuple-element.33.refs_1_.refs_2_, bf16[576,9216]{1,0:T(8,128)(2,1)} %get-tuple-element.34.refs_2_.refs_3_.refs_4_, bf16[576,9216]{1,0:T(8,128)(2,1)} %get-tuple-element.35.refs_3_.refs_5_.refs_6_, ...), custom_call_target="tpu_custom_call" | custom-call | flops 4076863488 | bytes 8699904 | tf_op jit(solution)/shard_map/add_products/pallas_call | solution.py:228
  116.6 0.4 collective-permute-done.6.refs_13_
  117.0 0.3 collective-permute-start.7
  117.4 1.7 collective-permute-start.13
  119.1 0.3 collective-permute-start.17
  119.4 15.4 %add_products.6 = (f32[576,512]{1,0:T(8,128)}, f32[576,512]{1,0:T(8,128)}) custom-call(s32[3]{0:T(128)} %pad_add_fusion.3.refs_0_, bf16[576,9216]{1,0:T(8,128)(2,1)} %get-tuple-element.33.refs_1_.refs_2_, bf16[576,9216]{1,0:T(8,128)(2,1)} %get-tuple-element.33.refs_1_.refs_2_, ...), custom_call_target="tpu_custom_call", output_to_operand_aliasing={{0}: (15, {}), {1}: (16, {})} | custom-call | flops 8153726976 | bytes 12681216 | tf_op jit(solution)/shard_map/add_products/pallas_call | solution.py:228
  134.9 1.9 collective-permute-start.3
  136.8 0.2 collective-permute-start.19
  137.0 0.3 collective-permute-start.8
  137.3 8.5 %collective-permute-done.17.refs_11_ = bf16[576,512]{1,0:T(8,128)(2,1)S(1)} collective-permute-done((bf16[576,512]{1,0:T(8,128)(2,1)}, bf16[576,512]{1,0:T(8,128)(2,1)S(1)}, u32[]{:S(2)}, u32[]{:S(2)}) %collective-permute-start.17) | collective-permute-done | bytes 589856 | tf_op jit(solution)/shard_map/ppermute | solution.py:269
  145.9 0.5 collective-permute-start.18
  146.4 15.4 %add_products.7 = (f32[576,512]{1,0:T(8,128)}, f32[576,512]{1,0:T(8,128)}) custom-call(s32[3]{0:T(128)} %pad_add_fusion.2.refs_0_, bf16[576,9216]{1,0:T(8,128)(2,1)} %get-tuple-element.33.refs_1_.refs_2_, bf16[576,9216]{1,0:T(8,128)(2,1)} %get-tuple-element.33.refs_1_.refs_2_, ...), custom_call_target="tpu_custom_call", output_to_operand_aliasing={{0}: (15, {}), {1}: (16, {})} | custom-call | flops 8153726976 | bytes 12681216 | tf_op jit(solution)/shard_map/add_products/pallas_call | solution.py:228
  161.8 0.1 collective-permute-start.4
  162.0 0.4 collective-permute-start.9
  162.4 0.8 copy-done.18
  163.2 0.2 copy-done.19
  163.4 0.2 copy-done.20
  163.6 15.4 %add_products.8 = (f32[576,512]{1,0:T(8,128)}, f32[576,512]{1,0:T(8,128)}) custom-call(s32[3]{0:T(128)} %pad_add_fusion.1.refs_0_, bf16[576,9216]{1,0:T(8,128)(2,1)} %get-tuple-element.33.refs_1_.refs_2_, bf16[576,9216]{1,0:T(8,128)(2,1)} %get-tuple-element.33.refs_1_.refs_2_, ...), custom_call_target="tpu_custom_call", output_to_operand_aliasing={{0}: (15, {}), {1}: (16, {})} | custom-call | flops 8153726976 | bytes 12681216 | tf_op jit(solution)/shard_map/add_products/pallas_call | solution.py:228
  179.1 0.8 copy-done.4
  179.9 0.2 copy-done.5
  180.0 10.0 %add_products.9 = (f32[576,512]{1,0:T(8,128)}, f32[576,512]{1,0:T(8,128)}, bf16[576,512]{1,0:T(8,128)(2,1)}, bf16[576,512]{1,0:T(8,128)(2,1)}, f32[3,2,512]{2,1,0:T(2,128)}) custom-call(s32[2]{0:T(128)} %pad_add_fusion.refs_0_, bf16[576,9216]{1,0:T(8,128)(2,1)} %get-tuple-element.33.refs_1_.refs_2_, ...), custom_call_target="tpu_custom_call", output_to_operand_aliasing={{0}: (8, {}), {1}: (9, {})} | custom-call | flops 4076863488 | bytes 8699904 | tf_op jit(solution)/shard_map/add_products/pallas_call | solution.py:228
  190.0 0.7 reshape.192
  190.7 21.3 %all-gather = f32[16,6,512]{2,1,0:T(8,128)S(1)} all-gather(f32[1,6,512]{2,1,0:T(8,128)S(1)} %reshape.192), channel_id=1, replica_groups=mesh['groups'=2,'prow'=16] {'prow'}, dimensions={0}, use_global_device_ids=true | all-gather | bytes 208896 | tf_op jit(solution)/shard_map/all_gather | solution.py:322
  212.0 0.7 reshape.193
  (79 shorter events, 0.6 us)
Async XLA Ops:
  0.6 8.9 %collective-permute-start.28 = (bf16[576,512]{1,0:T(8,128)(2,1)}, bf16[576,512]{1,0:T(8,128)(2,1)S(1)}, u32[]{:S(2)}, u32[]{:S(2)}) collective-permute-start(bf16[576,512]{1,0:T(8,128)(2,1)} %refs_10_.1), channel_id=1, source_target_pairs={{0,1},{1,0},{2,3},{3,2},{4,5},{5,4},{6,7},{7,6},{8,9},{9,8},{10,11... | collective-permute-start | bytes 1769480 | tf_op jit(solution)/shard_map/ppermute | solution.py:269
  1.1 17.0 %collective-permute-start = (bf16[576,512]{1,0:T(8,128)(2,1)}, bf16[576,512]{1,0:T(8,128)(2,1)S(1)}, u32[]{:S(2)}, u32[]{:S(2)}) collective-permute-start(bf16[576,512]{1,0:T(8,128)(2,1)} %refs_10_.1), channel_id=1, source_target_pairs={{0,4},{1,5},{2,0},{3,1},{4,8},{5,9},{6,2},{7,3},{8,12},{9,13},{10,... | collective-permute-start | bytes 1769480 | tf_op jit(solution)/shard_map/ppermute | solution.py:269
  3.8 28.1 %collective-permute-start.29 = (bf16[576,512]{1,0:T(8,128)(2,1)}, bf16[576,512]{1,0:T(8,128)(2,1)S(1)}, u32[]{:S(2)}, u32[]{:S(2)}) collective-permute-start(bf16[576,512]{1,0:T(8,128)(2,1)} %refs_11_.1), channel_id=1, source_target_pairs={{0,1},{1,0},{2,3},{3,2},{4,5},{5,4},{6,7},{7,6},{8,9},{9,8},{10,11... | collective-permute-start | bytes 1769480 | tf_op jit(solution)/shard_map/ppermute | solution.py:269
  4.0 26.6 %collective-permute-start.11 = (bf16[576,512]{1,0:T(8,128)(2,1)}, bf16[576,512]{1,0:T(8,128)(2,1)S(1)}, u32[]{:S(2)}, u32[]{:S(2)}) collective-permute-start(bf16[576,512]{1,0:T(8,128)(2,1)} %refs_11_.1), channel_id=1, source_target_pairs={{0,4},{1,5},{2,0},{3,1},{4,8},{5,9},{6,2},{7,3},{8,12},{9,13},{10,... | collective-permute-start | bytes 1769480 | tf_op jit(solution)/shard_map/ppermute | solution.py:269
  5.5 28.2 %collective-permute-start.15 = (bf16[576,512]{1,0:T(8,128)(2,1)}, bf16[576,512]{1,0:T(8,128)(2,1)}, u32[]{:S(2)}, u32[]{:S(2)}) collective-permute-start(bf16[576,512]{1,0:T(8,128)(2,1)} %refs_10_.1), channel_id=1, source_target_pairs={{4,0},{5,1},{0,2},{1,3},{8,4},{9,5},{2,6},{3,7},{12,8},{13,9},{6,1... | collective-permute-start | bytes 1769480 | tf_op jit(solution)/shard_map/ppermute | solution.py:269
  9.5 71.5 %copy-start = (bf16[576,512]{1,0:T(8,128)(2,1)}, bf16[576,512]{1,0:T(8,128)(2,1)S(1)}, u32[]{:S(2)}) copy-start(bf16[576,512]{1,0:T(8,128)(2,1)S(1)} %collective-permute-done.28.refs_5_) | copy-start | bytes 1769476
  9.5 25.8 %collective-permute-start.5 = (bf16[576,512]{1,0:T(8,128)(2,1)}, bf16[576,512]{1,0:T(8,128)(2,1)}, u32[]{:S(2)}, u32[]{:S(2)}) collective-permute-start(bf16[576,512]{1,0:T(8,128)(2,1)} %refs_11_.1), channel_id=1, source_target_pairs={{4,0},{5,1},{0,2},{1,3},{8,4},{9,5},{2,6},{3,7},{12,8},{13,9},{6,1... | collective-permute-start | bytes 1769480 | tf_op jit(solution)/shard_map/ppermute | solution.py:269
  18.1 62.9 %copy-start.6 = (bf16[576,512]{1,0:T(8,128)(2,1)}, bf16[576,512]{1,0:T(8,128)(2,1)S(1)}, u32[]{:S(2)}) copy-start(bf16[576,512]{1,0:T(8,128)(2,1)S(1)} %collective-permute-done.refs_7_) | copy-start | bytes 1769476
  18.1 17.2 %collective-permute-start.24 = (bf16[576,512]{1,0:T(8,128)(2,1)S(1)}, bf16[576,512]{1,0:T(8,128)(2,1)}, u32[]{:S(2)}, u32[]{:S(2)}) collective-permute-start(bf16[576,512]{1,0:T(8,128)(2,1)S(1)} %collective-permute-done.refs_7_), channel_id=1, source_target_pairs={{0,1},{1,0},{2,3},{3,2},{4,5},{5,4},{6,7},{7,6},{8,9},{9,8},{10,11... | collective-permute-start | bytes 1769480 | tf_op jit(solution)/shard_map/ppermute | solution.py:269
  30.5 50.5 %copy-start.7 = (bf16[576,512]{1,0:T(8,128)(2,1)}, bf16[576,512]{1,0:T(8,128)(2,1)S(1)}, u32[]{:S(2)}) copy-start(bf16[576,512]{1,0:T(8,128)(2,1)S(1)} %collective-permute-done.11.refs_9_) | copy-start | bytes 1769476
  30.5 5.4 %collective-permute-start.25 = (bf16[576,512]{1,0:T(8,128)(2,1)S(1)}, bf16[576,512]{1,0:T(8,128)(2,1)}, u32[]{:S(2)}, u32[]{:S(2)}) collective-permute-start(bf16[576,512]{1,0:T(8,128)(2,1)S(1)} %collective-permute-done.11.refs_9_), channel_id=1, source_target_pairs={{0,1},{1,0},{2,3},{3,2},{4,5},{5,4},{6,7},{7,6},{8,9},{9,8},{10,11... | collective-permute-start | bytes 1769480 | tf_op jit(solution)/shard_map/ppermute | solution.py:269
  31.9 49.1 %copy-start.1 = (bf16[576,512]{1,0:T(8,128)(2,1)}, bf16[576,512]{1,0:T(8,128)(2,1)S(1)}, u32[]{:S(2)}) copy-start(bf16[576,512]{1,0:T(8,128)(2,1)S(1)} %collective-permute-done.29.refs_7_) | copy-start | bytes 1769476
  31.9 69.7 %collective-permute-start.1 = (bf16[576,512]{1,0:T(8,128)(2,1)S(1)}, bf16[576,512]{1,0:T(8,128)(2,1)}, u32[]{:S(2)}, u32[]{:S(2)}) collective-permute-start(bf16[576,512]{1,0:T(8,128)(2,1)S(1)} %collective-permute-done.refs_7_), channel_id=1, source_target_pairs={{0,4},{1,5},{2,0},{3,1},{4,8},{5,9},{6,2},{7,3},{8,12},{9,13},{10,... | collective-permute-start | bytes 1769480 | tf_op jit(solution)/shard_map/ppermute | solution.py:269
  33.8 69.6 %collective-permute-start.12 = (bf16[576,512]{1,0:T(8,128)(2,1)S(1)}, bf16[576,512]{1,0:T(8,128)(2,1)}, u32[]{:S(2)}, u32[]{:S(2)}) collective-permute-start(bf16[576,512]{1,0:T(8,128)(2,1)S(1)} %collective-permute-done.11.refs_9_), channel_id=1, source_target_pairs={{0,4},{1,5},{2,0},{3,1},{4,8},{5,9},{6,2},{7,3},{8,12},{9,13},{10,... | collective-permute-start | bytes 1769480 | tf_op jit(solution)/shard_map/ppermute | solution.py:269
  35.4 65.9 %collective-permute-start.26 = (bf16[576,512]{1,0:T(8,128)(2,1)}, bf16[576,512]{1,0:T(8,128)(2,1)}, u32[]{:S(2)}, u32[]{:S(2)}) collective-permute-start(bf16[576,512]{1,0:T(8,128)(2,1)} %collective-permute-done.15.refs_11_), channel_id=1, source_target_pairs={{0,1},{1,0},{2,3},{3,2},{4,5},{5,4},{6,7},{7,6},{8,9},{9,8},{10,11... | collective-permute-start | bytes 1769480 | tf_op jit(solution)/shard_map/ppermute | solution.py:269
  35.4 68.2 %collective-permute-start.16 = (bf16[576,512]{1,0:T(8,128)(2,1)}, bf16[576,512]{1,0:T(8,128)(2,1)}, u32[]{:S(2)}, u32[]{:S(2)}) collective-permute-start(bf16[576,512]{1,0:T(8,128)(2,1)} %collective-permute-done.15.refs_11_), channel_id=1, source_target_pairs={{4,0},{5,1},{0,2},{1,3},{8,4},{9,5},{2,6},{3,7},{12,8},{13,9},{6,1... | collective-permute-start | bytes 1769480 | tf_op jit(solution)/shard_map/ppermute | solution.py:269
  35.9 65.8 %collective-permute-start.27 = (bf16[576,512]{1,0:T(8,128)(2,1)}, bf16[576,512]{1,0:T(8,128)(2,1)}, u32[]{:S(2)}, u32[]{:S(2)}) collective-permute-start(bf16[576,512]{1,0:T(8,128)(2,1)} %collective-permute-done.5.refs_13_), channel_id=1, source_target_pairs={{0,1},{1,0},{2,3},{3,2},{4,5},{5,4},{6,7},{7,6},{8,9},{9,8},{10,11... | collective-permute-start | bytes 1769480 | tf_op jit(solution)/shard_map/ppermute | solution.py:269
  101.2 15.8 %collective-permute-start.6 = (bf16[576,512]{1,0:T(8,128)(2,1)}, bf16[576,512]{1,0:T(8,128)(2,1)S(1)}, u32[]{:S(2)}, u32[]{:S(2)}) collective-permute-start(bf16[576,512]{1,0:T(8,128)(2,1)} %collective-permute-done.5.refs_13_), channel_id=1, source_target_pairs={{4,0},{5,1},{0,2},{1,3},{8,4},{9,5},{2,6},{3,7},{12,8},{13,9},{6,1... | collective-permute-start | bytes 1769480 | tf_op jit(solution)/shard_map/ppermute | solution.py:269
  101.6 15.4 %collective-permute-start.20 = (bf16[576,512]{1,0:T(8,128)(2,1)}, bf16[576,512]{1,0:T(8,128)(2,1)S(1)}, u32[]{:S(2)}, u32[]{:S(2)}) collective-permute-start(bf16[576,512]{1,0:T(8,128)(2,1)} %collective-permute-done.1.refs_7_), channel_id=1, source_target_pairs={{0,1},{1,0},{2,3},{3,2},{4,5},{5,4},{6,7},{7,6},{8,9},{9,8},{10,11... | collective-permute-start | bytes 1769480 | tf_op jit(solution)/shard_map/ppermute | solution.py:269
  101.7 17.8 %collective-permute-start.2 = (bf16[576,512]{1,0:T(8,128)(2,1)}, bf16[576,512]{1,0:T(8,128)(2,1)S(1)}, u32[]{:S(2)}, u32[]{:S(2)}) collective-permute-start(bf16[576,512]{1,0:T(8,128)(2,1)} %collective-permute-done.1.refs_7_), channel_id=1, source_target_pairs={{0,4},{1,5},{2,0},{3,1},{4,8},{5,9},{6,2},{7,3},{8,12},{9,13},{10,... | collective-permute-start | bytes 1769480 | tf_op jit(solution)/shard_map/ppermute | solution.py:269
  103.3 14.0 %collective-permute-start.21 = (bf16[576,512]{1,0:T(8,128)(2,1)}, bf16[576,512]{1,0:T(8,128)(2,1)S(1)}, u32[]{:S(2)}, u32[]{:S(2)}) collective-permute-start(bf16[576,512]{1,0:T(8,128)(2,1)} %collective-permute-done.12.refs_9_), channel_id=1, source_target_pairs={{0,1},{1,0},{2,3},{3,2},{4,5},{5,4},{6,7},{7,6},{8,9},{9,8},{10,11... | collective-permute-start | bytes 1769480 | tf_op jit(solution)/shard_map/ppermute | solution.py:269
  103.5 15.6 %collective-permute-start.22 = (bf16[576,512]{1,0:T(8,128)(2,1)}, bf16[576,512]{1,0:T(8,128)(2,1)S(1)}, u32[]{:S(2)}, u32[]{:S(2)}) collective-permute-start(bf16[576,512]{1,0:T(8,128)(2,1)} %collective-permute-done.16.refs_11_), channel_id=1, source_target_pairs={{0,1},{1,0},{2,3},{3,2},{4,5},{5,4},{6,7},{7,6},{8,9},{9,8},{10,11... | collective-permute-start | bytes 1769480 | tf_op jit(solution)/shard_map/ppermute | solution.py:269
  117.0 17.8 %copy-start.9 = (bf16[576,512]{1,0:T(8,128)(2,1)}, bf16[576,512]{1,0:T(8,128)(2,1)S(1)}, u32[]{:S(2)}) copy-start(bf16[576,512]{1,0:T(8,128)(2,1)S(1)} %collective-permute-done.6.refs_13_) | copy-start | bytes 1769476
  117.0 17.8 %collective-permute-start.23 = (bf16[576,512]{1,0:T(8,128)(2,1)S(1)}, bf16[576,512]{1,0:T(8,128)(2,1)S(1)}, u32[]{:S(2)}, u32[]{:S(2)}) collective-permute-start(bf16[576,512]{1,0:T(8,128)(2,1)S(1)} %collective-permute-done.6.refs_13_), channel_id=1, source_target_pairs={{0,1},{1,0},{2,3},{3,2},{4,5},{5,4},{6,7},{7,6},{8,9},{9,8},{10,11... | collective-permute-start | bytes 1769480 | tf_op jit(solution)/shard_map/ppermute | solution.py:269
  117.0 17.8 %copy-start.10 = (bf16[576,512]{1,0:T(8,128)(2,1)}, bf16[576,512]{1,0:T(8,128)(2,1)S(1)}, u32[]{:S(2)}) copy-start(bf16[576,512]{1,0:T(8,128)(2,1)S(1)} %collective-permute-done.20.refs_8_) | copy-start | bytes 1769476
  117.0 19.7 %collective-permute-start.7 = (bf16[576,512]{1,0:T(8,128)(2,1)S(1)}, bf16[576,512]{1,0:T(8,128)(2,1)S(1)}, u32[]{:S(2)}, u32[]{:S(2)}) collective-permute-start(bf16[576,512]{1,0:T(8,128)(2,1)S(1)} %collective-permute-done.6.refs_13_), channel_id=1, source_target_pairs={{4,0},{5,1},{0,2},{1,3},{8,4},{9,5},{2,6},{3,7},{12,8},{13,9},{6,1... | collective-permute-start | bytes 1769480 | tf_op jit(solution)/shard_map/ppermute | solution.py:269
  117.4 17.4 %copy-start.11 = (bf16[576,512]{1,0:T(8,128)(2,1)}, bf16[576,512]{1,0:T(8,128)(2,1)S(1)}, u32[]{:S(2)}) copy-start(bf16[576,512]{1,0:T(8,128)(2,1)S(1)} %collective-permute-done.21.refs_10_) | copy-start | bytes 1769476
  117.4 19.6 %collective-permute-start.13 = (bf16[576,512]{1,0:T(8,128)(2,1)}, bf16[576,512]{1,0:T(8,128)(2,1)S(1)}, u32[]{:S(2)}, u32[]{:S(2)}) collective-permute-start(bf16[576,512]{1,0:T(8,128)(2,1)} %collective-permute-done.12.refs_9_), channel_id=1, source_target_pairs={{0,4},{1,5},{2,0},{3,1},{4,8},{5,9},{6,2},{7,3},{8,12},{9,13},{10,... | collective-permute-start | bytes 1769480 | tf_op jit(solution)/shard_map/ppermute | solution.py:269
  119.1 15.7 %copy-start.13 = (bf16[576,512]{1,0:T(8,128)(2,1)}, bf16[576,512]{1,0:T(8,128)(2,1)S(1)}, u32[]{:S(2)}) copy-start(bf16[576,512]{1,0:T(8,128)(2,1)S(1)} %collective-permute-done.22.refs_12_) | copy-start | bytes 1769476
  119.1 26.7 %collective-permute-start.17 = (bf16[576,512]{1,0:T(8,128)(2,1)}, bf16[576,512]{1,0:T(8,128)(2,1)S(1)}, u32[]{:S(2)}, u32[]{:S(2)}) collective-permute-start(bf16[576,512]{1,0:T(8,128)(2,1)} %collective-permute-done.16.refs_11_), channel_id=1, source_target_pairs={{4,0},{5,1},{0,2},{1,3},{8,4},{9,5},{2,6},{3,7},{12,8},{13,9},{6,1... | collective-permute-start | bytes 1769480 | tf_op jit(solution)/shard_map/ppermute | solution.py:269
  119.4 15.4 %copy-start.8 = (bf16[576,512]{1,0:T(8,128)(2,1)}, bf16[576,512]{1,0:T(8,128)(2,1)S(1)}, u32[]{:S(2)}) copy-start(bf16[576,512]{1,0:T(8,128)(2,1)S(1)} %collective-permute-done.2.refs_7_) | copy-start | bytes 1769476
  119.4 26.4 %collective-permute-start.10 = (bf16[576,512]{1,0:T(8,128)(2,1)S(1)}, bf16[576,512]{1,0:T(8,128)(2,1)S(1)}, u32[]{:S(2)}, u32[]{:S(2)}) collective-permute-start(bf16[576,512]{1,0:T(8,128)(2,1)S(1)} %collective-permute-done.2.refs_7_), channel_id=1, source_target_pairs={{0,1},{1,0},{2,3},{3,2},{4,5},{5,4},{6,7},{7,6},{8,9},{9,8},{10,11... | collective-permute-start | bytes 1769480 | tf_op jit(solution)/shard_map/ppermute | solution.py:269
  134.9 11.5 %copy-start.17 = (bf16[576,512]{1,0:T(8,128)(2,1)}, bf16[576,512]{1,0:T(8,128)(2,1)S(1)}, u32[]{:S(2)}) copy-start(bf16[576,512]{1,0:T(8,128)(2,1)S(1)} %collective-permute-done.23.refs_14_) | copy-start | bytes 1769476
  134.9 26.9 %collective-permute-start.3 = (bf16[576,512]{1,0:T(8,128)(2,1)S(1)}, bf16[576,512]{1,0:T(8,128)(2,1)S(1)}, u32[]{:S(2)}, u32[]{:S(2)}) collective-permute-start(bf16[576,512]{1,0:T(8,128)(2,1)S(1)} %collective-permute-done.2.refs_7_), channel_id=1, source_target_pairs={{0,4},{1,5},{2,0},{3,1},{4,8},{5,9},{6,2},{7,3},{8,12},{9,13},{10,... | collective-permute-start | bytes 1769480 | tf_op jit(solution)/shard_map/ppermute | solution.py:269
  136.8 25.0 %copy-start.12 = (bf16[576,512]{1,0:T(8,128)(2,1)}, bf16[576,512]{1,0:T(8,128)(2,1)S(1)}, u32[]{:S(2)}) copy-start(bf16[576,512]{1,0:T(8,128)(2,1)S(1)} %collective-permute-done.7.refs_13_) | copy-start | bytes 1769476
  136.8 25.6 %collective-permute-start.19 = (bf16[576,512]{1,0:T(8,128)(2,1)S(1)}, bf16[576,512]{1,0:T(8,128)(2,1)S(1)}, u32[]{:S(2)}, u32[]{:S(2)}) collective-permute-start(bf16[576,512]{1,0:T(8,128)(2,1)S(1)} %collective-permute-done.7.refs_13_), channel_id=1, source_target_pairs={{0,1},{1,0},{2,3},{3,2},{4,5},{5,4},{6,7},{7,6},{8,9},{9,8},{10,11... | collective-permute-start | bytes 1769480 | tf_op jit(solution)/shard_map/ppermute | solution.py:269
  137.0 24.8 %copy-start.14 = (bf16[576,512]{1,0:T(8,128)(2,1)}, bf16[576,512]{1,0:T(8,128)(2,1)S(1)}, u32[]{:S(2)}) copy-start(bf16[576,512]{1,0:T(8,128)(2,1)S(1)} %collective-permute-done.13.refs_9_) | copy-start | bytes 1769476
  137.0 25.0 %collective-permute-start.8 = (bf16[576,512]{1,0:T(8,128)(2,1)S(1)}, bf16[576,512]{1,0:T(8,128)(2,1)S(1)}, u32[]{:S(2)}, u32[]{:S(2)}) collective-permute-start(bf16[576,512]{1,0:T(8,128)(2,1)S(1)} %collective-permute-done.7.refs_13_), channel_id=1, source_target_pairs={{4,0},{5,1},{0,2},{1,3},{8,4},{9,5},{2,6},{3,7},{12,8},{13,9},{6,1... | collective-permute-start | bytes 1769480 | tf_op jit(solution)/shard_map/ppermute | solution.py:269
  145.9 15.9 %copy-start.15 = (bf16[576,512]{1,0:T(8,128)(2,1)}, bf16[576,512]{1,0:T(8,128)(2,1)S(1)}, u32[]{:S(2)}) copy-start(bf16[576,512]{1,0:T(8,128)(2,1)S(1)} %collective-permute-done.17.refs_11_) | copy-start | bytes 1769476
  145.9 16.5 %collective-permute-start.14 = (bf16[576,512]{1,0:T(8,128)(2,1)S(1)}, bf16[576,512]{1,0:T(8,128)(2,1)S(1)}, u32[]{:S(2)}, u32[]{:S(2)}) collective-permute-start(bf16[576,512]{1,0:T(8,128)(2,1)S(1)} %collective-permute-done.13.refs_9_), channel_id=1, source_target_pairs={{0,1},{1,0},{2,3},{3,2},{4,5},{5,4},{6,7},{7,6},{8,9},{9,8},{10,11... | collective-permute-start | bytes 1769480 | tf_op jit(solution)/shard_map/ppermute | solution.py:269
  145.9 15.9 %copy-start.16 = (bf16[576,512]{1,0:T(8,128)(2,1)}, bf16[576,512]{1,0:T(8,128)(2,1)S(1)}, u32[]{:S(2)}) copy-start(bf16[576,512]{1,0:T(8,128)(2,1)S(1)} %collective-permute-done.10.refs_8_) | copy-start | bytes 1769476
  145.9 16.5 %collective-permute-start.18 = (bf16[576,512]{1,0:T(8,128)(2,1)S(1)}, bf16[576,512]{1,0:T(8,128)(2,1)S(1)}, u32[]{:S(2)}, u32[]{:S(2)}) collective-permute-start(bf16[576,512]{1,0:T(8,128)(2,1)S(1)} %collective-permute-done.17.refs_11_), channel_id=1, source_target_pairs={{0,1},{1,0},{2,3},{3,2},{4,5},{5,4},{6,7},{7,6},{8,9},{9,8},{10,11... | collective-permute-start | bytes 1769480 | tf_op jit(solution)/shard_map/ppermute | solution.py:269
  161.8 17.2 %copy-start.2 = (bf16[576,512]{1,0:T(8,128)(2,1)}, bf16[576,512]{1,0:T(8,128)(2,1)S(1)}, u32[]{:S(2)}) copy-start(bf16[576,512]{1,0:T(8,128)(2,1)S(1)} %collective-permute-done.3.refs_4_) | copy-start | bytes 1769476
  161.8 17.2 %collective-permute-start.4 = (bf16[576,512]{1,0:T(8,128)(2,1)S(1)}, bf16[576,512]{1,0:T(8,128)(2,1)S(1)}, u32[]{:S(2)}, u32[]{:S(2)}) collective-permute-start(bf16[576,512]{1,0:T(8,128)(2,1)S(1)} %collective-permute-done.3.refs_4_), channel_id=1, source_target_pairs={{0,1},{1,0},{2,3},{3,2},{4,5},{5,4},{6,7},{7,6},{8,9},{9,8},{10,11... | collective-permute-start | bytes 1769480 | tf_op jit(solution)/shard_map/ppermute | solution.py:269
  162.0 17.0 %copy-start.3 = (bf16[576,512]{1,0:T(8,128)(2,1)}, bf16[576,512]{1,0:T(8,128)(2,1)S(1)}, u32[]{:S(2)}) copy-start(bf16[576,512]{1,0:T(8,128)(2,1)S(1)} %collective-permute-done.8.refs_6_) | copy-start | bytes 1769476
  162.0 17.1 %collective-permute-start.9 = (bf16[576,512]{1,0:T(8,128)(2,1)S(1)}, bf16[576,512]{1,0:T(8,128)(2,1)S(1)}, u32[]{:S(2)}, u32[]{:S(2)}) collective-permute-start(bf16[576,512]{1,0:T(8,128)(2,1)S(1)} %collective-permute-done.8.refs_6_), channel_id=1, source_target_pairs={{0,1},{1,0},{2,3},{3,2},{4,5},{5,4},{6,7},{7,6},{8,9},{9,8},{10,11... | collective-permute-start | bytes 1769480 | tf_op jit(solution)/shard_map/ppermute | solution.py:269
  162.4 0.9 copy-start.18
  162.4 1.0 copy-start.19
  162.4 1.2 copy-start.20
  179.0 0.8 copy-start.4
  179.0 1.0 copy-start.5

commit v2 on v0

--- a/solution.py
+++ b/solution.py
@@ -1,9 +1,14 @@
+import functools
 import math
 
 import jax
 import jax.numpy as jnp
 from jax import lax
+from jax.experimental import pallas as pl
+from jax.experimental.pallas import tpu as pltpu
 from jax.sharding import PartitionSpec as P
+
+MIB = 1 << 20
 
 
 def swap_orbitals(block, orbitals):
@@ -19,7 +24,7 @@
     return jnp.dot(left, right, preferred_element_type=jnp.float32)
 
 
-def per_device(green_same, green_opp, interaction, pattern, occupation, hopping):
+def plain_form(green_same, green_opp, interaction, pattern, occupation, hopping):
     rows, width = green_same.shape
     orbitals = hopping.shape[0]
     pairs = orbitals * orbitals
@@ -43,31 +48,18 @@
     )
     kernel_direct = (polar_terms + pair_hopping).astype(jnp.bfloat16).reshape(rows, pairs)
     kernel_polar = polar_terms.astype(jnp.bfloat16).reshape(rows, pairs)
-    ladder_terms = (screened * ladder_factor[None]).astype(jnp.bfloat16)
-    kernel_ladder = ladder_terms.reshape(rows, pairs)
-    column_same, column_opp = (
-        lax.all_to_all(green_same, "prow", split_axis=1, concat_axis=0, tiled=True),
-        lax.all_to_all(green_opp, "prow", split_axis=1, concat_axis=0, tiled=True),
-    )
-    flipped_same = swap_orbitals(column_same, orbitals)
-    flipped_opp = swap_orbitals(column_opp, orbitals)
-    swapped_same, swapped_opp = (
-        lax.all_to_all(flipped_same, "prow", split_axis=0, concat_axis=1, tiled=True),
-        lax.all_to_all(flipped_opp, "prow", split_axis=0, concat_axis=1, tiled=True),
-    )
+    kernel_ladder = (screened * ladder_factor[None]).astype(jnp.bfloat16).reshape(rows, pairs)
     same_piece = lax.all_gather(green_same, "prow", axis=0, tiled=True)
     opp_piece = lax.all_gather(green_opp, "prow", axis=0, tiled=True)
-    swap_same = lax.all_gather(swapped_same, "prow", axis=0, tiled=True)
-    swap_opp = lax.all_gather(swapped_opp, "prow", axis=0, tiled=True)
     new_same = (
         product(kernel_direct, same_piece)
         + product(kernel_polar, opp_piece)
-        + product(kernel_ladder, swap_same)
+        + product(kernel_ladder, swap_orbitals(same_piece, orbitals))
     )
     new_opp = (
         product(kernel_direct, opp_piece)
         + product(kernel_polar, same_piece)
-        + product(kernel_ladder, swap_opp)
+        + product(kernel_ladder, swap_orbitals(opp_piece, orbitals))
     )
     next_same = (green_same.astype(jnp.float32) + 0.5 * new_same).astype(jnp.bfloat16)
     next_opp = (green_opp.astype(jnp.float32) + 0.5 * new_opp).astype(jnp.bfloat16)
@@ -76,6 +68,338 @@
     )
     collision = lax.psum(share, "prow")
     return (new_same, new_opp, next_same, next_opp, collision)
+
+
+def build_body(orbitals, low, high, pairs, *refs):
+    place_ref, inter_ref, pat_ref, hop_ref, occ_ref, pat4_ref, hop4_ref, eye4_ref, occ4_ref = refs[:9]
+    mixed_ref, polar_ref, turned_ref = refs[-3:]
+    span = 4 * orbitals
+    tiles = pairs // span
+    start = place_ref[0]
+    strips = range(0, high - low, 128)
+
+    @pl.loop(0, tiles)
+    def _(tile):
+        cols = pl.ds(pl.multiple_of(tile * span, 128), span)
+        for strip in strips:
+            size = min(128, high - low - strip)
+            piece = inter_ref[strip : strip + size, cols].T.astype(jnp.float32)
+            at = strip // 128 * pairs + tile * span
+            turned_ref[pl.ds(pl.multiple_of(at, 128), span), :size] = piece
+
+    group = lax.broadcasted_iota(jnp.int32, (1, span), 1) // orbitals
+    occ4 = occ4_ref[...]
+
+    @pl.loop(0, tiles)
+    def _(tile):
+        cols = pl.ds(pl.multiple_of(tile * span, 128), span)
+
+        def spread(values):
+            row = jnp.where(group == 0, values[0], values[1])
+            return jnp.where(group == 2, values[2], jnp.where(group == 3, values[3], row))
+
+        inner = [4 * tile + m for m in range(4)]
+        occ = spread([occ_ref[i] for i in inner])
+        polar_factor = occ - occ4
+        ladder_factor = (1.0 - occ4) - occ
+        facts = {}
+        for first in range(low // orbitals, -(-high // orbitals)):
+            here = start + first
+            linked = spread([pat_ref[here, i].astype(jnp.float32) for i in inner])
+            hop_row = spread([hop_ref[here, i] for i in inner])
+            unit = (group + 4 * tile == here).astype(jnp.float32)
+            linked4 = pat4_ref[pl.ds(here, 1), :]
+            facts[first] = (linked * polar_factor, linked4 * ladder_factor, hop_row, unit)
+        for strip in strips:
+            size = min(128, high - low - strip)
+            pieces = [
+                turned_ref[
+                    pl.ds(strip // 128 * pairs + 4 * tile + m, orbitals, stride=orbitals), :
+                ]
+                for m in range(4)
+            ]
+            block = jnp.concatenate(pieces, axis=0).astype(jnp.bfloat16).T[:size]
+            row = low + strip
+            while row < low + strip + size:
+                first, second = row // orbitals, row % orbitals
+                count = min(orbitals - second, low + strip + size - row)
+                there = slice(row - low, row - low + count)
+                polar_row, ladder_row, hop_row, unit = facts[first]
+                polar = inter_ref[there, cols].astype(jnp.float32) * polar_row
+                hop = (
+                    hop_row * eye4_ref[second : second + count]
+                    + unit * hop4_ref[second : second + count]
+                )
+                part = block[row - low - strip : row - low - strip + count]
+                ladder = (part.astype(jnp.float32) * ladder_row).astype(jnp.bfloat16)
+                direct = (polar + hop).astype(jnp.bfloat16).astype(jnp.float32)
+                held = polar.astype(jnp.bfloat16)
+                polar_ref[there, cols] = held
+                mixed_ref[there, cols] = (
+                    direct - held.astype(jnp.float32) + ladder.astype(jnp.float32)
+                ).astype(jnp.bfloat16)
+                row += count
+
+
+def build_rows(place, interaction, smalls, made, low, high):
+    rows, pairs = interaction.shape
+    pattern, hopping, occupation = smalls[:3]
+    orbitals = hopping.shape[0]
+    height = high - low
+    block = low // height
+    shape = jax.ShapeDtypeStruct((rows, pairs), jnp.bfloat16)
+    wide = pl.BlockSpec((height, pairs), lambda g, p: (block, 0))
+    smem = pl.BlockSpec(memory_space=pltpu.SMEM)
+    row4 = pl.BlockSpec((1, 4 * orbitals), lambda g, p: (0, 0))
+    small = pl.BlockSpec((orbitals, 4 * orbitals), lambda g, p: (0, 0))
+    return pl.pallas_call(
+        functools.partial(build_body, orbitals, low, high, pairs),
+        grid_spec=pltpu.PrefetchScalarGridSpec(
+            num_scalar_prefetch=1,
+            grid=(1,),
+            in_specs=[wide, smem, smem, smem, small, small, small, row4]
+            + [pl.BlockSpec(memory_space=pl.ANY)] * len(made),
+            out_specs=[wide] * 2,
+            scratch_shapes=[pltpu.VMEM((-(-height // 128) * pairs, 128), jnp.float32)],
+        ),
+        out_shape=[shape] * 2,
+        input_output_aliases={9 + n: n for n in range(len(made))},
+        compiler_params=pltpu.CompilerParams(vmem_limit_bytes=44 * MIB),
+        cost_estimate=pl.CostEstimate(
+            flops=20 * height * pairs, bytes_accessed=6 * height * pairs, transcendentals=0
+        ),
+        name="build_rows",
+    )(place, interaction, *smalls, *made)
+
+
+def step_body(chips, opening, closing, orbitals, scale, *refs):
+    place_ref = refs[0]
+    refs = list(refs[1:])
+    mixed_ref, polar_ref = refs.pop(0), refs.pop(0)
+    greens = [[[refs.pop(0) for _ in range(2)] for _ in range(2)] for _ in range(chips)]
+    sums = [] if opening else [refs.pop(0) for _ in range(3)]
+    olds = [refs.pop(0) for _ in range(2)] if closing else []
+    held = refs.pop()
+    totals = [refs.pop() for _ in range(3)][::-1] if closing else refs[:3]
+    core = place_ref[0]
+    rows = greens[0][0][0].shape[0]
+    now = pl.program_id(1)
+
+    for chip in range(chips):
+
+        @pl.when(now == chip)
+        def _():
+            for which in range(2):
+                lane = core if which == 0 else 1 - core
+                there = pl.ds(pl.multiple_of(lane * rows, 64), rows)
+                same, opp = greens[chip][0][which][...], greens[chip][1][which][...]
+                held[0, there, :] = same
+                held[1, there, :] = opp
+                both = same.astype(jnp.float32) + opp.astype(jnp.float32)
+                held[2, there, :] = both.astype(jnp.bfloat16)
+
+    @pl.when(now == 0)
+    def _():
+        for n in range(3):
+            if opening:
+                totals[n][...] = jnp.zeros_like(totals[n])
+            else:
+                totals[n][...] = sums[n][...]
+
+    totals[0][...] += product(mixed_ref[...], held[0])
+    totals[1][...] += product(mixed_ref[...], held[1])
+    totals[2][...] += product(polar_ref[...], held[2])
+    if closing:
+
+        @pl.when(now == chips - 1)
+        def _():
+            for first in range(rows // orbitals):
+                part = slice(first * orbitals, (first + 1) * orbitals)
+                shared = totals[2][part, :]
+                both = None
+                for kind in range(2):
+                    slope = totals[kind][part, :] + shared
+                    old = olds[kind][part, :].astype(jnp.float32)
+                    refs[kind][part, :] = slope
+                    refs[2 + kind][part, :] = (old + 0.5 * slope).astype(jnp.bfloat16)
+                    both = slope if both is None else both + slope
+                refs[4][first : first + 1, :] = jnp.sum(both, axis=0, keepdims=True) * scale
+
+
+def step(place, mats, greens, sums, olds, orbitals):
+    chips = len(greens)
+    opening, closing = not sums, bool(olds)
+    rows, width = greens[0][0][0].shape
+    wide = 2 * rows
+    span = min(width, 256)
+    tall = pl.BlockSpec((rows, span), lambda n, g, p: (0, n))
+    mat = pl.BlockSpec((rows, wide), lambda n, g, p: (0, p[1 + g]))
+    wide_sum = jax.ShapeDtypeStruct((rows, width), jnp.float32)
+    scratch = [pltpu.VMEM((3, wide, span), jnp.bfloat16)]
+    if closing:
+        out_specs = [tall] * 4 + [pl.BlockSpec((rows // orbitals, span), lambda n, g, p: (0, n))]
+        out_shape = [wide_sum] * 2 + [jax.ShapeDtypeStruct((rows, width), jnp.bfloat16)] * 2
+        out_shape += [jax.ShapeDtypeStruct((rows // orbitals, width), jnp.float32)]
+        scratch = [pltpu.VMEM((rows, span), jnp.float32)] * 3 + scratch
+    else:
+        out_specs, out_shape = [tall] * 3, [wide_sum] * 3
+    operands = list(mats)
+    operands += [greens[c][k][w] for c in range(chips) for k in range(2) for w in range(2)]
+    in_specs = [mat] * 2 + [tall] * (4 * chips)
+    aliases = {}
+    if not opening:
+        if not closing:
+            aliases = {1 + len(operands) + n: n for n in range(3)}
+        operands += list(sums)
+        in_specs += [tall] * 3
+    if closing:
+        operands += list(olds)
+        in_specs += [tall] * 2
+    return pl.pallas_call(
+        functools.partial(
+            step_body, chips, opening, closing, orbitals, 1.0 / math.sqrt(orbitals)
+        ),
+        grid_spec=pltpu.PrefetchScalarGridSpec(
+            num_scalar_prefetch=1,
+            grid=(width // span, chips),
+            in_specs=in_specs,
+            out_specs=out_specs,
+            scratch_shapes=scratch,
+        ),
+        out_shape=out_shape,
+        input_output_aliases=aliases,
+        compiler_params=pltpu.CompilerParams(vmem_limit_bytes=36 * MIB),
+        cost_estimate=pl.CostEstimate(
+            flops=6 * chips * rows * wide * width,
+            bytes_accessed=8 * chips * rows * wide + 24 * rows * width,
+            transcendentals=0,
+        ),
+        name="add_products",
+    )(place, *operands)
+
+
+def spread_blocks(block, index, stride, devices):
+    blocks = [block]
+    for other in range(1, 4):
+        pairs_of = [(d, d ^ (other * stride)) for d in range(devices)]
+        blocks.append(lax.ppermute(block, "prow", pairs_of))
+    part = index // stride % 4
+    low, high = part % 2 == 1, part // 2 == 1
+    b = [jnp.where(low, blocks[n ^ 1], blocks[n]) for n in range(4)]
+    b = [jnp.where(high, b[n ^ 2], b[n]) for n in range(4)]
+    return jnp.concatenate(b, axis=0)
+
+
+def after(value, *others):
+    return lax.optimization_barrier((value, *others))[0]
+
+
+def ring_form(green_same, green_opp, interaction, pattern, occupation, hopping):
+    rows, width = green_same.shape
+    orbitals = hopping.shape[0]
+    pairs = orbitals * orbitals
+    devices = pairs // rows
+    chips = devices // 2
+    me = lax.axis_index("prow")
+    core, chip = me % 2, me // 2
+    order = list(range(0, chips, 2)) + list(range(chips - 1, 0, -2))
+    spot = [order.index(c) for c in range(chips)]
+    ahead = [order[(spot[c] + 1) % chips] for c in range(chips)]
+    right = [(2 * c + k, 2 * ahead[c] + k) for c in range(chips) for k in range(2)]
+    left = [(b, a) for a, b in right]
+    across = [(d, d ^ 1) for d in range(devices)]
+    half = chips // 2
+    table = []
+    for c in range(chips):
+        line = [c]
+        for far in range(1, half + 1):
+            line += [order[(spot[c] - far) % chips], order[(spot[c] + far) % chips]]
+        table.append(line)
+    line = lax.dynamic_index_in_dim(jnp.array(table, jnp.int32), chip, 0, keepdims=False)
+
+    def send(block, pairs_of):
+        return lax.ppermute(block, "prow", pairs_of)
+
+    def both_ways(kind, blocks):
+        return [send(blocks[0], right), send(blocks[1], left)]
+
+    def share(blocks):
+        return [(block, send(block, across)) for block in blocks]
+
+    def place_of(low, high):
+        return jnp.concatenate([core[None].astype(jnp.int32), line[low:high]])
+
+    own = (green_same, green_opp)
+    moving = [both_ways(kind, [own[kind]] * 2) for kind in range(2)]
+    near = [share([own[kind]])[0] for kind in range(2)]
+
+    start = (me * (rows // orbitals)).astype(jnp.int32)[None]
+    smalls = (
+        pattern,
+        hopping,
+        occupation,
+        jnp.tile(pattern.astype(jnp.float32), (1, 4)),
+        jnp.tile(hopping, (1, 4)),
+        jnp.tile(jnp.eye(orbitals, dtype=jnp.float32), (1, 4)),
+        jnp.tile(occupation, 4)[None],
+    )
+    big = rows // 9 * 4
+    mats = build_rows(start, interaction, smalls, (), 0, big)
+
+    got = [[], []]
+    got[0] = [after(block, mats[0]) for block in moving[0]]
+    moving[0] = both_ways(0, got[0])
+    pair_same = share(got[0])
+    mats = build_rows(after(start, got[0][0]), interaction, smalls, mats, big, 2 * big)
+
+    got[1] = [after(block, mats[0]) for block in moving[1]]
+    moving[1] = both_ways(1, got[1])
+    pair_opp = share(got[1])
+    mats = build_rows(after(start, got[1][0]), interaction, smalls, mats, 2 * big, rows)
+
+    greens = [[near[0], near[1]]] + [[pair_same[n], pair_opp[n]] for n in range(2)]
+    sums = ()
+    for far in range(2, half):
+        got[0] = [after(block, mats[0]) for block in moving[0]]
+        last = far == half - 1
+        if last:
+            moving[0] = [send(got[0][0], right)]
+        else:
+            moving[0] = both_ways(0, got[0])
+        pair_same = share(got[0])
+        low = 0 if far == 2 else 2 * far - 3
+        sums = step(
+            after(place_of(low, 2 * far - 1), got[0][0]), mats, greens, sums, (), orbitals
+        )
+        got[1] = [after(block, sums[0]) for block in moving[1]]
+        if last:
+            moving[1] = [send(got[1][1], left)]
+        else:
+            moving[1] = both_ways(1, got[1])
+        pair_opp = share(got[1])
+        greens = [[pair_same[n], pair_opp[n]] for n in range(2)]
+        mats = [after(mats[0], got[1][0]), mats[1]]
+    low = 2 * half - 3
+    sums = step(place_of(low, low + 2), mats, greens, sums, (), orbitals)
+    far_same = share([after(moving[0][0], sums[0])])[0]
+    far_opp = share([after(moving[1][0], sums[0])])[0]
+    new_same, new_opp, next_same, next_opp, part = step(
+        place_of(low + 2, low + 3), mats, [[far_same, far_opp]], sums, own, orbitals
+    )
+    if devices == 16:
+        collision = spread_blocks(spread_blocks(part, me, 1, devices), me, 4, devices)
+    else:
+        collision = lax.all_gather(part, "prow", axis=0, tiled=True)
+    return (new_same, new_opp, next_same, next_opp, collision)
+
+
+def per_device(green_same, green_opp, interaction, pattern, occupation, hopping):
+    rows = green_same.shape[0]
+    orbitals = hopping.shape[0]
+    devices = orbitals * orbitals // rows
+    fits = rows % orbitals == 0 and rows % 576 == 0 and devices % 4 == 0 and devices >= 12
+    form = ring_form if fits else plain_form
+    return form(green_same, green_opp, interaction, pattern, occupation, hopping)
 
 
 def solution(mesh):

time: 498 us -> 162 us (0.33)
  blocking collectives: 141 us -> 0 us
  waiting for transfers between devices: 175 us -> 39.3 us
  Pallas kernels: 0 us -> 89.2 us
  matrix products: 69.7 us -> 0 us
  other arithmetic: 66 us -> 2.51 us
  starting transfers between devices: 0.38 us -> 25.2 us
  local copies, waits for them, and re-layouts: 27.6 us -> 4.27 us
  between operations: 14.1 us -> 0.88 us
    all_to_all x4 -> x0, blocking collectives: 141 us -> none  [the longest x1 37.4 us: per_device(): lax.all_to_all(green_same, 'prow', split_axis=1, concat_axis=0, tiled=True)]
    pallas_call x0 -> x7, Pallas kernels: none -> 89.2 us  [the longest x3 48.7 us: build_rows(): pl.pallas_call(functools.partial(build_body, orbitals, low, high, pairs),...]
    psum x1 -> x0, waiting for transfers between devices: 88 us -> none  [per_device(): collision = lax.psum(share, 'prow')]
    all_gather x4 -> x0, waiting for transfers between devices: 86 us -> none  [the longest x1 68.9 us: per_device(): swap_same = lax.all_gather(swapped_same, 'prow', axis=0, tiled=True)]
    dot_general x10 -> x0, matrix products: 69.7 us -> none  [the longest x6 67.4 us: product(): return jnp.dot(left, right, preferred_element_type=jnp.float32)]
    convert_element_type x2, other arithmetic: 53.9 us -> 0.81 us  [the longest x1 0.8 us: ring_form(): pattern.astype(jnp.float32)]
    ppermute x0 -> x36, waiting for transfers between devices: none -> 39.3 us  [the longest x30 32.8 us: send(): return lax.ppermute(block, 'prow', pairs_of)]
    ppermute x0 -> x36, starting transfers between devices: none -> 25.2 us  [the longest x30 18.9 us: send(): return lax.ppermute(block, 'prow', pairs_of)]
  transfers between devices with their start and end apart: 5 -> 36, of which waited for: 3 -> 12; matrix products, arithmetic and copies ran while one was open for 29% -> 2% of each run, Pallas kernels for 0% -> 51%
where the time goes in v2:
time: 162 us; the launch traced here: 161 us
  Pallas kernels  89.2 us (55%)
  waiting for transfers between devices  39.3 us (24%)
  starting transfers between devices  25.2 us (16%)
  local copies, waits for them, and re-layouts  4.27 us (3%)
  other arithmetic  2.51 us (2%)
    pallas_call x3, Pallas kernels, build_rows(): pl.pallas_call(functools.partial(build_body, orbitals, low, high, pairs),...  48.7 us
    pallas_call x4, Pallas kernels, step(): pl.pallas_call(functools.partial(step_body, chips, opening, closing, orbi...  40.6 us
    ppermute x30, waiting for transfers between devices, send(): return lax.ppermute(block, 'prow', pairs_of)  32.8 us
    ppermute x30, starting transfers between devices, send(): return lax.ppermute(block, 'prow', pairs_of)  18.9 us
    ppermute x6, waiting for transfers between devices, spread_blocks(): blocks.append(lax.ppermute(block, 'prow', pairs_of))  6.56 us
    ppermute x6, starting transfers between devices, spread_blocks(): blocks.append(lax.ppermute(block, 'prow', pairs_of))  6.31 us
  transfers between devices with their start and end apart: 36, of which 12 were waited for; matrix products, arithmetic and copies ran while one was open for 2% of the time, Pallas kernels for 51%

profile of v2, /device:TPU:0, one launch (start us, length us, event | category | flops | bytes accessed | tf_op | source)
XLA Modules:
  0.0 161.5 jit_solution(17920532284518271111)
XLA Ops:
  0.7 3.1 %collective-permute-start.1 = (bf16[576,512]{1,0:T(8,128)(2,1)}, bf16[576,512]{1,0:T(8,128)(2,1)S(1)}, u32[]{:S(2)}, u32[]{:S(2)}) collective-permute-start(bf16[576,512]{1,0:T(8,128)(2,1)} %refs_10_.1), channel_id=1, source_target_pairs={{0,4},{1,5},{2,0},{3,1},{4,8},{5,9},{6,2},{7,3},{8,12},{9,13},{10,... | collective-permute-start | bytes 1769480 | tf_op jit(solution)/shard_map/ppermute | solution.py:321
  3.7 0.0 collective-permute-start.8
  3.7 2.0 %collective-permute-start = (bf16[576,512]{1,0:T(8,128)(2,1)}, bf16[576,512]{1,0:T(8,128)(2,1)S(1)}, u32[]{:S(2)}, u32[]{:S(2)}) collective-permute-start(bf16[576,512]{1,0:T(8,128)(2,1)} %refs_11_.1), channel_id=1, source_target_pairs={{0,4},{1,5},{2,0},{3,1},{4,8},{5,9},{6,2},{7,3},{8,12},{9,13},{10,... | collective-permute-start | bytes 1769480 | tf_op jit(solution)/shard_map/ppermute | solution.py:321
  5.8 0.0 collective-permute-start.10
  5.8 12.3 %collective-permute-done.1.refs_7_ = bf16[576,512]{1,0:T(8,128)(2,1)S(1)} collective-permute-done((bf16[576,512]{1,0:T(8,128)(2,1)}, bf16[576,512]{1,0:T(8,128)(2,1)S(1)}, u32[]{:S(2)}, u32[]{:S(2)}) %collective-permute-start.1) | collective-permute-done | bytes 589856 | tf_op jit(solution)/shard_map/ppermute | solution.py:321
  18.1 0.8 convert_element_type.14
  18.9 0.1 tile.42.refs_5_
  19.1 0.1 tile.46.refs_7_
  19.3 0.1 tile.44.refs_6_
  19.5 0.1 broadcast_in_dim_tile.3.refs_8_
  19.6 19.0 %build_rows.3 = (bf16[576,9216]{1,0:T(8,128)(2,1)}, bf16[576,9216]{1,0:T(8,128)(2,1)}) custom-call(s32[1]{0:T(128)} %bitcast.2.refs_0_, bf16[576,9216]{1,0:T(8,128)(2,1)} %refs_1_.5, s32[96,96]{1,0:T(8,128)S(1)} %copy-done.4, f32[96,96]{1,0:T(8,128)S(1)} %copy-done.5, f32[96]{0:T(128)S(1)} %copy-done.6, f32[96,384]{1,0:T(8,128)S(1)} %tile.42.refs_5_, ...), custom_call_target="tpu_custom_call" | custom-call | flops 47185920 | bytes 14155776 | tf_op jit(solution)/shard_map/build_rows/pallas_call | solution.py:155
  38.6 2.1 %collective-permute-start.3 = (bf16[576,512]{1,0:T(8,128)(2,1)S(1)}, bf16[576,512]{1,0:T(8,128)(2,1)S(1)}, u32[]{:S(2)}, u32[]{:S(2)}) collective-permute-start(bf16[576,512]{1,0:T(8,128)(2,1)S(1)} %collective-permute-done.1.refs_7_), channel_id=1, source_target_pairs={{0,4},{1,5},{2,0},{3,1},{4,8},{5,9},{6,2},{7,3},{8,12},{9,13},{10,... | collective-permute-start | bytes 1769480 | tf_op jit(solution)/shard_map/ppermute | solution.py:321
  40.7 19.2 %build_rows.4 = (bf16[576,9216]{1,0:T(8,128)(2,1)}, bf16[576,9216]{1,0:T(8,128)(2,1)}) custom-call(s32[1]{0:T(128)} %bitcast.2.refs_0_, bf16[576,9216]{1,0:T(8,128)(2,1)} %refs_1_.5, s32[96,96]{1,0:T(8,128)S(1)} %copy-done.4, f32[96,96]{1,0:T(8,128)S(1)} %copy-done.5, f32[96]{0:T(128)S(1)} %copy-done.6, ...), custom_call_target="tpu_custom_call", output_to_operand_aliasing={{0}: (9, {}), {1}: (10, {})} | custom-call | flops 47185920 | bytes 14155776 | tf_op jit(solution)/shard_map/build_rows/pallas_call | solution.py:155
  59.9 0.2 collective-permute-start.6
  60.1 0.3 collective-permute-start.7
  60.4 0.2 collective-permute-start.11
  60.6 0.3 collective-permute-start.9
  60.9 0.7 constant_dynamic-slice_fusion
  61.6 0.1 collective-permute-start.18
  61.7 0.1 pad_add_fusion.1.refs_0_
  61.8 10.5 %build_rows.5 = (bf16[576,9216]{1,0:T(8,128)(2,1)}, bf16[576,9216]{1,0:T(8,128)(2,1)}) custom-call(s32[1]{0:T(128)} %bitcast.2.refs_0_, bf16[576,9216]{1,0:T(8,128)(2,1)} %refs_1_.5, s32[96,96]{1,0:T(8,128)S(1)} %copy-done.4, f32[96,96]{1,0:T(8,128)S(1)} %copy-done.5, f32[96]{0:T(128)S(1)} %copy-done.6, ...), custom_call_target="tpu_custom_call", output_to_operand_aliasing={{0}: (9, {}), {1}: (10, {})} | custom-call | flops 11796480 | bytes 3538944 | tf_op jit(solution)/shard_map/build_rows/pallas_call | solution.py:155
  72.3 2.0 %collective-permute-start.2 = (bf16[576,512]{1,0:T(8,128)(2,1)S(1)}, bf16[576,512]{1,0:T(8,128)(2,1)S(1)}, u32[]{:S(2)}, u32[]{:S(2)}) collective-permute-start(bf16[576,512]{1,0:T(8,128)(2,1)S(1)} %collective-permute-done.refs_9_), channel_id=1, source_target_pairs={{0,4},{1,5},{2,0},{3,1},{4,8},{5,9},{6,2},{7,3},{8,12},{9,13},{10,... | collective-permute-start | bytes 1769480 | tf_op jit(solution)/shard_map/ppermute | solution.py:321
  74.3 0.0 collective-permute-start.16
  74.3 13.8 %add_products.4 = (f32[576,512]{1,0:T(8,128)S(1)}, f32[576,512]{1,0:T(8,128)S(1)}, f32[576,512]{1,0:T(8,128)S(1)}) custom-call(s32[4]{0:T(128)S(1)} %pad_add_fusion.1.refs_0_, bf16[576,9216]{1,0:T(8,128)(2,1)} %get-tuple-element.70.refs_1_, bf16[576,9216]{1,0:T(8,128)(2,1)} %get-tuple-element.56.refs_2_, bf16[576,512]{1,0:T(8,128)(2,1)S(1)} %copy-done.2, ...), custom_call_target="tpu_custom_call" | custom-call | flops 6115295232 | bytes 23003136 | tf_op jit(solution)/shard_map/add_products/pallas_call | solution.py:258
  88.2 0.1 collective-permute-start.19
  88.2 1.9 %collective-permute-start.13 = (bf16[576,512]{1,0:T(8,128)(2,1)S(1)}, bf16[576,512]{1,0:T(8,128)(2,1)S(1)}, u32[]{:S(2)}, u32[]{:S(2)}) collective-permute-start(bf16[576,512]{1,0:T(8,128)(2,1)S(1)} %collective-permute-done.3.refs_3_), channel_id=1, source_target_pairs={{0,4},{1,5},{2,0},{3,1},{4,8},{5,9},{6,2},{7,3},{8,12},{9,13},{10,... | collective-permute-start | bytes 1769480 | tf_op jit(solution)/shard_map/ppermute | solution.py:321
  90.2 0.2 collective-permute-start.15
  90.3 0.3 collective-permute-start.14
  90.7 0.2 collective-permute-start.17
  90.8 1.2 collective-permute-start.25
  92.1 0.1 slice_bitcast_fusion
  92.1 0.1 pad_add_fusion.2.refs_0_
  92.2 11.8 %collective-permute-done.13.refs_3_ = bf16[576,512]{1,0:T(8,128)(2,1)S(1)} collective-permute-done((bf16[576,512]{1,0:T(8,128)(2,1)S(1)}, bf16[576,512]{1,0:T(8,128)(2,1)S(1)}, u32[]{:S(2)}, u32[]{:S(2)}) %collective-permute-start.13) | collective-permute-done | bytes 589856 | tf_op jit(solution)/shard_map/ppermute | solution.py:321
  104.1 1.7 %collective-permute-start.23 = (bf16[576,512]{1,0:T(8,128)(2,1)S(1)}, bf16[576,512]{1,0:T(8,128)(2,1)S(1)}, u32[]{:S(2)}, u32[]{:S(2)}) collective-permute-start(bf16[576,512]{1,0:T(8,128)(2,1)S(1)} %collective-permute-done.16.refs_7_), channel_id=1, source_target_pairs={{4,0},{5,1},{0,2},{1,3},{8,4},{9,5},{2,6},{3,7},{12,8},{13,9},{6,1... | collective-permute-start | bytes 1769480 | tf_op jit(solution)/shard_map/ppermute | solution.py:321
  105.8 0.3 collective-permute-start.12
  106.1 9.7 %add_products.5 = (f32[576,512]{1,0:T(8,128)S(1)}, f32[576,512]{1,0:T(8,128)S(1)}, f32[576,512]{1,0:T(8,128)S(1)}) custom-call(s32[3]{0:T(128)S(1)} %pad_add_fusion.2.refs_0_, bf16[576,9216]{1,0:T(8,128)(2,1)} %get-tuple-element.70.refs_1_, ...), custom_call_target="tpu_custom_call", output_to_operand_aliasing={{0}: (11, {}), {1}: (12, {}), {2}: (13, {})} | custom-call | flops 4076863488 | bytes 17694720 | tf_op jit(solution)/shard_map/add_products/pallas_call | solution.py:258
  115.8 0.1 collective-permute-start.26
  115.9 3.2 %collective-permute-done.23.refs_7_ = bf16[576,512]{1,0:T(8,128)(2,1)S(1)} collective-permute-done((bf16[576,512]{1,0:T(8,128)(2,1)S(1)}, bf16[576,512]{1,0:T(8,128)(2,1)S(1)}, u32[]{:S(2)}, u32[]{:S(2)}) %collective-permute-start.23) | collective-permute-done | bytes 589856 | tf_op jit(solution)/shard_map/ppermute | solution.py:321
  119.1 1.3 collective-permute-done.12.refs_5_
  120.4 0.5 collective-permute-start.21
  120.9 1.5 collective-permute-start.28
  122.5 0.5 collective-permute-start.20
  123.0 0.1 pad_add_fusion.3.refs_0_
  123.0 0.2 collective-permute-done.21.refs_4_
  123.3 10.0 %add_products.6 = (f32[576,512]{1,0:T(8,128)S(1)}, f32[576,512]{1,0:T(8,128)S(1)}, f32[576,512]{1,0:T(8,128)S(1)}) custom-call(s32[3]{0:T(128)S(1)} %pad_add_fusion.3.refs_0_, bf16[576,9216]{1,0:T(8,128)(2,1)} %get-tuple-element.70.refs_1_, ...), custom_call_target="tpu_custom_call", output_to_operand_aliasing={{0}: (11, {}), {1}: (12, {}), {2}: (13, {})} | custom-call | flops 4076863488 | bytes 17694720 | tf_op jit(solution)/shard_map/add_products/pallas_call | solution.py:258
  133.3 1.0 copy-done
  134.3 1.9 %collective-permute-done.28.refs_5_ = bf16[576,512]{1,0:T(8,128)(2,1)S(1)} collective-permute-done((bf16[576,512]{1,0:T(8,128)(2,1)S(1)}, bf16[576,512]{1,0:T(8,128)(2,1)S(1)}, u32[]{:S(2)}, u32[]{:S(2)}) %collective-permute-start.28) | collective-permute-done | bytes 589856 | tf_op jit(solution)/shard_map/ppermute | solution.py:321
  136.2 1.2 collective-permute-done.20.refs_3_
  137.4 0.6 slice.24
  138.0 0.7 pad_add_fusion.refs_0_
  138.7 0.7 collective-permute-done.27.refs_4_
  139.5 1.3 copy-done.1
  140.7 7.1 %add_products.7 = (f32[576,512]{1,0:T(8,128)}, f32[576,512]{1,0:T(8,128)}, bf16[576,512]{1,0:T(8,128)(2,1)}, bf16[576,512]{1,0:T(8,128)(2,1)}, f32[6,512]{1,0:T(8,128)S(1)}) custom-call(s32[2]{0:T(128)S(1)} %pad_add_fusion.refs_0_, bf16[576,9216]{1,0:T(8,128)(2,1)S(1)} %bitcast.10, bf16[576,9216]{1,0:T(8,128)(2,1)} %get-tuple-element.56.refs_2_, ...), custom_call_target="tpu_custom_call" | custom-call | flops 2038431744 | bytes 12386304 | tf_op jit(solution)/shard_map/add_products/pallas_call | solution.py:258
  147.8 1.4 collective-permute-start.30
  149.2 0.4 collective-permute-start.31
  149.6 0.1 collective-permute-start.32
  149.7 1.3 collective-permute-done.30
  151.0 1.9 %collective-permute-done.31 = f32[6,512]{1,0:T(8,128)S(1)} collective-permute-done((f32[6,512]{1,0:T(8,128)S(1)}, f32[6,512]{1,0:T(8,128)S(1)}, u32[]{:S(2)}, u32[]{:S(2)}) %collective-permute-start.31) | collective-permute-done | bytes 12320 | tf_op jit(solution)/shard_map/ppermute | solution.py:285
  153.0 2.4 %collective-permute-start.33 = (f32[24,512]{1,0:T(8,128)S(1)}, f32[24,512]{1,0:T(8,128)S(1)}, u32[]{:S(2)}, u32[]{:S(2)}) collective-permute-start(f32[24,512]{1,0:T(8,128)S(1)} %pad_maximum_fusion.1), channel_id=1, source_target_pairs={{0,12},{1,13},{2,14},{3,15},{4,8},{5,9},{6,10},{7,11},{8,4},{9,5},... | collective-permute-start | bytes 147464 | tf_op jit(solution)/shard_map/ppermute | solution.py:285
  155.4 0.7 collective-permute-start.34
  156.1 1.4 collective-permute-start.35
  157.4 1.5 collective-permute-done.33
  158.9 1.8 %collective-permute-done.34 = f32[24,512]{1,0:T(8,128)S(1)} collective-permute-done((f32[24,512]{1,0:T(8,128)S(1)}, f32[24,512]{1,0:T(8,128)S(1)}, u32[]{:S(2)}, u32[]{:S(2)}) %collective-permute-start.34) | collective-permute-done | bytes 49184 | tf_op jit(solution)/shard_map/ppermute | solution.py:285
  160.8 0.7 pad_maximum_fusion
  (58 shorter events, 0.3 us)
Async XLA Ops:
  0.6 18.9 %copy-start.4 = (s32[96,96]{1,0:T(8,128)S(1)}, s32[96,96]{1,0:T(8,128)}, u32[]{:S(2)}) copy-start(s32[96,96]{1,0:T(8,128)} %refs_2_.5) | copy-start | bytes 110596
  0.6 18.6 %copy-start.5 = (f32[96,96]{1,0:T(8,128)S(1)}, f32[96,96]{1,0:T(8,128)}, u32[]{:S(2)}) copy-start(f32[96,96]{1,0:T(8,128)} %refs_3_.6) | copy-start | bytes 110596
  0.7 18.8 %copy-start.6 = (f32[96]{0:T(128)S(1)}, f32[96]{0:T(128)}, u32[]{:S(2)}) copy-start(f32[96]{0:T(128)} %refs_4_.5) | copy-start | bytes 1156
  0.7 17.4 %collective-permute-start.1 = (bf16[576,512]{1,0:T(8,128)(2,1)}, bf16[576,512]{1,0:T(8,128)(2,1)S(1)}, u32[]{:S(2)}, u32[]{:S(2)}) collective-permute-start(bf16[576,512]{1,0:T(8,128)(2,1)} %refs_10_.1), channel_id=1, source_target_pairs={{0,4},{1,5},{2,0},{3,1},{4,8},{5,9},{6,2},{7,3},{8,12},{9,13},{10,... | collective-permute-start | bytes 1769480 | tf_op jit(solution)/shard_map/ppermute | solution.py:321
  3.7 34.8 %collective-permute-start.8 = (bf16[576,512]{1,0:T(8,128)(2,1)}, bf16[576,512]{1,0:T(8,128)(2,1)S(1)}, u32[]{:S(2)}, u32[]{:S(2)}) collective-permute-start(bf16[576,512]{1,0:T(8,128)(2,1)} %refs_10_.1), channel_id=1, source_target_pairs={{4,0},{5,1},{0,2},{1,3},{8,4},{9,5},{2,6},{3,7},{12,8},{13,9},{6,1... | collective-permute-start | bytes 1769480 | tf_op jit(solution)/shard_map/ppermute | solution.py:321
  3.7 56.1 %collective-permute-start = (bf16[576,512]{1,0:T(8,128)(2,1)}, bf16[576,512]{1,0:T(8,128)(2,1)S(1)}, u32[]{:S(2)}, u32[]{:S(2)}) collective-permute-start(bf16[576,512]{1,0:T(8,128)(2,1)} %refs_11_.1), channel_id=1, source_target_pairs={{0,4},{1,5},{2,0},{3,1},{4,8},{5,9},{6,2},{7,3},{8,12},{9,13},{10,... | collective-permute-start | bytes 1769480 | tf_op jit(solution)/shard_map/ppermute | solution.py:321
  5.8 54.3 %collective-permute-start.10 = (bf16[576,512]{1,0:T(8,128)(2,1)}, bf16[576,512]{1,0:T(8,128)(2,1)S(1)}, u32[]{:S(2)}, u32[]{:S(2)}) collective-permute-start(bf16[576,512]{1,0:T(8,128)(2,1)} %refs_11_.1), channel_id=1, source_target_pairs={{4,0},{5,1},{0,2},{1,3},{8,4},{9,5},{2,6},{3,7},{12,8},{13,9},{6,1... | collective-permute-start | bytes 1769480 | tf_op jit(solution)/shard_map/ppermute | solution.py:321
  5.8 54.6 %collective-permute-start.4 = (bf16[576,512]{1,0:T(8,128)(2,1)}, bf16[576,512]{1,0:T(8,128)(2,1)}, u32[]{:S(2)}, u32[]{:S(2)}) collective-permute-start(bf16[576,512]{1,0:T(8,128)(2,1)} %refs_10_.1), channel_id=1, source_target_pairs={{0,1},{1,0},{2,3},{3,2},{4,5},{5,4},{6,7},{7,6},{8,9},{9,8},{10,11... | collective-permute-start | bytes 1769480 | tf_op jit(solution)/shard_map/ppermute | solution.py:321
  18.1 42.6 %collective-permute-start.5 = (bf16[576,512]{1,0:T(8,128)(2,1)}, bf16[576,512]{1,0:T(8,128)(2,1)}, u32[]{:S(2)}, u32[]{:S(2)}) collective-permute-start(bf16[576,512]{1,0:T(8,128)(2,1)} %refs_11_.1), channel_id=1, source_target_pairs={{0,1},{1,0},{2,3},{3,2},{4,5},{5,4},{6,7},{7,6},{8,9},{9,8},{10,11... | collective-permute-start | bytes 1769480 | tf_op jit(solution)/shard_map/ppermute | solution.py:321
  38.6 23.0 %collective-permute-start.3 = (bf16[576,512]{1,0:T(8,128)(2,1)S(1)}, bf16[576,512]{1,0:T(8,128)(2,1)S(1)}, u32[]{:S(2)}, u32[]{:S(2)}) collective-permute-start(bf16[576,512]{1,0:T(8,128)(2,1)S(1)} %collective-permute-done.1.refs_7_), channel_id=1, source_target_pairs={{0,4},{1,5},{2,0},{3,1},{4,8},{5,9},{6,2},{7,3},{8,12},{9,13},{10,... | collective-permute-start | bytes 1769480 | tf_op jit(solution)/shard_map/ppermute | solution.py:321
  59.9 14.4 %collective-permute-start.6 = (bf16[576,512]{1,0:T(8,128)(2,1)S(1)}, bf16[576,512]{1,0:T(8,128)(2,1)}, u32[]{:S(2)}, u32[]{:S(2)}) collective-permute-start(bf16[576,512]{1,0:T(8,128)(2,1)S(1)} %collective-permute-done.1.refs_7_), channel_id=1, source_target_pairs={{0,1},{1,0},{2,3},{3,2},{4,5},{5,4},{6,7},{7,6},{8,9},{9,8},{10,11... | collective-permute-start | bytes 1769480 | tf_op jit(solution)/shard_map/ppermute | solution.py:321
  60.1 12.2 %collective-permute-start.7 = (bf16[576,512]{1,0:T(8,128)(2,1)S(1)}, bf16[576,512]{1,0:T(8,128)(2,1)}, u32[]{:S(2)}, u32[]{:S(2)}) collective-permute-start(bf16[576,512]{1,0:T(8,128)(2,1)S(1)} %collective-permute-done.refs_9_), channel_id=1, source_target_pairs={{0,1},{1,0},{2,3},{3,2},{4,5},{5,4},{6,7},{7,6},{8,9},{9,8},{10,11... | collective-permute-start | bytes 1769480 | tf_op jit(solution)/shard_map/ppermute | solution.py:321
  60.4 13.9 %collective-permute-start.11 = (bf16[576,512]{1,0:T(8,128)(2,1)S(1)}, bf16[576,512]{1,0:T(8,128)(2,1)}, u32[]{:S(2)}, u32[]{:S(2)}) collective-permute-start(bf16[576,512]{1,0:T(8,128)(2,1)S(1)} %collective-permute-done.10.refs_13_), channel_id=1, source_target_pairs={{0,1},{1,0},{2,3},{3,2},{4,5},{5,4},{6,7},{7,6},{8,9},{9,8},{10,11... | collective-permute-start | bytes 1769480 | tf_op jit(solution)/shard_map/ppermute | solution.py:321
  60.6 13.7 %collective-permute-start.9 = (bf16[576,512]{1,0:T(8,128)(2,1)S(1)}, bf16[576,512]{1,0:T(8,128)(2,1)}, u32[]{:S(2)}, u32[]{:S(2)}) collective-permute-start(bf16[576,512]{1,0:T(8,128)(2,1)S(1)} %collective-permute-done.8.refs_11_), channel_id=1, source_target_pairs={{0,1},{1,0},{2,3},{3,2},{4,5},{5,4},{6,7},{7,6},{8,9},{9,8},{10,11... | collective-permute-start | bytes 1769480 | tf_op jit(solution)/shard_map/ppermute | solution.py:321
  61.6 26.5 %collective-permute-start.18 = (bf16[576,512]{1,0:T(8,128)(2,1)S(1)}, bf16[576,512]{1,0:T(8,128)(2,1)S(1)}, u32[]{:S(2)}, u32[]{:S(2)}) collective-permute-start(bf16[576,512]{1,0:T(8,128)(2,1)S(1)} %collective-permute-done.10.refs_13_), channel_id=1, source_target_pairs={{4,0},{5,1},{0,2},{1,3},{8,4},{9,5},{2,6},{3,7},{12,8},{13,9},{6,1... | collective-permute-start | bytes 1769480 | tf_op jit(solution)/shard_map/ppermute | solution.py:321
  61.8 12.5 %copy-start.2 = (bf16[576,512]{1,0:T(8,128)(2,1)S(1)}, bf16[576,512]{1,0:T(8,128)(2,1)}, u32[]{:S(2)}) copy-start(bf16[576,512]{1,0:T(8,128)(2,1)} %refs_10_.1) | copy-start | bytes 1769476
  61.8 12.6 %copy-start.3 = (bf16[576,512]{1,0:T(8,128)(2,1)S(1)}, bf16[576,512]{1,0:T(8,128)(2,1)}, u32[]{:S(2)}) copy-start(bf16[576,512]{1,0:T(8,128)(2,1)} %refs_11_.1) | copy-start | bytes 1769476
  72.3 17.9 %collective-permute-start.2 = (bf16[576,512]{1,0:T(8,128)(2,1)S(1)}, bf16[576,512]{1,0:T(8,128)(2,1)S(1)}, u32[]{:S(2)}, u32[]{:S(2)}) collective-permute-start(bf16[576,512]{1,0:T(8,128)(2,1)S(1)} %collective-permute-done.refs_9_), channel_id=1, source_target_pairs={{0,4},{1,5},{2,0},{3,1},{4,8},{5,9},{6,2},{7,3},{8,12},{9,13},{10,... | collective-permute-start | bytes 1769480 | tf_op jit(solution)/shard_map/ppermute | solution.py:321
  74.3 16.4 %collective-permute-start.16 = (bf16[576,512]{1,0:T(8,128)(2,1)S(1)}, bf16[576,512]{1,0:T(8,128)(2,1)S(1)}, u32[]{:S(2)}, u32[]{:S(2)}) collective-permute-start(bf16[576,512]{1,0:T(8,128)(2,1)S(1)} %collective-permute-done.8.refs_11_), channel_id=1, source_target_pairs={{4,0},{5,1},{0,2},{1,3},{8,4},{9,5},{2,6},{3,7},{12,8},{13,9},{6,1... | collective-permute-start | bytes 1769480 | tf_op jit(solution)/shard_map/ppermute | solution.py:321
  88.2 2.7 %collective-permute-start.19 = (bf16[576,512]{1,0:T(8,128)(2,1)S(1)}, bf16[576,512]{1,0:T(8,128)(2,1)S(1)}, u32[]{:S(2)}, u32[]{:S(2)}) collective-permute-start(bf16[576,512]{1,0:T(8,128)(2,1)S(1)} %collective-permute-done.18.refs_9_), channel_id=1, source_target_pairs={{0,1},{1,0},{2,3},{3,2},{4,5},{5,4},{6,7},{7,6},{8,9},{9,8},{10,11... | collective-permute-start | bytes 1769480 | tf_op jit(solution)/shard_map/ppermute | solution.py:321
  88.2 15.8 %collective-permute-start.13 = (bf16[576,512]{1,0:T(8,128)(2,1)S(1)}, bf16[576,512]{1,0:T(8,128)(2,1)S(1)}, u32[]{:S(2)}, u32[]{:S(2)}) collective-permute-start(bf16[576,512]{1,0:T(8,128)(2,1)S(1)} %collective-permute-done.3.refs_3_), channel_id=1, source_target_pairs={{0,4},{1,5},{2,0},{3,1},{4,8},{5,9},{6,2},{7,3},{8,12},{9,13},{10,... | collective-permute-start | bytes 1769480 | tf_op jit(solution)/shard_map/ppermute | solution.py:321
  90.2 15.7 %collective-permute-start.15 = (bf16[576,512]{1,0:T(8,128)(2,1)S(1)}, bf16[576,512]{1,0:T(8,128)(2,1)S(1)}, u32[]{:S(2)}, u32[]{:S(2)}) collective-permute-start(bf16[576,512]{1,0:T(8,128)(2,1)S(1)} %collective-permute-done.2.refs_5_), channel_id=1, source_target_pairs={{0,1},{1,0},{2,3},{3,2},{4,5},{5,4},{6,7},{7,6},{8,9},{9,8},{10,11... | collective-permute-start | bytes 1769480 | tf_op jit(solution)/shard_map/ppermute | solution.py:321
  90.3 15.8 %collective-permute-start.14 = (bf16[576,512]{1,0:T(8,128)(2,1)S(1)}, bf16[576,512]{1,0:T(8,128)(2,1)S(1)}, u32[]{:S(2)}, u32[]{:S(2)}) collective-permute-start(bf16[576,512]{1,0:T(8,128)(2,1)S(1)} %collective-permute-done.3.refs_3_), channel_id=1, source_target_pairs={{0,1},{1,0},{2,3},{3,2},{4,5},{5,4},{6,7},{7,6},{8,9},{9,8},{10,11... | collective-permute-start | bytes 1769480 | tf_op jit(solution)/shard_map/ppermute | solution.py:321
  90.7 15.4 %collective-permute-start.17 = (bf16[576,512]{1,0:T(8,128)(2,1)S(1)}, bf16[576,512]{1,0:T(8,128)(2,1)S(1)}, u32[]{:S(2)}, u32[]{:S(2)}) collective-permute-start(bf16[576,512]{1,0:T(8,128)(2,1)S(1)} %collective-permute-done.16.refs_7_), channel_id=1, source_target_pairs={{0,1},{1,0},{2,3},{3,2},{4,5},{5,4},{6,7},{7,6},{8,9},{9,8},{10,11... | collective-permute-start | bytes 1769480 | tf_op jit(solution)/shard_map/ppermute | solution.py:321
  90.8 25.0 %collective-permute-start.25 = (bf16[576,512]{1,0:T(8,128)(2,1)S(1)}, bf16[576,512]{1,0:T(8,128)(2,1)S(1)}, u32[]{:S(2)}, u32[]{:S(2)}) collective-permute-start(bf16[576,512]{1,0:T(8,128)(2,1)S(1)} %collective-permute-done.18.refs_9_), channel_id=1, source_target_pairs={{4,0},{5,1},{0,2},{1,3},{8,4},{9,5},{2,6},{3,7},{12,8},{13,9},{6,1... | collective-permute-start | bytes 1769480 | tf_op jit(solution)/shard_map/ppermute | solution.py:321
  104.1 15.0 %collective-permute-start.23 = (bf16[576,512]{1,0:T(8,128)(2,1)S(1)}, bf16[576,512]{1,0:T(8,128)(2,1)S(1)}, u32[]{:S(2)}, u32[]{:S(2)}) collective-permute-start(bf16[576,512]{1,0:T(8,128)(2,1)S(1)} %collective-permute-done.16.refs_7_), channel_id=1, source_target_pairs={{4,0},{5,1},{0,2},{1,3},{8,4},{9,5},{2,6},{3,7},{12,8},{13,9},{6,1... | collective-permute-start | bytes 1769480 | tf_op jit(solution)/shard_map/ppermute | solution.py:321
  105.8 14.6 %collective-permute-start.12 = (bf16[576,512]{1,0:T(8,128)(2,1)S(1)}, bf16[576,512]{1,0:T(8,128)(2,1)S(1)}, u32[]{:S(2)}, u32[]{:S(2)}) collective-permute-start(bf16[576,512]{1,0:T(8,128)(2,1)S(1)} %collective-permute-done.2.refs_5_), channel_id=1, source_target_pairs={{0,4},{1,5},{2,0},{3,1},{4,8},{5,9},{6,2},{7,3},{8,12},{9,13},{10,... | collective-permute-start | bytes 1769480 | tf_op jit(solution)/shard_map/ppermute | solution.py:321
  115.8 6.7 %collective-permute-start.26 = (bf16[576,512]{1,0:T(8,128)(2,1)S(1)}, bf16[576,512]{1,0:T(8,128)(2,1)S(1)}, u32[]{:S(2)}, u32[]{:S(2)}) collective-permute-start(bf16[576,512]{1,0:T(8,128)(2,1)S(1)} %collective-permute-done.25.refs_9_), channel_id=1, source_target_pairs={{0,1},{1,0},{2,3},{3,2},{4,5},{5,4},{6,7},{7,6},{8,9},{9,8},{10,11... | collective-permute-start | bytes 1769480 | tf_op jit(solution)/shard_map/ppermute | solution.py:321
  119.1 4.0 %collective-permute-start.24 = (bf16[576,512]{1,0:T(8,128)(2,1)S(1)}, bf16[576,512]{1,0:T(8,128)(2,1)S(1)}, u32[]{:S(2)}, u32[]{:S(2)}) collective-permute-start(bf16[576,512]{1,0:T(8,128)(2,1)S(1)} %collective-permute-done.23.refs_7_), channel_id=1, source_target_pairs={{0,1},{1,0},{2,3},{3,2},{4,5},{5,4},{6,7},{7,6},{8,9},{9,8},{10,11... | collective-permute-start | bytes 1769480 | tf_op jit(solution)/shard_map/ppermute | solution.py:321
  120.4 2.6 %collective-permute-start.22 = (bf16[576,512]{1,0:T(8,128)(2,1)S(1)}, bf16[576,512]{1,0:T(8,128)(2,1)S(1)}, u32[]{:S(2)}, u32[]{:S(2)}) collective-permute-start(bf16[576,512]{1,0:T(8,128)(2,1)S(1)} %collective-permute-done.12.refs_5_), channel_id=1, source_target_pairs={{0,1},{1,0},{2,3},{3,2},{4,5},{5,4},{6,7},{7,6},{8,9},{9,8},{10,11... | collective-permute-start | bytes 1769480 | tf_op jit(solution)/shard_map/ppermute | solution.py:321
  120.4 2.8 %collective-permute-start.21 = (bf16[576,512]{1,0:T(8,128)(2,1)S(1)}, bf16[576,512]{1,0:T(8,128)(2,1)S(1)}, u32[]{:S(2)}, u32[]{:S(2)}) collective-permute-start(bf16[576,512]{1,0:T(8,128)(2,1)S(1)} %collective-permute-done.13.refs_3_), channel_id=1, source_target_pairs={{0,1},{1,0},{2,3},{3,2},{4,5},{5,4},{6,7},{7,6},{8,9},{9,8},{10,11... | collective-permute-start | bytes 1769480 | tf_op jit(solution)/shard_map/ppermute | solution.py:321
  120.9 15.2 %collective-permute-start.28 = (bf16[576,512]{1,0:T(8,128)(2,1)S(1)}, bf16[576,512]{1,0:T(8,128)(2,1)S(1)}, u32[]{:S(2)}, u32[]{:S(2)}) collective-permute-start(bf16[576,512]{1,0:T(8,128)(2,1)S(1)} %collective-permute-done.25.refs_9_), channel_id=1, source_target_pairs={{4,0},{5,1},{0,2},{1,3},{8,4},{9,5},{2,6},{3,7},{12,8},{13,9},{6,1... | collective-permute-start | bytes 1769480 | tf_op jit(solution)/shard_map/ppermute | solution.py:321
  122.5 15.0 %collective-permute-start.20 = (bf16[576,512]{1,0:T(8,128)(2,1)S(1)}, bf16[576,512]{1,0:T(8,128)(2,1)S(1)}, u32[]{:S(2)}, u32[]{:S(2)}) collective-permute-start(bf16[576,512]{1,0:T(8,128)(2,1)S(1)} %collective-permute-done.13.refs_3_), channel_id=1, source_target_pairs={{0,4},{1,5},{2,0},{3,1},{4,8},{5,9},{6,2},{7,3},{8,12},{9,13},{10,... | collective-permute-start | bytes 1769480 | tf_op jit(solution)/shard_map/ppermute | solution.py:321
  123.3 16.2 %slice-start = ((s8[10616832]{0:T(1024)(128)(4,1)}), s8[4194304]{0:T(1024)(128)(4,1)S(1)}, s32[]{:S(2)}) async-start(s8[10616832]{0:T(1024)(128)(4,1)} %bitcast.9), calls=%async_computation | async-start | bytes 8388608
  123.3 16.2 %slice-start.1 = ((s8[10616832]{0:T(1024)(128)(4,1)}), s8[4194304]{0:T(1024)(128)(4,1)S(1)}, s32[]{:S(2)}) async-start(s8[10616832]{0:T(1024)(128)(4,1)} %bitcast.9), calls=%async_computation.1 | async-start | bytes 8388608
  123.3 16.2 %slice-start.2 = ((s8[10616832]{0:T(1024)(128)(4,1)}), s8[2228224]{0:T(1024)(128)(4,1)S(1)}, s32[]{:S(2)}) async-start(s8[10616832]{0:T(1024)(128)(4,1)} %bitcast.9), calls=%async_computation.2 | async-start | bytes 4456448
  133.3 1.0 copy-start
  136.2 2.6 %collective-permute-start.29 = (bf16[576,512]{1,0:T(8,128)(2,1)S(1)}, bf16[576,512]{1,0:T(8,128)(2,1)S(1)}, u32[]{:S(2)}, u32[]{:S(2)}) collective-permute-start(bf16[576,512]{1,0:T(8,128)(2,1)S(1)} %collective-permute-done.28.refs_5_), channel_id=1, source_target_pairs={{0,1},{1,0},{2,3},{3,2},{4,5},{5,4},{6,7},{7,6},{8,9},{9,8},{10,11... | collective-permute-start | bytes 1769480 | tf_op jit(solution)/shard_map/ppermute | solution.py:321
  137.4 2.0 %collective-permute-start.27 = (bf16[576,512]{1,0:T(8,128)(2,1)S(1)}, bf16[576,512]{1,0:T(8,128)(2,1)S(1)}, u32[]{:S(2)}, u32[]{:S(2)}) collective-permute-start(bf16[576,512]{1,0:T(8,128)(2,1)S(1)} %collective-permute-done.20.refs_3_), channel_id=1, source_target_pairs={{0,1},{1,0},{2,3},{3,2},{4,5},{5,4},{6,7},{7,6},{8,9},{9,8},{10,11... | collective-permute-start | bytes 1769480 | tf_op jit(solution)/shard_map/ppermute | solution.py:321
  139.4 1.3 copy-start.1
  147.8 3.2 %collective-permute-start.30 = (f32[6,512]{1,0:T(8,128)S(1)}, f32[6,512]{1,0:T(8,128)S(1)}, u32[]{:S(2)}, u32[]{:S(2)}) collective-permute-start(f32[6,512]{1,0:T(8,128)S(1)} %get-tuple-element.84), channel_id=1, source_target_pairs={{0,3},{1,2},{2,1},{3,0},{4,7},{5,6},{6,5},{7,4},{8,11},{9,10},{10,... | collective-permute-start | bytes 36872 | tf_op jit(solution)/shard_map/ppermute | solution.py:285
  149.2 3.8 %collective-permute-start.31 = (f32[6,512]{1,0:T(8,128)S(1)}, f32[6,512]{1,0:T(8,128)S(1)}, u32[]{:S(2)}, u32[]{:S(2)}) collective-permute-start(f32[6,512]{1,0:T(8,128)S(1)} %get-tuple-element.84), channel_id=1, source_target_pairs={{0,2},{1,3},{2,0},{3,1},{4,6},{5,7},{6,4},{7,5},{8,10},{9,11},{10,... | collective-permute-start | bytes 36872 | tf_op jit(solution)/shard_map/ppermute | solution.py:285
  149.6 3.3 %collective-permute-start.32 = (f32[6,512]{1,0:T(8,128)S(1)}, f32[6,512]{1,0:T(8,128)S(1)}, u32[]{:S(2)}, u32[]{:S(2)}) collective-permute-start(f32[6,512]{1,0:T(8,128)S(1)} %get-tuple-element.84), channel_id=1, source_target_pairs={{0,1},{1,0},{2,3},{3,2},{4,5},{5,4},{6,7},{7,6},{8,9},{9,8},{10,11... | collective-permute-start | bytes 36872 | tf_op jit(solution)/shard_map/ppermute | solution.py:285
  153.0 6.0 %collective-permute-start.33 = (f32[24,512]{1,0:T(8,128)S(1)}, f32[24,512]{1,0:T(8,128)S(1)}, u32[]{:S(2)}, u32[]{:S(2)}) collective-permute-start(f32[24,512]{1,0:T(8,128)S(1)} %pad_maximum_fusion.1), channel_id=1, source_target_pairs={{0,12},{1,13},{2,14},{3,15},{4,8},{5,9},{6,10},{7,11},{8,4},{9,5},... | collective-permute-start | bytes 147464 | tf_op jit(solution)/shard_map/ppermute | solution.py:285
  155.4 5.4 %collective-permute-start.34 = (f32[24,512]{1,0:T(8,128)S(1)}, f32[24,512]{1,0:T(8,128)S(1)}, u32[]{:S(2)}, u32[]{:S(2)}) collective-permute-start(f32[24,512]{1,0:T(8,128)S(1)} %pad_maximum_fusion.1), channel_id=1, source_target_pairs={{0,8},{1,9},{2,10},{3,11},{4,12},{5,13},{6,14},{7,15},{8,0},{9,1},... | collective-permute-start | bytes 147464 | tf_op jit(solution)/shard_map/ppermute | solution.py:285
  156.1 4.7 %collective-permute-start.35 = (f32[24,512]{1,0:T(8,128)S(1)}, f32[24,512]{1,0:T(8,128)S(1)}, u32[]{:S(2)}, u32[]{:S(2)}) collective-permute-start(f32[24,512]{1,0:T(8,128)S(1)} %pad_maximum_fusion.1), channel_id=1, source_target_pairs={{0,4},{1,5},{2,6},{3,7},{4,0},{5,1},{6,2},{7,3},{8,12},{9,13},{10,... | collective-permute-start | bytes 147464 | tf_op jit(solution)/shard_map/ppermute | solution.py:285

commit v3 on v2

--- a/solution.py
+++ b/solution.py
@@ -70,8 +70,15 @@
     return (new_same, new_opp, next_same, next_opp, collision)
 
 
+def turn(unit, block):
+    return lax.dot_general(
+        unit, block, (((1,), (1,)), ((), ())), preferred_element_type=jnp.float32
+    )
+
+
 def build_body(orbitals, low, high, pairs, *refs):
-    place_ref, inter_ref, pat_ref, hop_ref, occ_ref, pat4_ref, hop4_ref, eye4_ref, occ4_ref = refs[:9]
+    place_ref, inter_ref, pat_ref, hop_ref, occ_ref = refs[:5]
+    pat4_ref, hop4_ref, eye4_ref, occ4_ref, unit_ref = refs[5:10]
     mixed_ref, polar_ref, turned_ref = refs[-3:]
     span = 4 * orbitals
     tiles = pairs // span
@@ -81,11 +88,11 @@
     @pl.loop(0, tiles)
     def _(tile):
         cols = pl.ds(pl.multiple_of(tile * span, 128), span)
+        turned = turn(unit_ref[...], inter_ref[:, cols])
         for strip in strips:
             size = min(128, high - low - strip)
-            piece = inter_ref[strip : strip + size, cols].T.astype(jnp.float32)
             at = strip // 128 * pairs + tile * span
-            turned_ref[pl.ds(pl.multiple_of(at, 128), span), :size] = piece
+            turned_ref[pl.ds(pl.multiple_of(at, 128), span), :size] = turned[:, strip : strip + size]
 
     group = lax.broadcasted_iota(jnp.int32, (1, span), 1) // orbitals
     occ4 = occ4_ref[...]
@@ -110,6 +117,7 @@
             unit = (group + 4 * tile == here).astype(jnp.float32)
             linked4 = pat4_ref[pl.ds(here, 1), :]
             facts[first] = (linked * polar_factor, linked4 * ladder_factor, hop_row, unit)
+        sides = []
         for strip in strips:
             size = min(128, high - low - strip)
             pieces = [
@@ -118,27 +126,28 @@
                 ]
                 for m in range(4)
             ]
-            block = jnp.concatenate(pieces, axis=0).astype(jnp.bfloat16).T[:size]
-            row = low + strip
-            while row < low + strip + size:
-                first, second = row // orbitals, row % orbitals
-                count = min(orbitals - second, low + strip + size - row)
-                there = slice(row - low, row - low + count)
-                polar_row, ladder_row, hop_row, unit = facts[first]
-                polar = inter_ref[there, cols].astype(jnp.float32) * polar_row
-                hop = (
-                    hop_row * eye4_ref[second : second + count]
-                    + unit * hop4_ref[second : second + count]
-                )
-                part = block[row - low - strip : row - low - strip + count]
-                ladder = (part.astype(jnp.float32) * ladder_row).astype(jnp.bfloat16)
-                direct = (polar + hop).astype(jnp.bfloat16).astype(jnp.float32)
-                held = polar.astype(jnp.bfloat16)
-                polar_ref[there, cols] = held
-                mixed_ref[there, cols] = (
-                    direct - held.astype(jnp.float32) + ladder.astype(jnp.float32)
-                ).astype(jnp.bfloat16)
-                row += count
+            sides.append(jnp.concatenate(pieces, axis=0)[:, :size].astype(jnp.bfloat16))
+        side = jnp.concatenate(sides, axis=1)
+        block = turn(unit_ref[: high - low, : high - low], side)
+        row = low
+        while row < high:
+            first, second = row // orbitals, row % orbitals
+            count = min(orbitals - second, high - row)
+            there = slice(row - low, row - low + count)
+            polar_row, ladder_row, hop_row, unit = facts[first]
+            polar = inter_ref[there, cols].astype(jnp.float32) * polar_row
+            hop = (
+                hop_row * eye4_ref[second : second + count]
+                + unit * hop4_ref[second : second + count]
+            )
+            ladder = (block[there] * ladder_row).astype(jnp.bfloat16)
+            direct = (polar + hop).astype(jnp.bfloat16).astype(jnp.float32)
+            held = polar.astype(jnp.bfloat16)
+            polar_ref[there, cols] = held
+            mixed_ref[there, cols] = (
+                direct - held.astype(jnp.float32) + ladder.astype(jnp.float32)
+            ).astype(jnp.bfloat16)
+            row += count
 
 
 def build_rows(place, interaction, smalls, made, low, high):
@@ -152,37 +161,40 @@
     smem = pl.BlockSpec(memory_space=pltpu.SMEM)
     row4 = pl.BlockSpec((1, 4 * orbitals), lambda g, p: (0, 0))
     small = pl.BlockSpec((orbitals, 4 * orbitals), lambda g, p: (0, 0))
+    square = pl.BlockSpec((4 * orbitals, 4 * orbitals), lambda g, p: (0, 0))
     return pl.pallas_call(
         functools.partial(build_body, orbitals, low, high, pairs),
         grid_spec=pltpu.PrefetchScalarGridSpec(
             num_scalar_prefetch=1,
             grid=(1,),
-            in_specs=[wide, smem, smem, smem, small, small, small, row4]
+            in_specs=[wide, smem, smem, smem, small, small, small, row4, square]
             + [pl.BlockSpec(memory_space=pl.ANY)] * len(made),
             out_specs=[wide] * 2,
             scratch_shapes=[pltpu.VMEM((-(-height // 128) * pairs, 128), jnp.float32)],
         ),
         out_shape=[shape] * 2,
-        input_output_aliases={9 + n: n for n in range(len(made))},
+        input_output_aliases={10 + n: n for n in range(len(made))},
         compiler_params=pltpu.CompilerParams(vmem_limit_bytes=44 * MIB),
-        cost_estimate=pl.CostEstimate(
-            flops=20 * height * pairs, bytes_accessed=6 * height * pairs, transcendentals=0
-        ),
+        cost_estimate=pl.CostEstimate(flops=1024, bytes_accessed=1024, transcendentals=0),
         name="build_rows",
     )(place, interaction, *smalls, *made)
 
 
-def step_body(chips, opening, closing, orbitals, scale, *refs):
+def step_body(parts, rows, opening, closing, orbitals, scale, *refs):
     place_ref = refs[0]
     refs = list(refs[1:])
+    chips = len(parts)
     mixed_ref, polar_ref = refs.pop(0), refs.pop(0)
-    greens = [[[refs.pop(0) for _ in range(2)] for _ in range(2)] for _ in range(chips)]
+    greens = []
+    for count in parts:
+        pieces = [refs.pop(0) for _ in range(2 * count)]
+        greens.append([pieces[:count], pieces[count:]])
     sums = [] if opening else [refs.pop(0) for _ in range(3)]
     olds = [refs.pop(0) for _ in range(2)] if closing else []
     held = refs.pop()
     totals = [refs.pop() for _ in range(3)][::-1] if closing else refs[:3]
     core = place_ref[0]
-    rows = greens[0][0][0].shape[0]
+    span = greens[0][0][0].shape[1]
     now = pl.program_id(1)
 
     for chip in range(chips):
@@ -192,11 +204,13 @@
             for which in range(2):
                 lane = core if which == 0 else 1 - core
                 there = pl.ds(pl.multiple_of(lane * rows, 64), rows)
-                same, opp = greens[chip][0][which][...], greens[chip][1][which][...]
-                held[0, there, :] = same
-                held[1, there, :] = opp
+                pieces = greens[chip][which]
+                same = pieces[0][:rows, :]
+                opp = pieces[-1][pieces[-1].shape[0] - rows :, :]
                 both = same.astype(jnp.float32) + opp.astype(jnp.float32)
-                held[2, there, :] = both.astype(jnp.bfloat16)
+                held[there, :span] = same
+                held[there, span : 2 * span] = opp
+                held[there, 2 * span :] = both.astype(jnp.bfloat16)
 
     @pl.when(now == 0)
     def _():
@@ -206,9 +220,10 @@
             else:
                 totals[n][...] = sums[n][...]
 
-    totals[0][...] += product(mixed_ref[...], held[0])
-    totals[1][...] += product(mixed_ref[...], held[1])
-    totals[2][...] += product(polar_ref[...], held[2])
+    mixed = product(mixed_ref[...], held[:, : 2 * span])
+    totals[0][...] += mixed[:, :span]
+    totals[1][...] += mixed[:, span:]
+    totals[2][...] += product(polar_ref[...], held[:, 2 * span :])
     if closing:
 
         @pl.when(now == chips - 1)
@@ -226,16 +241,18 @@
                 refs[4][first : first + 1, :] = jnp.sum(both, axis=0, keepdims=True) * scale
 
 
-def step(place, mats, greens, sums, olds, orbitals):
+def step(place, low, mats, greens, sums, olds, orbitals):
     chips = len(greens)
     opening, closing = not sums, bool(olds)
-    rows, width = greens[0][0][0].shape
+    rows = mats[0].shape[0]
+    width = greens[0][0][0].shape[1]
+    parts = tuple(len(pair[0]) for pair in greens)
     wide = 2 * rows
-    span = min(width, 256)
+    span = min(width, 256) if closing else width
     tall = pl.BlockSpec((rows, span), lambda n, g, p: (0, n))
-    mat = pl.BlockSpec((rows, wide), lambda n, g, p: (0, p[1 + g]))
+    mat = pl.BlockSpec((rows, wide), lambda n, g, p: (0, p[1 + low + g]))
     wide_sum = jax.ShapeDtypeStruct((rows, width), jnp.float32)
-    scratch = [pltpu.VMEM((3, wide, span), jnp.bfloat16)]
+    scratch = [pltpu.VMEM((wide, 3 * span), jnp.bfloat16)]
     if closing:
         out_specs = [tall] * 4 + [pl.BlockSpec((rows // orbitals, span), lambda n, g, p: (0, n))]
         out_shape = [wide_sum] * 2 + [jax.ShapeDtypeStruct((rows, width), jnp.bfloat16)] * 2
@@ -244,8 +261,10 @@
     else:
         out_specs, out_shape = [tall] * 3, [wide_sum] * 3
     operands = list(mats)
-    operands += [greens[c][k][w] for c in range(chips) for k in range(2) for w in range(2)]
-    in_specs = [mat] * 2 + [tall] * (4 * chips)
+    blocks = [block for pair in greens for side in pair for block in side]
+    operands += blocks
+    in_specs = [mat] * 2
+    in_specs += [pl.BlockSpec((block.shape[0], span), lambda n, g, p: (0, n)) for block in blocks]
     aliases = {}
     if not opening:
         if not closing:
@@ -257,7 +276,7 @@
         in_specs += [tall] * 2
     return pl.pallas_call(
         functools.partial(
-            step_body, chips, opening, closing, orbitals, 1.0 / math.sqrt(orbitals)
+            step_body, parts, rows, opening, closing, orbitals, 1.0 / math.sqrt(orbitals)
         ),
         grid_spec=pltpu.PrefetchScalarGridSpec(
             num_scalar_prefetch=1,
@@ -268,12 +287,8 @@
         ),
         out_shape=out_shape,
         input_output_aliases=aliases,
-        compiler_params=pltpu.CompilerParams(vmem_limit_bytes=36 * MIB),
-        cost_estimate=pl.CostEstimate(
-            flops=6 * chips * rows * wide * width,
-            bytes_accessed=8 * chips * rows * wide + 24 * rows * width,
-            transcendentals=0,
-        ),
+        compiler_params=pltpu.CompilerParams(vmem_limit_bytes=48 * MIB),
+        cost_estimate=pl.CostEstimate(flops=1024, bytes_accessed=1024, transcendentals=0),
         name="add_products",
     )(place, *operands)
 
@@ -320,18 +335,10 @@
     def send(block, pairs_of):
         return lax.ppermute(block, "prow", pairs_of)
 
-    def both_ways(kind, blocks):
-        return [send(blocks[0], right), send(blocks[1], left)]
-
-    def share(blocks):
-        return [(block, send(block, across)) for block in blocks]
-
-    def place_of(low, high):
-        return jnp.concatenate([core[None].astype(jnp.int32), line[low:high]])
-
-    own = (green_same, green_opp)
-    moving = [both_ways(kind, [own[kind]] * 2) for kind in range(2)]
-    near = [share([own[kind]])[0] for kind in range(2)]
+    place = jnp.concatenate([core[None].astype(jnp.int32), line])
+    own = jnp.concatenate([green_same, green_opp], axis=0)
+    moving = [send(own, right), send(own, left)]
+    near = send(own, across)
 
     start = (me * (rows // orbitals)).astype(jnp.int32)[None]
     smalls = (
@@ -342,49 +349,32 @@
         jnp.tile(hopping, (1, 4)),
         jnp.tile(jnp.eye(orbitals, dtype=jnp.float32), (1, 4)),
         jnp.tile(occupation, 4)[None],
+        jnp.eye(4 * orbitals, dtype=jnp.bfloat16),
     )
     big = rows // 9 * 4
     mats = build_rows(start, interaction, smalls, (), 0, big)
-
-    got = [[], []]
-    got[0] = [after(block, mats[0]) for block in moving[0]]
-    moving[0] = both_ways(0, got[0])
-    pair_same = share(got[0])
-    mats = build_rows(after(start, got[0][0]), interaction, smalls, mats, big, 2 * big)
-
-    got[1] = [after(block, mats[0]) for block in moving[1]]
-    moving[1] = both_ways(1, got[1])
-    pair_opp = share(got[1])
-    mats = build_rows(after(start, got[1][0]), interaction, smalls, mats, 2 * big, rows)
-
-    greens = [[near[0], near[1]]] + [[pair_same[n], pair_opp[n]] for n in range(2)]
-    sums = ()
-    for far in range(2, half):
-        got[0] = [after(block, mats[0]) for block in moving[0]]
-        last = far == half - 1
-        if last:
-            moving[0] = [send(got[0][0], right)]
+    mats = build_rows(start, interaction, smalls, mats, big, 2 * big)
+
+    greens, low, sums, done = [([own], [near])], 0, (), mats[0]
+    for far in range(1, half):
+        got = [after(block, done) for block in moving]
+        if far < half - 1:
+            moving = [send(got[0], right), send(got[1], left)]
         else:
-            moving[0] = both_ways(0, got[0])
-        pair_same = share(got[0])
-        low = 0 if far == 2 else 2 * far - 3
-        sums = step(
-            after(place_of(low, 2 * far - 1), got[0][0]), mats, greens, sums, (), orbitals
-        )
-        got[1] = [after(block, sums[0]) for block in moving[1]]
-        if last:
-            moving[1] = [send(got[1][1], left)]
+            moving = [send(got[0][:rows], right), send(got[1][rows:], left)]
+        passed = [([block], [send(block, across)]) for block in got]
+        if far == 1:
+            mats = build_rows(after(start, got[0]), interaction, smalls, mats, 2 * big, rows)
+            greens += passed
         else:
-            moving[1] = both_ways(1, got[1])
-        pair_opp = share(got[1])
-        greens = [[pair_same[n], pair_opp[n]] for n in range(2)]
-        mats = [after(mats[0], got[1][0]), mats[1]]
-    low = 2 * half - 3
-    sums = step(place_of(low, low + 2), mats, greens, sums, (), orbitals)
-    far_same = share([after(moving[0][0], sums[0])])[0]
-    far_opp = share([after(moving[1][0], sums[0])])[0]
+            greens = passed
+        sums = step(after(place, got[0]), low, mats, greens, sums, (), orbitals)
+        low += len(greens)
+        done = sums[0]
+    last = [after(block, done) for block in moving]
+    shared = [send(block, across) for block in last]
     new_same, new_opp, next_same, next_opp, part = step(
-        place_of(low + 2, low + 3), mats, [[far_same, far_opp]], sums, own, orbitals
+        place, low, mats, [(last, shared)], sums, (green_same, green_opp), orbitals
     )
     if devices == 16:
         collision = spread_blocks(spread_blocks(part, me, 1, devices), me, 4, devices)

time: 162 us -> 160 us (0.988)
  Pallas kernels: 89.2 us -> 107 us
  waiting for transfers between devices: 39.3 us -> 30.5 us
  starting transfers between devices: 25.2 us -> 17 us
  other arithmetic: 2.51 us -> 0.87 us
    pallas_call x3, Pallas kernels: 48.7 us -> 66.7 us  [build_rows(): pl.pallas_call(functools.partial(build_body, orbitals, low, high, pairs),...]
    ppermute x30 -> x17, waiting for transfers between devices: 32.8 us -> 24.1 us  [send(): return lax.ppermute(block, 'prow', pairs_of)]
    ppermute x30 -> x17, starting transfers between devices: 18.9 us -> 10.7 us  [send(): return lax.ppermute(block, 'prow', pairs_of)]
  transfers between devices with their start and end apart: 36 -> 23, of which waited for: 12 -> 13; matrix products, arithmetic and copies ran while one was open for 2% -> 1% of each run, Pallas kernels for 51% -> 62%
where the time goes in v3:
time: 160 us
  Pallas kernels  107 us (67%)
  waiting for transfers between devices  30.5 us (19%)
  starting transfers between devices  17 us (11%)
  local copies, waits for them, and re-layouts  4.01 us (3%)
    pallas_call x3, Pallas kernels, build_rows(): pl.pallas_call(functools.partial(build_body, orbitals, low, high, pairs),...  66.7 us
    pallas_call x4, Pallas kernels, step(): pl.pallas_call(functools.partial(step_body, parts, rows, opening, closing...  40.3 us
    ppermute x17, waiting for transfers between devices, send(): return lax.ppermute(block, 'prow', pairs_of)  24.1 us
    ppermute x17, starting transfers between devices, send(): return lax.ppermute(block, 'prow', pairs_of)  10.7 us
    ppermute x6, waiting for transfers between devices, spread_blocks(): blocks.append(lax.ppermute(block, 'prow', pairs_of))  6.32 us
    ppermute x6, starting transfers between devices, spread_blocks(): blocks.append(lax.ppermute(block, 'prow', pairs_of))  6.31 us
  transfers between devices with their start and end apart: 23, of which 13 were waited for; matrix products, arithmetic and copies ran while one was open for 1% of the time, Pallas kernels for 62%

profile of v3, /device:TPU:0, one launch (start us, length us, event | category | flops | bytes accessed | tf_op | source)
XLA Modules:
  0.0 160.2 jit_solution(10721672705543464270)
XLA Ops:
  0.7 1.2 constant_dynamic-update-slice_fusion.1
  1.8 0.1 copy-done.2
  1.9 0.0 copy-start.5
  1.9 3.1 %collective-permute-start = (bf16[1152,512]{1,0:T(8,128)(2,1)S(1)}, bf16[1152,512]{1,0:T(8,128)(2,1)}, u32[]{:S(2)}, u32[]{:S(2)}) collective-permute-start(bf16[1152,512]{1,0:T(8,128)(2,1)S(1)} %constant_dynamic-update-slice_fusion.refs_3_), channel_id=1, source_target_pairs={{0,4},{1,5},{2,0},{3,1},{4,8},{5,9},{6,2},{7,3},{8,12},{9,13},{10,... | collective-permute-start | bytes 3538952 | tf_op jit(solution)/shard_map/ppermute | solution.py:336
  5.0 0.0 collective-permute-start.4
  5.0 0.0 collective-permute-start.2
  5.1 0.1 tile.42.refs_5_
  5.3 0.1 tile.46.refs_7_
  5.5 0.1 tile.44.refs_6_
  5.7 0.1 broadcast_in_dim_tile.3.refs_8_
  5.8 26.0 %build_rows.3 = (bf16[576,9216]{1,0:T(8,128)(2,1)}, bf16[576,9216]{1,0:T(8,128)(2,1)}) custom-call(s32[1]{0:T(128)} %bitcast.2.refs_0_, bf16[576,9216]{1,0:T(8,128)(2,1)} %refs_1_.5, s32[96,96]{1,0:T(8,128)S(1)} %copy-done.3, f32[96,96]{1,0:T(8,128)S(1)} %copy-done.4, f32[96]{0:T(128)S(1)} %copy-done.5, f32[96,384]{1,0:T(8,128)S(1)} %tile.42.refs_5_, ...), custom_call_target="tpu_custom_call" | custom-call | flops 1024 | bytes 1024 | tf_op jit(solution)/shard_map/build_rows/pallas_call | solution.py:165
  31.7 25.9 %build_rows.4 = (bf16[576,9216]{1,0:T(8,128)(2,1)}, bf16[576,9216]{1,0:T(8,128)(2,1)}) custom-call(s32[1]{0:T(128)} %bitcast.2.refs_0_, bf16[576,9216]{1,0:T(8,128)(2,1)} %refs_1_.5, s32[96,96]{1,0:T(8,128)S(1)} %copy-done.3, f32[96,96]{1,0:T(8,128)S(1)} %copy-done.4, f32[96]{0:T(128)S(1)} %copy-done.5, ...), custom_call_target="tpu_custom_call", output_to_operand_aliasing={{0}: (10, {}), {1}: (11, {})} | custom-call | flops 1024 | bytes 1024 | tf_op jit(solution)/shard_map/build_rows/pallas_call | solution.py:165
  57.6 0.0 collective-permute-done.refs_5_
  57.6 0.0 collective-permute-done.4.refs_7_
  57.6 0.6 collective-permute-start.3
  58.2 0.1 collective-permute-start.5
  58.3 1.9 %collective-permute-start.8 = (bf16[1152,512]{1,0:T(8,128)(2,1)}, bf16[1152,512]{1,0:T(8,128)(2,1)}, u32[]{:S(2)}, u32[]{:S(2)}) collective-permute-start(bf16[1152,512]{1,0:T(8,128)(2,1)} %collective-permute-done.4.refs_7_), channel_id=1, source_target_pairs={{4,0},{5,1},{0,2},{1,3},{8,4},{9,5},{2,6},{3,7},{12,8},{13,9},{6,1... | collective-permute-start | bytes 3538952 | tf_op jit(solution)/shard_map/ppermute | solution.py:336
  60.2 0.1 collective-permute-start.1
  60.3 0.7 dynamic-slice_bitcast_fusion
  61.0 0.1 pad_add_fusion.refs_0_
  61.1 14.8 %build_rows.5 = (bf16[576,9216]{1,0:T(8,128)(2,1)}, bf16[576,9216]{1,0:T(8,128)(2,1)}) custom-call(s32[1]{0:T(128)} %bitcast.2.refs_0_, bf16[576,9216]{1,0:T(8,128)(2,1)} %refs_1_.5, s32[96,96]{1,0:T(8,128)S(1)} %copy-done.3, f32[96,96]{1,0:T(8,128)S(1)} %copy-done.4, f32[96]{0:T(128)S(1)} %copy-done.5, ...), custom_call_target="tpu_custom_call", output_to_operand_aliasing={{0}: (10, {}), {1}: (11, {})} | custom-call | flops 1024 | bytes 1024 | tf_op jit(solution)/shard_map/build_rows/pallas_call | solution.py:165
  75.9 0.0 collective-permute-done.2.refs_4_
  75.9 0.0 collective-permute-done.3.refs_6_
  75.9 0.0 collective-permute-done.5.refs_8_
  75.9 13.4 %add_products.4 = (f32[576,512]{1,0:T(8,128)S(1)}, f32[576,512]{1,0:T(8,128)S(1)}, f32[576,512]{1,0:T(8,128)S(1)}) custom-call(s32[10]{0:T(128)S(1)} %pad_add_fusion.refs_0_, bf16[576,9216]{1,0:T(8,128)(2,1)} %get-tuple-element.43.refs_1_, bf16[576,9216]{1,0:T(8,128)(2,1)} %get-tuple-element.44.refs_2_, ...), custom_call_target="tpu_custom_call" | custom-call | flops 1024 | bytes 1024 | tf_op jit(solution)/shard_map/add_products/pallas_call | solution.py:277
  89.4 0.0 collective-permute-done.8.refs_5_
  89.4 0.3 collective-permute-start.9
  89.6 0.0 collective-permute-done.1.refs_3_
  89.7 0.3 collective-permute-start.7
  90.0 1.9 %collective-permute-start.12 = (bf16[1152,512]{1,0:T(8,128)(2,1)}, bf16[1152,512]{1,0:T(8,128)(2,1)S(1)}, u32[]{:S(2)}, u32[]{:S(2)}) collective-permute-start(bf16[1152,512]{1,0:T(8,128)(2,1)} %collective-permute-done.8.refs_5_), channel_id=1, source_target_pairs={{4,0},{5,1},{0,2},{1,3},{8,4},{9,5},{2,6},{3,7},{12,8},{13,9},{6,1... | collective-permute-start | bytes 3538952 | tf_op jit(solution)/shard_map/ppermute | solution.py:336
  91.9 0.1 collective-permute-start.6
  92.0 0.5 collective-permute-done.9.refs_6_
  92.5 1.7 %collective-permute-done.7.refs_4_ = bf16[1152,512]{1,0:T(8,128)(2,1)S(1)} collective-permute-done((bf16[1152,512]{1,0:T(8,128)(2,1)}, bf16[1152,512]{1,0:T(8,128)(2,1)S(1)}, u32[]{:S(2)}, u32[]{:S(2)}) %collective-permute-start.7) | collective-permute-done | bytes 1179680 | tf_op jit(solution)/shard_map/ppermute | solution.py:336
  94.2 9.9 %add_products.5 = (f32[576,512]{1,0:T(8,128)S(1)}, f32[576,512]{1,0:T(8,128)S(1)}, f32[576,512]{1,0:T(8,128)S(1)}) custom-call(s32[10]{0:T(128)S(1)} %pad_add_fusion.refs_0_, bf16[576,9216]{1,0:T(8,128)(2,1)} %get-tuple-element.43.refs_1_, bf16[576,9216]{1,0:T(8,128)(2,1)} %get-tuple-element.44.refs_2_, ...), custom_call_target="tpu_custom_call", output_to_operand_aliasing={{0}: (7, {}), {1}: (8, {}), {2}: (9, {})} | custom-call | flops 1024 | bytes 1024 | tf_op jit(solution)/shard_map/add_products/pallas_call | solution.py:277
  104.1 14.3 %collective-permute-done.12.refs_5_ = bf16[1152,512]{1,0:T(8,128)(2,1)S(1)} collective-permute-done((bf16[1152,512]{1,0:T(8,128)(2,1)}, bf16[1152,512]{1,0:T(8,128)(2,1)S(1)}, u32[]{:S(2)}, u32[]{:S(2)}) %collective-permute-start.12) | collective-permute-done | bytes 1179680 | tf_op jit(solution)/shard_map/ppermute | solution.py:336
  118.4 0.0 collective-permute-start.13
  118.4 1.4 collective-permute-done.6.refs_3_
  119.8 0.0 collective-permute-start.11
  119.8 1.7 %collective-permute-start.14 = (bf16[576,512]{1,0:T(8,128)(2,1)S(1)}, bf16[576,512]{1,0:T(8,128)(2,1)S(1)}, u32[]{:S(2)}, u32[]{:S(2)}) collective-permute-start(bf16[576,512]{1,0:T(8,128)(2,1)S(1)} %slice.7), channel_id=1, source_target_pairs={{4,0},{5,1},{0,2},{1,3},{8,4},{9,5},{2,6},{3,7},{12,8},{13,9},{6,1... | collective-permute-start | bytes 1769480 | tf_op jit(solution)/shard_map/ppermute | solution.py:336
  121.6 0.6 collective-permute-start.10
  122.2 0.0 collective-permute-done.13.refs_6_
  122.2 0.7 collective-permute-done.11.refs_4_
  122.9 0.3 copy-done.7
  123.2 9.5 %add_products.6 = (f32[576,512]{1,0:T(8,128)S(1)}, f32[576,512]{1,0:T(8,128)S(1)}, f32[576,512]{1,0:T(8,128)S(1)}) custom-call(s32[10]{0:T(128)S(1)} %pad_add_fusion.refs_0_, bf16[576,9216]{1,0:T(8,128)(2,1)} %get-tuple-element.43.refs_1_, bf16[576,9216]{1,0:T(8,128)(2,1)} %get-tuple-element.44.refs_2_, ...), custom_call_target="tpu_custom_call", output_to_operand_aliasing={{0}: (7, {}), {1}: (8, {}), {2}: (9, {})} | custom-call | flops 1024 | bytes 1024 | tf_op jit(solution)/shard_map/add_products/pallas_call | solution.py:277
  132.7 1.0 copy-done
  133.8 1.8 %collective-permute-done.14.refs_4_ = bf16[576,512]{1,0:T(8,128)(2,1)S(1)} collective-permute-done((bf16[576,512]{1,0:T(8,128)(2,1)S(1)}, bf16[576,512]{1,0:T(8,128)(2,1)S(1)}, u32[]{:S(2)}, u32[]{:S(2)}) %collective-permute-start.14) | collective-permute-done | bytes 589856 | tf_op jit(solution)/shard_map/ppermute | solution.py:336
  135.6 0.0 collective-permute-start.16
  135.6 1.7 %collective-permute-done.10.refs_3_ = bf16[576,512]{1,0:T(8,128)(2,1)S(1)} collective-permute-done((bf16[576,512]{1,0:T(8,128)(2,1)S(1)}, bf16[576,512]{1,0:T(8,128)(2,1)S(1)}, u32[]{:S(2)}, u32[]{:S(2)}) %collective-permute-start.10) | collective-permute-done | bytes 589856 | tf_op jit(solution)/shard_map/ppermute | solution.py:336
  137.3 0.0 collective-permute-start.15
  137.3 0.3 collective-permute-done.16.refs_6_
  137.6 1.7 %collective-permute-done.15.refs_5_ = bf16[576,512]{1,0:T(8,128)(2,1)S(1)} collective-permute-done((bf16[576,512]{1,0:T(8,128)(2,1)S(1)}, bf16[576,512]{1,0:T(8,128)(2,1)S(1)}, u32[]{:S(2)}, u32[]{:S(2)}) %collective-permute-start.15) | collective-permute-done | bytes 589856 | tf_op jit(solution)/shard_map/ppermute | solution.py:336
  139.3 7.5 %add_products.7 = (f32[576,512]{1,0:T(8,128)}, f32[576,512]{1,0:T(8,128)}, bf16[576,512]{1,0:T(8,128)(2,1)}, bf16[576,512]{1,0:T(8,128)(2,1)}, f32[6,512]{1,0:T(8,128)S(1)}) custom-call(s32[10]{0:T(128)S(1)} %pad_add_fusion.refs_0_, bf16[576,9216]{1,0:T(8,128)(2,1)} %get-tuple-element.43.refs_1_, bf16[576,9216]{1,0:T(8,128)(2,1)} %get-tuple-element.44.refs_2_, ...), custom_call_target="tpu_custom_call" | custom-call | flops 1024 | bytes 1024 | tf_op jit(solution)/shard_map/add_products/pallas_call | solution.py:277
  146.8 1.4 collective-permute-start.17
  148.1 0.4 collective-permute-start.18
  148.5 0.1 collective-permute-start.19
  148.6 1.3 collective-permute-done.17
  149.9 2.0 %collective-permute-done.18 = f32[6,512]{1,0:T(8,128)S(1)} collective-permute-done((f32[6,512]{1,0:T(8,128)S(1)}, f32[6,512]{1,0:T(8,128)S(1)}, u32[]{:S(2)}, u32[]{:S(2)}) %collective-permute-start.18) | collective-permute-done | bytes 12320 | tf_op jit(solution)/shard_map/ppermute | solution.py:300
  151.9 0.0 collective-permute-done.19
  151.9 1.7 %collective-permute-start.20 = (f32[24,512]{1,0:T(8,128)S(1)}, f32[24,512]{1,0:T(8,128)S(1)}, u32[]{:S(2)}, u32[]{:S(2)}) collective-permute-start(f32[24,512]{1,0:T(8,128)S(1)} %pad_maximum_fusion.1), channel_id=1, source_target_pairs={{0,12},{1,13},{2,14},{3,15},{4,8},{5,9},{6,10},{7,11},{8,4},{9,5},... | collective-permute-start | bytes 147464 | tf_op jit(solution)/shard_map/ppermute | solution.py:300
  153.7 1.3 collective-permute-start.21
  155.0 1.4 collective-permute-start.22
  156.4 2.0 %collective-permute-done.20 = f32[24,512]{1,0:T(8,128)S(1)} collective-permute-done((f32[24,512]{1,0:T(8,128)S(1)}, f32[24,512]{1,0:T(8,128)S(1)}, u32[]{:S(2)}, u32[]{:S(2)}) %collective-permute-start.20) | collective-permute-done | bytes 49184 | tf_op jit(solution)/shard_map/ppermute | solution.py:300
  158.4 1.0 collective-permute-done.21
  159.5 0.7 pad_maximum_fusion
  (28 shorter events, 0.4 us)
Async XLA Ops:
  0.6 1.2 copy-start.2
  0.6 4.4 %copy-start.3 = (s32[96,96]{1,0:T(8,128)S(1)}, s32[96,96]{1,0:T(8,128)}, u32[]{:S(2)}) copy-start(s32[96,96]{1,0:T(8,128)} %refs_2_.5) | copy-start | bytes 110596
  1.9 3.6 %copy-start.4 = (f32[96,96]{1,0:T(8,128)S(1)}, f32[96,96]{1,0:T(8,128)}, u32[]{:S(2)}) copy-start(f32[96,96]{1,0:T(8,128)} %refs_3_.5) | copy-start | bytes 110596
  1.9 3.7 %copy-start.5 = (f32[96]{0:T(128)S(1)}, f32[96]{0:T(128)}, u32[]{:S(2)}) copy-start(f32[96]{0:T(128)} %refs_4_.5) | copy-start | bytes 1156
  1.9 55.7 %collective-permute-start = (bf16[1152,512]{1,0:T(8,128)(2,1)S(1)}, bf16[1152,512]{1,0:T(8,128)(2,1)}, u32[]{:S(2)}, u32[]{:S(2)}) collective-permute-start(bf16[1152,512]{1,0:T(8,128)(2,1)S(1)} %constant_dynamic-update-slice_fusion.refs_3_), channel_id=1, source_target_pairs={{0,4},{1,5},{2,0},{3,1},{4,8},{5,9},{6,2},{7,3},{8,12},{9,13},{10,... | collective-permute-start | bytes 3538952 | tf_op jit(solution)/shard_map/ppermute | solution.py:336
  5.0 52.6 %collective-permute-start.4 = (bf16[1152,512]{1,0:T(8,128)(2,1)S(1)}, bf16[1152,512]{1,0:T(8,128)(2,1)}, u32[]{:S(2)}, u32[]{:S(2)}) collective-permute-start(bf16[1152,512]{1,0:T(8,128)(2,1)S(1)} %constant_dynamic-update-slice_fusion.refs_3_), channel_id=1, source_target_pairs={{4,0},{5,1},{0,2},{1,3},{8,4},{9,5},{2,6},{3,7},{12,8},{13,9},{6,1... | collective-permute-start | bytes 3538952 | tf_op jit(solution)/shard_map/ppermute | solution.py:336
  5.0 70.9 %collective-permute-start.2 = (bf16[1152,512]{1,0:T(8,128)(2,1)S(1)}, bf16[1152,512]{1,0:T(8,128)(2,1)}, u32[]{:S(2)}, u32[]{:S(2)}) collective-permute-start(bf16[1152,512]{1,0:T(8,128)(2,1)S(1)} %constant_dynamic-update-slice_fusion.refs_3_), channel_id=1, source_target_pairs={{0,1},{1,0},{2,3},{3,2},{4,5},{5,4},{6,7},{7,6},{8,9},{9,8},{10,11... | collective-permute-start | bytes 3538952 | tf_op jit(solution)/shard_map/ppermute | solution.py:336
  57.6 18.3 %collective-permute-start.3 = (bf16[1152,512]{1,0:T(8,128)(2,1)}, bf16[1152,512]{1,0:T(8,128)(2,1)}, u32[]{:S(2)}, u32[]{:S(2)}) collective-permute-start(bf16[1152,512]{1,0:T(8,128)(2,1)} %collective-permute-done.refs_5_), channel_id=1, source_target_pairs={{0,1},{1,0},{2,3},{3,2},{4,5},{5,4},{6,7},{7,6},{8,9},{9,8},{10,11... | collective-permute-start | bytes 3538952 | tf_op jit(solution)/shard_map/ppermute | solution.py:336
  58.2 17.7 %collective-permute-start.5 = (bf16[1152,512]{1,0:T(8,128)(2,1)}, bf16[1152,512]{1,0:T(8,128)(2,1)}, u32[]{:S(2)}, u32[]{:S(2)}) collective-permute-start(bf16[1152,512]{1,0:T(8,128)(2,1)} %collective-permute-done.4.refs_7_), channel_id=1, source_target_pairs={{0,1},{1,0},{2,3},{3,2},{4,5},{5,4},{6,7},{7,6},{8,9},{9,8},{10,11... | collective-permute-start | bytes 3538952 | tf_op jit(solution)/shard_map/ppermute | solution.py:336
  58.3 31.1 %collective-permute-start.8 = (bf16[1152,512]{1,0:T(8,128)(2,1)}, bf16[1152,512]{1,0:T(8,128)(2,1)}, u32[]{:S(2)}, u32[]{:S(2)}) collective-permute-start(bf16[1152,512]{1,0:T(8,128)(2,1)} %collective-permute-done.4.refs_7_), channel_id=1, source_target_pairs={{4,0},{5,1},{0,2},{1,3},{8,4},{9,5},{2,6},{3,7},{12,8},{13,9},{6,1... | collective-permute-start | bytes 3538952 | tf_op jit(solution)/shard_map/ppermute | solution.py:336
  60.2 29.4 %collective-permute-start.1 = (bf16[1152,512]{1,0:T(8,128)(2,1)}, bf16[1152,512]{1,0:T(8,128)(2,1)}, u32[]{:S(2)}, u32[]{:S(2)}) collective-permute-start(bf16[1152,512]{1,0:T(8,128)(2,1)} %collective-permute-done.refs_5_), channel_id=1, source_target_pairs={{0,4},{1,5},{2,0},{3,1},{4,8},{5,9},{6,2},{7,3},{8,12},{9,13},{10,... | collective-permute-start | bytes 3538952 | tf_op jit(solution)/shard_map/ppermute | solution.py:336
  89.4 3.1 %collective-permute-start.9 = (bf16[1152,512]{1,0:T(8,128)(2,1)}, bf16[1152,512]{1,0:T(8,128)(2,1)S(1)}, u32[]{:S(2)}, u32[]{:S(2)}) collective-permute-start(bf16[1152,512]{1,0:T(8,128)(2,1)} %collective-permute-done.8.refs_5_), channel_id=1, source_target_pairs={{0,1},{1,0},{2,3},{3,2},{4,5},{5,4},{6,7},{7,6},{8,9},{9,8},{10,11... | collective-permute-start | bytes 3538952 | tf_op jit(solution)/shard_map/ppermute | solution.py:336
  89.7 4.5 %collective-permute-start.7 = (bf16[1152,512]{1,0:T(8,128)(2,1)}, bf16[1152,512]{1,0:T(8,128)(2,1)S(1)}, u32[]{:S(2)}, u32[]{:S(2)}) collective-permute-start(bf16[1152,512]{1,0:T(8,128)(2,1)} %collective-permute-done.1.refs_3_), channel_id=1, source_target_pairs={{0,1},{1,0},{2,3},{3,2},{4,5},{5,4},{6,7},{7,6},{8,9},{9,8},{10,11... | collective-permute-start | bytes 3538952 | tf_op jit(solution)/shard_map/ppermute | solution.py:336
  90.0 28.4 %collective-permute-start.12 = (bf16[1152,512]{1,0:T(8,128)(2,1)}, bf16[1152,512]{1,0:T(8,128)(2,1)S(1)}, u32[]{:S(2)}, u32[]{:S(2)}) collective-permute-start(bf16[1152,512]{1,0:T(8,128)(2,1)} %collective-permute-done.8.refs_5_), channel_id=1, source_target_pairs={{4,0},{5,1},{0,2},{1,3},{8,4},{9,5},{2,6},{3,7},{12,8},{13,9},{6,1... | collective-permute-start | bytes 3538952 | tf_op jit(solution)/shard_map/ppermute | solution.py:336
  91.9 27.9 %collective-permute-start.6 = (bf16[1152,512]{1,0:T(8,128)(2,1)}, bf16[1152,512]{1,0:T(8,128)(2,1)S(1)}, u32[]{:S(2)}, u32[]{:S(2)}) collective-permute-start(bf16[1152,512]{1,0:T(8,128)(2,1)} %collective-permute-done.1.refs_3_), channel_id=1, source_target_pairs={{0,4},{1,5},{2,0},{3,1},{4,8},{5,9},{6,2},{7,3},{8,12},{9,13},{10,... | collective-permute-start | bytes 3538952 | tf_op jit(solution)/shard_map/ppermute | solution.py:336
  92.5 1.7 %copy-start.8 = (bf16[1152,512]{1,0:T(8,128)(2,1)}, bf16[1152,512]{1,0:T(8,128)(2,1)S(1)}, u32[]{:S(2)}) copy-start(bf16[1152,512]{1,0:T(8,128)(2,1)S(1)} %collective-permute-done.9.refs_6_) | copy-start | bytes 3538948
  118.4 3.2 %copy-start.6 = (bf16[1152,512]{1,0:T(8,128)(2,1)}, bf16[1152,512]{1,0:T(8,128)(2,1)S(1)}, u32[]{:S(2)}) copy-start(bf16[1152,512]{1,0:T(8,128)(2,1)S(1)} %collective-permute-done.12.refs_5_) | copy-start | bytes 3538948
  118.4 3.8 %collective-permute-start.13 = (bf16[1152,512]{1,0:T(8,128)(2,1)S(1)}, bf16[1152,512]{1,0:T(8,128)(2,1)S(1)}, u32[]{:S(2)}, u32[]{:S(2)}) collective-permute-start(bf16[1152,512]{1,0:T(8,128)(2,1)S(1)} %collective-permute-done.12.refs_5_), channel_id=1, source_target_pairs={{0,1},{1,0},{2,3},{3,2},{4,5},{5,4},{6,7},{7,6},{8,9},{9,8},{10,11... | collective-permute-start | bytes 3538952 | tf_op jit(solution)/shard_map/ppermute | solution.py:336
  119.8 3.1 %collective-permute-start.11 = (bf16[1152,512]{1,0:T(8,128)(2,1)S(1)}, bf16[1152,512]{1,0:T(8,128)(2,1)S(1)}, u32[]{:S(2)}, u32[]{:S(2)}) collective-permute-start(bf16[1152,512]{1,0:T(8,128)(2,1)S(1)} %collective-permute-done.6.refs_3_), channel_id=1, source_target_pairs={{0,1},{1,0},{2,3},{3,2},{4,5},{5,4},{6,7},{7,6},{8,9},{9,8},{10,11... | collective-permute-start | bytes 3538952 | tf_op jit(solution)/shard_map/ppermute | solution.py:336
  119.8 15.8 %collective-permute-start.14 = (bf16[576,512]{1,0:T(8,128)(2,1)S(1)}, bf16[576,512]{1,0:T(8,128)(2,1)S(1)}, u32[]{:S(2)}, u32[]{:S(2)}) collective-permute-start(bf16[576,512]{1,0:T(8,128)(2,1)S(1)} %slice.7), channel_id=1, source_target_pairs={{4,0},{5,1},{0,2},{1,3},{8,4},{9,5},{2,6},{3,7},{12,8},{13,9},{6,1... | collective-permute-start | bytes 1769480 | tf_op jit(solution)/shard_map/ppermute | solution.py:336
  121.6 15.7 %collective-permute-start.10 = (bf16[576,512]{1,0:T(8,128)(2,1)S(1)}, bf16[576,512]{1,0:T(8,128)(2,1)S(1)}, u32[]{:S(2)}, u32[]{:S(2)}) collective-permute-start(bf16[576,512]{1,0:T(8,128)(2,1)S(1)} %slice.6), channel_id=1, source_target_pairs={{0,4},{1,5},{2,0},{3,1},{4,8},{5,9},{6,2},{7,3},{8,12},{9,13},{10,... | collective-permute-start | bytes 1769480 | tf_op jit(solution)/shard_map/ppermute | solution.py:336
  122.2 1.0 copy-start.7
  123.2 16.1 %copy-start.1 = (bf16[576,512]{1,0:T(8,128)(2,1)S(1)}, bf16[576,512]{1,0:T(8,128)(2,1)}, u32[]{:S(2)}) copy-start(bf16[576,512]{1,0:T(8,128)(2,1)} %refs_10_.1) | copy-start | bytes 1769476
  132.7 1.1 copy-start
  135.6 2.0 %collective-permute-start.16 = (bf16[576,512]{1,0:T(8,128)(2,1)S(1)}, bf16[576,512]{1,0:T(8,128)(2,1)S(1)}, u32[]{:S(2)}, u32[]{:S(2)}) collective-permute-start(bf16[576,512]{1,0:T(8,128)(2,1)S(1)} %collective-permute-done.14.refs_4_), channel_id=1, source_target_pairs={{0,1},{1,0},{2,3},{3,2},{4,5},{5,4},{6,7},{7,6},{8,9},{9,8},{10,11... | collective-permute-start | bytes 1769480 | tf_op jit(solution)/shard_map/ppermute | solution.py:336
  137.3 2.0 %collective-permute-start.15 = (bf16[576,512]{1,0:T(8,128)(2,1)S(1)}, bf16[576,512]{1,0:T(8,128)(2,1)S(1)}, u32[]{:S(2)}, u32[]{:S(2)}) collective-permute-start(bf16[576,512]{1,0:T(8,128)(2,1)S(1)} %collective-permute-done.10.refs_3_), channel_id=1, source_target_pairs={{0,1},{1,0},{2,3},{3,2},{4,5},{5,4},{6,7},{7,6},{8,9},{9,8},{10,11... | collective-permute-start | bytes 1769480 | tf_op jit(solution)/shard_map/ppermute | solution.py:336
  146.8 3.2 %collective-permute-start.17 = (f32[6,512]{1,0:T(8,128)S(1)}, f32[6,512]{1,0:T(8,128)S(1)}, u32[]{:S(2)}, u32[]{:S(2)}) collective-permute-start(f32[6,512]{1,0:T(8,128)S(1)} %get-tuple-element.68), channel_id=1, source_target_pairs={{0,3},{1,2},{2,1},{3,0},{4,7},{5,6},{6,5},{7,4},{8,11},{9,10},{10,... | collective-permute-start | bytes 36872 | tf_op jit(solution)/shard_map/ppermute | solution.py:300
  148.1 3.8 %collective-permute-start.18 = (f32[6,512]{1,0:T(8,128)S(1)}, f32[6,512]{1,0:T(8,128)S(1)}, u32[]{:S(2)}, u32[]{:S(2)}) collective-permute-start(f32[6,512]{1,0:T(8,128)S(1)} %get-tuple-element.68), channel_id=1, source_target_pairs={{0,2},{1,3},{2,0},{3,1},{4,6},{5,7},{6,4},{7,5},{8,10},{9,11},{10,... | collective-permute-start | bytes 36872 | tf_op jit(solution)/shard_map/ppermute | solution.py:300
  148.5 3.4 %collective-permute-start.19 = (f32[6,512]{1,0:T(8,128)S(1)}, f32[6,512]{1,0:T(8,128)S(1)}, u32[]{:S(2)}, u32[]{:S(2)}) collective-permute-start(f32[6,512]{1,0:T(8,128)S(1)} %get-tuple-element.68), channel_id=1, source_target_pairs={{0,1},{1,0},{2,3},{3,2},{4,5},{5,4},{6,7},{7,6},{8,9},{9,8},{10,11... | collective-permute-start | bytes 36872 | tf_op jit(solution)/shard_map/ppermute | solution.py:300
  151.9 6.5 %collective-permute-start.20 = (f32[24,512]{1,0:T(8,128)S(1)}, f32[24,512]{1,0:T(8,128)S(1)}, u32[]{:S(2)}, u32[]{:S(2)}) collective-permute-start(f32[24,512]{1,0:T(8,128)S(1)} %pad_maximum_fusion.1), channel_id=1, source_target_pairs={{0,12},{1,13},{2,14},{3,15},{4,8},{5,9},{6,10},{7,11},{8,4},{9,5},... | collective-permute-start | bytes 147464 | tf_op jit(solution)/shard_map/ppermute | solution.py:300
  153.7 5.7 %collective-permute-start.21 = (f32[24,512]{1,0:T(8,128)S(1)}, f32[24,512]{1,0:T(8,128)S(1)}, u32[]{:S(2)}, u32[]{:S(2)}) collective-permute-start(f32[24,512]{1,0:T(8,128)S(1)} %pad_maximum_fusion.1), channel_id=1, source_target_pairs={{0,8},{1,9},{2,10},{3,11},{4,12},{5,13},{6,14},{7,15},{8,0},{9,1},... | collective-permute-start | bytes 147464 | tf_op jit(solution)/shard_map/ppermute | solution.py:300
  155.0 4.5 %collective-permute-start.22 = (f32[24,512]{1,0:T(8,128)S(1)}, f32[24,512]{1,0:T(8,128)S(1)}, u32[]{:S(2)}, u32[]{:S(2)}) collective-permute-start(f32[24,512]{1,0:T(8,128)S(1)} %pad_maximum_fusion.1), channel_id=1, source_target_pairs={{0,4},{1,5},{2,6},{3,7},{4,0},{5,1},{6,2},{7,3},{8,12},{9,13},{10,... | collective-permute-start | bytes 147464 | tf_op jit(solution)/shard_map/ppermute | solution.py:300

commit v4 on v3

--- a/solution.py
+++ b/solution.py
@@ -70,29 +70,28 @@
     return (new_same, new_opp, next_same, next_opp, collision)
 
 
-def turn(unit, block):
-    return lax.dot_general(
-        unit, block, (((1,), (1,)), ((), ())), preferred_element_type=jnp.float32
-    )
-
-
 def build_body(orbitals, low, high, pairs, *refs):
     place_ref, inter_ref, pat_ref, hop_ref, occ_ref = refs[:5]
-    pat4_ref, hop4_ref, eye4_ref, occ4_ref, unit_ref = refs[5:10]
+    pat4_ref, hop4_ref, eye4_ref, occ4_ref = refs[5:9]
     mixed_ref, polar_ref, turned_ref = refs[-3:]
     span = 4 * orbitals
     tiles = pairs // span
     start = place_ref[0]
     strips = range(0, high - low, 128)
 
-    @pl.loop(0, tiles)
+    pitch = orbitals + 1
+    room = orbitals * pitch
+
+    @pl.loop(0, tiles // 2)
     def _(tile):
-        cols = pl.ds(pl.multiple_of(tile * span, 128), span)
-        turned = turn(unit_ref[...], inter_ref[:, cols])
+        cols = pl.ds(pl.multiple_of(tile * 2 * span, 128), 2 * span)
         for strip in strips:
             size = min(128, high - low - strip)
-            at = strip // 128 * pairs + tile * span
-            turned_ref[pl.ds(pl.multiple_of(at, 128), span), :size] = turned[:, strip : strip + size]
+            turned = inter_ref[strip : strip + size, cols].astype(jnp.float32).T
+            at = pl.multiple_of(strip // 128 * room + tile * 8 * pitch, 8)
+            for m in range(8):
+                there = pl.ds(at + m * pitch, orbitals)
+                turned_ref[there, :size] = turned[m * orbitals : (m + 1) * orbitals]
 
     group = lax.broadcasted_iota(jnp.int32, (1, span), 1) // orbitals
     occ4 = occ4_ref[...]
@@ -117,18 +116,17 @@
             unit = (group + 4 * tile == here).astype(jnp.float32)
             linked4 = pat4_ref[pl.ds(here, 1), :]
             facts[first] = (linked * polar_factor, linked4 * ladder_factor, hop_row, unit)
-        sides = []
+        blocks = []
         for strip in strips:
             size = min(128, high - low - strip)
             pieces = [
                 turned_ref[
-                    pl.ds(strip // 128 * pairs + 4 * tile + m, orbitals, stride=orbitals), :
+                    pl.ds(strip // 128 * room + 4 * tile + m, orbitals, stride=pitch), :
                 ]
                 for m in range(4)
             ]
-            sides.append(jnp.concatenate(pieces, axis=0)[:, :size].astype(jnp.bfloat16))
-        side = jnp.concatenate(sides, axis=1)
-        block = turn(unit_ref[: high - low, : high - low], side)
+            blocks.append(jnp.concatenate(pieces, axis=0).T[:size])
+        block = jnp.concatenate(blocks, axis=0)
         row = low
         while row < high:
             first, second = row // orbitals, row % orbitals
@@ -161,19 +159,18 @@
     smem = pl.BlockSpec(memory_space=pltpu.SMEM)
     row4 = pl.BlockSpec((1, 4 * orbitals), lambda g, p: (0, 0))
     small = pl.BlockSpec((orbitals, 4 * orbitals), lambda g, p: (0, 0))
-    square = pl.BlockSpec((4 * orbitals, 4 * orbitals), lambda g, p: (0, 0))
     return pl.pallas_call(
         functools.partial(build_body, orbitals, low, high, pairs),
         grid_spec=pltpu.PrefetchScalarGridSpec(
             num_scalar_prefetch=1,
             grid=(1,),
-            in_specs=[wide, smem, smem, smem, small, small, small, row4, square]
+            in_specs=[wide, smem, smem, smem, small, small, small, row4]
             + [pl.BlockSpec(memory_space=pl.ANY)] * len(made),
             out_specs=[wide] * 2,
-            scratch_shapes=[pltpu.VMEM((-(-height // 128) * pairs, 128), jnp.float32)],
+            scratch_shapes=[pltpu.VMEM((-(-height // 128) * orbitals * (orbitals + 1), 128), jnp.float32)],
         ),
         out_shape=[shape] * 2,
-        input_output_aliases={10 + n: n for n in range(len(made))},
+        input_output_aliases={9 + n: n for n in range(len(made))},
         compiler_params=pltpu.CompilerParams(vmem_limit_bytes=44 * MIB),
         cost_estimate=pl.CostEstimate(flops=1024, bytes_accessed=1024, transcendentals=0),
         name="build_rows",
@@ -349,7 +346,6 @@
         jnp.tile(hopping, (1, 4)),
         jnp.tile(jnp.eye(orbitals, dtype=jnp.float32), (1, 4)),
         jnp.tile(occupation, 4)[None],
-        jnp.eye(4 * orbitals, dtype=jnp.bfloat16),
     )
     big = rows // 9 * 4
     mats = build_rows(start, interaction, smalls, (), 0, big)

time: 160 us -> 134 us (0.84)
  Pallas kernels: 107 us -> 76 us
  waiting for transfers between devices: 30.5 us -> 36 us
    pallas_call x3, Pallas kernels: 66.7 us -> 36.1 us  [build_rows(): pl.pallas_call(functools.partial(build_body, orbitals, low, high, pairs),...]
    ppermute x17, waiting for transfers between devices: 24.1 us -> 30.3 us  [send(): return lax.ppermute(block, 'prow', pairs_of)]
  transfers between devices with their start and end apart: 23 -> 23, of which waited for: 13 -> 14; matrix products, arithmetic and copies ran while one was open for 1% -> 1% of each run, Pallas kernels for 62% -> 51%
where the time goes in v4:
time: 134 us
  Pallas kernels  76 us (57%)
  waiting for transfers between devices  36 us (27%)
  starting transfers between devices  16.4 us (12%)
  local copies, waits for them, and re-layouts  3.72 us (3%)
    pallas_call x4, Pallas kernels, step(): pl.pallas_call(functools.partial(step_body, parts, rows, opening, closing...  39.9 us
    pallas_call x3, Pallas kernels, build_rows(): pl.pallas_call(functools.partial(build_body, orbitals, low, high, pairs),...  36.1 us
    ppermute x17, waiting for transfers between devices, send(): return lax.ppermute(block, 'prow', pairs_of)  30.3 us
    ppermute x17, starting transfers between devices, send(): return lax.ppermute(block, 'prow', pairs_of)  10.1 us
    ppermute x6, starting transfers between devices, spread_blocks(): blocks.append(lax.ppermute(block, 'prow', pairs_of))  6.31 us
    ppermute x6, waiting for transfers between devices, spread_blocks(): blocks.append(lax.ppermute(block, 'prow', pairs_of))  5.73 us
  transfers between devices with their start and end apart: 23, of which 14 were waited for; matrix products, arithmetic and copies ran while one was open for 1% of the time, Pallas kernels for 51%

profile of v4, /device:TPU:0, one launch (start us, length us, event | category | flops | bytes accessed | tf_op | source)
XLA Modules:
  0.0 133.9 jit_solution(2921534960440395205)
XLA Ops:
  0.7 1.2 constant_dynamic-update-slice_fusion.1
  1.8 0.1 copy-done.2
  1.9 0.0 copy-start.5
  1.9 3.1 %collective-permute-start = (bf16[1152,512]{1,0:T(8,128)(2,1)S(1)}, bf16[1152,512]{1,0:T(8,128)(2,1)}, u32[]{:S(2)}, u32[]{:S(2)}) collective-permute-start(bf16[1152,512]{1,0:T(8,128)(2,1)S(1)} %constant_dynamic-update-slice_fusion.refs_3_), channel_id=1, source_target_pairs={{0,4},{1,5},{2,0},{3,1},{4,8},{5,9},{6,2},{7,3},{8,12},{9,13},{10,... | collective-permute-start | bytes 3538952 | tf_op jit(solution)/shard_map/ppermute | solution.py:333
  5.0 0.0 collective-permute-start.4
  5.0 0.0 collective-permute-start.2
  5.1 0.1 tile.42.refs_5_
  5.3 0.1 tile.46.refs_7_
  5.5 0.1 tile.44.refs_6_
  5.7 0.1 broadcast_in_dim_tile.3.refs_8_
  5.7 13.8 %build_rows.3 = (bf16[576,9216]{1,0:T(8,128)(2,1)}, bf16[576,9216]{1,0:T(8,128)(2,1)}) custom-call(s32[1]{0:T(128)} %bitcast.2.refs_0_, bf16[576,9216]{1,0:T(8,128)(2,1)} %refs_1_.5, s32[96,96]{1,0:T(8,128)S(1)} %copy-done.3, f32[96,96]{1,0:T(8,128)S(1)} %copy-done.4, f32[96]{0:T(128)S(1)} %copy-done.5, f32[96,384]{1,0:T(8,128)S(1)} %tile.42.refs_5_, ...), custom_call_target="tpu_custom_call" | custom-call | flops 1024 | bytes 1024 | tf_op jit(solution)/shard_map/build_rows/pallas_call | solution.py:162
  19.6 14.0 %build_rows.4 = (bf16[576,9216]{1,0:T(8,128)(2,1)}, bf16[576,9216]{1,0:T(8,128)(2,1)}) custom-call(s32[1]{0:T(128)} %bitcast.2.refs_0_, bf16[576,9216]{1,0:T(8,128)(2,1)} %refs_1_.5, s32[96,96]{1,0:T(8,128)S(1)} %copy-done.3, f32[96,96]{1,0:T(8,128)S(1)} %copy-done.4, f32[96]{0:T(128)S(1)} %copy-done.5, ...), custom_call_target="tpu_custom_call", output_to_operand_aliasing={{0}: (9, {}), {1}: (10, {})} | custom-call | flops 1024 | bytes 1024 | tf_op jit(solution)/shard_map/build_rows/pallas_call | solution.py:162
  33.6 0.0 collective-permute-done.refs_5_
  33.6 0.0 collective-permute-done.4.refs_7_
  33.6 0.6 collective-permute-start.3
  34.2 0.1 collective-permute-start.5
  34.3 2.0 %collective-permute-start.8 = (bf16[1152,512]{1,0:T(8,128)(2,1)}, bf16[1152,512]{1,0:T(8,128)(2,1)}, u32[]{:S(2)}, u32[]{:S(2)}) collective-permute-start(bf16[1152,512]{1,0:T(8,128)(2,1)} %collective-permute-done.4.refs_7_), channel_id=1, source_target_pairs={{4,0},{5,1},{0,2},{1,3},{8,4},{9,5},{2,6},{3,7},{12,8},{13,9},{6,1... | collective-permute-start | bytes 3538952 | tf_op jit(solution)/shard_map/ppermute | solution.py:333
  36.2 0.1 collective-permute-start.1
  36.3 0.7 dynamic-slice_bitcast_fusion
  37.0 0.1 pad_add_fusion.refs_0_
  37.1 8.2 %build_rows.5 = (bf16[576,9216]{1,0:T(8,128)(2,1)}, bf16[576,9216]{1,0:T(8,128)(2,1)}) custom-call(s32[1]{0:T(128)} %bitcast.2.refs_0_, bf16[576,9216]{1,0:T(8,128)(2,1)} %refs_1_.5, s32[96,96]{1,0:T(8,128)S(1)} %copy-done.3, f32[96,96]{1,0:T(8,128)S(1)} %copy-done.4, f32[96]{0:T(128)S(1)} %copy-done.5, ...), custom_call_target="tpu_custom_call", output_to_operand_aliasing={{0}: (9, {}), {1}: (10, {})} | custom-call | flops 1024 | bytes 1024 | tf_op jit(solution)/shard_map/build_rows/pallas_call | solution.py:162
  45.3 0.0 collective-permute-done.2.refs_4_
  45.3 0.0 collective-permute-done.3.refs_6_
  45.3 0.0 collective-permute-done.5.refs_8_
  45.3 13.4 %add_products.4 = (f32[576,512]{1,0:T(8,128)S(1)}, f32[576,512]{1,0:T(8,128)S(1)}, f32[576,512]{1,0:T(8,128)S(1)}) custom-call(s32[10]{0:T(128)S(1)} %pad_add_fusion.refs_0_, bf16[576,9216]{1,0:T(8,128)(2,1)} %get-tuple-element.43.refs_1_, bf16[576,9216]{1,0:T(8,128)(2,1)} %get-tuple-element.44.refs_2_, ...), custom_call_target="tpu_custom_call" | custom-call | flops 1024 | bytes 1024 | tf_op jit(solution)/shard_map/add_products/pallas_call | solution.py:274
  58.7 4.4 %collective-permute-done.8.refs_5_ = bf16[1152,512]{1,0:T(8,128)(2,1)} collective-permute-done((bf16[1152,512]{1,0:T(8,128)(2,1)}, bf16[1152,512]{1,0:T(8,128)(2,1)}, u32[]{:S(2)}, u32[]{:S(2)}) %collective-permute-start.8) | collective-permute-done | bytes 1179680 | tf_op jit(solution)/shard_map/ppermute | solution.py:333
  63.2 0.0 collective-permute-start.9
  63.2 1.3 collective-permute-done.1.refs_3_
  64.5 0.0 collective-permute-start.7
  64.5 1.6 %collective-permute-start.12 = (bf16[1152,512]{1,0:T(8,128)(2,1)}, bf16[1152,512]{1,0:T(8,128)(2,1)S(1)}, u32[]{:S(2)}, u32[]{:S(2)}) collective-permute-start(bf16[1152,512]{1,0:T(8,128)(2,1)} %collective-permute-done.8.refs_5_), channel_id=1, source_target_pairs={{4,0},{5,1},{0,2},{1,3},{8,4},{9,5},{2,6},{3,7},{12,8},{13,9},{6,1... | collective-permute-start | bytes 3538952 | tf_op jit(solution)/shard_map/ppermute | solution.py:333
  66.1 0.4 collective-permute-start.6
  66.5 0.0 collective-permute-done.9.refs_6_
  66.5 1.2 collective-permute-done.7.refs_4_
  67.7 9.5 %add_products.5 = (f32[576,512]{1,0:T(8,128)S(1)}, f32[576,512]{1,0:T(8,128)S(1)}, f32[576,512]{1,0:T(8,128)S(1)}) custom-call(s32[10]{0:T(128)S(1)} %pad_add_fusion.refs_0_, bf16[576,9216]{1,0:T(8,128)(2,1)} %get-tuple-element.43.refs_1_, bf16[576,9216]{1,0:T(8,128)(2,1)} %get-tuple-element.44.refs_2_, ...), custom_call_target="tpu_custom_call", output_to_operand_aliasing={{0}: (7, {}), {1}: (8, {}), {2}: (9, {})} | custom-call | flops 1024 | bytes 1024 | tf_op jit(solution)/shard_map/add_products/pallas_call | solution.py:274
  77.2 15.9 %collective-permute-done.12.refs_5_ = bf16[1152,512]{1,0:T(8,128)(2,1)S(1)} collective-permute-done((bf16[1152,512]{1,0:T(8,128)(2,1)}, bf16[1152,512]{1,0:T(8,128)(2,1)S(1)}, u32[]{:S(2)}, u32[]{:S(2)}) %collective-permute-start.12) | collective-permute-done | bytes 1179680 | tf_op jit(solution)/shard_map/ppermute | solution.py:333
  93.1 0.0 collective-permute-start.13
  93.1 1.1 collective-permute-done.6.refs_3_
  94.2 0.0 collective-permute-start.11
  94.2 1.6 %collective-permute-start.14 = (bf16[576,512]{1,0:T(8,128)(2,1)S(1)}, bf16[576,512]{1,0:T(8,128)(2,1)S(1)}, u32[]{:S(2)}, u32[]{:S(2)}) collective-permute-start(bf16[576,512]{1,0:T(8,128)(2,1)S(1)} %slice.7), channel_id=1, source_target_pairs={{4,0},{5,1},{0,2},{1,3},{8,4},{9,5},{2,6},{3,7},{12,8},{13,9},{6,1... | collective-permute-start | bytes 1769480 | tf_op jit(solution)/shard_map/ppermute | solution.py:333
  95.9 0.7 collective-permute-start.10
  96.6 0.0 collective-permute-done.13.refs_6_
  96.6 1.0 collective-permute-done.11.refs_4_
  97.6 9.5 %add_products.6 = (f32[576,512]{1,0:T(8,128)S(1)}, f32[576,512]{1,0:T(8,128)S(1)}, f32[576,512]{1,0:T(8,128)S(1)}) custom-call(s32[10]{0:T(128)S(1)} %pad_add_fusion.refs_0_, bf16[576,9216]{1,0:T(8,128)(2,1)} %get-tuple-element.43.refs_1_, bf16[576,9216]{1,0:T(8,128)(2,1)} %get-tuple-element.44.refs_2_, ...), custom_call_target="tpu_custom_call", output_to_operand_aliasing={{0}: (7, {}), {1}: (8, {}), {2}: (9, {})} | custom-call | flops 1024 | bytes 1024 | tf_op jit(solution)/shard_map/add_products/pallas_call | solution.py:274
  107.1 1.0 copy-done
  108.2 1.8 %collective-permute-done.14.refs_4_ = bf16[576,512]{1,0:T(8,128)(2,1)S(1)} collective-permute-done((bf16[576,512]{1,0:T(8,128)(2,1)S(1)}, bf16[576,512]{1,0:T(8,128)(2,1)S(1)}, u32[]{:S(2)}, u32[]{:S(2)}) %collective-permute-start.14) | collective-permute-done | bytes 589856 | tf_op jit(solution)/shard_map/ppermute | solution.py:333
  110.0 0.0 collective-permute-start.16
  110.0 1.6 %collective-permute-done.10.refs_3_ = bf16[576,512]{1,0:T(8,128)(2,1)S(1)} collective-permute-done((bf16[576,512]{1,0:T(8,128)(2,1)S(1)}, bf16[576,512]{1,0:T(8,128)(2,1)S(1)}, u32[]{:S(2)}, u32[]{:S(2)}) %collective-permute-start.10) | collective-permute-done | bytes 589856 | tf_op jit(solution)/shard_map/ppermute | solution.py:333
  111.6 0.0 collective-permute-start.15
  111.6 0.4 collective-permute-done.16.refs_6_
  112.0 1.6 %collective-permute-done.15.refs_5_ = bf16[576,512]{1,0:T(8,128)(2,1)S(1)} collective-permute-done((bf16[576,512]{1,0:T(8,128)(2,1)S(1)}, bf16[576,512]{1,0:T(8,128)(2,1)S(1)}, u32[]{:S(2)}, u32[]{:S(2)}) %collective-permute-start.15) | collective-permute-done | bytes 589856 | tf_op jit(solution)/shard_map/ppermute | solution.py:333
  113.6 7.5 %add_products.7 = (f32[576,512]{1,0:T(8,128)}, f32[576,512]{1,0:T(8,128)}, bf16[576,512]{1,0:T(8,128)(2,1)}, bf16[576,512]{1,0:T(8,128)(2,1)}, f32[6,512]{1,0:T(8,128)S(1)}) custom-call(s32[10]{0:T(128)S(1)} %pad_add_fusion.refs_0_, bf16[576,9216]{1,0:T(8,128)(2,1)} %get-tuple-element.43.refs_1_, bf16[576,9216]{1,0:T(8,128)(2,1)} %get-tuple-element.44.refs_2_, ...), custom_call_target="tpu_custom_call" | custom-call | flops 1024 | bytes 1024 | tf_op jit(solution)/shard_map/add_products/pallas_call | solution.py:274
  121.0 1.3 collective-permute-start.17
  122.4 0.5 collective-permute-start.18
  122.8 0.1 collective-permute-start.19
  122.9 1.3 collective-permute-done.17
  124.2 1.9 %collective-permute-done.18 = f32[6,512]{1,0:T(8,128)S(1)} collective-permute-done((f32[6,512]{1,0:T(8,128)S(1)}, f32[6,512]{1,0:T(8,128)S(1)}, u32[]{:S(2)}, u32[]{:S(2)}) %collective-permute-start.18) | collective-permute-done | bytes 12320 | tf_op jit(solution)/shard_map/ppermute | solution.py:297
  126.1 0.0 collective-permute-done.19
  126.2 0.8 collective-permute-start.20
  127.0 1.5 %collective-permute-start.21 = (f32[24,512]{1,0:T(8,128)S(1)}, f32[24,512]{1,0:T(8,128)S(1)}, u32[]{:S(2)}, u32[]{:S(2)}) collective-permute-start(f32[24,512]{1,0:T(8,128)S(1)} %pad_maximum_fusion.1), channel_id=1, source_target_pairs={{0,8},{1,9},{2,10},{3,11},{4,12},{5,13},{6,14},{7,15},{8,0},{9,1},... | collective-permute-start | bytes 147464 | tf_op jit(solution)/shard_map/ppermute | solution.py:297
  128.5 2.1 %collective-permute-start.22 = (f32[24,512]{1,0:T(8,128)S(1)}, f32[24,512]{1,0:T(8,128)S(1)}, u32[]{:S(2)}, u32[]{:S(2)}) collective-permute-start(f32[24,512]{1,0:T(8,128)S(1)} %pad_maximum_fusion.1), channel_id=1, source_target_pairs={{0,4},{1,5},{2,6},{3,7},{4,0},{5,1},{6,2},{7,3},{8,12},{9,13},{10,... | collective-permute-start | bytes 147464 | tf_op jit(solution)/shard_map/ppermute | solution.py:297
  130.6 1.6 %collective-permute-done.20 = f32[24,512]{1,0:T(8,128)S(1)} collective-permute-done((f32[24,512]{1,0:T(8,128)S(1)}, f32[24,512]{1,0:T(8,128)S(1)}, u32[]{:S(2)}, u32[]{:S(2)}) %collective-permute-start.20) | collective-permute-done | bytes 49184 | tf_op jit(solution)/shard_map/ppermute | solution.py:297
  132.2 0.9 collective-permute-done.21
  133.1 0.0 collective-permute-done.22
  133.2 0.7 pad_maximum_fusion
  (27 shorter events, 0.3 us)
Async XLA Ops:
  0.6 1.2 copy-start.2
  0.6 4.4 %copy-start.3 = (s32[96,96]{1,0:T(8,128)S(1)}, s32[96,96]{1,0:T(8,128)}, u32[]{:S(2)}) copy-start(s32[96,96]{1,0:T(8,128)} %refs_2_.5) | copy-start | bytes 110596
  1.9 3.6 %copy-start.4 = (f32[96,96]{1,0:T(8,128)S(1)}, f32[96,96]{1,0:T(8,128)}, u32[]{:S(2)}) copy-start(f32[96,96]{1,0:T(8,128)} %refs_3_.5) | copy-start | bytes 110596
  1.9 3.7 %copy-start.5 = (f32[96]{0:T(128)S(1)}, f32[96]{0:T(128)}, u32[]{:S(2)}) copy-start(f32[96]{0:T(128)} %refs_4_.5) | copy-start | bytes 1156
  1.9 31.7 %collective-permute-start = (bf16[1152,512]{1,0:T(8,128)(2,1)S(1)}, bf16[1152,512]{1,0:T(8,128)(2,1)}, u32[]{:S(2)}, u32[]{:S(2)}) collective-permute-start(bf16[1152,512]{1,0:T(8,128)(2,1)S(1)} %constant_dynamic-update-slice_fusion.refs_3_), channel_id=1, source_target_pairs={{0,4},{1,5},{2,0},{3,1},{4,8},{5,9},{6,2},{7,3},{8,12},{9,13},{10,... | collective-permute-start | bytes 3538952 | tf_op jit(solution)/shard_map/ppermute | solution.py:333
  5.0 28.6 %collective-permute-start.4 = (bf16[1152,512]{1,0:T(8,128)(2,1)S(1)}, bf16[1152,512]{1,0:T(8,128)(2,1)}, u32[]{:S(2)}, u32[]{:S(2)}) collective-permute-start(bf16[1152,512]{1,0:T(8,128)(2,1)S(1)} %constant_dynamic-update-slice_fusion.refs_3_), channel_id=1, source_target_pairs={{4,0},{5,1},{0,2},{1,3},{8,4},{9,5},{2,6},{3,7},{12,8},{13,9},{6,1... | collective-permute-start | bytes 3538952 | tf_op jit(solution)/shard_map/ppermute | solution.py:333
  5.0 40.3 %collective-permute-start.2 = (bf16[1152,512]{1,0:T(8,128)(2,1)S(1)}, bf16[1152,512]{1,0:T(8,128)(2,1)}, u32[]{:S(2)}, u32[]{:S(2)}) collective-permute-start(bf16[1152,512]{1,0:T(8,128)(2,1)S(1)} %constant_dynamic-update-slice_fusion.refs_3_), channel_id=1, source_target_pairs={{0,1},{1,0},{2,3},{3,2},{4,5},{5,4},{6,7},{7,6},{8,9},{9,8},{10,11... | collective-permute-start | bytes 3538952 | tf_op jit(solution)/shard_map/ppermute | solution.py:333
  33.6 11.7 %collective-permute-start.3 = (bf16[1152,512]{1,0:T(8,128)(2,1)}, bf16[1152,512]{1,0:T(8,128)(2,1)}, u32[]{:S(2)}, u32[]{:S(2)}) collective-permute-start(bf16[1152,512]{1,0:T(8,128)(2,1)} %collective-permute-done.refs_5_), channel_id=1, source_target_pairs={{0,1},{1,0},{2,3},{3,2},{4,5},{5,4},{6,7},{7,6},{8,9},{9,8},{10,11... | collective-permute-start | bytes 3538952 | tf_op jit(solution)/shard_map/ppermute | solution.py:333
  34.2 11.1 %collective-permute-start.5 = (bf16[1152,512]{1,0:T(8,128)(2,1)}, bf16[1152,512]{1,0:T(8,128)(2,1)}, u32[]{:S(2)}, u32[]{:S(2)}) collective-permute-start(bf16[1152,512]{1,0:T(8,128)(2,1)} %collective-permute-done.4.refs_7_), channel_id=1, source_target_pairs={{0,1},{1,0},{2,3},{3,2},{4,5},{5,4},{6,7},{7,6},{8,9},{9,8},{10,11... | collective-permute-start | bytes 3538952 | tf_op jit(solution)/shard_map/ppermute | solution.py:333
  34.3 28.9 %collective-permute-start.8 = (bf16[1152,512]{1,0:T(8,128)(2,1)}, bf16[1152,512]{1,0:T(8,128)(2,1)}, u32[]{:S(2)}, u32[]{:S(2)}) collective-permute-start(bf16[1152,512]{1,0:T(8,128)(2,1)} %collective-permute-done.4.refs_7_), channel_id=1, source_target_pairs={{4,0},{5,1},{0,2},{1,3},{8,4},{9,5},{2,6},{3,7},{12,8},{13,9},{6,1... | collective-permute-start | bytes 3538952 | tf_op jit(solution)/shard_map/ppermute | solution.py:333
  36.2 28.2 %collective-permute-start.1 = (bf16[1152,512]{1,0:T(8,128)(2,1)}, bf16[1152,512]{1,0:T(8,128)(2,1)S(1)}, u32[]{:S(2)}, u32[]{:S(2)}) collective-permute-start(bf16[1152,512]{1,0:T(8,128)(2,1)} %collective-permute-done.refs_5_), channel_id=1, source_target_pairs={{0,4},{1,5},{2,0},{3,1},{4,8},{5,9},{6,2},{7,3},{8,12},{9,13},{10,... | collective-permute-start | bytes 3538952 | tf_op jit(solution)/shard_map/ppermute | solution.py:333
  63.2 3.4 %collective-permute-start.9 = (bf16[1152,512]{1,0:T(8,128)(2,1)}, bf16[1152,512]{1,0:T(8,128)(2,1)S(1)}, u32[]{:S(2)}, u32[]{:S(2)}) collective-permute-start(bf16[1152,512]{1,0:T(8,128)(2,1)} %collective-permute-done.8.refs_5_), channel_id=1, source_target_pairs={{0,1},{1,0},{2,3},{3,2},{4,5},{5,4},{6,7},{7,6},{8,9},{9,8},{10,11... | collective-permute-start | bytes 3538952 | tf_op jit(solution)/shard_map/ppermute | solution.py:333
  64.5 3.2 %collective-permute-start.7 = (bf16[1152,512]{1,0:T(8,128)(2,1)S(1)}, bf16[1152,512]{1,0:T(8,128)(2,1)S(1)}, u32[]{:S(2)}, u32[]{:S(2)}) collective-permute-start(bf16[1152,512]{1,0:T(8,128)(2,1)S(1)} %collective-permute-done.1.refs_3_), channel_id=1, source_target_pairs={{0,1},{1,0},{2,3},{3,2},{4,5},{5,4},{6,7},{7,6},{8,9},{9,8},{10,11... | collective-permute-start | bytes 3538952 | tf_op jit(solution)/shard_map/ppermute | solution.py:333
  64.5 28.6 %collective-permute-start.12 = (bf16[1152,512]{1,0:T(8,128)(2,1)}, bf16[1152,512]{1,0:T(8,128)(2,1)S(1)}, u32[]{:S(2)}, u32[]{:S(2)}) collective-permute-start(bf16[1152,512]{1,0:T(8,128)(2,1)} %collective-permute-done.8.refs_5_), channel_id=1, source_target_pairs={{4,0},{5,1},{0,2},{1,3},{8,4},{9,5},{2,6},{3,7},{12,8},{13,9},{6,1... | collective-permute-start | bytes 3538952 | tf_op jit(solution)/shard_map/ppermute | solution.py:333
  66.1 28.1 %collective-permute-start.6 = (bf16[1152,512]{1,0:T(8,128)(2,1)S(1)}, bf16[1152,512]{1,0:T(8,128)(2,1)S(1)}, u32[]{:S(2)}, u32[]{:S(2)}) collective-permute-start(bf16[1152,512]{1,0:T(8,128)(2,1)S(1)} %collective-permute-done.1.refs_3_), channel_id=1, source_target_pairs={{0,4},{1,5},{2,0},{3,1},{4,8},{5,9},{6,2},{7,3},{8,12},{9,13},{10,... | collective-permute-start | bytes 3538952 | tf_op jit(solution)/shard_map/ppermute | solution.py:333
  66.5 1.2 copy-start.8
  93.1 2.8 %copy-start.6 = (bf16[1152,512]{1,0:T(8,128)(2,1)}, bf16[1152,512]{1,0:T(8,128)(2,1)S(1)}, u32[]{:S(2)}) copy-start(bf16[1152,512]{1,0:T(8,128)(2,1)S(1)} %collective-permute-done.12.refs_5_) | copy-start | bytes 3538948
  93.1 3.5 %collective-permute-start.13 = (bf16[1152,512]{1,0:T(8,128)(2,1)S(1)}, bf16[1152,512]{1,0:T(8,128)(2,1)S(1)}, u32[]{:S(2)}, u32[]{:S(2)}) collective-permute-start(bf16[1152,512]{1,0:T(8,128)(2,1)S(1)} %collective-permute-done.12.refs_5_), channel_id=1, source_target_pairs={{0,1},{1,0},{2,3},{3,2},{4,5},{5,4},{6,7},{7,6},{8,9},{9,8},{10,11... | collective-permute-start | bytes 3538952 | tf_op jit(solution)/shard_map/ppermute | solution.py:333
  94.2 3.5 %collective-permute-start.11 = (bf16[1152,512]{1,0:T(8,128)(2,1)S(1)}, bf16[1152,512]{1,0:T(8,128)(2,1)S(1)}, u32[]{:S(2)}, u32[]{:S(2)}) collective-permute-start(bf16[1152,512]{1,0:T(8,128)(2,1)S(1)} %collective-permute-done.6.refs_3_), channel_id=1, source_target_pairs={{0,1},{1,0},{2,3},{3,2},{4,5},{5,4},{6,7},{7,6},{8,9},{9,8},{10,11... | collective-permute-start | bytes 3538952 | tf_op jit(solution)/shard_map/ppermute | solution.py:333
  94.2 15.8 %collective-permute-start.14 = (bf16[576,512]{1,0:T(8,128)(2,1)S(1)}, bf16[576,512]{1,0:T(8,128)(2,1)S(1)}, u32[]{:S(2)}, u32[]{:S(2)}) collective-permute-start(bf16[576,512]{1,0:T(8,128)(2,1)S(1)} %slice.7), channel_id=1, source_target_pairs={{4,0},{5,1},{0,2},{1,3},{8,4},{9,5},{2,6},{3,7},{12,8},{13,9},{6,1... | collective-permute-start | bytes 1769480 | tf_op jit(solution)/shard_map/ppermute | solution.py:333
  95.9 15.7 %collective-permute-start.10 = (bf16[576,512]{1,0:T(8,128)(2,1)S(1)}, bf16[576,512]{1,0:T(8,128)(2,1)S(1)}, u32[]{:S(2)}, u32[]{:S(2)}) collective-permute-start(bf16[576,512]{1,0:T(8,128)(2,1)S(1)} %slice.6), channel_id=1, source_target_pairs={{0,4},{1,5},{2,0},{3,1},{4,8},{5,9},{6,2},{7,3},{8,12},{9,13},{10,... | collective-permute-start | bytes 1769480 | tf_op jit(solution)/shard_map/ppermute | solution.py:333
  96.6 1.0 copy-start.7
  97.6 16.0 %copy-start.1 = (bf16[576,512]{1,0:T(8,128)(2,1)S(1)}, bf16[576,512]{1,0:T(8,128)(2,1)}, u32[]{:S(2)}) copy-start(bf16[576,512]{1,0:T(8,128)(2,1)} %refs_10_.1) | copy-start | bytes 1769476
  107.1 1.1 copy-start
  110.0 2.0 %collective-permute-start.16 = (bf16[576,512]{1,0:T(8,128)(2,1)S(1)}, bf16[576,512]{1,0:T(8,128)(2,1)S(1)}, u32[]{:S(2)}, u32[]{:S(2)}) collective-permute-start(bf16[576,512]{1,0:T(8,128)(2,1)S(1)} %collective-permute-done.14.refs_4_), channel_id=1, source_target_pairs={{0,1},{1,0},{2,3},{3,2},{4,5},{5,4},{6,7},{7,6},{8,9},{9,8},{10,11... | collective-permute-start | bytes 1769480 | tf_op jit(solution)/shard_map/ppermute | solution.py:333
  111.6 2.0 %collective-permute-start.15 = (bf16[576,512]{1,0:T(8,128)(2,1)S(1)}, bf16[576,512]{1,0:T(8,128)(2,1)S(1)}, u32[]{:S(2)}, u32[]{:S(2)}) collective-permute-start(bf16[576,512]{1,0:T(8,128)(2,1)S(1)} %collective-permute-done.10.refs_3_), channel_id=1, source_target_pairs={{0,1},{1,0},{2,3},{3,2},{4,5},{5,4},{6,7},{7,6},{8,9},{9,8},{10,11... | collective-permute-start | bytes 1769480 | tf_op jit(solution)/shard_map/ppermute | solution.py:333
  121.0 3.2 %collective-permute-start.17 = (f32[6,512]{1,0:T(8,128)S(1)}, f32[6,512]{1,0:T(8,128)S(1)}, u32[]{:S(2)}, u32[]{:S(2)}) collective-permute-start(f32[6,512]{1,0:T(8,128)S(1)} %get-tuple-element.68), channel_id=1, source_target_pairs={{0,3},{1,2},{2,1},{3,0},{4,7},{5,6},{6,5},{7,4},{8,11},{9,10},{10,... | collective-permute-start | bytes 36872 | tf_op jit(solution)/shard_map/ppermute | solution.py:297
  122.4 3.8 %collective-permute-start.18 = (f32[6,512]{1,0:T(8,128)S(1)}, f32[6,512]{1,0:T(8,128)S(1)}, u32[]{:S(2)}, u32[]{:S(2)}) collective-permute-start(f32[6,512]{1,0:T(8,128)S(1)} %get-tuple-element.68), channel_id=1, source_target_pairs={{0,2},{1,3},{2,0},{3,1},{4,6},{5,7},{6,4},{7,5},{8,10},{9,11},{10,... | collective-permute-start | bytes 36872 | tf_op jit(solution)/shard_map/ppermute | solution.py:297
  122.8 3.3 %collective-permute-start.19 = (f32[6,512]{1,0:T(8,128)S(1)}, f32[6,512]{1,0:T(8,128)S(1)}, u32[]{:S(2)}, u32[]{:S(2)}) collective-permute-start(f32[6,512]{1,0:T(8,128)S(1)} %get-tuple-element.68), channel_id=1, source_target_pairs={{0,1},{1,0},{2,3},{3,2},{4,5},{5,4},{6,7},{7,6},{8,9},{9,8},{10,11... | collective-permute-start | bytes 36872 | tf_op jit(solution)/shard_map/ppermute | solution.py:297
  126.2 6.1 %collective-permute-start.20 = (f32[24,512]{1,0:T(8,128)S(1)}, f32[24,512]{1,0:T(8,128)S(1)}, u32[]{:S(2)}, u32[]{:S(2)}) collective-permute-start(f32[24,512]{1,0:T(8,128)S(1)} %pad_maximum_fusion.1), channel_id=1, source_target_pairs={{0,12},{1,13},{2,14},{3,15},{4,8},{5,9},{6,10},{7,11},{8,4},{9,5},... | collective-permute-start | bytes 147464 | tf_op jit(solution)/shard_map/ppermute | solution.py:297
  127.0 6.1 %collective-permute-start.21 = (f32[24,512]{1,0:T(8,128)S(1)}, f32[24,512]{1,0:T(8,128)S(1)}, u32[]{:S(2)}, u32[]{:S(2)}) collective-permute-start(f32[24,512]{1,0:T(8,128)S(1)} %pad_maximum_fusion.1), channel_id=1, source_target_pairs={{0,8},{1,9},{2,10},{3,11},{4,12},{5,13},{6,14},{7,15},{8,0},{9,1},... | collective-permute-start | bytes 147464 | tf_op jit(solution)/shard_map/ppermute | solution.py:297
  128.5 4.6 %collective-permute-start.22 = (f32[24,512]{1,0:T(8,128)S(1)}, f32[24,512]{1,0:T(8,128)S(1)}, u32[]{:S(2)}, u32[]{:S(2)}) collective-permute-start(f32[24,512]{1,0:T(8,128)S(1)} %pad_maximum_fusion.1), channel_id=1, source_target_pairs={{0,4},{1,5},{2,6},{3,7},{4,0},{5,1},{6,2},{7,3},{8,12},{9,13},{10,... | collective-permute-start | bytes 147464 | tf_op jit(solution)/shard_map/ppermute | solution.py:297

commit v5 on v4

--- a/solution.py
+++ b/solution.py
@@ -70,7 +70,7 @@
     return (new_same, new_opp, next_same, next_opp, collision)
 
 
-def build_body(orbitals, low, high, pairs, *refs):
+def build_body(orbitals, low, high, pairs, only, *refs):
     place_ref, inter_ref, pat_ref, hop_ref, occ_ref = refs[:5]
     pat4_ref, hop4_ref, eye4_ref, occ4_ref = refs[5:9]
     mixed_ref, polar_ref, turned_ref = refs[-3:]
@@ -78,6 +78,21 @@
     tiles = pairs // span
     start = place_ref[0]
     strips = range(0, high - low, 128)
+    if only is not None:
+        kept = refs[9:-3]
+
+        @pl.when(place_ref[1] == only)
+        def _():
+            build_body(orbitals, low, high, pairs, None, *refs)
+
+        if kept:
+
+            @pl.when(place_ref[1] != only)
+            def _():
+                mixed_ref[...] = kept[0][...]
+                polar_ref[...] = kept[1][...]
+
+        return
 
     pitch = orbitals + 1
     room = orbitals * pitch
@@ -148,7 +163,7 @@
             row += count
 
 
-def build_rows(place, interaction, smalls, made, low, high):
+def build_rows(place, interaction, smalls, made, low, high, only=None):
     rows, pairs = interaction.shape
     pattern, hopping, occupation = smalls[:3]
     orbitals = hopping.shape[0]
@@ -160,12 +175,12 @@
     row4 = pl.BlockSpec((1, 4 * orbitals), lambda g, p: (0, 0))
     small = pl.BlockSpec((orbitals, 4 * orbitals), lambda g, p: (0, 0))
     return pl.pallas_call(
-        functools.partial(build_body, orbitals, low, high, pairs),
+        functools.partial(build_body, orbitals, low, high, pairs, only),
         grid_spec=pltpu.PrefetchScalarGridSpec(
             num_scalar_prefetch=1,
             grid=(1,),
             in_specs=[wide, smem, smem, smem, small, small, small, row4]
-            + [pl.BlockSpec(memory_space=pl.ANY)] * len(made),
+            + [pl.BlockSpec(memory_space=pl.ANY) if only is None else wide] * len(made),
             out_specs=[wide] * 2,
             scratch_shapes=[pltpu.VMEM((-(-height // 128) * orbitals * (orbitals + 1), 128), jnp.float32)],
         ),
@@ -333,11 +348,7 @@
         return lax.ppermute(block, "prow", pairs_of)
 
     place = jnp.concatenate([core[None].astype(jnp.int32), line])
-    own = jnp.concatenate([green_same, green_opp], axis=0)
-    moving = [send(own, right), send(own, left)]
-    near = send(own, across)
-
-    start = (me * (rows // orbitals)).astype(jnp.int32)[None]
+    start = jnp.stack([me * (rows // orbitals), core]).astype(jnp.int32)
     smalls = (
         pattern,
         hopping,
@@ -348,10 +359,13 @@
         jnp.tile(occupation, 4)[None],
     )
     big = rows // 9 * 4
-    mats = build_rows(start, interaction, smalls, (), 0, big)
-    mats = build_rows(start, interaction, smalls, mats, big, 2 * big)
-
-    greens, low, sums, done = [([own], [near])], 0, (), mats[0]
+    mats = build_rows(start, interaction, smalls, (), 2 * big, rows, only=1)
+    own = after(jnp.concatenate([green_same, green_opp], axis=0), mats[0])
+    moving = [send(own, right), send(own, left)]
+    near = send(own, across)
+    mats = build_rows(after(start, own), interaction, smalls, mats, 0, big)
+
+    chips_in, low, sums, done = [([own], [near])], 0, (), mats[0]
     for far in range(1, half):
         got = [after(block, done) for block in moving]
         if far < half - 1:
@@ -360,12 +374,16 @@
             moving = [send(got[0][:rows], right), send(got[1][rows:], left)]
         passed = [([block], [send(block, across)]) for block in got]
         if far == 1:
-            mats = build_rows(after(start, got[0]), interaction, smalls, mats, 2 * big, rows)
-            greens += passed
-        else:
-            greens = passed
-        sums = step(after(place, got[0]), low, mats, greens, sums, (), orbitals)
-        low += len(greens)
+            mats = build_rows(after(start, got[0]), interaction, smalls, mats, big, 2 * big)
+            mats = build_rows(start, interaction, smalls, mats, 2 * big, rows, only=0)
+            chips_in += passed
+            done = mats[0]
+            continue
+        if far == 2:
+            sums = step(after(place, got[0]), low, mats, chips_in, sums, (), orbitals)
+            low += len(chips_in)
+        sums = step(after(place, got[0]), low, mats, passed, sums, (), orbitals)
+        low += len(passed)
         done = sums[0]
     last = [after(block, done) for block in moving]
     shared = [send(block, across) for block in last]

time: 134 us -> 139 us (1.037)
  waiting for transfers between devices: 36 us -> 21.8 us
  Pallas kernels: 76 us -> 82.2 us
  starting transfers between devices: 16.4 us -> 22.2 us
  local copies, waits for them, and re-layouts: 3.72 us -> 9.34 us
    ppermute x17, waiting for transfers between devices: 30.3 us -> 16.6 us  [send(): return lax.ppermute(block, 'prow', pairs_of)]
    pallas_call x3 -> x4, Pallas kernels: 36.1 us -> 41.9 us  [build_rows(): pl.pallas_call(functools.partial(build_body, orbitals, low, high, pairs,...]
    ppermute x17, starting transfers between devices: 10.1 us -> 15.9 us  [send(): return lax.ppermute(block, 'prow', pairs_of)]
    unnamed x19 -> x22, local copies, waits for them, and re-layouts: 2.29 us -> 6.09 us
  transfers between devices with their start and end apart: 23 -> 23, of which waited for: 14 -> 11; matrix products, arithmetic and copies ran while one was open for 1% -> 1% of each run, Pallas kernels for 51% -> 51%
where the time goes in v5:
time: 139 us; the launch traced here: 138 us
  Pallas kernels  82.2 us (59%)
  starting transfers between devices  22.2 us (16%)
  waiting for transfers between devices  21.8 us (16%)
  local copies, waits for them, and re-layouts  9.34 us (7%)
  other arithmetic  1.88 us (1%)
    pallas_call x4, Pallas kernels, build_rows(): pl.pallas_call(functools.partial(build_body, orbitals, low, high, pairs,...  41.9 us
    pallas_call x4, Pallas kernels, step(): pl.pallas_call(functools.partial(step_body, parts, rows, opening, closing...  40.3 us
    ppermute x17, waiting for transfers between devices, send(): return lax.ppermute(block, 'prow', pairs_of)  16.6 us
    ppermute x17, starting transfers between devices, send(): return lax.ppermute(block, 'prow', pairs_of)  15.9 us
    ppermute x6, starting transfers between devices, spread_blocks(): blocks.append(lax.ppermute(block, 'prow', pairs_of))  6.31 us
    unnamed x22, local copies, waits for them, and re-layouts  6.09 us
    ppermute x6, waiting for transfers between devices, spread_blocks(): blocks.append(lax.ppermute(block, 'prow', pairs_of))  5.17 us
  transfers between devices with their start and end apart: 23, of which 11 were waited for; matrix products, arithmetic and copies ran while one was open for 1% of the time, Pallas kernels for 51%

profile of v5, /device:TPU:0, one launch (start us, length us, event | category | flops | bytes accessed | tf_op | source)
XLA Modules:
  0.0 138.2 jit_solution(3191553929691255417)
XLA Ops:
  0.7 0.9 convert_element_type.16
  1.6 0.1 tile.46.refs_5_
  1.8 0.8 tile.47
  2.6 0.1 tile.48.refs_6_
  2.8 0.1 tile.50.refs_7_
  3.0 0.1 broadcast_in_dim_tile.3.refs_8_
  3.0 0.1 pad_add_fusion.1.refs_0_
  3.1 0.1 pad_maximum_fusion.refs_3_
  3.2 0.7 copy-done.3
  3.9 0.0 copy-done.4
  4.0 4.1 %build_rows.4 = (bf16[576,9216]{1,0:T(8,128)(2,1)}, bf16[576,9216]{1,0:T(8,128)(2,1)}) custom-call(s32[2]{0:T(128)S(1)} %pad_add_fusion.1.refs_0_, bf16[576,9216]{1,0:T(8,128)(2,1)} %refs_1_.7, s32[96,96]{1,0:T(8,128)S(1)} %copy-done.3, f32[96,96]{1,0:T(8,128)S(1)} %copy-done.4, f32[96]{0:T(128)S(1)} %copy-done.7, f32[96,384]{1,0:T(8,128)S(1)} %tile.46.refs_5_, ...), custom_call_target="tpu_custom_call" | custom-call | flops 1024 | bytes 1024 | tf_op jit(solution)/shard_map/build_rows/pallas_call | solution.py:177
  8.1 3.0 %collective-permute-start = (bf16[1152,512]{1,0:T(8,128)(2,1)S(1)}, bf16[1152,512]{1,0:T(8,128)(2,1)S(1)}, u32[]{:S(2)}, u32[]{:S(2)}) collective-permute-start(bf16[1152,512]{1,0:T(8,128)(2,1)S(1)} %pad_maximum_fusion.refs_3_), channel_id=1, source_target_pairs={{0,4},{1,5},{2,0},{3,1},{4,8},{5,9},{6,2},{7,3},{8,12},{9,13},{10,... | collective-permute-start | bytes 3538952 | tf_op jit(solution)/shard_map/ppermute | solution.py:348
  11.1 14.4 %build_rows.5 = (bf16[576,9216]{1,0:T(8,128)(2,1)}, bf16[576,9216]{1,0:T(8,128)(2,1)}) custom-call(s32[2]{0:T(128)S(1)} %pad_add_fusion.1.refs_0_, bf16[576,9216]{1,0:T(8,128)(2,1)} %refs_1_.7, s32[96,96]{1,0:T(8,128)S(1)} %copy-done.3, f32[96,96]{1,0:T(8,128)S(1)} %copy-done.4, f32[96]{0:T(128)S(1)} %copy-done.7, ...), custom_call_target="tpu_custom_call", output_to_operand_aliasing={{0}: (9, {}), {1}: (10, {})} | custom-call | flops 1024 | bytes 1024 | tf_op jit(solution)/shard_map/build_rows/pallas_call | solution.py:177
  25.5 8.4 %collective-permute-done.refs_5_ = bf16[1152,512]{1,0:T(8,128)(2,1)S(1)} collective-permute-done((bf16[1152,512]{1,0:T(8,128)(2,1)S(1)}, bf16[1152,512]{1,0:T(8,128)(2,1)S(1)}, u32[]{:S(2)}, u32[]{:S(2)}) %collective-permute-start) | collective-permute-done | bytes 1179680 | tf_op jit(solution)/shard_map/ppermute | solution.py:348
  34.0 2.4 %collective-permute-start.1 = (bf16[1152,512]{1,0:T(8,128)(2,1)S(1)}, bf16[1152,512]{1,0:T(8,128)(2,1)}, u32[]{:S(2)}, u32[]{:S(2)}) collective-permute-start(bf16[1152,512]{1,0:T(8,128)(2,1)S(1)} %collective-permute-done.refs_5_), channel_id=1, source_target_pairs={{0,4},{1,5},{2,0},{3,1},{4,8},{5,9},{6,2},{7,3},{8,12},{9,13},{10,... | collective-permute-start | bytes 3538952 | tf_op jit(solution)/shard_map/ppermute | solution.py:348
  36.3 0.4 collective-permute-done.4.refs_7_
  36.7 3.5 %collective-permute-start.7 = (bf16[1152,512]{1,0:T(8,128)(2,1)S(1)}, bf16[1152,512]{1,0:T(8,128)(2,1)S(1)}, u32[]{:S(2)}, u32[]{:S(2)}) collective-permute-start(bf16[1152,512]{1,0:T(8,128)(2,1)S(1)} %pad_maximum_fusion.refs_3_), channel_id=1, source_target_pairs={{0,1},{1,0},{2,3},{3,2},{4,5},{5,4},{6,7},{7,6},{8,9},{9,8},{10,11... | collective-permute-start | bytes 3538952 | tf_op jit(solution)/shard_map/ppermute | solution.py:348
  40.2 0.0 collective-permute-start.8
  40.2 0.5 collective-permute-start.9
  40.7 14.5 %build_rows.6 = (bf16[576,9216]{1,0:T(8,128)(2,1)}, bf16[576,9216]{1,0:T(8,128)(2,1)}) custom-call(s32[2]{0:T(128)S(1)} %pad_add_fusion.1.refs_0_, bf16[576,9216]{1,0:T(8,128)(2,1)} %refs_1_.7, s32[96,96]{1,0:T(8,128)S(1)} %copy-done.3, f32[96,96]{1,0:T(8,128)S(1)} %copy-done.4, f32[96]{0:T(128)S(1)} %copy-done.7, ...), custom_call_target="tpu_custom_call", output_to_operand_aliasing={{0}: (9, {}), {1}: (10, {})} | custom-call | flops 1024 | bytes 1024 | tf_op jit(solution)/shard_map/build_rows/pallas_call | solution.py:177
  55.2 8.9 %build_rows.7 = (bf16[576,9216]{1,0:T(8,128)(2,1)}, bf16[576,9216]{1,0:T(8,128)(2,1)}) custom-call(s32[2]{0:T(128)S(1)} %pad_add_fusion.1.refs_0_, bf16[576,9216]{1,0:T(8,128)(2,1)} %refs_1_.7, s32[96,96]{1,0:T(8,128)S(1)} %copy-done.3, f32[96,96]{1,0:T(8,128)S(1)} %copy-done.4, f32[96]{0:T(128)S(1)} %copy-done.7, ...), custom_call_target="tpu_custom_call", output_to_operand_aliasing={{0}: (9, {}), {1}: (10, {})} | custom-call | flops 1024 | bytes 1024 | tf_op jit(solution)/shard_map/build_rows/pallas_call | solution.py:177
  64.1 0.0 collective-permute-done.1.refs_3_
  64.1 0.0 collective-permute-start.3
  64.1 0.0 collective-permute-done.5.refs_5_
  64.1 1.5 %collective-permute-start.6 = (bf16[1152,512]{1,0:T(8,128)(2,1)}, bf16[1152,512]{1,0:T(8,128)(2,1)}, u32[]{:S(2)}, u32[]{:S(2)}) collective-permute-start(bf16[1152,512]{1,0:T(8,128)(2,1)} %collective-permute-done.5.refs_5_), channel_id=1, source_target_pairs={{0,1},{1,0},{2,3},{3,2},{4,5},{5,4},{6,7},{7,6},{8,9},{9,8},{10,11... | collective-permute-start | bytes 3538952 | tf_op jit(solution)/shard_map/ppermute | solution.py:348
  65.7 1.0 copy-done.5
  66.7 1.6 %collective-permute-start.2 = (bf16[1152,512]{1,0:T(8,128)(2,1)}, bf16[1152,512]{1,0:T(8,128)(2,1)S(1)}, u32[]{:S(2)}, u32[]{:S(2)}) collective-permute-start(bf16[1152,512]{1,0:T(8,128)(2,1)} %collective-permute-done.1.refs_3_), channel_id=1, source_target_pairs={{0,4},{1,5},{2,0},{3,1},{4,8},{5,9},{6,2},{7,3},{8,12},{9,13},{10,... | collective-permute-start | bytes 3538952 | tf_op jit(solution)/shard_map/ppermute | solution.py:348
  68.3 0.0 collective-permute-done.8.refs_6_
  68.3 1.0 copy-done.10
  69.3 0.4 collective-permute-start.12
  69.7 0.7 dynamic-slice_bitcast_fusion
  70.4 0.1 pad_add_fusion.refs_0_
  70.5 0.0 collective-permute-done.9.refs_8_
  70.5 1.3 copy-done.6
  71.8 13.1 %add_products.4 = (f32[576,512]{1,0:T(8,128)S(1)}, f32[576,512]{1,0:T(8,128)S(1)}, f32[576,512]{1,0:T(8,128)S(1)}) custom-call(s32[10]{0:T(128)S(1)} %pad_add_fusion.refs_0_, bf16[576,9216]{1,0:T(8,128)(2,1)} %get-tuple-element.50.refs_1_, bf16[576,9216]{1,0:T(8,128)(2,1)} %get-tuple-element.51.refs_2_, bf16[1152,512]{1,0:T(8,128)(2,1)S(1)} %pad_maximum_fusion.refs_3_, ...), custom_call_target="tpu_custom_call" | custom-call | flops 1024 | bytes 1024 | tf_op jit(solution)/shard_map/add_products/pallas_call | solution.py:289
  84.9 0.0 collective-permute-done.3.refs_4_
  84.9 10.2 %add_products.5 = (f32[576,512]{1,0:T(8,128)S(1)}, f32[576,512]{1,0:T(8,128)S(1)}, f32[576,512]{1,0:T(8,128)S(1)}) custom-call(s32[10]{0:T(128)S(1)} %pad_add_fusion.refs_0_, bf16[576,9216]{1,0:T(8,128)(2,1)} %get-tuple-element.50.refs_1_, bf16[576,9216]{1,0:T(8,128)(2,1)} %get-tuple-element.51.refs_2_, ...), custom_call_target="tpu_custom_call", output_to_operand_aliasing={{0}: (7, {}), {1}: (8, {}), {2}: (9, {})} | custom-call | flops 1024 | bytes 1024 | tf_op jit(solution)/shard_map/add_products/pallas_call | solution.py:289
  95.1 0.1 collective-permute-start.11
  95.2 2.0 %collective-permute-done.12.refs_5_ = bf16[1152,512]{1,0:T(8,128)(2,1)} collective-permute-done((bf16[1152,512]{1,0:T(8,128)(2,1)}, bf16[1152,512]{1,0:T(8,128)(2,1)}, u32[]{:S(2)}, u32[]{:S(2)}) %collective-permute-start.12) | collective-permute-done | bytes 1179680 | tf_op jit(solution)/shard_map/ppermute | solution.py:348
  97.3 1.6 %collective-permute-start.10 = (bf16[576,512]{1,0:T(8,128)(2,1)S(1)}, bf16[576,512]{1,0:T(8,128)(2,1)S(1)}, u32[]{:S(2)}, u32[]{:S(2)}) collective-permute-start(bf16[576,512]{1,0:T(8,128)(2,1)S(1)} %slice.6), channel_id=1, source_target_pairs={{0,4},{1,5},{2,0},{3,1},{4,8},{5,9},{6,2},{7,3},{8,12},{9,13},{10,... | collective-permute-start | bytes 1769480 | tf_op jit(solution)/shard_map/ppermute | solution.py:348
  98.9 1.1 slice.7
  100.0 0.7 collective-permute-start.14
  100.7 0.0 collective-permute-done.11.refs_4_
  100.7 0.0 collective-permute-done.13.refs_6_
  100.7 1.0 copy-done.8
  101.7 9.5 %add_products.6 = (f32[576,512]{1,0:T(8,128)S(1)}, f32[576,512]{1,0:T(8,128)S(1)}, f32[576,512]{1,0:T(8,128)S(1)}) custom-call(s32[10]{0:T(128)S(1)} %pad_add_fusion.refs_0_, bf16[576,9216]{1,0:T(8,128)(2,1)} %get-tuple-element.50.refs_1_, bf16[576,9216]{1,0:T(8,128)(2,1)} %get-tuple-element.51.refs_2_, ...), custom_call_target="tpu_custom_call", output_to_operand_aliasing={{0}: (7, {}), {1}: (8, {}), {2}: (9, {})} | custom-call | flops 1024 | bytes 1024 | tf_op jit(solution)/shard_map/add_products/pallas_call | solution.py:289
  111.2 1.0 copy-done
  112.2 0.8 collective-permute-done.10.refs_3_
  113.0 2.6 %collective-permute-done.14.refs_4_ = bf16[576,512]{1,0:T(8,128)(2,1)S(1)} collective-permute-done((bf16[576,512]{1,0:T(8,128)(2,1)S(1)}, bf16[576,512]{1,0:T(8,128)(2,1)S(1)}, u32[]{:S(2)}, u32[]{:S(2)}) %collective-permute-start.14) | collective-permute-done | bytes 589856 | tf_op jit(solution)/shard_map/ppermute | solution.py:348
  115.7 0.5 collective-permute-start.16
  116.2 1.5 %collective-permute-done.15.refs_5_ = bf16[576,512]{1,0:T(8,128)(2,1)S(1)} collective-permute-done((bf16[576,512]{1,0:T(8,128)(2,1)S(1)}, bf16[576,512]{1,0:T(8,128)(2,1)S(1)}, u32[]{:S(2)}, u32[]{:S(2)}) %collective-permute-start.15) | collective-permute-done | bytes 589856 | tf_op jit(solution)/shard_map/ppermute | solution.py:348
  117.7 0.8 collective-permute-done.16.refs_6_
  118.5 7.5 %add_products.7 = (f32[576,512]{1,0:T(8,128)}, f32[576,512]{1,0:T(8,128)}, bf16[576,512]{1,0:T(8,128)(2,1)}, bf16[576,512]{1,0:T(8,128)(2,1)}, f32[6,512]{1,0:T(8,128)S(1)}) custom-call(s32[10]{0:T(128)S(1)} %pad_add_fusion.refs_0_, bf16[576,9216]{1,0:T(8,128)(2,1)} %get-tuple-element.50.refs_1_, bf16[576,9216]{1,0:T(8,128)(2,1)} %get-tuple-element.51.refs_2_, ...), custom_call_target="tpu_custom_call" | custom-call | flops 1024 | bytes 1024 | tf_op jit(solution)/shard_map/add_products/pallas_call | solution.py:289
  126.0 0.2 collective-permute-start.17
  126.2 1.6 %collective-permute-start.18 = (f32[6,512]{1,0:T(8,128)S(1)}, f32[6,512]{1,0:T(8,128)S(1)}, u32[]{:S(2)}, u32[]{:S(2)}) collective-permute-start(f32[6,512]{1,0:T(8,128)S(1)} %get-tuple-element.74), channel_id=1, source_target_pairs={{0,2},{1,3},{2,0},{3,1},{4,6},{5,7},{6,4},{7,5},{8,10},{9,11},{10,... | collective-permute-start | bytes 36872 | tf_op jit(solution)/shard_map/ppermute | solution.py:312
  127.8 0.1 collective-permute-start.19
  127.9 1.3 collective-permute-done.17
  129.2 0.8 collective-permute-done.18
  130.0 1.7 %collective-permute-start.20 = (f32[24,512]{1,0:T(8,128)S(1)}, f32[24,512]{1,0:T(8,128)S(1)}, u32[]{:S(2)}, u32[]{:S(2)}) collective-permute-start(f32[24,512]{1,0:T(8,128)S(1)} %pad_maximum_fusion.2), channel_id=1, source_target_pairs={{0,12},{1,13},{2,14},{3,15},{4,8},{5,9},{6,10},{7,11},{8,4},{9,5},... | collective-permute-start | bytes 147464 | tf_op jit(solution)/shard_map/ppermute | solution.py:312
  131.7 1.2 collective-permute-start.21
  132.9 1.5 %collective-permute-start.22 = (f32[24,512]{1,0:T(8,128)S(1)}, f32[24,512]{1,0:T(8,128)S(1)}, u32[]{:S(2)}, u32[]{:S(2)}) collective-permute-start(f32[24,512]{1,0:T(8,128)S(1)} %pad_maximum_fusion.2), channel_id=1, source_target_pairs={{0,4},{1,5},{2,6},{3,7},{4,0},{5,1},{6,2},{7,3},{8,12},{9,13},{10,... | collective-permute-start | bytes 147464 | tf_op jit(solution)/shard_map/ppermute | solution.py:312
  134.4 2.0 %collective-permute-done.20 = f32[24,512]{1,0:T(8,128)S(1)} collective-permute-done((f32[24,512]{1,0:T(8,128)S(1)}, f32[24,512]{1,0:T(8,128)S(1)}, u32[]{:S(2)}, u32[]{:S(2)}) %collective-permute-start.20) | collective-permute-done | bytes 49184 | tf_op jit(solution)/shard_map/ppermute | solution.py:312
  136.4 1.1 collective-permute-done.21
  137.6 0.7 pad_maximum_fusion.1
  (32 shorter events, 0.2 us)
Async XLA Ops:
  0.6 2.3 %copy-start.7 = (f32[96]{0:T(128)S(1)}, f32[96]{0:T(128)}, u32[]{:S(2)}) copy-start(f32[96]{0:T(128)} %refs_4_.7) | copy-start | bytes 1156
  0.6 2.5 %copy-start.1 = (bf16[576,512]{1,0:T(8,128)(2,1)S(1)}, bf16[576,512]{1,0:T(8,128)(2,1)}, u32[]{:S(2)}) copy-start(bf16[576,512]{1,0:T(8,128)(2,1)} %refs_11_.1) | copy-start | bytes 1769476
  0.7 2.5 %copy-start.2 = (bf16[576,512]{1,0:T(8,128)(2,1)S(1)}, bf16[576,512]{1,0:T(8,128)(2,1)}, u32[]{:S(2)}) copy-start(bf16[576,512]{1,0:T(8,128)(2,1)} %refs_10_.1) | copy-start | bytes 1769476
  3.1 0.8 copy-start.3
  3.1 0.8 copy-start.4
  8.1 25.8 %collective-permute-start = (bf16[1152,512]{1,0:T(8,128)(2,1)S(1)}, bf16[1152,512]{1,0:T(8,128)(2,1)S(1)}, u32[]{:S(2)}, u32[]{:S(2)}) collective-permute-start(bf16[1152,512]{1,0:T(8,128)(2,1)S(1)} %pad_maximum_fusion.refs_3_), channel_id=1, source_target_pairs={{0,4},{1,5},{2,0},{3,1},{4,8},{5,9},{6,2},{7,3},{8,12},{9,13},{10,... | collective-permute-start | bytes 3538952 | tf_op jit(solution)/shard_map/ppermute | solution.py:348
  11.1 25.6 %collective-permute-start.4 = (bf16[1152,512]{1,0:T(8,128)(2,1)S(1)}, bf16[1152,512]{1,0:T(8,128)(2,1)}, u32[]{:S(2)}, u32[]{:S(2)}) collective-permute-start(bf16[1152,512]{1,0:T(8,128)(2,1)S(1)} %pad_maximum_fusion.refs_3_), channel_id=1, source_target_pairs={{4,0},{5,1},{0,2},{1,3},{8,4},{9,5},{2,6},{3,7},{12,8},{13,9},{6,1... | collective-permute-start | bytes 3538952 | tf_op jit(solution)/shard_map/ppermute | solution.py:348
  34.0 21.3 %copy-start.9 = (bf16[1152,512]{1,0:T(8,128)(2,1)}, bf16[1152,512]{1,0:T(8,128)(2,1)S(1)}, u32[]{:S(2)}) copy-start(bf16[1152,512]{1,0:T(8,128)(2,1)S(1)} %collective-permute-done.refs_5_) | copy-start | bytes 3538948
  34.0 30.2 %collective-permute-start.1 = (bf16[1152,512]{1,0:T(8,128)(2,1)S(1)}, bf16[1152,512]{1,0:T(8,128)(2,1)}, u32[]{:S(2)}, u32[]{:S(2)}) collective-permute-start(bf16[1152,512]{1,0:T(8,128)(2,1)S(1)} %collective-permute-done.refs_5_), channel_id=1, source_target_pairs={{0,4},{1,5},{2,0},{3,1},{4,8},{5,9},{6,2},{7,3},{8,12},{9,13},{10,... | collective-permute-start | bytes 3538952 | tf_op jit(solution)/shard_map/ppermute | solution.py:348
  36.7 27.4 %collective-permute-start.5 = (bf16[1152,512]{1,0:T(8,128)(2,1)}, bf16[1152,512]{1,0:T(8,128)(2,1)}, u32[]{:S(2)}, u32[]{:S(2)}) collective-permute-start(bf16[1152,512]{1,0:T(8,128)(2,1)} %collective-permute-done.4.refs_7_), channel_id=1, source_target_pairs={{4,0},{5,1},{0,2},{1,3},{8,4},{9,5},{2,6},{3,7},{12,8},{13,9},{6,1... | collective-permute-start | bytes 3538952 | tf_op jit(solution)/shard_map/ppermute | solution.py:348
  36.7 29.0 %collective-permute-start.7 = (bf16[1152,512]{1,0:T(8,128)(2,1)S(1)}, bf16[1152,512]{1,0:T(8,128)(2,1)S(1)}, u32[]{:S(2)}, u32[]{:S(2)}) collective-permute-start(bf16[1152,512]{1,0:T(8,128)(2,1)S(1)} %pad_maximum_fusion.refs_3_), channel_id=1, source_target_pairs={{0,1},{1,0},{2,3},{3,2},{4,5},{5,4},{6,7},{7,6},{8,9},{9,8},{10,11... | collective-permute-start | bytes 3538952 | tf_op jit(solution)/shard_map/ppermute | solution.py:348
  40.2 28.1 %collective-permute-start.8 = (bf16[1152,512]{1,0:T(8,128)(2,1)S(1)}, bf16[1152,512]{1,0:T(8,128)(2,1)S(1)}, u32[]{:S(2)}, u32[]{:S(2)}) collective-permute-start(bf16[1152,512]{1,0:T(8,128)(2,1)S(1)} %collective-permute-done.refs_5_), channel_id=1, source_target_pairs={{0,1},{1,0},{2,3},{3,2},{4,5},{5,4},{6,7},{7,6},{8,9},{9,8},{10,11... | collective-permute-start | bytes 3538952 | tf_op jit(solution)/shard_map/ppermute | solution.py:348
  40.2 30.3 %collective-permute-start.9 = (bf16[1152,512]{1,0:T(8,128)(2,1)}, bf16[1152,512]{1,0:T(8,128)(2,1)}, u32[]{:S(2)}, u32[]{:S(2)}) collective-permute-start(bf16[1152,512]{1,0:T(8,128)(2,1)} %collective-permute-done.4.refs_7_), channel_id=1, source_target_pairs={{0,1},{1,0},{2,3},{3,2},{4,5},{5,4},{6,7},{7,6},{8,9},{9,8},{10,11... | collective-permute-start | bytes 3538952 | tf_op jit(solution)/shard_map/ppermute | solution.py:348
  64.1 20.8 %collective-permute-start.3 = (bf16[1152,512]{1,0:T(8,128)(2,1)}, bf16[1152,512]{1,0:T(8,128)(2,1)}, u32[]{:S(2)}, u32[]{:S(2)}) collective-permute-start(bf16[1152,512]{1,0:T(8,128)(2,1)} %collective-permute-done.1.refs_3_), channel_id=1, source_target_pairs={{0,1},{1,0},{2,3},{3,2},{4,5},{5,4},{6,7},{7,6},{8,9},{9,8},{10,11... | collective-permute-start | bytes 3538952 | tf_op jit(solution)/shard_map/ppermute | solution.py:348
  64.1 20.7 %collective-permute-start.6 = (bf16[1152,512]{1,0:T(8,128)(2,1)}, bf16[1152,512]{1,0:T(8,128)(2,1)}, u32[]{:S(2)}, u32[]{:S(2)}) collective-permute-start(bf16[1152,512]{1,0:T(8,128)(2,1)} %collective-permute-done.5.refs_5_), channel_id=1, source_target_pairs={{0,1},{1,0},{2,3},{3,2},{4,5},{5,4},{6,7},{7,6},{8,9},{9,8},{10,11... | collective-permute-start | bytes 3538952 | tf_op jit(solution)/shard_map/ppermute | solution.py:348
  65.7 1.0 copy-start.5
  66.7 28.4 %collective-permute-start.2 = (bf16[1152,512]{1,0:T(8,128)(2,1)}, bf16[1152,512]{1,0:T(8,128)(2,1)S(1)}, u32[]{:S(2)}, u32[]{:S(2)}) collective-permute-start(bf16[1152,512]{1,0:T(8,128)(2,1)} %collective-permute-done.1.refs_3_), channel_id=1, source_target_pairs={{0,4},{1,5},{2,0},{3,1},{4,8},{5,9},{6,2},{7,3},{8,12},{9,13},{10,... | collective-permute-start | bytes 3538952 | tf_op jit(solution)/shard_map/ppermute | solution.py:348
  68.3 1.0 copy-start.10
  69.3 27.9 %collective-permute-start.12 = (bf16[1152,512]{1,0:T(8,128)(2,1)}, bf16[1152,512]{1,0:T(8,128)(2,1)}, u32[]{:S(2)}, u32[]{:S(2)}) collective-permute-start(bf16[1152,512]{1,0:T(8,128)(2,1)} %collective-permute-done.5.refs_5_), channel_id=1, source_target_pairs={{4,0},{5,1},{0,2},{1,3},{8,4},{9,5},{2,6},{3,7},{12,8},{13,9},{6,1... | collective-permute-start | bytes 3538952 | tf_op jit(solution)/shard_map/ppermute | solution.py:348
  70.5 1.3 copy-start.6
  95.1 5.5 %collective-permute-start.11 = (bf16[1152,512]{1,0:T(8,128)(2,1)S(1)}, bf16[1152,512]{1,0:T(8,128)(2,1)S(1)}, u32[]{:S(2)}, u32[]{:S(2)}) collective-permute-start(bf16[1152,512]{1,0:T(8,128)(2,1)S(1)} %collective-permute-done.2.refs_3_), channel_id=1, source_target_pairs={{0,1},{1,0},{2,3},{3,2},{4,5},{5,4},{6,7},{7,6},{8,9},{9,8},{10,11... | collective-permute-start | bytes 3538952 | tf_op jit(solution)/shard_map/ppermute | solution.py:348
  97.2 3.5 %collective-permute-start.13 = (bf16[1152,512]{1,0:T(8,128)(2,1)}, bf16[1152,512]{1,0:T(8,128)(2,1)S(1)}, u32[]{:S(2)}, u32[]{:S(2)}) collective-permute-start(bf16[1152,512]{1,0:T(8,128)(2,1)} %collective-permute-done.12.refs_5_), channel_id=1, source_target_pairs={{0,1},{1,0},{2,3},{3,2},{4,5},{5,4},{6,7},{7,6},{8,9},{9,8},{10,11... | collective-permute-start | bytes 3538952 | tf_op jit(solution)/shard_map/ppermute | solution.py:348
  97.3 15.8 %collective-permute-start.10 = (bf16[576,512]{1,0:T(8,128)(2,1)S(1)}, bf16[576,512]{1,0:T(8,128)(2,1)S(1)}, u32[]{:S(2)}, u32[]{:S(2)}) collective-permute-start(bf16[576,512]{1,0:T(8,128)(2,1)S(1)} %slice.6), channel_id=1, source_target_pairs={{0,4},{1,5},{2,0},{3,1},{4,8},{5,9},{6,2},{7,3},{8,12},{9,13},{10,... | collective-permute-start | bytes 1769480 | tf_op jit(solution)/shard_map/ppermute | solution.py:348
  100.0 15.7 %collective-permute-start.14 = (bf16[576,512]{1,0:T(8,128)(2,1)S(1)}, bf16[576,512]{1,0:T(8,128)(2,1)S(1)}, u32[]{:S(2)}, u32[]{:S(2)}) collective-permute-start(bf16[576,512]{1,0:T(8,128)(2,1)S(1)} %slice.7), channel_id=1, source_target_pairs={{4,0},{5,1},{0,2},{1,3},{8,4},{9,5},{2,6},{3,7},{12,8},{13,9},{6,1... | collective-permute-start | bytes 1769480 | tf_op jit(solution)/shard_map/ppermute | solution.py:348
  100.7 1.0 copy-start.8
  111.2 1.0 copy-start
  115.7 2.0 %collective-permute-start.15 = (bf16[576,512]{1,0:T(8,128)(2,1)S(1)}, bf16[576,512]{1,0:T(8,128)(2,1)S(1)}, u32[]{:S(2)}, u32[]{:S(2)}) collective-permute-start(bf16[576,512]{1,0:T(8,128)(2,1)S(1)} %collective-permute-done.10.refs_3_), channel_id=1, source_target_pairs={{0,1},{1,0},{2,3},{3,2},{4,5},{5,4},{6,7},{7,6},{8,9},{9,8},{10,11... | collective-permute-start | bytes 1769480 | tf_op jit(solution)/shard_map/ppermute | solution.py:348
  115.7 2.8 %collective-permute-start.16 = (bf16[576,512]{1,0:T(8,128)(2,1)S(1)}, bf16[576,512]{1,0:T(8,128)(2,1)S(1)}, u32[]{:S(2)}, u32[]{:S(2)}) collective-permute-start(bf16[576,512]{1,0:T(8,128)(2,1)S(1)} %collective-permute-done.14.refs_4_), channel_id=1, source_target_pairs={{0,1},{1,0},{2,3},{3,2},{4,5},{5,4},{6,7},{7,6},{8,9},{9,8},{10,11... | collective-permute-start | bytes 1769480 | tf_op jit(solution)/shard_map/ppermute | solution.py:348
  126.0 3.2 %collective-permute-start.17 = (f32[6,512]{1,0:T(8,128)S(1)}, f32[6,512]{1,0:T(8,128)S(1)}, u32[]{:S(2)}, u32[]{:S(2)}) collective-permute-start(f32[6,512]{1,0:T(8,128)S(1)} %get-tuple-element.74), channel_id=1, source_target_pairs={{0,3},{1,2},{2,1},{3,0},{4,7},{5,6},{6,5},{7,4},{8,11},{9,10},{10,... | collective-permute-start | bytes 36872 | tf_op jit(solution)/shard_map/ppermute | solution.py:312
  126.2 3.8 %collective-permute-start.18 = (f32[6,512]{1,0:T(8,128)S(1)}, f32[6,512]{1,0:T(8,128)S(1)}, u32[]{:S(2)}, u32[]{:S(2)}) collective-permute-start(f32[6,512]{1,0:T(8,128)S(1)} %get-tuple-element.74), channel_id=1, source_target_pairs={{0,2},{1,3},{2,0},{3,1},{4,6},{5,7},{6,4},{7,5},{8,10},{9,11},{10,... | collective-permute-start | bytes 36872 | tf_op jit(solution)/shard_map/ppermute | solution.py:312
  127.8 2.2 %collective-permute-start.19 = (f32[6,512]{1,0:T(8,128)S(1)}, f32[6,512]{1,0:T(8,128)S(1)}, u32[]{:S(2)}, u32[]{:S(2)}) collective-permute-start(f32[6,512]{1,0:T(8,128)S(1)} %get-tuple-element.74), channel_id=1, source_target_pairs={{0,1},{1,0},{2,3},{3,2},{4,5},{5,4},{6,7},{7,6},{8,9},{9,8},{10,11... | collective-permute-start | bytes 36872 | tf_op jit(solution)/shard_map/ppermute | solution.py:312
  130.0 6.4 %collective-permute-start.20 = (f32[24,512]{1,0:T(8,128)S(1)}, f32[24,512]{1,0:T(8,128)S(1)}, u32[]{:S(2)}, u32[]{:S(2)}) collective-permute-start(f32[24,512]{1,0:T(8,128)S(1)} %pad_maximum_fusion.2), channel_id=1, source_target_pairs={{0,12},{1,13},{2,14},{3,15},{4,8},{5,9},{6,10},{7,11},{8,4},{9,5},... | collective-permute-start | bytes 147464 | tf_op jit(solution)/shard_map/ppermute | solution.py:312
  131.7 5.9 %collective-permute-start.21 = (f32[24,512]{1,0:T(8,128)S(1)}, f32[24,512]{1,0:T(8,128)S(1)}, u32[]{:S(2)}, u32[]{:S(2)}) collective-permute-start(f32[24,512]{1,0:T(8,128)S(1)} %pad_maximum_fusion.2), channel_id=1, source_target_pairs={{0,8},{1,9},{2,10},{3,11},{4,12},{5,13},{6,14},{7,15},{8,0},{9,1},... | collective-permute-start | bytes 147464 | tf_op jit(solution)/shard_map/ppermute | solution.py:312
  132.9 4.6 %collective-permute-start.22 = (f32[24,512]{1,0:T(8,128)S(1)}, f32[24,512]{1,0:T(8,128)S(1)}, u32[]{:S(2)}, u32[]{:S(2)}) collective-permute-start(f32[24,512]{1,0:T(8,128)S(1)} %pad_maximum_fusion.2), channel_id=1, source_target_pairs={{0,4},{1,5},{2,6},{3,7},{4,0},{5,1},{6,2},{7,3},{8,12},{9,13},{10,... | collective-permute-start | bytes 147464 | tf_op jit(solution)/shard_map/ppermute | solution.py:312

commit v6 on v4

--- a/solution.py
+++ b/solution.py
@@ -154,6 +154,7 @@
     orbitals = hopping.shape[0]
     height = high - low
     block = low // height
+    assert low % height == 0
     shape = jax.ShapeDtypeStruct((rows, pairs), jnp.bfloat16)
     wide = pl.BlockSpec((height, pairs), lambda g, p: (block, 0))
     smem = pl.BlockSpec(memory_space=pltpu.SMEM)
@@ -235,7 +236,9 @@
                     refs[kind][part, :] = slope
                     refs[2 + kind][part, :] = (old + 0.5 * slope).astype(jnp.bfloat16)
                     both = slope if both is None else both + slope
-                refs[4][first : first + 1, :] = jnp.sum(both, axis=0, keepdims=True) * scale
+                summed = jnp.sum(both, axis=0, keepdims=True) * scale
+                for copy in range(first, refs[4].shape[0], rows // orbitals):
+                    refs[4][copy : copy + 1, :] = summed
 
 
 def step(place, low, mats, greens, sums, olds, orbitals):
@@ -251,9 +254,9 @@
     wide_sum = jax.ShapeDtypeStruct((rows, width), jnp.float32)
     scratch = [pltpu.VMEM((wide, 3 * span), jnp.bfloat16)]
     if closing:
-        out_specs = [tall] * 4 + [pl.BlockSpec((rows // orbitals, span), lambda n, g, p: (0, n))]
+        out_specs = [tall] * 4 + [pl.BlockSpec((orbitals, span), lambda n, g, p: (0, n))]
         out_shape = [wide_sum] * 2 + [jax.ShapeDtypeStruct((rows, width), jnp.bfloat16)] * 2
-        out_shape += [jax.ShapeDtypeStruct((rows // orbitals, width), jnp.float32)]
+        out_shape += [jax.ShapeDtypeStruct((orbitals, width), jnp.float32)]
         scratch = [pltpu.VMEM((rows, span), jnp.float32)] * 3 + scratch
     else:
         out_specs, out_shape = [tall] * 3, [wide_sum] * 3
@@ -290,18 +293,6 @@
     )(place, *operands)
 
 
-def spread_blocks(block, index, stride, devices):
-    blocks = [block]
-    for other in range(1, 4):
-        pairs_of = [(d, d ^ (other * stride)) for d in range(devices)]
-        blocks.append(lax.ppermute(block, "prow", pairs_of))
-    part = index // stride % 4
-    low, high = part % 2 == 1, part // 2 == 1
-    b = [jnp.where(low, blocks[n ^ 1], blocks[n]) for n in range(4)]
-    b = [jnp.where(high, b[n ^ 2], b[n]) for n in range(4)]
-    return jnp.concatenate(b, axis=0)
-
-
 def after(value, *others):
     return lax.optimization_barrier((value, *others))[0]
 
@@ -313,29 +304,28 @@
     devices = pairs // rows
     chips = devices // 2
     me = lax.axis_index("prow")
-    core, chip = me % 2, me // 2
+    core = me % 2
     order = list(range(0, chips, 2)) + list(range(chips - 1, 0, -2))
     spot = [order.index(c) for c in range(chips)]
-    ahead = [order[(spot[c] + 1) % chips] for c in range(chips)]
-    right = [(2 * c + k, 2 * ahead[c] + k) for c in range(chips) for k in range(2)]
-    left = [(b, a) for a, b in right]
+    half = chips // 2
+
+    def away(device, far):
+        way = 1 if device % 2 == 0 else -1
+        return order[(spot[device // 2] - way * far) % chips]
+
+    first_way = [(2 * away(d, 1) + d % 2, d) for d in range(devices)]
+    second_way = [(b, a) for a, b in first_way]
     across = [(d, d ^ 1) for d in range(devices)]
-    half = chips // 2
     table = []
-    for c in range(chips):
-        line = [c]
+    for d in range(devices):
+        line = [d % 2, d // 2]
         for far in range(1, half + 1):
-            line += [order[(spot[c] - far) % chips], order[(spot[c] + far) % chips]]
+            line += [away(d, far), away(d, -far)]
         table.append(line)
-    line = lax.dynamic_index_in_dim(jnp.array(table, jnp.int32), chip, 0, keepdims=False)
+    place = lax.dynamic_index_in_dim(jnp.array(table, jnp.int32), me, 0, keepdims=False)
 
     def send(block, pairs_of):
         return lax.ppermute(block, "prow", pairs_of)
-
-    place = jnp.concatenate([core[None].astype(jnp.int32), line])
-    own = jnp.concatenate([green_same, green_opp], axis=0)
-    moving = [send(own, right), send(own, left)]
-    near = send(own, across)
 
     start = (me * (rows // orbitals)).astype(jnp.int32)[None]
     smalls = (
@@ -347,35 +337,46 @@
         jnp.tile(jnp.eye(orbitals, dtype=jnp.float32), (1, 4)),
         jnp.tile(occupation, 4)[None],
     )
-    big = rows // 9 * 4
-    mats = build_rows(start, interaction, smalls, (), 0, big)
-    mats = build_rows(start, interaction, smalls, mats, big, 2 * big)
-
-    greens, low, sums, done = [([own], [near])], 0, (), mats[0]
+
+    def build(when, made, strip):
+        low = 128 * strip
+        return build_rows(when, interaction, smalls, made, low, min(low + 128, rows))
+
+    strips = -(-rows // 128)
+    own = jnp.concatenate([green_same, green_opp], axis=0)
+    moving = [send(own, first_way), None]
+    mats = build(start, (), 0)
+    own_later = after(own, mats[0])
+    moving[1] = send(own_later, second_way)
+    near = send(own_later, across)
+    mats = build(start, mats, 1)
+
+    chips_in, low, sums, done, made = [([own], [near])], 0, (), mats[0], 2
     for far in range(1, half):
-        got = [after(block, done) for block in moving]
-        if far < half - 1:
-            moving = [send(got[0], right), send(got[1], left)]
-        else:
-            moving = [send(got[0][:rows], right), send(got[1][rows:], left)]
-        passed = [([block], [send(block, across)]) for block in got]
-        if far == 1:
-            mats = build_rows(after(start, got[0]), interaction, smalls, mats, 2 * big, rows)
-            greens += passed
-        else:
-            greens = passed
-        sums = step(after(place, got[0]), low, mats, greens, sums, (), orbitals)
-        low += len(greens)
-        done = sums[0]
-    last = [after(block, done) for block in moving]
+        got, passed = [], []
+        for turn in range(2):
+            block = after(moving[turn], done)
+            onward = block if far < half - 1 else block[turn * rows : (turn + 1) * rows]
+            moving[turn] = send(onward, second_way if turn else first_way)
+            got.append(block)
+            passed.append(send(block, across))
+            if made < strips:
+                mats = build(after(start, block), mats, made)
+                made += 1
+                done = mats[0]
+            if far > 1 and turn == (far == 2) and made == strips:
+                sums = step(after(place, block), low, mats, chips_in, sums, (), orbitals)
+                low += len(chips_in)
+                chips_in, done = [], sums[0]
+        chips_in = chips_in + [([got[0]], [passed[1]]), ([got[1]], [passed[0]])]
+    sums = step(place, low, mats, chips_in, sums, (), orbitals)
+    low += len(chips_in)
+    last = [after(block, sums[0]) for block in moving]
     shared = [send(block, across) for block in last]
     new_same, new_opp, next_same, next_opp, part = step(
         place, low, mats, [(last, shared)], sums, (green_same, green_opp), orbitals
     )
-    if devices == 16:
-        collision = spread_blocks(spread_blocks(part, me, 1, devices), me, 4, devices)
-    else:
-        collision = lax.all_gather(part, "prow", axis=0, tiled=True)
+    collision = lax.all_to_all(part, "prow", split_axis=0, concat_axis=0, tiled=True)
     return (new_same, new_opp, next_same, next_opp, collision)
 
 

time: 134 us -> 135 us (level)
  waiting for transfers between devices: 36 us -> 8.29 us
  blocking collectives: 0 us -> 16 us
  Pallas kernels: 76 us -> 86.7 us
  local copies, waits for them, and re-layouts: 3.72 us -> 9.82 us
  starting transfers between devices: 16.4 us -> 13.3 us
    ppermute x17, waiting for transfers between devices: 30.3 us -> 8.29 us  [send(): return lax.ppermute(block, 'prow', pairs_of)]
    all_to_all x0 -> x1, blocking collectives: none -> 16 us  [ring_form(): lax.all_to_all(part, 'prow', split_axis=0, concat_axis=0, tiled=True)]
    pallas_call x3 -> x5, Pallas kernels: 36.1 us -> 46.4 us  [build_rows(): pl.pallas_call(functools.partial(build_body, orbitals, low, high, pairs),...]
    ppermute x6 -> x0, starting transfers between devices: 6.31 us -> none  [spread_blocks(): blocks.append(lax.ppermute(block, 'prow', pairs_of))]
    ppermute x6 -> x0, waiting for transfers between devices: 5.73 us -> none  [spread_blocks(): blocks.append(lax.ppermute(block, 'prow', pairs_of))]
    unnamed x19 -> x23, local copies, waits for them, and re-layouts: 2.29 us -> 6.6 us
    ppermute x17, starting transfers between devices: 10.1 us -> 13.3 us  [send(): return lax.ppermute(block, 'prow', pairs_of)]
  transfers between devices with their start and end apart: 23 -> 17, of which waited for: 14 -> 7; matrix products, arithmetic and copies ran while one was open for 1% -> 2% of each run, Pallas kernels for 51% -> 59%
where the time goes in v6:
time: 135 us
  Pallas kernels  86.7 us (64%)
  blocking collectives  16 us (12%)
  starting transfers between devices  13.3 us (10%)
  local copies, waits for them, and re-layouts  9.82 us (7%)
  waiting for transfers between devices  8.29 us (6%)
    pallas_call x5, Pallas kernels, build_rows(): pl.pallas_call(functools.partial(build_body, orbitals, low, high, pairs),...  46.4 us
    pallas_call x4, Pallas kernels, step(): pl.pallas_call(functools.partial(step_body, parts, rows, opening, closing...  40.3 us
    all_to_all x1, blocking collectives, ring_form(): lax.all_to_all(part, 'prow', split_axis=0, concat_axis=0, tiled=True)  16 us
    ppermute x17, starting transfers between devices, send(): return lax.ppermute(block, 'prow', pairs_of)  13.3 us
    ppermute x17, waiting for transfers between devices, send(): return lax.ppermute(block, 'prow', pairs_of)  8.29 us
    unnamed x23, local copies, waits for them, and re-layouts  6.6 us
  transfers between devices with their start and end apart: 17, of which 7 were waited for; matrix products, arithmetic and copies ran while one was open for 2% of the time, Pallas kernels for 59%

profile of v6, /device:TPU:0, one launch (start us, length us, event | category | flops | bytes accessed | tf_op | source)
XLA Modules:
  0.0 134.9 jit_solution(2179611436657544506)
XLA Ops:
  0.6 0.0 copy-start.2
  0.6 0.0 copy-start.3
  0.7 1.2 constant_dynamic-update-slice_fusion.1
  1.8 0.1 copy-done.2
  1.9 0.0 copy-start.7
  1.9 3.1 %collective-permute-start = (bf16[1152,512]{1,0:T(8,128)(2,1)S(1)}, bf16[1152,512]{1,0:T(8,128)(2,1)}, u32[]{:S(2)}, u32[]{:S(2)}) collective-permute-start(bf16[1152,512]{1,0:T(8,128)(2,1)S(1)} %constant_dynamic-update-slice_fusion.refs_3_), channel_id=1, source_target_pairs={{2,0},{5,1},{6,2},{1,3},{0,4},{9,5},{10,6},{3,7},{4,8},{13,9},{14,... | collective-permute-start | bytes 3538952 | tf_op jit(solution)/shard_map/ppermute | solution.py:328
  5.0 0.0 copy-done.3
  5.1 0.1 tile.50.refs_5_
  5.3 0.1 tile.54.refs_7_
  5.5 0.1 tile.52.refs_6_
  5.6 0.1 broadcast_in_dim_tile.3.refs_8_
  5.7 9.6 %build_rows.5 = (bf16[576,9216]{1,0:T(8,128)(2,1)}, bf16[576,9216]{1,0:T(8,128)(2,1)}) custom-call(s32[1]{0:T(128)} %bitcast.1.refs_0_, bf16[576,9216]{1,0:T(8,128)(2,1)} %refs_1_.9, s32[96,96]{1,0:T(8,128)S(1)} %copy-done.3, f32[96,96]{1,0:T(8,128)S(1)} %copy-done.4, f32[96]{0:T(128)S(1)} %copy-done.7, f32[96,384]{1,0:T(8,128)S(1)} %tile.50.refs_5_, ...), custom_call_target="tpu_custom_call" | custom-call | flops 1024 | bytes 1024 | tf_op jit(solution)/shard_map/build_rows/pallas_call | solution.py:163
  15.3 0.2 collective-permute-start.2
  15.5 9.4 %build_rows.6 = (bf16[576,9216]{1,0:T(8,128)(2,1)}, bf16[576,9216]{1,0:T(8,128)(2,1)}) custom-call(s32[1]{0:T(128)} %bitcast.1.refs_0_, bf16[576,9216]{1,0:T(8,128)(2,1)} %refs_1_.9, s32[96,96]{1,0:T(8,128)S(1)} %copy-done.3, f32[96,96]{1,0:T(8,128)S(1)} %copy-done.4, f32[96]{0:T(128)S(1)} %copy-done.7, ...), custom_call_target="tpu_custom_call", output_to_operand_aliasing={{0}: (9, {}), {1}: (10, {})} | custom-call | flops 1024 | bytes 1024 | tf_op jit(solution)/shard_map/build_rows/pallas_call | solution.py:163
  25.0 0.0 collective-permute-done.refs_5_
  25.0 1.8 %collective-permute-start.1 = (bf16[1152,512]{1,0:T(8,128)(2,1)}, bf16[1152,512]{1,0:T(8,128)(2,1)}, u32[]{:S(2)}, u32[]{:S(2)}) collective-permute-start(bf16[1152,512]{1,0:T(8,128)(2,1)} %collective-permute-done.refs_5_), channel_id=1, source_target_pairs={{2,0},{5,1},{6,2},{1,3},{0,4},{9,5},{10,6},{3,7},{4,8},{13,9},{14,... | collective-permute-start | bytes 3538952 | tf_op jit(solution)/shard_map/ppermute | solution.py:328
  26.8 9.5 %build_rows.7 = (bf16[576,9216]{1,0:T(8,128)(2,1)}, bf16[576,9216]{1,0:T(8,128)(2,1)}) custom-call(s32[1]{0:T(128)} %bitcast.1.refs_0_, bf16[576,9216]{1,0:T(8,128)(2,1)} %refs_1_.9, s32[96,96]{1,0:T(8,128)S(1)} %copy-done.3, f32[96,96]{1,0:T(8,128)S(1)} %copy-done.4, f32[96]{0:T(128)S(1)} %copy-done.7, ...), custom_call_target="tpu_custom_call", output_to_operand_aliasing={{0}: (9, {}), {1}: (10, {})} | custom-call | flops 1024 | bytes 1024 | tf_op jit(solution)/shard_map/build_rows/pallas_call | solution.py:163
  36.3 0.0 collective-permute-done.2.refs_7_
  36.3 0.2 collective-permute-start.4
  36.5 0.5 collective-permute-start.5
  37.0 0.0 collective-permute-start.6
  37.0 0.5 collective-permute-start.7
  37.5 9.6 %build_rows.8 = (bf16[576,9216]{1,0:T(8,128)(2,1)}, bf16[576,9216]{1,0:T(8,128)(2,1)}) custom-call(s32[1]{0:T(128)} %bitcast.1.refs_0_, bf16[576,9216]{1,0:T(8,128)(2,1)} %refs_1_.9, s32[96,96]{1,0:T(8,128)S(1)} %copy-done.3, f32[96,96]{1,0:T(8,128)S(1)} %copy-done.4, f32[96]{0:T(128)S(1)} %copy-done.7, ...), custom_call_target="tpu_custom_call", output_to_operand_aliasing={{0}: (9, {}), {1}: (10, {})} | custom-call | flops 1024 | bytes 1024 | tf_op jit(solution)/shard_map/build_rows/pallas_call | solution.py:163
  47.1 3.6 %collective-permute-done.1.refs_3_ = bf16[1152,512]{1,0:T(8,128)(2,1)} collective-permute-done((bf16[1152,512]{1,0:T(8,128)(2,1)}, bf16[1152,512]{1,0:T(8,128)(2,1)}, u32[]{:S(2)}, u32[]{:S(2)}) %collective-permute-start.1) | collective-permute-done | bytes 1179680 | tf_op jit(solution)/shard_map/ppermute | solution.py:328
  50.8 2.4 %collective-permute-start.3 = (bf16[1152,512]{1,0:T(8,128)(2,1)}, bf16[1152,512]{1,0:T(8,128)(2,1)S(1)}, u32[]{:S(2)}, u32[]{:S(2)}) collective-permute-start(bf16[1152,512]{1,0:T(8,128)(2,1)} %collective-permute-done.1.refs_3_), channel_id=1, source_target_pairs={{2,0},{5,1},{6,2},{1,3},{0,4},{9,5},{10,6},{3,7},{4,8},{13,9},{14,... | collective-permute-start | bytes 3538952 | tf_op jit(solution)/shard_map/ppermute | solution.py:328
  53.1 8.2 %build_rows.9 = (bf16[576,9216]{1,0:T(8,128)(2,1)}, bf16[576,9216]{1,0:T(8,128)(2,1)}) custom-call(s32[1]{0:T(128)} %bitcast.1.refs_0_, bf16[576,9216]{1,0:T(8,128)(2,1)} %refs_1_.9, s32[96,96]{1,0:T(8,128)S(1)} %copy-done.3, f32[96,96]{1,0:T(8,128)S(1)} %copy-done.4, f32[96]{0:T(128)S(1)} %copy-done.7, ...), custom_call_target="tpu_custom_call", output_to_operand_aliasing={{0}: (9, {}), {1}: (10, {})} | custom-call | flops 1024 | bytes 1024 | tf_op jit(solution)/shard_map/build_rows/pallas_call | solution.py:163
  61.3 0.9 collective-permute-done.4.refs_5_
  62.2 0.0 collective-permute-start.10
  62.2 0.0 collective-permute-done.5.refs_4_
  62.2 1.0 copy-done.5
  63.2 0.5 collective-permute-start.11
  63.7 0.0 collective-permute-done.6.refs_6_
  63.7 1.0 copy-done.10
  64.8 0.2 collective-permute-start.9
  65.0 0.7 dynamic-slice_bitcast_fusion.refs_0_
  65.7 0.0 collective-permute-done.7.refs_8_
  65.7 1.3 copy-done.6
  66.9 13.1 %add_products.4 = (f32[576,512]{1,0:T(8,128)S(1)}, f32[576,512]{1,0:T(8,128)S(1)}, f32[576,512]{1,0:T(8,128)S(1)}) custom-call(s32[10]{0:T(128)S(1)} %dynamic-slice_bitcast_fusion.refs_0_, bf16[576,9216]{1,0:T(8,128)(2,1)} %get-tuple-element.58.refs_1_, bf16[576,9216]{1,0:T(8,128)(2,1)} %get-tuple-element.59.refs_2_, ...), custom_call_target="tpu_custom_call" | custom-call | flops 1024 | bytes 1024 | tf_op jit(solution)/shard_map/add_products/pallas_call | solution.py:277
  80.0 0.0 collective-permute-done.3.refs_3_
  80.0 0.0 collective-permute-done.10.refs_4_
  80.0 0.0 collective-permute-done.11.refs_6_
  80.0 10.2 %add_products.5 = (f32[576,512]{1,0:T(8,128)S(1)}, f32[576,512]{1,0:T(8,128)S(1)}, f32[576,512]{1,0:T(8,128)S(1)}) custom-call(s32[10]{0:T(128)S(1)} %dynamic-slice_bitcast_fusion.refs_0_, bf16[576,9216]{1,0:T(8,128)(2,1)} %get-tuple-element.58.refs_1_, ...), custom_call_target="tpu_custom_call", output_to_operand_aliasing={{0}: (7, {}), {1}: (8, {}), {2}: (9, {})} | custom-call | flops 1024 | bytes 1024 | tf_op jit(solution)/shard_map/add_products/pallas_call | solution.py:277
  90.3 0.0 collective-permute-done.9.refs_5_
  90.3 1.2 collective-permute-start.12
  91.5 0.1 collective-permute-start.13
  91.5 1.1 slice.7
  92.6 1.2 collective-permute-start.14
  93.9 1.1 collective-permute-start.8
  95.0 0.0 collective-permute-done.12.refs_4_
  95.0 0.6 collective-permute-done.13.refs_6_
  95.6 1.0 copy-done.8
  96.6 9.5 %add_products.6 = (f32[576,512]{1,0:T(8,128)S(1)}, f32[576,512]{1,0:T(8,128)S(1)}, f32[576,512]{1,0:T(8,128)S(1)}) custom-call(s32[10]{0:T(128)S(1)} %dynamic-slice_bitcast_fusion.refs_0_, bf16[576,9216]{1,0:T(8,128)(2,1)} %get-tuple-element.58.refs_1_, ...), custom_call_target="tpu_custom_call", output_to_operand_aliasing={{0}: (7, {}), {1}: (8, {}), {2}: (9, {})} | custom-call | flops 1024 | bytes 1024 | tf_op jit(solution)/shard_map/add_products/pallas_call | solution.py:277
  106.1 0.0 copy-start
  106.2 1.0 copy-done
  107.2 0.7 collective-permute-done.14.refs_4_
  107.9 0.0 collective-permute-start.16
  107.9 0.5 collective-permute-done.8.refs_3_
  108.4 0.4 collective-permute-start.15
  108.7 1.2 collective-permute-done.16.refs_6_
  109.9 0.8 collective-permute-done.15.refs_5_
  110.7 0.0 copy-done.1
  110.7 7.5 %add_products.7 = (f32[576,512]{1,0:T(8,128)}, f32[576,512]{1,0:T(8,128)}, bf16[576,512]{1,0:T(8,128)(2,1)}, bf16[576,512]{1,0:T(8,128)(2,1)}, f32[96,512]{1,0:T(8,128)S(1)}) custom-call(s32[10]{0:T(128)S(1)} %dynamic-slice_bitcast_fusion.refs_0_, bf16[576,9216]{1,0:T(8,128)(2,1)} %get-tuple-element.58.refs_1_, bf16[576,9216]{1,0:T(8,128)(2,1)} %get-tuple-element.59.refs_2_, ...), custom_call_target="tpu_custom_call" | custom-call | flops 1024 | bytes 1024 | tf_op jit(solution)/shard_map/add_products/pallas_call | solution.py:277
  118.2 16.0 %all_to_all.12 = f32[16,6,512]{2,1,0:T(8,128)S(1)} all-to-all(f32[16,6,512]{2,1,0:T(8,128)S(1)} %all_to_all.8), channel_id=1, replica_groups=mesh['groups'=2,'prow'=16] {'prow'}, dimensions={0} | all-to-all | bytes 393216 | tf_op jit(solution)/shard_map/all_to_all | solution.py:379
  134.2 0.7 all_to_all.10
  (19 shorter events, 0.2 us)
Async XLA Ops:
  0.6 1.2 copy-start.2
  0.6 4.4 %copy-start.3 = (s32[96,96]{1,0:T(8,128)S(1)}, s32[96,96]{1,0:T(8,128)}, u32[]{:S(2)}) copy-start(s32[96,96]{1,0:T(8,128)} %refs_2_.9) | copy-start | bytes 110596
  1.9 3.6 %copy-start.4 = (f32[96,96]{1,0:T(8,128)S(1)}, f32[96,96]{1,0:T(8,128)}, u32[]{:S(2)}) copy-start(f32[96,96]{1,0:T(8,128)} %refs_3_.9) | copy-start | bytes 110596
  1.9 3.7 %copy-start.7 = (f32[96]{0:T(128)S(1)}, f32[96]{0:T(128)}, u32[]{:S(2)}) copy-start(f32[96]{0:T(128)} %refs_4_.9) | copy-start | bytes 1156
  1.9 23.0 %collective-permute-start = (bf16[1152,512]{1,0:T(8,128)(2,1)S(1)}, bf16[1152,512]{1,0:T(8,128)(2,1)}, u32[]{:S(2)}, u32[]{:S(2)}) collective-permute-start(bf16[1152,512]{1,0:T(8,128)(2,1)S(1)} %constant_dynamic-update-slice_fusion.refs_3_), channel_id=1, source_target_pairs={{2,0},{5,1},{6,2},{1,3},{0,4},{9,5},{10,6},{3,7},{4,8},{13,9},{14,... | collective-permute-start | bytes 3538952 | tf_op jit(solution)/shard_map/ppermute | solution.py:328
  15.3 20.9 %collective-permute-start.2 = (bf16[1152,512]{1,0:T(8,128)(2,1)S(1)}, bf16[1152,512]{1,0:T(8,128)(2,1)S(1)}, u32[]{:S(2)}, u32[]{:S(2)}) collective-permute-start(bf16[1152,512]{1,0:T(8,128)(2,1)S(1)} %constant_dynamic-update-slice_fusion.refs_3_), channel_id=1, source_target_pairs={{0,2},{1,5},{2,6},{3,1},{4,0},{5,9},{6,10},{7,3},{8,4},{9,13},{10,... | collective-permute-start | bytes 3538952 | tf_op jit(solution)/shard_map/ppermute | solution.py:328
  25.0 25.8 %collective-permute-start.1 = (bf16[1152,512]{1,0:T(8,128)(2,1)}, bf16[1152,512]{1,0:T(8,128)(2,1)}, u32[]{:S(2)}, u32[]{:S(2)}) collective-permute-start(bf16[1152,512]{1,0:T(8,128)(2,1)} %collective-permute-done.refs_5_), channel_id=1, source_target_pairs={{2,0},{5,1},{6,2},{1,3},{0,4},{9,5},{10,6},{3,7},{4,8},{13,9},{14,... | collective-permute-start | bytes 3538952 | tf_op jit(solution)/shard_map/ppermute | solution.py:328
  36.3 10.9 %copy-start.9 = (bf16[1152,512]{1,0:T(8,128)(2,1)}, bf16[1152,512]{1,0:T(8,128)(2,1)S(1)}, u32[]{:S(2)}) copy-start(bf16[1152,512]{1,0:T(8,128)(2,1)S(1)} %collective-permute-done.2.refs_7_) | copy-start | bytes 3538948
  36.3 25.9 %collective-permute-start.4 = (bf16[1152,512]{1,0:T(8,128)(2,1)S(1)}, bf16[1152,512]{1,0:T(8,128)(2,1)}, u32[]{:S(2)}, u32[]{:S(2)}) collective-permute-start(bf16[1152,512]{1,0:T(8,128)(2,1)S(1)} %collective-permute-done.2.refs_7_), channel_id=1, source_target_pairs={{0,2},{1,5},{2,6},{3,1},{4,0},{5,9},{6,10},{7,3},{8,4},{9,13},{10,... | collective-permute-start | bytes 3538952 | tf_op jit(solution)/shard_map/ppermute | solution.py:328
  36.5 25.7 %collective-permute-start.5 = (bf16[1152,512]{1,0:T(8,128)(2,1)S(1)}, bf16[1152,512]{1,0:T(8,128)(2,1)S(1)}, u32[]{:S(2)}, u32[]{:S(2)}) collective-permute-start(bf16[1152,512]{1,0:T(8,128)(2,1)S(1)} %constant_dynamic-update-slice_fusion.refs_3_), channel_id=1, source_target_pairs={{0,1},{1,0},{2,3},{3,2},{4,5},{5,4},{6,7},{7,6},{8,9},{9,8},{10,11... | collective-permute-start | bytes 3538952 | tf_op jit(solution)/shard_map/ppermute | solution.py:328
  37.0 26.7 %collective-permute-start.6 = (bf16[1152,512]{1,0:T(8,128)(2,1)S(1)}, bf16[1152,512]{1,0:T(8,128)(2,1)S(1)}, u32[]{:S(2)}, u32[]{:S(2)}) collective-permute-start(bf16[1152,512]{1,0:T(8,128)(2,1)S(1)} %collective-permute-done.2.refs_7_), channel_id=1, source_target_pairs={{0,1},{1,0},{2,3},{3,2},{4,5},{5,4},{6,7},{7,6},{8,9},{9,8},{10,11... | collective-permute-start | bytes 3538952 | tf_op jit(solution)/shard_map/ppermute | solution.py:328
  37.0 28.6 %collective-permute-start.7 = (bf16[1152,512]{1,0:T(8,128)(2,1)}, bf16[1152,512]{1,0:T(8,128)(2,1)}, u32[]{:S(2)}, u32[]{:S(2)}) collective-permute-start(bf16[1152,512]{1,0:T(8,128)(2,1)} %collective-permute-done.refs_5_), channel_id=1, source_target_pairs={{0,1},{1,0},{2,3},{3,2},{4,5},{5,4},{6,7},{7,6},{8,9},{9,8},{10,11... | collective-permute-start | bytes 3538952 | tf_op jit(solution)/shard_map/ppermute | solution.py:328
  50.8 29.2 %collective-permute-start.3 = (bf16[1152,512]{1,0:T(8,128)(2,1)}, bf16[1152,512]{1,0:T(8,128)(2,1)S(1)}, u32[]{:S(2)}, u32[]{:S(2)}) collective-permute-start(bf16[1152,512]{1,0:T(8,128)(2,1)} %collective-permute-done.1.refs_3_), channel_id=1, source_target_pairs={{2,0},{5,1},{6,2},{1,3},{0,4},{9,5},{10,6},{3,7},{4,8},{13,9},{14,... | collective-permute-start | bytes 3538952 | tf_op jit(solution)/shard_map/ppermute | solution.py:328
  62.2 17.8 %collective-permute-start.10 = (bf16[1152,512]{1,0:T(8,128)(2,1)}, bf16[1152,512]{1,0:T(8,128)(2,1)}, u32[]{:S(2)}, u32[]{:S(2)}) collective-permute-start(bf16[1152,512]{1,0:T(8,128)(2,1)} %collective-permute-done.4.refs_5_), channel_id=1, source_target_pairs={{0,1},{1,0},{2,3},{3,2},{4,5},{5,4},{6,7},{7,6},{8,9},{9,8},{10,11... | collective-permute-start | bytes 3538952 | tf_op jit(solution)/shard_map/ppermute | solution.py:328
  62.2 1.0 copy-start.5
  63.2 16.8 %collective-permute-start.11 = (bf16[1152,512]{1,0:T(8,128)(2,1)}, bf16[1152,512]{1,0:T(8,128)(2,1)}, u32[]{:S(2)}, u32[]{:S(2)}) collective-permute-start(bf16[1152,512]{1,0:T(8,128)(2,1)} %collective-permute-done.1.refs_3_), channel_id=1, source_target_pairs={{0,1},{1,0},{2,3},{3,2},{4,5},{5,4},{6,7},{7,6},{8,9},{9,8},{10,11... | collective-permute-start | bytes 3538952 | tf_op jit(solution)/shard_map/ppermute | solution.py:328
  63.7 1.0 copy-start.10
  64.8 25.5 %collective-permute-start.9 = (bf16[1152,512]{1,0:T(8,128)(2,1)}, bf16[1152,512]{1,0:T(8,128)(2,1)}, u32[]{:S(2)}, u32[]{:S(2)}) collective-permute-start(bf16[1152,512]{1,0:T(8,128)(2,1)} %collective-permute-done.4.refs_5_), channel_id=1, source_target_pairs={{0,2},{1,5},{2,6},{3,1},{4,0},{5,9},{6,10},{7,3},{8,4},{9,13},{10,... | collective-permute-start | bytes 3538952 | tf_op jit(solution)/shard_map/ppermute | solution.py:328
  65.7 1.3 copy-start.6
  90.3 4.8 %collective-permute-start.12 = (bf16[1152,512]{1,0:T(8,128)(2,1)}, bf16[1152,512]{1,0:T(8,128)(2,1)S(1)}, u32[]{:S(2)}, u32[]{:S(2)}) collective-permute-start(bf16[1152,512]{1,0:T(8,128)(2,1)} %collective-permute-done.9.refs_5_), channel_id=1, source_target_pairs={{0,1},{1,0},{2,3},{3,2},{4,5},{5,4},{6,7},{7,6},{8,9},{9,8},{10,11... | collective-permute-start | bytes 3538952 | tf_op jit(solution)/shard_map/ppermute | solution.py:328
  91.5 4.2 %collective-permute-start.13 = (bf16[1152,512]{1,0:T(8,128)(2,1)S(1)}, bf16[1152,512]{1,0:T(8,128)(2,1)S(1)}, u32[]{:S(2)}, u32[]{:S(2)}) collective-permute-start(bf16[1152,512]{1,0:T(8,128)(2,1)S(1)} %collective-permute-done.3.refs_3_), channel_id=1, source_target_pairs={{0,1},{1,0},{2,3},{3,2},{4,5},{5,4},{6,7},{7,6},{8,9},{9,8},{10,11... | collective-permute-start | bytes 3538952 | tf_op jit(solution)/shard_map/ppermute | solution.py:328
  92.6 15.2 %collective-permute-start.14 = (bf16[576,512]{1,0:T(8,128)(2,1)S(1)}, bf16[576,512]{1,0:T(8,128)(2,1)S(1)}, u32[]{:S(2)}, u32[]{:S(2)}) collective-permute-start(bf16[576,512]{1,0:T(8,128)(2,1)S(1)} %slice.7), channel_id=1, source_target_pairs={{0,2},{1,5},{2,6},{3,1},{4,0},{5,9},{6,10},{7,3},{8,4},{9,13},{10,... | collective-permute-start | bytes 1769480 | tf_op jit(solution)/shard_map/ppermute | solution.py:328
  93.9 14.5 %collective-permute-start.8 = (bf16[576,512]{1,0:T(8,128)(2,1)S(1)}, bf16[576,512]{1,0:T(8,128)(2,1)S(1)}, u32[]{:S(2)}, u32[]{:S(2)}) collective-permute-start(bf16[576,512]{1,0:T(8,128)(2,1)S(1)} %slice.6), channel_id=1, source_target_pairs={{2,0},{5,1},{6,2},{1,3},{0,4},{9,5},{10,6},{3,7},{4,8},{13,9},{14,... | collective-permute-start | bytes 1769480 | tf_op jit(solution)/shard_map/ppermute | solution.py:328
  95.6 1.0 copy-start.8
  96.6 14.1 %copy-start.1 = (bf16[576,512]{1,0:T(8,128)(2,1)S(1)}, bf16[576,512]{1,0:T(8,128)(2,1)}, u32[]{:S(2)}) copy-start(bf16[576,512]{1,0:T(8,128)(2,1)} %refs_10_.1) | copy-start | bytes 1769476
  106.1 1.1 copy-start
  107.9 2.0 %collective-permute-start.16 = (bf16[576,512]{1,0:T(8,128)(2,1)S(1)}, bf16[576,512]{1,0:T(8,128)(2,1)S(1)}, u32[]{:S(2)}, u32[]{:S(2)}) collective-permute-start(bf16[576,512]{1,0:T(8,128)(2,1)S(1)} %collective-permute-done.14.refs_4_), channel_id=1, source_target_pairs={{0,1},{1,0},{2,3},{3,2},{4,5},{5,4},{6,7},{7,6},{8,9},{9,8},{10,11... | collective-permute-start | bytes 1769480 | tf_op jit(solution)/shard_map/ppermute | solution.py:328
  108.4 2.4 %collective-permute-start.15 = (bf16[576,512]{1,0:T(8,128)(2,1)S(1)}, bf16[576,512]{1,0:T(8,128)(2,1)S(1)}, u32[]{:S(2)}, u32[]{:S(2)}) collective-permute-start(bf16[576,512]{1,0:T(8,128)(2,1)S(1)} %collective-permute-done.8.refs_3_), channel_id=1, source_target_pairs={{0,1},{1,0},{2,3},{3,2},{4,5},{5,4},{6,7},{7,6},{8,9},{9,8},{10,11... | collective-permute-start | bytes 1769480 | tf_op jit(solution)/shard_map/ppermute | solution.py:328

commit v7 on v6

--- a/solution.py
+++ b/solution.py
@@ -82,23 +82,29 @@
     pitch = orbitals + 1
     room = orbitals * pitch
 
-    @pl.loop(0, tiles // 2)
-    def _(tile):
-        cols = pl.ds(pl.multiple_of(tile * 2 * span, 128), 2 * span)
-        for strip in strips:
-            size = min(128, high - low - strip)
-            turned = inter_ref[strip : strip + size, cols].astype(jnp.float32).T
-            at = pl.multiple_of(strip // 128 * room + tile * 8 * pitch, 8)
-            for m in range(8):
-                there = pl.ds(at + m * pitch, orbitals)
-                turned_ref[there, :size] = turned[m * orbitals : (m + 1) * orbitals]
+    @pl.when(pl.program_id(0) == 0)
+    def _():
+        @pl.loop(0, tiles // 2)
+        def _(tile):
+            cols = pl.ds(pl.multiple_of(tile * 2 * span, 128), 2 * span)
+            for strip in strips:
+                size = min(128, high - low - strip)
+                turned = inter_ref[strip : strip + size, cols].astype(jnp.float32).T
+                at = pl.multiple_of(strip // 128 * room + tile * 8 * pitch, 8)
+                for m in range(8):
+                    there = pl.ds(at + m * pitch, orbitals)
+                    turned_ref[there, :size] = turned[m * orbitals : (m + 1) * orbitals]
 
     group = lax.broadcasted_iota(jnp.int32, (1, span), 1) // orbitals
     occ4 = occ4_ref[...]
 
-    @pl.loop(0, tiles)
-    def _(tile):
+    per_chunk = mixed_ref.shape[1] // span
+
+    @pl.loop(0, per_chunk, unroll=2)
+    def _(step):
+        tile = pl.program_id(0) * per_chunk + step
         cols = pl.ds(pl.multiple_of(tile * span, 128), span)
+        out_cols = pl.ds(pl.multiple_of(step * span, 128), span)
 
         def spread(values):
             row = jnp.where(group == 0, values[0], values[1])
@@ -141,8 +147,8 @@
             ladder = (block[there] * ladder_row).astype(jnp.bfloat16)
             direct = (polar + hop).astype(jnp.bfloat16).astype(jnp.float32)
             held = polar.astype(jnp.bfloat16)
-            polar_ref[there, cols] = held
-            mixed_ref[there, cols] = (
+            polar_ref[there, out_cols] = held
+            mixed_ref[there, out_cols] = (
                 direct - held.astype(jnp.float32) + ladder.astype(jnp.float32)
             ).astype(jnp.bfloat16)
             row += count
@@ -155,8 +161,11 @@
     height = high - low
     block = low // height
     assert low % height == 0
-    shape = jax.ShapeDtypeStruct((rows, pairs), jnp.bfloat16)
-    wide = pl.BlockSpec((height, pairs), lambda g, p: (block, 0))
+    shape = pltpu.HBM((rows, pairs), jnp.bfloat16)
+    chunks = 4
+    once = pl.Buffered(1)
+    wide = pl.BlockSpec((height, pairs), lambda g, p: (block, 0), pipeline_mode=once)
+    chunk = pl.BlockSpec((height, pairs // chunks), lambda g, p: (block, g))
     smem = pl.BlockSpec(memory_space=pltpu.SMEM)
     row4 = pl.BlockSpec((1, 4 * orbitals), lambda g, p: (0, 0))
     small = pl.BlockSpec((orbitals, 4 * orbitals), lambda g, p: (0, 0))
@@ -164,15 +173,15 @@
         functools.partial(build_body, orbitals, low, high, pairs),
         grid_spec=pltpu.PrefetchScalarGridSpec(
             num_scalar_prefetch=1,
-            grid=(1,),
+            grid=(chunks,),
             in_specs=[wide, smem, smem, smem, small, small, small, row4]
             + [pl.BlockSpec(memory_space=pl.ANY)] * len(made),
-            out_specs=[wide] * 2,
+            out_specs=[chunk] * 2,
             scratch_shapes=[pltpu.VMEM((-(-height // 128) * orbitals * (orbitals + 1), 128), jnp.float32)],
         ),
         out_shape=[shape] * 2,
         input_output_aliases={9 + n: n for n in range(len(made))},
-        compiler_params=pltpu.CompilerParams(vmem_limit_bytes=44 * MIB),
+        compiler_params=pltpu.CompilerParams(vmem_limit_bytes=28 * MIB),
         cost_estimate=pl.CostEstimate(flops=1024, bytes_accessed=1024, transcendentals=0),
         name="build_rows",
     )(place, interaction, *smalls, *made)
@@ -236,9 +245,7 @@
                     refs[kind][part, :] = slope
                     refs[2 + kind][part, :] = (old + 0.5 * slope).astype(jnp.bfloat16)
                     both = slope if both is None else both + slope
-                summed = jnp.sum(both, axis=0, keepdims=True) * scale
-                for copy in range(first, refs[4].shape[0], rows // orbitals):
-                    refs[4][copy : copy + 1, :] = summed
+                refs[4][first : first + 1, :] = jnp.sum(both, axis=0, keepdims=True) * scale
 
 
 def step(place, low, mats, greens, sums, olds, orbitals):
@@ -254,23 +261,27 @@
     wide_sum = jax.ShapeDtypeStruct((rows, width), jnp.float32)
     scratch = [pltpu.VMEM((wide, 3 * span), jnp.bfloat16)]
     if closing:
-        out_specs = [tall] * 4 + [pl.BlockSpec((orbitals, span), lambda n, g, p: (0, n))]
+        out_specs = [tall] * 4 + [pl.BlockSpec((rows // orbitals, span), lambda n, g, p: (0, n))]
         out_shape = [wide_sum] * 2 + [jax.ShapeDtypeStruct((rows, width), jnp.bfloat16)] * 2
-        out_shape += [jax.ShapeDtypeStruct((orbitals, width), jnp.float32)]
+        out_shape += [jax.ShapeDtypeStruct((rows // orbitals, width), jnp.float32)]
         scratch = [pltpu.VMEM((rows, span), jnp.float32)] * 3 + scratch
     else:
         out_specs, out_shape = [tall] * 3, [wide_sum] * 3
-    operands = list(mats)
+    operands = [pltpu.with_memory_space_constraint(mat_, pltpu.HBM) for mat_ in mats]
     blocks = [block for pair in greens for side in pair for block in side]
     operands += blocks
     in_specs = [mat] * 2
-    in_specs += [pl.BlockSpec((block.shape[0], span), lambda n, g, p: (0, n)) for block in blocks]
+    mode = pl.Buffered(1 if span == width else 2)
+    in_specs += [
+        pl.BlockSpec((block.shape[0], span), lambda n, g, p: (0, n), pipeline_mode=mode)
+        for block in blocks
+    ]
     aliases = {}
     if not opening:
         if not closing:
             aliases = {1 + len(operands) + n: n for n in range(3)}
         operands += list(sums)
-        in_specs += [tall] * 3
+        in_specs += [pl.BlockSpec((rows, span), lambda n, g, p: (0, n), pipeline_mode=mode)] * 3
     if closing:
         operands += list(olds)
         in_specs += [tall] * 2
@@ -287,10 +298,22 @@
         ),
         out_shape=out_shape,
         input_output_aliases=aliases,
-        compiler_params=pltpu.CompilerParams(vmem_limit_bytes=48 * MIB),
+        compiler_params=pltpu.CompilerParams(vmem_limit_bytes=36 * MIB),
         cost_estimate=pl.CostEstimate(flops=1024, bytes_accessed=1024, transcendentals=0),
         name="add_products",
     )(place, *operands)
+
+
+def spread_blocks(block, index, stride, devices):
+    blocks = [block]
+    for other in range(1, 4):
+        pairs_of = [(d, d ^ (other * stride)) for d in range(devices)]
+        blocks.append(lax.ppermute(block, "prow", pairs_of))
+    part = index // stride % 4
+    low, high = part % 2 == 1, part // 2 == 1
+    b = [jnp.where(low, blocks[n ^ 1], blocks[n]) for n in range(4)]
+    b = [jnp.where(high, b[n ^ 2], b[n]) for n in range(4)]
+    return jnp.concatenate(b, axis=0)
 
 
 def after(value, *others):
@@ -320,13 +343,14 @@
     for d in range(devices):
         line = [d % 2, d // 2]
         for far in range(1, half + 1):
-            line += [away(d, far), away(d, -far)]
+            line += [away(d, -far), away(d, far)]
         table.append(line)
     place = lax.dynamic_index_in_dim(jnp.array(table, jnp.int32), me, 0, keepdims=False)
 
     def send(block, pairs_of):
         return lax.ppermute(block, "prow", pairs_of)
 
+    interaction = pltpu.with_memory_space_constraint(interaction, pltpu.HBM)
     start = (me * (rows // orbitals)).astype(jnp.int32)[None]
     smalls = (
         pattern,
@@ -338,11 +362,12 @@
         jnp.tile(occupation, 4)[None],
     )
 
-    def build(when, made, strip):
-        low = 128 * strip
-        return build_rows(when, interaction, smalls, made, low, min(low + 128, rows))
-
-    strips = -(-rows // 128)
+    big = rows // 9 * 4
+    cuts = [(0, big), (big, 2 * big), (2 * big, rows)]
+
+    def build(when, made, part):
+        return build_rows(when, interaction, smalls, made, *cuts[part])
+
     own = jnp.concatenate([green_same, green_opp], axis=0)
     moving = [send(own, first_way), None]
     mats = build(start, (), 0)
@@ -351,7 +376,8 @@
     near = send(own_later, across)
     mats = build(start, mats, 1)
 
-    chips_in, low, sums, done, made = [([own], [near])], 0, (), mats[0], 2
+    low, sums, done = 0, (), mats[0]
+    waiting = [([own], [near])]
     for far in range(1, half):
         got, passed = [], []
         for turn in range(2):
@@ -360,23 +386,29 @@
             moving[turn] = send(onward, second_way if turn else first_way)
             got.append(block)
             passed.append(send(block, across))
-            if made < strips:
-                mats = build(after(start, block), mats, made)
-                made += 1
+            if far == 1 and turn == 0:
+                mats = build(after(start, block), mats, 2)
                 done = mats[0]
-            if far > 1 and turn == (far == 2) and made == strips:
-                sums = step(after(place, block), low, mats, chips_in, sums, (), orbitals)
-                low += len(chips_in)
-                chips_in, done = [], sums[0]
-        chips_in = chips_in + [([got[0]], [passed[1]]), ([got[1]], [passed[0]])]
-    sums = step(place, low, mats, chips_in, sums, (), orbitals)
-    low += len(chips_in)
+                continue
+            later = []
+            if turn == 1:
+                came = [([got[1]], [passed[0]]), ([got[0]], [passed[1]])]
+                split = 0 if far == 1 else 1
+                waiting, later = waiting + came[:split], came[split:]
+            sums = step(after(place, block), low, mats, waiting, sums, (), orbitals)
+            low += len(waiting)
+            waiting, done = later, sums[0]
+    sums = step(place, low, mats, waiting, sums, (), orbitals)
+    low += len(waiting)
     last = [after(block, sums[0]) for block in moving]
     shared = [send(block, across) for block in last]
     new_same, new_opp, next_same, next_opp, part = step(
         place, low, mats, [(last, shared)], sums, (green_same, green_opp), orbitals
     )
-    collision = lax.all_to_all(part, "prow", split_axis=0, concat_axis=0, tiled=True)
+    if devices == 16:
+        collision = spread_blocks(spread_blocks(part, me, 1, devices), me, 4, devices)
+    else:
+        collision = lax.all_gather(part, "prow", axis=0, tiled=True)
     return (new_same, new_opp, next_same, next_opp, collision)
 
 

time: 135 us -> 128 us (0.948)
  blocking collectives: 16 us -> 0 us
  waiting for transfers between devices: 8.29 us -> 24 us
  Pallas kernels: 86.7 us -> 76.6 us
  starting transfers between devices: 13.3 us -> 19.4 us
  local copies, waits for them, and re-layouts: 9.82 us -> 5.07 us
  other arithmetic: 0.02 us -> 1.38 us
    all_to_all x1 -> x0, blocking collectives: 16 us -> none  [ring_form(): lax.all_to_all(part, 'prow', split_axis=0, concat_axis=0, tiled=True)]
    pallas_call x5 -> x3, Pallas kernels: 46.4 us -> 30.8 us  [build_rows(): pl.pallas_call(functools.partial(build_body, orbitals, low, high, pairs),...]
    ppermute x17, waiting for transfers between devices: 8.29 us -> 16.6 us  [send(): return lax.ppermute(block, 'prow', pairs_of)]
    ppermute x0 -> x6, waiting for transfers between devices: none -> 7.33 us  [spread_blocks(): blocks.append(lax.ppermute(block, 'prow', pairs_of))]
    ppermute x0 -> x6, starting transfers between devices: none -> 6.31 us  [spread_blocks(): blocks.append(lax.ppermute(block, 'prow', pairs_of))]
    pallas_call x4 -> x7, Pallas kernels: 40.3 us -> 45.8 us  [step(): pl.pallas_call(functools.partial(step_body, parts, rows, opening, closing...]
    unnamed x23 -> x11, local copies, waits for them, and re-layouts: 6.6 us -> 1.24 us
    another operation x2, local copies, waits for them, and re-layouts: 0.18 us -> 1.78 us  [ring_form(): jnp.tile(hopping, (1, 4))]
  transfers between devices with their start and end apart: 17 -> 23, of which waited for: 7 -> 12; matrix products, arithmetic and copies ran while one was open for 2% -> 3% of each run, Pallas kernels for 59% -> 54%
where the time goes in v7:
time: 128 us; the launch traced here: 127 us
  Pallas kernels  76.6 us (60%)
  waiting for transfers between devices  24 us (19%)
  starting transfers between devices  19.4 us (15%)
  local copies, waits for them, and re-layouts  5.07 us (4%)
  other arithmetic  1.38 us (1%)
    pallas_call x7, Pallas kernels, step(): pl.pallas_call(functools.partial(step_body, parts, rows, opening, closing...  45.8 us
    pallas_call x3, Pallas kernels, build_rows(): pl.pallas_call(functools.partial(build_body, orbitals, low, high, pairs),...  30.8 us
    ppermute x17, waiting for transfers between devices, send(): return lax.ppermute(block, 'prow', pairs_of)  16.6 us
    ppermute x17, starting transfers between devices, send(): return lax.ppermute(block, 'prow', pairs_of)  13.1 us
    ppermute x6, waiting for transfers between devices, spread_blocks(): blocks.append(lax.ppermute(block, 'prow', pairs_of))  7.33 us
    ppermute x6, starting transfers between devices, spread_blocks(): blocks.append(lax.ppermute(block, 'prow', pairs_of))  6.31 us
  transfers between devices with their start and end apart: 23, of which 12 were waited for; matrix products, arithmetic and copies ran while one was open for 3% of the time, Pallas kernels for 54%

profile of v7, /device:TPU:0, one launch (start us, length us, event | category | flops | bytes accessed | tf_op | source)
XLA Modules:
  0.0 127.3 jit_solution(3496886113135030202)
XLA Ops:
  0.7 1.2 constant_dynamic-update-slice_fusion.1
  1.8 0.1 copy-done.1
  1.9 0.0 copy-start.4
  1.9 3.1 %collective-permute-start = (bf16[1152,512]{1,0:T(8,128)(2,1)S(1)}, bf16[1152,512]{1,0:T(8,128)(2,1)S(1)}, u32[]{:S(2)}, u32[]{:S(2)}) collective-permute-start(bf16[1152,512]{1,0:T(8,128)(2,1)S(1)} %constant_dynamic-update-slice_fusion.refs_3_), channel_id=1, source_target_pairs={{2,0},{5,1},{6,2},{1,3},{0,4},{9,5},{10,6},{3,7},{4,8},{13,9},{14,... | collective-permute-start | bytes 3538952 | tf_op jit(solution)/shard_map/ppermute | solution.py:351
  5.0 0.6 fusion
  5.7 0.1 tile.42.refs_5_
  5.8 0.8 tile.45
  6.7 0.1 tile.46.refs_7_
  6.8 0.7 tile.43
  7.5 1.1 tile.44.refs_6_
  8.6 0.1 broadcast_in_dim_tile.3.refs_8_
  8.7 11.8 %build_rows.3 = (bf16[576,9216]{1,0:T(8,128)(2,1)}, bf16[576,9216]{1,0:T(8,128)(2,1)}) custom-call(s32[1]{0:T(128)} %bitcast.1.refs_0_, bf16[576,9216]{1,0:T(8,128)(2,1)} %refs_1_.5, s32[96,96]{1,0:T(8,128)S(1)} %copy-done.2, f32[96,96]{1,0:T(8,128)S(1)} %copy-done.3, f32[96]{0:T(128)S(1)} %copy-done.4, f32[96,384]{1,0:T(8,128)S(1)} %tile.42.refs_5_, ...), custom_call_target="tpu_custom_call" | custom-call | flops 1024 | bytes 1024 | tf_op jit(solution)/shard_map/build_rows/pallas_call | solution.py:172
  20.5 0.0 collective-permute-start.2
  20.5 0.0 collective-permute-start.3
  20.5 11.9 %build_rows.4 = (bf16[576,9216]{1,0:T(8,128)(2,1)}, bf16[576,9216]{1,0:T(8,128)(2,1)}) custom-call(s32[1]{0:T(128)} %bitcast.1.refs_0_, bf16[576,9216]{1,0:T(8,128)(2,1)} %refs_1_.5, s32[96,96]{1,0:T(8,128)S(1)} %copy-done.2, f32[96,96]{1,0:T(8,128)S(1)} %copy-done.3, f32[96]{0:T(128)S(1)} %copy-done.4, ...), custom_call_target="tpu_custom_call", output_to_operand_aliasing={{0}: (9, {}), {1}: (10, {})} | custom-call | flops 1024 | bytes 1024 | tf_op jit(solution)/shard_map/build_rows/pallas_call | solution.py:172
  32.4 0.0 collective-permute-done.refs_5_
  32.4 2.0 %collective-permute-start.1 = (bf16[1152,512]{1,0:T(8,128)(2,1)S(1)}, bf16[1152,512]{1,0:T(8,128)(2,1)}, u32[]{:S(2)}, u32[]{:S(2)}) collective-permute-start(bf16[1152,512]{1,0:T(8,128)(2,1)S(1)} %collective-permute-done.refs_5_), channel_id=1, source_target_pairs={{2,0},{5,1},{6,2},{1,3},{0,4},{9,5},{10,6},{3,7},{4,8},{13,9},{14,... | collective-permute-start | bytes 3538952 | tf_op jit(solution)/shard_map/ppermute | solution.py:351
  34.4 7.1 %build_rows.5 = (bf16[576,9216]{1,0:T(8,128)(2,1)}, bf16[576,9216]{1,0:T(8,128)(2,1)}) custom-call(s32[1]{0:T(128)} %bitcast.1.refs_0_, bf16[576,9216]{1,0:T(8,128)(2,1)} %refs_1_.5, s32[96,96]{1,0:T(8,128)S(1)} %copy-done.2, f32[96,96]{1,0:T(8,128)S(1)} %copy-done.3, f32[96]{0:T(128)S(1)} %copy-done.4, ...), custom_call_target="tpu_custom_call", output_to_operand_aliasing={{0}: (9, {}), {1}: (10, {})} | custom-call | flops 1024 | bytes 1024 | tf_op jit(solution)/shard_map/build_rows/pallas_call | solution.py:172
  41.5 0.0 collective-permute-done.2.refs_3_
  41.5 0.2 collective-permute-start.7
  41.7 0.3 collective-permute-start.6
  42.1 1.3 %collective-permute-start.5 = (bf16[1152,512]{1,0:T(8,128)(2,1)}, bf16[1152,512]{1,0:T(8,128)(2,1)}, u32[]{:S(2)}, u32[]{:S(2)}) collective-permute-start(bf16[1152,512]{1,0:T(8,128)(2,1)} %collective-permute-done.2.refs_3_), channel_id=1, source_target_pairs={{0,2},{1,5},{2,6},{3,1},{4,0},{5,9},{6,10},{7,3},{8,4},{9,13},{10,... | collective-permute-start | bytes 3538952 | tf_op jit(solution)/shard_map/ppermute | solution.py:351
  43.4 0.7 dynamic-slice_bitcast_fusion.refs_0_
  44.1 5.8 %add_products.7 = (f32[576,512]{1,0:T(8,128)S(1)}, f32[576,512]{1,0:T(8,128)S(1)}, f32[576,512]{1,0:T(8,128)S(1)}) custom-call(s32[10]{0:T(128)S(1)} %dynamic-slice_bitcast_fusion.refs_0_, bf16[576,9216]{1,0:T(8,128)(2,1)} %get-tuple-element.55.refs_1_, bf16[576,9216]{1,0:T(8,128)(2,1)} %get-tuple-element.56.refs_2_, ...), custom_call_target="tpu_custom_call" | custom-call | flops 1024 | bytes 1024 | tf_op jit(solution)/shard_map/add_products/pallas_call | solution.py:288
  49.9 2.4 %collective-permute-done.1.refs_3_ = bf16[1152,512]{1,0:T(8,128)(2,1)} collective-permute-done((bf16[1152,512]{1,0:T(8,128)(2,1)S(1)}, bf16[1152,512]{1,0:T(8,128)(2,1)}, u32[]{:S(2)}, u32[]{:S(2)}) %collective-permute-start.1) | collective-permute-done | bytes 1179680 | tf_op jit(solution)/shard_map/ppermute | solution.py:351
  52.3 0.7 collective-permute-start.8
  53.0 1.8 %collective-permute-start.4 = (bf16[1152,512]{1,0:T(8,128)(2,1)}, bf16[1152,512]{1,0:T(8,128)(2,1)S(1)}, u32[]{:S(2)}, u32[]{:S(2)}) collective-permute-start(bf16[1152,512]{1,0:T(8,128)(2,1)} %collective-permute-done.1.refs_3_), channel_id=1, source_target_pairs={{2,0},{5,1},{6,2},{1,3},{0,4},{9,5},{10,6},{3,7},{4,8},{13,9},{14,... | collective-permute-start | bytes 3538952 | tf_op jit(solution)/shard_map/ppermute | solution.py:351
  54.8 9.9 %add_products.8 = (f32[576,512]{1,0:T(8,128)S(1)}, f32[576,512]{1,0:T(8,128)S(1)}, f32[576,512]{1,0:T(8,128)S(1)}) custom-call(s32[10]{0:T(128)S(1)} %dynamic-slice_bitcast_fusion.refs_0_, bf16[576,9216]{1,0:T(8,128)(2,1)} %get-tuple-element.55.refs_1_, ...), custom_call_target="tpu_custom_call", output_to_operand_aliasing={{0}: (7, {}), {1}: (8, {}), {2}: (9, {})} | custom-call | flops 1024 | bytes 1024 | tf_op jit(solution)/shard_map/add_products/pallas_call | solution.py:288
  64.6 3.0 %collective-permute-done.5.refs_3_ = bf16[1152,512]{1,0:T(8,128)(2,1)} collective-permute-done((bf16[1152,512]{1,0:T(8,128)(2,1)}, bf16[1152,512]{1,0:T(8,128)(2,1)}, u32[]{:S(2)}, u32[]{:S(2)}) %collective-permute-start.5) | collective-permute-done | bytes 1179680 | tf_op jit(solution)/shard_map/ppermute | solution.py:351
  67.6 0.0 collective-permute-start.11
  67.6 0.5 collective-permute-start.10
  68.1 0.0 collective-permute-done.8.refs_4_
  68.1 5.9 %add_products.9 = (f32[576,512]{1,0:T(8,128)S(1)}, f32[576,512]{1,0:T(8,128)S(1)}, f32[576,512]{1,0:T(8,128)S(1)}) custom-call(s32[10]{0:T(128)S(1)} %dynamic-slice_bitcast_fusion.refs_0_, bf16[576,9216]{1,0:T(8,128)(2,1)} %get-tuple-element.55.refs_1_, ...), custom_call_target="tpu_custom_call", output_to_operand_aliasing={{0}: (5, {}), {1}: (6, {}), {2}: (7, {})} | custom-call | flops 1024 | bytes 1024 | tf_op jit(solution)/shard_map/add_products/pallas_call | solution.py:288
  74.0 3.0 %collective-permute-done.4.refs_3_ = bf16[1152,512]{1,0:T(8,128)(2,1)S(1)} collective-permute-done((bf16[1152,512]{1,0:T(8,128)(2,1)}, bf16[1152,512]{1,0:T(8,128)(2,1)S(1)}, u32[]{:S(2)}, u32[]{:S(2)}) %collective-permute-start.4) | collective-permute-done | bytes 1179680 | tf_op jit(solution)/shard_map/ppermute | solution.py:351
  77.0 0.8 collective-permute-start.13
  77.8 0.0 collective-permute-done.11.refs_4_
  77.8 5.9 %add_products.10 = (f32[576,512]{1,0:T(8,128)S(1)}, f32[576,512]{1,0:T(8,128)S(1)}, f32[576,512]{1,0:T(8,128)S(1)}) custom-call(s32[10]{0:T(128)S(1)} %dynamic-slice_bitcast_fusion.refs_0_, bf16[576,9216]{1,0:T(8,128)(2,1)} %get-tuple-element.55.refs_1_, ...), custom_call_target="tpu_custom_call", output_to_operand_aliasing={{0}: (5, {}), {1}: (6, {}), {2}: (7, {})} | custom-call | flops 1024 | bytes 1024 | tf_op jit(solution)/shard_map/add_products/pallas_call | solution.py:288
  83.7 3.5 %collective-permute-done.10.refs_3_ = bf16[1152,512]{1,0:T(8,128)(2,1)S(1)} collective-permute-done((bf16[1152,512]{1,0:T(8,128)(2,1)}, bf16[1152,512]{1,0:T(8,128)(2,1)S(1)}, u32[]{:S(2)}, u32[]{:S(2)}) %collective-permute-start.10) | collective-permute-done | bytes 1179680 | tf_op jit(solution)/shard_map/ppermute | solution.py:351
  87.3 1.1 collective-permute-start.14
  88.4 1.0 collective-permute-start.9
  89.5 0.0 collective-permute-done.13.refs_4_
  89.5 5.5 %add_products.11 = (f32[576,512]{1,0:T(8,128)S(1)}, f32[576,512]{1,0:T(8,128)S(1)}, f32[576,512]{1,0:T(8,128)S(1)}) custom-call(s32[10]{0:T(128)S(1)} %dynamic-slice_bitcast_fusion.refs_0_, bf16[576,9216]{1,0:T(8,128)(2,1)} %get-tuple-element.55.refs_1_, ...), custom_call_target="tpu_custom_call", output_to_operand_aliasing={{0}: (5, {}), {1}: (6, {}), {2}: (7, {})} | custom-call | flops 1024 | bytes 1024 | tf_op jit(solution)/shard_map/add_products/pallas_call | solution.py:288
  95.0 0.0 collective-permute-done.12.refs_4_
  95.0 0.0 copy-start
  95.0 5.5 %add_products.12 = (f32[576,512]{1,0:T(8,128)S(1)}, f32[576,512]{1,0:T(8,128)S(1)}, f32[576,512]{1,0:T(8,128)S(1)}) custom-call(s32[10]{0:T(128)S(1)} %dynamic-slice_bitcast_fusion.refs_0_, bf16[576,9216]{1,0:T(8,128)(2,1)} %get-tuple-element.55.refs_1_, ...), custom_call_target="tpu_custom_call", output_to_operand_aliasing={{0}: (5, {}), {1}: (6, {}), {2}: (7, {})} | custom-call | flops 1024 | bytes 1024 | tf_op jit(solution)/shard_map/add_products/pallas_call | solution.py:288
  100.5 2.1 %collective-permute-done.14.refs_4_ = bf16[576,512]{1,0:T(8,128)(2,1)S(1)} collective-permute-done((bf16[576,512]{1,0:T(8,128)(2,1)S(1)}, bf16[576,512]{1,0:T(8,128)(2,1)S(1)}, u32[]{:S(2)}, u32[]{:S(2)}) %collective-permute-start.14) | collective-permute-done | bytes 589856 | tf_op jit(solution)/shard_map/ppermute | solution.py:351
  102.6 0.5 collective-permute-done.9.refs_3_
  103.1 0.3 collective-permute-start.15
  103.4 1.3 collective-permute-done.16.refs_6_
  104.6 0.8 collective-permute-done.15.refs_5_
  105.5 7.4 %add_products.13 = (f32[576,512]{1,0:T(8,128)}, f32[576,512]{1,0:T(8,128)}, bf16[576,512]{1,0:T(8,128)(2,1)}, bf16[576,512]{1,0:T(8,128)(2,1)}, f32[6,512]{1,0:T(8,128)S(1)}) custom-call(s32[10]{0:T(128)S(1)} %dynamic-slice_bitcast_fusion.refs_0_, bf16[576,9216]{1,0:T(8,128)(2,1)} %get-tuple-element.55.refs_1_, bf16[576,9216]{1,0:T(8,128)(2,1)} %get-tuple-element.56.refs_2_, ...), custom_call_target="tpu_custom_call" | custom-call | flops 1024 | bytes 1024 | tf_op jit(solution)/shard_map/add_products/pallas_call | solution.py:288
  112.8 1.4 %collective-permute-start.17 = (f32[6,512]{1,0:T(8,128)S(1)}, f32[6,512]{1,0:T(8,128)S(1)}, u32[]{:S(2)}, u32[]{:S(2)}) collective-permute-start(f32[6,512]{1,0:T(8,128)S(1)} %get-tuple-element.92), channel_id=1, source_target_pairs={{0,3},{1,2},{2,1},{3,0},{4,7},{5,6},{6,5},{7,4},{8,11},{9,10},{10,... | collective-permute-start | bytes 36872 | tf_op jit(solution)/shard_map/ppermute | solution.py:311
  114.2 0.4 collective-permute-start.18
  114.6 0.1 collective-permute-start.19
  114.7 1.3 %collective-permute-done.17 = f32[6,512]{1,0:T(8,128)S(1)} collective-permute-done((f32[6,512]{1,0:T(8,128)S(1)}, f32[6,512]{1,0:T(8,128)S(1)}, u32[]{:S(2)}, u32[]{:S(2)}) %collective-permute-start.17) | collective-permute-done | bytes 12320 | tf_op jit(solution)/shard_map/ppermute | solution.py:311
  116.0 2.0 %collective-permute-done.18 = f32[6,512]{1,0:T(8,128)S(1)} collective-permute-done((f32[6,512]{1,0:T(8,128)S(1)}, f32[6,512]{1,0:T(8,128)S(1)}, u32[]{:S(2)}, u32[]{:S(2)}) %collective-permute-start.18) | collective-permute-done | bytes 12320 | tf_op jit(solution)/shard_map/ppermute | solution.py:311
  118.0 0.0 collective-permute-done.19
  118.0 3.5 %collective-permute-start.20 = (f32[24,512]{1,0:T(8,128)S(1)}, f32[24,512]{1,0:T(8,128)S(1)}, u32[]{:S(2)}, u32[]{:S(2)}) collective-permute-start(f32[24,512]{1,0:T(8,128)S(1)} %pad_maximum_fusion.1), channel_id=1, source_target_pairs={{0,12},{1,13},{2,14},{3,15},{4,8},{5,9},{6,10},{7,11},{8,4},{9,5},... | collective-permute-start | bytes 147464 | tf_op jit(solution)/shard_map/ppermute | solution.py:311
  121.5 0.0 collective-permute-start.21
  121.5 0.9 collective-permute-start.22
  122.5 1.7 %collective-permute-done.20 = f32[24,512]{1,0:T(8,128)S(1)} collective-permute-done((f32[24,512]{1,0:T(8,128)S(1)}, f32[24,512]{1,0:T(8,128)S(1)}, u32[]{:S(2)}, u32[]{:S(2)}) %collective-permute-start.20) | collective-permute-done | bytes 49184 | tf_op jit(solution)/shard_map/ppermute | solution.py:311
  124.1 2.4 %collective-permute-done.21 = f32[24,512]{1,0:T(8,128)S(1)} collective-permute-done((f32[24,512]{1,0:T(8,128)S(1)}, f32[24,512]{1,0:T(8,128)S(1)}, u32[]{:S(2)}, u32[]{:S(2)}) %collective-permute-start.21) | collective-permute-done | bytes 49184 | tf_op jit(solution)/shard_map/ppermute | solution.py:311
  126.5 0.0 collective-permute-done.22
  126.6 0.7 pad_maximum_fusion
  (21 shorter events, 0.2 us)
Async XLA Ops:
  0.6 1.2 copy-start.1
  0.6 5.0 %copy-start.2 = (s32[96,96]{1,0:T(8,128)S(1)}, s32[96,96]{1,0:T(8,128)}, u32[]{:S(2)}) copy-start(s32[96,96]{1,0:T(8,128)} %refs_2_.5) | copy-start | bytes 110596
  1.9 5.0 %copy-start.3 = (f32[96,96]{1,0:T(8,128)S(1)}, f32[96,96]{1,0:T(8,128)}, u32[]{:S(2)}) copy-start(f32[96,96]{1,0:T(8,128)} %refs_3_.5) | copy-start | bytes 110596
  1.9 6.7 %copy-start.4 = (f32[96]{0:T(128)S(1)}, f32[96]{0:T(128)}, u32[]{:S(2)}) copy-start(f32[96]{0:T(128)} %refs_4_.5) | copy-start | bytes 1156
  1.9 30.5 %collective-permute-start = (bf16[1152,512]{1,0:T(8,128)(2,1)S(1)}, bf16[1152,512]{1,0:T(8,128)(2,1)S(1)}, u32[]{:S(2)}, u32[]{:S(2)}) collective-permute-start(bf16[1152,512]{1,0:T(8,128)(2,1)S(1)} %constant_dynamic-update-slice_fusion.refs_3_), channel_id=1, source_target_pairs={{2,0},{5,1},{6,2},{1,3},{0,4},{9,5},{10,6},{3,7},{4,8},{13,9},{14,... | collective-permute-start | bytes 3538952 | tf_op jit(solution)/shard_map/ppermute | solution.py:351
  20.5 21.1 %collective-permute-start.2 = (bf16[1152,512]{1,0:T(8,128)(2,1)S(1)}, bf16[1152,512]{1,0:T(8,128)(2,1)}, u32[]{:S(2)}, u32[]{:S(2)}) collective-permute-start(bf16[1152,512]{1,0:T(8,128)(2,1)S(1)} %constant_dynamic-update-slice_fusion.refs_3_), channel_id=1, source_target_pairs={{0,2},{1,5},{2,6},{3,1},{4,0},{5,9},{6,10},{7,3},{8,4},{9,13},{10,... | collective-permute-start | bytes 3538952 | tf_op jit(solution)/shard_map/ppermute | solution.py:351
  20.5 23.6 %collective-permute-start.3 = (bf16[1152,512]{1,0:T(8,128)(2,1)S(1)}, bf16[1152,512]{1,0:T(8,128)(2,1)}, u32[]{:S(2)}, u32[]{:S(2)}) collective-permute-start(bf16[1152,512]{1,0:T(8,128)(2,1)S(1)} %constant_dynamic-update-slice_fusion.refs_3_), channel_id=1, source_target_pairs={{0,1},{1,0},{2,3},{3,2},{4,5},{5,4},{6,7},{7,6},{8,9},{9,8},{10,11... | collective-permute-start | bytes 3538952 | tf_op jit(solution)/shard_map/ppermute | solution.py:351
  32.4 19.9 %collective-permute-start.1 = (bf16[1152,512]{1,0:T(8,128)(2,1)S(1)}, bf16[1152,512]{1,0:T(8,128)(2,1)}, u32[]{:S(2)}, u32[]{:S(2)}) collective-permute-start(bf16[1152,512]{1,0:T(8,128)(2,1)S(1)} %collective-permute-done.refs_5_), channel_id=1, source_target_pairs={{2,0},{5,1},{6,2},{1,3},{0,4},{9,5},{10,6},{3,7},{4,8},{13,9},{14,... | collective-permute-start | bytes 3538952 | tf_op jit(solution)/shard_map/ppermute | solution.py:351
  41.5 13.2 %collective-permute-start.7 = (bf16[1152,512]{1,0:T(8,128)(2,1)}, bf16[1152,512]{1,0:T(8,128)(2,1)}, u32[]{:S(2)}, u32[]{:S(2)}) collective-permute-start(bf16[1152,512]{1,0:T(8,128)(2,1)} %collective-permute-done.2.refs_3_), channel_id=1, source_target_pairs={{0,1},{1,0},{2,3},{3,2},{4,5},{5,4},{6,7},{7,6},{8,9},{9,8},{10,11... | collective-permute-start | bytes 3538952 | tf_op jit(solution)/shard_map/ppermute | solution.py:351
  41.7 13.0 %collective-permute-start.6 = (bf16[1152,512]{1,0:T(8,128)(2,1)S(1)}, bf16[1152,512]{1,0:T(8,128)(2,1)}, u32[]{:S(2)}, u32[]{:S(2)}) collective-permute-start(bf16[1152,512]{1,0:T(8,128)(2,1)S(1)} %collective-permute-done.refs_5_), channel_id=1, source_target_pairs={{0,1},{1,0},{2,3},{3,2},{4,5},{5,4},{6,7},{7,6},{8,9},{9,8},{10,11... | collective-permute-start | bytes 3538952 | tf_op jit(solution)/shard_map/ppermute | solution.py:351
  42.1 25.6 %collective-permute-start.5 = (bf16[1152,512]{1,0:T(8,128)(2,1)}, bf16[1152,512]{1,0:T(8,128)(2,1)}, u32[]{:S(2)}, u32[]{:S(2)}) collective-permute-start(bf16[1152,512]{1,0:T(8,128)(2,1)} %collective-permute-done.2.refs_3_), channel_id=1, source_target_pairs={{0,2},{1,5},{2,6},{3,1},{4,0},{5,9},{6,10},{7,3},{8,4},{9,13},{10,... | collective-permute-start | bytes 3538952 | tf_op jit(solution)/shard_map/ppermute | solution.py:351
  52.3 15.8 %collective-permute-start.8 = (bf16[1152,512]{1,0:T(8,128)(2,1)}, bf16[1152,512]{1,0:T(8,128)(2,1)S(1)}, u32[]{:S(2)}, u32[]{:S(2)}) collective-permute-start(bf16[1152,512]{1,0:T(8,128)(2,1)} %collective-permute-done.1.refs_3_), channel_id=1, source_target_pairs={{0,1},{1,0},{2,3},{3,2},{4,5},{5,4},{6,7},{7,6},{8,9},{9,8},{10,11... | collective-permute-start | bytes 3538952 | tf_op jit(solution)/shard_map/ppermute | solution.py:351
  53.0 24.0 %collective-permute-start.4 = (bf16[1152,512]{1,0:T(8,128)(2,1)}, bf16[1152,512]{1,0:T(8,128)(2,1)S(1)}, u32[]{:S(2)}, u32[]{:S(2)}) collective-permute-start(bf16[1152,512]{1,0:T(8,128)(2,1)} %collective-permute-done.1.refs_3_), channel_id=1, source_target_pairs={{2,0},{5,1},{6,2},{1,3},{0,4},{9,5},{10,6},{3,7},{4,8},{13,9},{14,... | collective-permute-start | bytes 3538952 | tf_op jit(solution)/shard_map/ppermute | solution.py:351
  67.6 10.2 %collective-permute-start.11 = (bf16[1152,512]{1,0:T(8,128)(2,1)}, bf16[1152,512]{1,0:T(8,128)(2,1)S(1)}, u32[]{:S(2)}, u32[]{:S(2)}) collective-permute-start(bf16[1152,512]{1,0:T(8,128)(2,1)} %collective-permute-done.5.refs_3_), channel_id=1, source_target_pairs={{0,1},{1,0},{2,3},{3,2},{4,5},{5,4},{6,7},{7,6},{8,9},{9,8},{10,11... | collective-permute-start | bytes 3538952 | tf_op jit(solution)/shard_map/ppermute | solution.py:351
  67.6 19.6 %collective-permute-start.10 = (bf16[1152,512]{1,0:T(8,128)(2,1)}, bf16[1152,512]{1,0:T(8,128)(2,1)S(1)}, u32[]{:S(2)}, u32[]{:S(2)}) collective-permute-start(bf16[1152,512]{1,0:T(8,128)(2,1)} %collective-permute-done.5.refs_3_), channel_id=1, source_target_pairs={{0,2},{1,5},{2,6},{3,1},{4,0},{5,9},{6,10},{7,3},{8,4},{9,13},{10,... | collective-permute-start | bytes 3538952 | tf_op jit(solution)/shard_map/ppermute | solution.py:351
  77.0 12.5 %collective-permute-start.13 = (bf16[1152,512]{1,0:T(8,128)(2,1)S(1)}, bf16[1152,512]{1,0:T(8,128)(2,1)S(1)}, u32[]{:S(2)}, u32[]{:S(2)}) collective-permute-start(bf16[1152,512]{1,0:T(8,128)(2,1)S(1)} %collective-permute-done.4.refs_3_), channel_id=1, source_target_pairs={{0,1},{1,0},{2,3},{3,2},{4,5},{5,4},{6,7},{7,6},{8,9},{9,8},{10,11... | collective-permute-start | bytes 3538952 | tf_op jit(solution)/shard_map/ppermute | solution.py:351
  87.2 7.8 %collective-permute-start.12 = (bf16[1152,512]{1,0:T(8,128)(2,1)S(1)}, bf16[1152,512]{1,0:T(8,128)(2,1)S(1)}, u32[]{:S(2)}, u32[]{:S(2)}) collective-permute-start(bf16[1152,512]{1,0:T(8,128)(2,1)S(1)} %collective-permute-done.10.refs_3_), channel_id=1, source_target_pairs={{0,1},{1,0},{2,3},{3,2},{4,5},{5,4},{6,7},{7,6},{8,9},{9,8},{10,11... | collective-permute-start | bytes 3538952 | tf_op jit(solution)/shard_map/ppermute | solution.py:351
  87.3 15.3 %collective-permute-start.14 = (bf16[576,512]{1,0:T(8,128)(2,1)S(1)}, bf16[576,512]{1,0:T(8,128)(2,1)S(1)}, u32[]{:S(2)}, u32[]{:S(2)}) collective-permute-start(bf16[576,512]{1,0:T(8,128)(2,1)S(1)} %slice.7), channel_id=1, source_target_pairs={{0,2},{1,5},{2,6},{3,1},{4,0},{5,9},{6,10},{7,3},{8,4},{9,13},{10,... | collective-permute-start | bytes 1769480 | tf_op jit(solution)/shard_map/ppermute | solution.py:351
  88.4 14.6 %collective-permute-start.9 = (bf16[576,512]{1,0:T(8,128)(2,1)S(1)}, bf16[576,512]{1,0:T(8,128)(2,1)S(1)}, u32[]{:S(2)}, u32[]{:S(2)}) collective-permute-start(bf16[576,512]{1,0:T(8,128)(2,1)S(1)} %slice.6), channel_id=1, source_target_pairs={{2,0},{5,1},{6,2},{1,3},{0,4},{9,5},{10,6},{3,7},{4,8},{13,9},{14,... | collective-permute-start | bytes 1769480 | tf_op jit(solution)/shard_map/ppermute | solution.py:351
  95.0 10.5 %copy-start = (bf16[576,512]{1,0:T(8,128)(2,1)S(1)}, bf16[576,512]{1,0:T(8,128)(2,1)}, u32[]{:S(2)}) copy-start(bf16[576,512]{1,0:T(8,128)(2,1)} %refs_10_.1) | copy-start | bytes 1769476
  102.6 2.0 %collective-permute-start.16 = (bf16[576,512]{1,0:T(8,128)(2,1)S(1)}, bf16[576,512]{1,0:T(8,128)(2,1)S(1)}, u32[]{:S(2)}, u32[]{:S(2)}) collective-permute-start(bf16[576,512]{1,0:T(8,128)(2,1)S(1)} %collective-permute-done.14.refs_4_), channel_id=1, source_target_pairs={{0,1},{1,0},{2,3},{3,2},{4,5},{5,4},{6,7},{7,6},{8,9},{9,8},{10,11... | collective-permute-start | bytes 1769480 | tf_op jit(solution)/shard_map/ppermute | solution.py:351
  103.1 2.4 %collective-permute-start.15 = (bf16[576,512]{1,0:T(8,128)(2,1)S(1)}, bf16[576,512]{1,0:T(8,128)(2,1)S(1)}, u32[]{:S(2)}, u32[]{:S(2)}) collective-permute-start(bf16[576,512]{1,0:T(8,128)(2,1)S(1)} %collective-permute-done.9.refs_3_), channel_id=1, source_target_pairs={{0,1},{1,0},{2,3},{3,2},{4,5},{5,4},{6,7},{7,6},{8,9},{9,8},{10,11... | collective-permute-start | bytes 1769480 | tf_op jit(solution)/shard_map/ppermute | solution.py:351
  112.8 3.2 %collective-permute-start.17 = (f32[6,512]{1,0:T(8,128)S(1)}, f32[6,512]{1,0:T(8,128)S(1)}, u32[]{:S(2)}, u32[]{:S(2)}) collective-permute-start(f32[6,512]{1,0:T(8,128)S(1)} %get-tuple-element.92), channel_id=1, source_target_pairs={{0,3},{1,2},{2,1},{3,0},{4,7},{5,6},{6,5},{7,4},{8,11},{9,10},{10,... | collective-permute-start | bytes 36872 | tf_op jit(solution)/shard_map/ppermute | solution.py:311
  114.2 3.8 %collective-permute-start.18 = (f32[6,512]{1,0:T(8,128)S(1)}, f32[6,512]{1,0:T(8,128)S(1)}, u32[]{:S(2)}, u32[]{:S(2)}) collective-permute-start(f32[6,512]{1,0:T(8,128)S(1)} %get-tuple-element.92), channel_id=1, source_target_pairs={{0,2},{1,3},{2,0},{3,1},{4,6},{5,7},{6,4},{7,5},{8,10},{9,11},{10,... | collective-permute-start | bytes 36872 | tf_op jit(solution)/shard_map/ppermute | solution.py:311
  114.6 3.4 %collective-permute-start.19 = (f32[6,512]{1,0:T(8,128)S(1)}, f32[6,512]{1,0:T(8,128)S(1)}, u32[]{:S(2)}, u32[]{:S(2)}) collective-permute-start(f32[6,512]{1,0:T(8,128)S(1)} %get-tuple-element.92), channel_id=1, source_target_pairs={{0,1},{1,0},{2,3},{3,2},{4,5},{5,4},{6,7},{7,6},{8,9},{9,8},{10,11... | collective-permute-start | bytes 36872 | tf_op jit(solution)/shard_map/ppermute | solution.py:311
  118.0 6.1 %collective-permute-start.20 = (f32[24,512]{1,0:T(8,128)S(1)}, f32[24,512]{1,0:T(8,128)S(1)}, u32[]{:S(2)}, u32[]{:S(2)}) collective-permute-start(f32[24,512]{1,0:T(8,128)S(1)} %pad_maximum_fusion.1), channel_id=1, source_target_pairs={{0,12},{1,13},{2,14},{3,15},{4,8},{5,9},{6,10},{7,11},{8,4},{9,5},... | collective-permute-start | bytes 147464 | tf_op jit(solution)/shard_map/ppermute | solution.py:311
  121.5 5.0 %collective-permute-start.21 = (f32[24,512]{1,0:T(8,128)S(1)}, f32[24,512]{1,0:T(8,128)S(1)}, u32[]{:S(2)}, u32[]{:S(2)}) collective-permute-start(f32[24,512]{1,0:T(8,128)S(1)} %pad_maximum_fusion.1), channel_id=1, source_target_pairs={{0,8},{1,9},{2,10},{3,11},{4,12},{5,13},{6,14},{7,15},{8,0},{9,1},... | collective-permute-start | bytes 147464 | tf_op jit(solution)/shard_map/ppermute | solution.py:311
  121.5 5.0 %collective-permute-start.22 = (f32[24,512]{1,0:T(8,128)S(1)}, f32[24,512]{1,0:T(8,128)S(1)}, u32[]{:S(2)}, u32[]{:S(2)}) collective-permute-start(f32[24,512]{1,0:T(8,128)S(1)} %pad_maximum_fusion.1), channel_id=1, source_target_pairs={{0,4},{1,5},{2,6},{3,7},{4,0},{5,1},{6,2},{7,3},{8,12},{9,13},{10,... | collective-permute-start | bytes 147464 | tf_op jit(solution)/shard_map/ppermute | solution.py:311

commit v8 on v7

--- a/solution.py
+++ b/solution.py
@@ -3,6 +3,7 @@
 
 import jax
 import jax.numpy as jnp
+import numpy as np
 from jax import lax
 from jax.experimental import pallas as pl
 from jax.experimental.pallas import tpu as pltpu
@@ -72,7 +73,7 @@
 
 def build_body(orbitals, low, high, pairs, *refs):
     place_ref, inter_ref, pat_ref, hop_ref, occ_ref = refs[:5]
-    pat4_ref, hop4_ref, eye4_ref, occ4_ref = refs[5:9]
+    both4_ref, eye4_ref, occ4_ref = refs[5:8]
     mixed_ref, polar_ref, turned_ref = refs[-3:]
     span = 4 * orbitals
     tiles = pairs // span
@@ -120,7 +121,7 @@
             linked = spread([pat_ref[here, i].astype(jnp.float32) for i in inner])
             hop_row = spread([hop_ref[here, i] for i in inner])
             unit = (group + 4 * tile == here).astype(jnp.float32)
-            linked4 = pat4_ref[pl.ds(here, 1), :]
+            linked4 = both4_ref[pl.ds(here, 1), :]
             facts[first] = (linked * polar_factor, linked4 * ladder_factor, hop_row, unit)
         blocks = []
         for strip in strips:
@@ -142,7 +143,7 @@
             polar = inter_ref[there, cols].astype(jnp.float32) * polar_row
             hop = (
                 hop_row * eye4_ref[second : second + count]
-                + unit * hop4_ref[second : second + count]
+                + unit * both4_ref[orbitals + second : orbitals + second + count]
             )
             ladder = (block[there] * ladder_row).astype(jnp.bfloat16)
             direct = (polar + hop).astype(jnp.bfloat16).astype(jnp.float32)
@@ -169,18 +170,19 @@
     smem = pl.BlockSpec(memory_space=pltpu.SMEM)
     row4 = pl.BlockSpec((1, 4 * orbitals), lambda g, p: (0, 0))
     small = pl.BlockSpec((orbitals, 4 * orbitals), lambda g, p: (0, 0))
+    twice = pl.BlockSpec((2 * orbitals, 4 * orbitals), lambda g, p: (0, 0))
     return pl.pallas_call(
         functools.partial(build_body, orbitals, low, high, pairs),
         grid_spec=pltpu.PrefetchScalarGridSpec(
             num_scalar_prefetch=1,
             grid=(chunks,),
-            in_specs=[wide, smem, smem, smem, small, small, small, row4]
+            in_specs=[wide, smem, smem, smem, twice, small, row4]
             + [pl.BlockSpec(memory_space=pl.ANY)] * len(made),
             out_specs=[chunk] * 2,
             scratch_shapes=[pltpu.VMEM((-(-height // 128) * orbitals * (orbitals + 1), 128), jnp.float32)],
         ),
         out_shape=[shape] * 2,
-        input_output_aliases={9 + n: n for n in range(len(made))},
+        input_output_aliases={8 + n: n for n in range(len(made))},
         compiler_params=pltpu.CompilerParams(vmem_limit_bytes=28 * MIB),
         cost_estimate=pl.CostEstimate(flops=1024, bytes_accessed=1024, transcendentals=0),
         name="build_rows",
@@ -356,14 +358,13 @@
         pattern,
         hopping,
         occupation,
-        jnp.tile(pattern.astype(jnp.float32), (1, 4)),
-        jnp.tile(hopping, (1, 4)),
-        jnp.tile(jnp.eye(orbitals, dtype=jnp.float32), (1, 4)),
-        jnp.tile(occupation, 4)[None],
+        jnp.concatenate([jnp.concatenate([pattern.astype(jnp.float32), hopping], axis=0)] * 4, axis=1),
+        jnp.array(np.tile(np.eye(orbitals, dtype=np.float32), (1, 4))),
+        jnp.concatenate([occupation] * 4)[None],
     )
 
     big = rows // 9 * 4
-    cuts = [(0, big), (big, 2 * big), (2 * big, rows)]
+    cuts = [(2 * big, rows), (0, big), (big, 2 * big)]
 
     def build(when, made, part):
         return build_rows(when, interaction, smalls, made, *cuts[part])

time: 128 us -> 123 us (0.961)
  local copies, waits for them, and re-layouts: 5.07 us -> 2.07 us
  waiting for transfers between devices: 24 us -> 21.2 us
  starting transfers between devices: 19.4 us -> 21.3 us
    ppermute x17, waiting for transfers between devices: 16.6 us -> 13.5 us  [send(): return lax.ppermute(block, 'prow', pairs_of)]
    another operation x8 -> x0, local copies, waits for them, and re-layouts: 3.02 us -> none  [the longest x2 1.78 us: ring_form(): jnp.tile(hopping, (1, 4))]
    ppermute x17, starting transfers between devices: 13.1 us -> 14.7 us  [send(): return lax.ppermute(block, 'prow', pairs_of)]
  transfers between devices with their start and end apart: 23 -> 23, of which waited for: 12 -> 13; matrix products, arithmetic and copies ran while one was open for 3% -> 1% of each run, Pallas kernels for 54% -> 56%
where the time goes in v8:
time: 123 us
  Pallas kernels  76.5 us (62%)
  starting transfers between devices  21.3 us (17%)
  waiting for transfers between devices  21.2 us (17%)
  local copies, waits for them, and re-layouts  2.07 us (2%)
    pallas_call x7, Pallas kernels, step(): pl.pallas_call(functools.partial(step_body, parts, rows, opening, closing...  45.9 us
    pallas_call x3, Pallas kernels, build_rows(): pl.pallas_call(functools.partial(build_body, orbitals, low, high, pairs),...  30.6 us
    ppermute x17, starting transfers between devices, send(): return lax.ppermute(block, 'prow', pairs_of)  14.7 us
    ppermute x17, waiting for transfers between devices, send(): return lax.ppermute(block, 'prow', pairs_of)  13.5 us
    ppermute x6, waiting for transfers between devices, spread_blocks(): blocks.append(lax.ppermute(block, 'prow', pairs_of))  7.69 us
    ppermute x6, starting transfers between devices, spread_blocks(): blocks.append(lax.ppermute(block, 'prow', pairs_of))  6.58 us
  transfers between devices with their start and end apart: 23, of which 13 were waited for; matrix products, arithmetic and copies ran while one was open for 1% of the time, Pallas kernels for 56%

profile of v8, /device:TPU:0, one launch (start us, length us, event | category | flops | bytes accessed | tf_op | source)
XLA Modules:
  0.0 122.9 jit_solution(17952054073999594094)
XLA Ops:
  0.6 0.0 copy-start.2
  0.7 1.2 constant_dynamic-update-slice_fusion.1
  1.9 0.1 copy-done.1
  2.0 3.1 %collective-permute-start = (bf16[1152,512]{1,0:T(8,128)(2,1)S(1)}, bf16[1152,512]{1,0:T(8,128)(2,1)}, u32[]{:S(2)}, u32[]{:S(2)}) collective-permute-start(bf16[1152,512]{1,0:T(8,128)(2,1)S(1)} %constant_dynamic-update-slice_fusion.refs_3_), channel_id=1, source_target_pairs={{2,0},{5,1},{6,2},{1,3},{0,4},{9,5},{10,6},{3,7},{4,8},{13,9},{14,... | collective-permute-start | bytes 3538952 | tf_op jit(solution)/shard_map/ppermute | solution.py:353
  5.1 0.1 pad_maximum_fusion.2
  5.1 0.2 maximum_maximum_fusion.refs_5_
  5.4 7.1 %build_rows.3 = (bf16[576,9216]{1,0:T(8,128)(2,1)}, bf16[576,9216]{1,0:T(8,128)(2,1)}) custom-call(s32[1]{0:T(128)} %bitcast.1.refs_0_, bf16[576,9216]{1,0:T(8,128)(2,1)} %refs_1_.5, s32[96,96]{1,0:T(8,128)S(1)} %copy-done.3, f32[96,96]{1,0:T(8,128)S(1)} %copy-done.4, f32[96]{0:T(128)S(1)} %copy-done.5, f32[192,384]{1,0:T(8,128)S(1)} %maximum_maximum_fusion.refs_5_, ...), custom_call_target="tpu_custom_call" | custom-call | flops 1024 | bytes 1024 | tf_op jit(solution)/shard_map/build_rows/pallas_call | solution.py:174
  12.5 0.0 collective-permute-start.2
  12.5 0.0 collective-permute-start.3
  12.5 11.7 %build_rows.4 = (bf16[576,9216]{1,0:T(8,128)(2,1)}, bf16[576,9216]{1,0:T(8,128)(2,1)}) custom-call(s32[1]{0:T(128)} %bitcast.1.refs_0_, bf16[576,9216]{1,0:T(8,128)(2,1)} %refs_1_.5, s32[96,96]{1,0:T(8,128)S(1)} %copy-done.3, f32[96,96]{1,0:T(8,128)S(1)} %copy-done.4, f32[96]{0:T(128)S(1)} %copy-done.5, ...), custom_call_target="tpu_custom_call", output_to_operand_aliasing={{0}: (8, {}), {1}: (9, {})} | custom-call | flops 1024 | bytes 1024 | tf_op jit(solution)/shard_map/build_rows/pallas_call | solution.py:174
  24.3 0.7 collective-permute-done.refs_5_
  25.0 2.6 %collective-permute-start.1 = (bf16[1152,512]{1,0:T(8,128)(2,1)}, bf16[1152,512]{1,0:T(8,128)(2,1)S(1)}, u32[]{:S(2)}, u32[]{:S(2)}) collective-permute-start(bf16[1152,512]{1,0:T(8,128)(2,1)} %collective-permute-done.refs_5_), channel_id=1, source_target_pairs={{2,0},{5,1},{6,2},{1,3},{0,4},{9,5},{10,6},{3,7},{4,8},{13,9},{14,... | collective-permute-start | bytes 3538952 | tf_op jit(solution)/shard_map/ppermute | solution.py:353
  27.6 11.7 %build_rows.5 = (bf16[576,9216]{1,0:T(8,128)(2,1)}, bf16[576,9216]{1,0:T(8,128)(2,1)}) custom-call(s32[1]{0:T(128)} %bitcast.1.refs_0_, bf16[576,9216]{1,0:T(8,128)(2,1)} %refs_1_.5, s32[96,96]{1,0:T(8,128)S(1)} %copy-done.3, f32[96,96]{1,0:T(8,128)S(1)} %copy-done.4, f32[96]{0:T(128)S(1)} %copy-done.5, ...), custom_call_target="tpu_custom_call", output_to_operand_aliasing={{0}: (8, {}), {1}: (9, {})} | custom-call | flops 1024 | bytes 1024 | tf_op jit(solution)/shard_map/build_rows/pallas_call | solution.py:174
  39.3 0.0 collective-permute-done.2.refs_3_
  39.3 0.0 collective-permute-start.7
  39.3 0.5 collective-permute-start.6
  39.8 0.0 collective-permute-start.5
  39.8 0.7 dynamic-slice_bitcast_fusion.refs_0_
  40.5 0.0 collective-permute-done.3.refs_4_
  40.5 5.8 %add_products.7 = (f32[576,512]{1,0:T(8,128)S(1)}, f32[576,512]{1,0:T(8,128)S(1)}, f32[576,512]{1,0:T(8,128)S(1)}) custom-call(s32[10]{0:T(128)S(1)} %dynamic-slice_bitcast_fusion.refs_0_, bf16[576,9216]{1,0:T(8,128)(2,1)} %get-tuple-element.55.refs_1_, bf16[576,9216]{1,0:T(8,128)(2,1)} %get-tuple-element.56.refs_2_, ...), custom_call_target="tpu_custom_call" | custom-call | flops 1024 | bytes 1024 | tf_op jit(solution)/shard_map/add_products/pallas_call | solution.py:290
  46.3 0.2 collective-permute-done.1.refs_3_
  46.5 1.1 collective-permute-start.8
  47.6 1.5 %collective-permute-start.4 = (bf16[1152,512]{1,0:T(8,128)(2,1)S(1)}, bf16[1152,512]{1,0:T(8,128)(2,1)S(1)}, u32[]{:S(2)}, u32[]{:S(2)}) collective-permute-start(bf16[1152,512]{1,0:T(8,128)(2,1)S(1)} %collective-permute-done.1.refs_3_), channel_id=1, source_target_pairs={{2,0},{5,1},{6,2},{1,3},{0,4},{9,5},{10,6},{3,7},{4,8},{13,9},{14,... | collective-permute-start | bytes 3538952 | tf_op jit(solution)/shard_map/ppermute | solution.py:353
  49.2 0.0 collective-permute-done.7.refs_6_
  49.2 0.0 collective-permute-done.6.refs_4_
  49.2 10.2 %add_products.8 = (f32[576,512]{1,0:T(8,128)S(1)}, f32[576,512]{1,0:T(8,128)S(1)}, f32[576,512]{1,0:T(8,128)S(1)}) custom-call(s32[10]{0:T(128)S(1)} %dynamic-slice_bitcast_fusion.refs_0_, bf16[576,9216]{1,0:T(8,128)(2,1)} %get-tuple-element.55.refs_1_, ...), custom_call_target="tpu_custom_call", output_to_operand_aliasing={{0}: (7, {}), {1}: (8, {}), {2}: (9, {})} | custom-call | flops 1024 | bytes 1024 | tf_op jit(solution)/shard_map/add_products/pallas_call | solution.py:290
  59.4 2.9 %collective-permute-done.5.refs_3_ = bf16[1152,512]{1,0:T(8,128)(2,1)} collective-permute-done((bf16[1152,512]{1,0:T(8,128)(2,1)}, bf16[1152,512]{1,0:T(8,128)(2,1)}, u32[]{:S(2)}, u32[]{:S(2)}) %collective-permute-start.5) | collective-permute-done | bytes 1179680 | tf_op jit(solution)/shard_map/ppermute | solution.py:353
  62.3 1.0 collective-permute-start.11
  63.3 1.6 %collective-permute-start.10 = (bf16[1152,512]{1,0:T(8,128)(2,1)}, bf16[1152,512]{1,0:T(8,128)(2,1)S(1)}, u32[]{:S(2)}, u32[]{:S(2)}) collective-permute-start(bf16[1152,512]{1,0:T(8,128)(2,1)} %collective-permute-done.5.refs_3_), channel_id=1, source_target_pairs={{0,2},{1,5},{2,6},{3,1},{4,0},{5,9},{6,10},{7,3},{8,4},{9,13},{10,... | collective-permute-start | bytes 3538952 | tf_op jit(solution)/shard_map/ppermute | solution.py:353
  64.8 0.0 collective-permute-done.8.refs_4_
  64.9 5.9 %add_products.9 = (f32[576,512]{1,0:T(8,128)S(1)}, f32[576,512]{1,0:T(8,128)S(1)}, f32[576,512]{1,0:T(8,128)S(1)}) custom-call(s32[10]{0:T(128)S(1)} %dynamic-slice_bitcast_fusion.refs_0_, bf16[576,9216]{1,0:T(8,128)(2,1)} %get-tuple-element.55.refs_1_, ...), custom_call_target="tpu_custom_call", output_to_operand_aliasing={{0}: (5, {}), {1}: (6, {}), {2}: (7, {})} | custom-call | flops 1024 | bytes 1024 | tf_op jit(solution)/shard_map/add_products/pallas_call | solution.py:290
  70.7 2.6 %collective-permute-done.4.refs_3_ = bf16[1152,512]{1,0:T(8,128)(2,1)S(1)} collective-permute-done((bf16[1152,512]{1,0:T(8,128)(2,1)S(1)}, bf16[1152,512]{1,0:T(8,128)(2,1)S(1)}, u32[]{:S(2)}, u32[]{:S(2)}) %collective-permute-start.4) | collective-permute-done | bytes 1179680 | tf_op jit(solution)/shard_map/ppermute | solution.py:353
  73.3 0.0 collective-permute-start.13
  73.3 0.0 collective-permute-done.11.refs_4_
  73.3 5.5 %add_products.10 = (f32[576,512]{1,0:T(8,128)S(1)}, f32[576,512]{1,0:T(8,128)S(1)}, f32[576,512]{1,0:T(8,128)S(1)}) custom-call(s32[10]{0:T(128)S(1)} %dynamic-slice_bitcast_fusion.refs_0_, bf16[576,9216]{1,0:T(8,128)(2,1)} %get-tuple-element.55.refs_1_, ...), custom_call_target="tpu_custom_call", output_to_operand_aliasing={{0}: (5, {}), {1}: (6, {}), {2}: (7, {})} | custom-call | flops 1024 | bytes 1024 | tf_op jit(solution)/shard_map/add_products/pallas_call | solution.py:290
  78.8 2.7 %collective-permute-done.10.refs_3_ = bf16[1152,512]{1,0:T(8,128)(2,1)S(1)} collective-permute-done((bf16[1152,512]{1,0:T(8,128)(2,1)}, bf16[1152,512]{1,0:T(8,128)(2,1)S(1)}, u32[]{:S(2)}, u32[]{:S(2)}) %collective-permute-start.10) | collective-permute-done | bytes 1179680 | tf_op jit(solution)/shard_map/ppermute | solution.py:353
  81.6 0.6 collective-permute-start.12
  82.2 2.1 %collective-permute-start.14 = (bf16[576,512]{1,0:T(8,128)(2,1)S(1)}, bf16[576,512]{1,0:T(8,128)(2,1)S(1)}, u32[]{:S(2)}, u32[]{:S(2)}) collective-permute-start(bf16[576,512]{1,0:T(8,128)(2,1)S(1)} %slice.7), channel_id=1, source_target_pairs={{0,2},{1,5},{2,6},{3,1},{4,0},{5,9},{6,10},{7,3},{8,4},{9,13},{10,... | collective-permute-start | bytes 1769480 | tf_op jit(solution)/shard_map/ppermute | solution.py:353
  84.3 0.1 collective-permute-start.9
  84.5 0.0 collective-permute-done.13.refs_4_
  84.5 5.5 %add_products.11 = (f32[576,512]{1,0:T(8,128)S(1)}, f32[576,512]{1,0:T(8,128)S(1)}, f32[576,512]{1,0:T(8,128)S(1)}) custom-call(s32[10]{0:T(128)S(1)} %dynamic-slice_bitcast_fusion.refs_0_, bf16[576,9216]{1,0:T(8,128)(2,1)} %get-tuple-element.55.refs_1_, ...), custom_call_target="tpu_custom_call", output_to_operand_aliasing={{0}: (5, {}), {1}: (6, {}), {2}: (7, {})} | custom-call | flops 1024 | bytes 1024 | tf_op jit(solution)/shard_map/add_products/pallas_call | solution.py:290
  90.0 0.0 collective-permute-done.12.refs_4_
  90.0 0.0 copy-start
  90.0 5.5 %add_products.12 = (f32[576,512]{1,0:T(8,128)S(1)}, f32[576,512]{1,0:T(8,128)S(1)}, f32[576,512]{1,0:T(8,128)S(1)}) custom-call(s32[10]{0:T(128)S(1)} %dynamic-slice_bitcast_fusion.refs_0_, bf16[576,9216]{1,0:T(8,128)(2,1)} %get-tuple-element.55.refs_1_, ...), custom_call_target="tpu_custom_call", output_to_operand_aliasing={{0}: (5, {}), {1}: (6, {}), {2}: (7, {})} | custom-call | flops 1024 | bytes 1024 | tf_op jit(solution)/shard_map/add_products/pallas_call | solution.py:290
  95.6 2.1 %collective-permute-done.14.refs_4_ = bf16[576,512]{1,0:T(8,128)(2,1)S(1)} collective-permute-done((bf16[576,512]{1,0:T(8,128)(2,1)S(1)}, bf16[576,512]{1,0:T(8,128)(2,1)S(1)}, u32[]{:S(2)}, u32[]{:S(2)}) %collective-permute-start.14) | collective-permute-done | bytes 589856 | tf_op jit(solution)/shard_map/ppermute | solution.py:353
  97.7 0.0 collective-permute-start.16
  97.7 0.1 collective-permute-done.9.refs_3_
  97.8 0.6 collective-permute-start.15
  98.4 1.3 %collective-permute-done.16.refs_6_ = bf16[576,512]{1,0:T(8,128)(2,1)S(1)} collective-permute-done((bf16[576,512]{1,0:T(8,128)(2,1)S(1)}, bf16[576,512]{1,0:T(8,128)(2,1)S(1)}, u32[]{:S(2)}, u32[]{:S(2)}) %collective-permute-start.16) | collective-permute-done | bytes 589856 | tf_op jit(solution)/shard_map/ppermute | solution.py:353
  99.7 0.8 collective-permute-done.15.refs_5_
  100.5 7.4 %add_products.13 = (f32[576,512]{1,0:T(8,128)}, f32[576,512]{1,0:T(8,128)}, bf16[576,512]{1,0:T(8,128)(2,1)}, bf16[576,512]{1,0:T(8,128)(2,1)}, f32[6,512]{1,0:T(8,128)S(1)}) custom-call(s32[10]{0:T(128)S(1)} %dynamic-slice_bitcast_fusion.refs_0_, bf16[576,9216]{1,0:T(8,128)(2,1)} %get-tuple-element.55.refs_1_, bf16[576,9216]{1,0:T(8,128)(2,1)} %get-tuple-element.56.refs_2_, ...), custom_call_target="tpu_custom_call" | custom-call | flops 1024 | bytes 1024 | tf_op jit(solution)/shard_map/add_products/pallas_call | solution.py:290
  107.9 1.7 %collective-permute-start.17 = (f32[6,512]{1,0:T(8,128)S(1)}, f32[6,512]{1,0:T(8,128)S(1)}, u32[]{:S(2)}, u32[]{:S(2)}) collective-permute-start(f32[6,512]{1,0:T(8,128)S(1)} %get-tuple-element.92), channel_id=1, source_target_pairs={{0,3},{1,2},{2,1},{3,0},{4,7},{5,6},{6,5},{7,4},{8,11},{9,10},{10,... | collective-permute-start | bytes 36872 | tf_op jit(solution)/shard_map/ppermute | solution.py:313
  109.7 0.3 collective-permute-start.18
  110.0 0.1 collective-permute-start.19
  110.0 1.1 collective-permute-done.17
  111.1 2.3 %collective-permute-done.18 = f32[6,512]{1,0:T(8,128)S(1)} collective-permute-done((f32[6,512]{1,0:T(8,128)S(1)}, f32[6,512]{1,0:T(8,128)S(1)}, u32[]{:S(2)}, u32[]{:S(2)}) %collective-permute-start.18) | collective-permute-done | bytes 12320 | tf_op jit(solution)/shard_map/ppermute | solution.py:313
  113.4 0.0 collective-permute-done.19
  113.5 3.8 %collective-permute-start.20 = (f32[24,512]{1,0:T(8,128)S(1)}, f32[24,512]{1,0:T(8,128)S(1)}, u32[]{:S(2)}, u32[]{:S(2)}) collective-permute-start(f32[24,512]{1,0:T(8,128)S(1)} %pad_maximum_fusion.1), channel_id=1, source_target_pairs={{0,12},{1,13},{2,14},{3,15},{4,8},{5,9},{6,10},{7,11},{8,4},{9,5},... | collective-permute-start | bytes 147464 | tf_op jit(solution)/shard_map/ppermute | solution.py:313
  117.2 0.0 collective-permute-start.21
  117.2 0.7 collective-permute-start.22
  117.9 1.9 %collective-permute-done.20 = f32[24,512]{1,0:T(8,128)S(1)} collective-permute-done((f32[24,512]{1,0:T(8,128)S(1)}, f32[24,512]{1,0:T(8,128)S(1)}, u32[]{:S(2)}, u32[]{:S(2)}) %collective-permute-start.20) | collective-permute-done | bytes 49184 | tf_op jit(solution)/shard_map/ppermute | solution.py:313
  119.8 2.4 %collective-permute-done.21 = f32[24,512]{1,0:T(8,128)S(1)} collective-permute-done((f32[24,512]{1,0:T(8,128)S(1)}, f32[24,512]{1,0:T(8,128)S(1)}, u32[]{:S(2)}, u32[]{:S(2)}) %collective-permute-start.21) | collective-permute-done | bytes 49184 | tf_op jit(solution)/shard_map/ppermute | solution.py:313
  122.2 0.0 collective-permute-done.22
  122.3 0.7 pad_maximum_fusion
  (17 shorter events, 0.2 us)
Async XLA Ops:
  0.6 4.7 %copy-start.2 = (f32[96,384]{1,0:T(8,128)S(1)}, f32[96,384]{1,0:T(8,128)}, u32[]{:S(2)}) copy-start(f32[96,384]{1,0:T(8,128)} %constant.82.clone.refs_6_) | copy-start | bytes 442372
  0.6 1.3 %copy-start.1 = (bf16[576,512]{1,0:T(8,128)(2,1)S(1)}, bf16[576,512]{1,0:T(8,128)(2,1)}, u32[]{:S(2)}) copy-start(bf16[576,512]{1,0:T(8,128)(2,1)} %refs_11_.1) | copy-start | bytes 1769476
  0.7 4.4 %copy-start.3 = (s32[96,96]{1,0:T(8,128)S(1)}, s32[96,96]{1,0:T(8,128)}, u32[]{:S(2)}) copy-start(s32[96,96]{1,0:T(8,128)} %refs_2_.5) | copy-start | bytes 110596
  0.7 4.4 %copy-start.5 = (f32[96]{0:T(128)S(1)}, f32[96]{0:T(128)}, u32[]{:S(2)}) copy-start(f32[96]{0:T(128)} %refs_4_.5) | copy-start | bytes 1156
  0.7 4.5 %copy-start.4 = (f32[96,96]{1,0:T(8,128)S(1)}, f32[96,96]{1,0:T(8,128)}, u32[]{:S(2)}) copy-start(f32[96,96]{1,0:T(8,128)} %refs_3_.5) | copy-start | bytes 110596
  2.0 23.0 %collective-permute-start = (bf16[1152,512]{1,0:T(8,128)(2,1)S(1)}, bf16[1152,512]{1,0:T(8,128)(2,1)}, u32[]{:S(2)}, u32[]{:S(2)}) collective-permute-start(bf16[1152,512]{1,0:T(8,128)(2,1)S(1)} %constant_dynamic-update-slice_fusion.refs_3_), channel_id=1, source_target_pairs={{2,0},{5,1},{6,2},{1,3},{0,4},{9,5},{10,6},{3,7},{4,8},{13,9},{14,... | collective-permute-start | bytes 3538952 | tf_op jit(solution)/shard_map/ppermute | solution.py:353
  12.5 26.7 %collective-permute-start.2 = (bf16[1152,512]{1,0:T(8,128)(2,1)S(1)}, bf16[1152,512]{1,0:T(8,128)(2,1)}, u32[]{:S(2)}, u32[]{:S(2)}) collective-permute-start(bf16[1152,512]{1,0:T(8,128)(2,1)S(1)} %constant_dynamic-update-slice_fusion.refs_3_), channel_id=1, source_target_pairs={{0,2},{1,5},{2,6},{3,1},{4,0},{5,9},{6,10},{7,3},{8,4},{9,13},{10,... | collective-permute-start | bytes 3538952 | tf_op jit(solution)/shard_map/ppermute | solution.py:353
  12.5 28.0 %collective-permute-start.3 = (bf16[1152,512]{1,0:T(8,128)(2,1)S(1)}, bf16[1152,512]{1,0:T(8,128)(2,1)}, u32[]{:S(2)}, u32[]{:S(2)}) collective-permute-start(bf16[1152,512]{1,0:T(8,128)(2,1)S(1)} %constant_dynamic-update-slice_fusion.refs_3_), channel_id=1, source_target_pairs={{0,1},{1,0},{2,3},{3,2},{4,5},{5,4},{6,7},{7,6},{8,9},{9,8},{10,11... | collective-permute-start | bytes 3538952 | tf_op jit(solution)/shard_map/ppermute | solution.py:353
  25.0 21.5 %collective-permute-start.1 = (bf16[1152,512]{1,0:T(8,128)(2,1)}, bf16[1152,512]{1,0:T(8,128)(2,1)S(1)}, u32[]{:S(2)}, u32[]{:S(2)}) collective-permute-start(bf16[1152,512]{1,0:T(8,128)(2,1)} %collective-permute-done.refs_5_), channel_id=1, source_target_pairs={{2,0},{5,1},{6,2},{1,3},{0,4},{9,5},{10,6},{3,7},{4,8},{13,9},{14,... | collective-permute-start | bytes 3538952 | tf_op jit(solution)/shard_map/ppermute | solution.py:353
  39.3 9.9 %collective-permute-start.7 = (bf16[1152,512]{1,0:T(8,128)(2,1)}, bf16[1152,512]{1,0:T(8,128)(2,1)}, u32[]{:S(2)}, u32[]{:S(2)}) collective-permute-start(bf16[1152,512]{1,0:T(8,128)(2,1)} %collective-permute-done.2.refs_3_), channel_id=1, source_target_pairs={{0,1},{1,0},{2,3},{3,2},{4,5},{5,4},{6,7},{7,6},{8,9},{9,8},{10,11... | collective-permute-start | bytes 3538952 | tf_op jit(solution)/shard_map/ppermute | solution.py:353
  39.3 9.9 %collective-permute-start.6 = (bf16[1152,512]{1,0:T(8,128)(2,1)}, bf16[1152,512]{1,0:T(8,128)(2,1)}, u32[]{:S(2)}, u32[]{:S(2)}) collective-permute-start(bf16[1152,512]{1,0:T(8,128)(2,1)} %collective-permute-done.refs_5_), channel_id=1, source_target_pairs={{0,1},{1,0},{2,3},{3,2},{4,5},{5,4},{6,7},{7,6},{8,9},{9,8},{10,11... | collective-permute-start | bytes 3538952 | tf_op jit(solution)/shard_map/ppermute | solution.py:353
  39.8 22.5 %collective-permute-start.5 = (bf16[1152,512]{1,0:T(8,128)(2,1)}, bf16[1152,512]{1,0:T(8,128)(2,1)}, u32[]{:S(2)}, u32[]{:S(2)}) collective-permute-start(bf16[1152,512]{1,0:T(8,128)(2,1)} %collective-permute-done.2.refs_3_), channel_id=1, source_target_pairs={{0,2},{1,5},{2,6},{3,1},{4,0},{5,9},{6,10},{7,3},{8,4},{9,13},{10,... | collective-permute-start | bytes 3538952 | tf_op jit(solution)/shard_map/ppermute | solution.py:353
  46.5 18.3 %collective-permute-start.8 = (bf16[1152,512]{1,0:T(8,128)(2,1)S(1)}, bf16[1152,512]{1,0:T(8,128)(2,1)S(1)}, u32[]{:S(2)}, u32[]{:S(2)}) collective-permute-start(bf16[1152,512]{1,0:T(8,128)(2,1)S(1)} %collective-permute-done.1.refs_3_), channel_id=1, source_target_pairs={{0,1},{1,0},{2,3},{3,2},{4,5},{5,4},{6,7},{7,6},{8,9},{9,8},{10,11... | collective-permute-start | bytes 3538952 | tf_op jit(solution)/shard_map/ppermute | solution.py:353
  47.6 25.7 %collective-permute-start.4 = (bf16[1152,512]{1,0:T(8,128)(2,1)S(1)}, bf16[1152,512]{1,0:T(8,128)(2,1)S(1)}, u32[]{:S(2)}, u32[]{:S(2)}) collective-permute-start(bf16[1152,512]{1,0:T(8,128)(2,1)S(1)} %collective-permute-done.1.refs_3_), channel_id=1, source_target_pairs={{2,0},{5,1},{6,2},{1,3},{0,4},{9,5},{10,6},{3,7},{4,8},{13,9},{14,... | collective-permute-start | bytes 3538952 | tf_op jit(solution)/shard_map/ppermute | solution.py:353
  62.3 11.0 %collective-permute-start.11 = (bf16[1152,512]{1,0:T(8,128)(2,1)}, bf16[1152,512]{1,0:T(8,128)(2,1)S(1)}, u32[]{:S(2)}, u32[]{:S(2)}) collective-permute-start(bf16[1152,512]{1,0:T(8,128)(2,1)} %collective-permute-done.5.refs_3_), channel_id=1, source_target_pairs={{0,1},{1,0},{2,3},{3,2},{4,5},{5,4},{6,7},{7,6},{8,9},{9,8},{10,11... | collective-permute-start | bytes 3538952 | tf_op jit(solution)/shard_map/ppermute | solution.py:353
  63.3 18.3 %collective-permute-start.10 = (bf16[1152,512]{1,0:T(8,128)(2,1)}, bf16[1152,512]{1,0:T(8,128)(2,1)S(1)}, u32[]{:S(2)}, u32[]{:S(2)}) collective-permute-start(bf16[1152,512]{1,0:T(8,128)(2,1)} %collective-permute-done.5.refs_3_), channel_id=1, source_target_pairs={{0,2},{1,5},{2,6},{3,1},{4,0},{5,9},{6,10},{7,3},{8,4},{9,13},{10,... | collective-permute-start | bytes 3538952 | tf_op jit(solution)/shard_map/ppermute | solution.py:353
  73.3 11.2 %collective-permute-start.13 = (bf16[1152,512]{1,0:T(8,128)(2,1)S(1)}, bf16[1152,512]{1,0:T(8,128)(2,1)S(1)}, u32[]{:S(2)}, u32[]{:S(2)}) collective-permute-start(bf16[1152,512]{1,0:T(8,128)(2,1)S(1)} %collective-permute-done.4.refs_3_), channel_id=1, source_target_pairs={{0,1},{1,0},{2,3},{3,2},{4,5},{5,4},{6,7},{7,6},{8,9},{9,8},{10,11... | collective-permute-start | bytes 3538952 | tf_op jit(solution)/shard_map/ppermute | solution.py:353
  81.6 8.4 %collective-permute-start.12 = (bf16[1152,512]{1,0:T(8,128)(2,1)S(1)}, bf16[1152,512]{1,0:T(8,128)(2,1)S(1)}, u32[]{:S(2)}, u32[]{:S(2)}) collective-permute-start(bf16[1152,512]{1,0:T(8,128)(2,1)S(1)} %collective-permute-done.10.refs_3_), channel_id=1, source_target_pairs={{0,1},{1,0},{2,3},{3,2},{4,5},{5,4},{6,7},{7,6},{8,9},{9,8},{10,11... | collective-permute-start | bytes 3538952 | tf_op jit(solution)/shard_map/ppermute | solution.py:353
  82.2 15.5 %collective-permute-start.14 = (bf16[576,512]{1,0:T(8,128)(2,1)S(1)}, bf16[576,512]{1,0:T(8,128)(2,1)S(1)}, u32[]{:S(2)}, u32[]{:S(2)}) collective-permute-start(bf16[576,512]{1,0:T(8,128)(2,1)S(1)} %slice.7), channel_id=1, source_target_pairs={{0,2},{1,5},{2,6},{3,1},{4,0},{5,9},{6,10},{7,3},{8,4},{9,13},{10,... | collective-permute-start | bytes 1769480 | tf_op jit(solution)/shard_map/ppermute | solution.py:353
  84.3 13.5 %collective-permute-start.9 = (bf16[576,512]{1,0:T(8,128)(2,1)S(1)}, bf16[576,512]{1,0:T(8,128)(2,1)S(1)}, u32[]{:S(2)}, u32[]{:S(2)}) collective-permute-start(bf16[576,512]{1,0:T(8,128)(2,1)S(1)} %slice.6), channel_id=1, source_target_pairs={{2,0},{5,1},{6,2},{1,3},{0,4},{9,5},{10,6},{3,7},{4,8},{13,9},{14,... | collective-permute-start | bytes 1769480 | tf_op jit(solution)/shard_map/ppermute | solution.py:353
  90.0 10.5 %copy-start = (bf16[576,512]{1,0:T(8,128)(2,1)S(1)}, bf16[576,512]{1,0:T(8,128)(2,1)}, u32[]{:S(2)}) copy-start(bf16[576,512]{1,0:T(8,128)(2,1)} %refs_10_.1) | copy-start | bytes 1769476
  97.7 2.0 %collective-permute-start.16 = (bf16[576,512]{1,0:T(8,128)(2,1)S(1)}, bf16[576,512]{1,0:T(8,128)(2,1)S(1)}, u32[]{:S(2)}, u32[]{:S(2)}) collective-permute-start(bf16[576,512]{1,0:T(8,128)(2,1)S(1)} %collective-permute-done.14.refs_4_), channel_id=1, source_target_pairs={{0,1},{1,0},{2,3},{3,2},{4,5},{5,4},{6,7},{7,6},{8,9},{9,8},{10,11... | collective-permute-start | bytes 1769480 | tf_op jit(solution)/shard_map/ppermute | solution.py:353
  97.8 2.7 %collective-permute-start.15 = (bf16[576,512]{1,0:T(8,128)(2,1)S(1)}, bf16[576,512]{1,0:T(8,128)(2,1)S(1)}, u32[]{:S(2)}, u32[]{:S(2)}) collective-permute-start(bf16[576,512]{1,0:T(8,128)(2,1)S(1)} %collective-permute-done.9.refs_3_), channel_id=1, source_target_pairs={{0,1},{1,0},{2,3},{3,2},{4,5},{5,4},{6,7},{7,6},{8,9},{9,8},{10,11... | collective-permute-start | bytes 1769480 | tf_op jit(solution)/shard_map/ppermute | solution.py:353
  107.9 3.2 %collective-permute-start.17 = (f32[6,512]{1,0:T(8,128)S(1)}, f32[6,512]{1,0:T(8,128)S(1)}, u32[]{:S(2)}, u32[]{:S(2)}) collective-permute-start(f32[6,512]{1,0:T(8,128)S(1)} %get-tuple-element.92), channel_id=1, source_target_pairs={{0,3},{1,2},{2,1},{3,0},{4,7},{5,6},{6,5},{7,4},{8,11},{9,10},{10,... | collective-permute-start | bytes 36872 | tf_op jit(solution)/shard_map/ppermute | solution.py:313
  109.7 3.8 %collective-permute-start.18 = (f32[6,512]{1,0:T(8,128)S(1)}, f32[6,512]{1,0:T(8,128)S(1)}, u32[]{:S(2)}, u32[]{:S(2)}) collective-permute-start(f32[6,512]{1,0:T(8,128)S(1)} %get-tuple-element.92), channel_id=1, source_target_pairs={{0,2},{1,3},{2,0},{3,1},{4,6},{5,7},{6,4},{7,5},{8,10},{9,11},{10,... | collective-permute-start | bytes 36872 | tf_op jit(solution)/shard_map/ppermute | solution.py:313
  110.0 3.5 %collective-permute-start.19 = (f32[6,512]{1,0:T(8,128)S(1)}, f32[6,512]{1,0:T(8,128)S(1)}, u32[]{:S(2)}, u32[]{:S(2)}) collective-permute-start(f32[6,512]{1,0:T(8,128)S(1)} %get-tuple-element.92), channel_id=1, source_target_pairs={{0,1},{1,0},{2,3},{3,2},{4,5},{5,4},{6,7},{7,6},{8,9},{9,8},{10,11... | collective-permute-start | bytes 36872 | tf_op jit(solution)/shard_map/ppermute | solution.py:313
  113.5 6.4 %collective-permute-start.20 = (f32[24,512]{1,0:T(8,128)S(1)}, f32[24,512]{1,0:T(8,128)S(1)}, u32[]{:S(2)}, u32[]{:S(2)}) collective-permute-start(f32[24,512]{1,0:T(8,128)S(1)} %pad_maximum_fusion.1), channel_id=1, source_target_pairs={{0,12},{1,13},{2,14},{3,15},{4,8},{5,9},{6,10},{7,11},{8,4},{9,5},... | collective-permute-start | bytes 147464 | tf_op jit(solution)/shard_map/ppermute | solution.py:313
  117.2 5.0 %collective-permute-start.21 = (f32[24,512]{1,0:T(8,128)S(1)}, f32[24,512]{1,0:T(8,128)S(1)}, u32[]{:S(2)}, u32[]{:S(2)}) collective-permute-start(f32[24,512]{1,0:T(8,128)S(1)} %pad_maximum_fusion.1), channel_id=1, source_target_pairs={{0,8},{1,9},{2,10},{3,11},{4,12},{5,13},{6,14},{7,15},{8,0},{9,1},... | collective-permute-start | bytes 147464 | tf_op jit(solution)/shard_map/ppermute | solution.py:313
  117.2 5.0 %collective-permute-start.22 = (f32[24,512]{1,0:T(8,128)S(1)}, f32[24,512]{1,0:T(8,128)S(1)}, u32[]{:S(2)}, u32[]{:S(2)}) collective-permute-start(f32[24,512]{1,0:T(8,128)S(1)} %pad_maximum_fusion.1), channel_id=1, source_target_pairs={{0,4},{1,5},{2,6},{3,7},{4,0},{5,1},{6,2},{7,3},{8,12},{9,13},{10,... | collective-permute-start | bytes 147464 | tf_op jit(solution)/shard_map/ppermute | solution.py:313

commit v9 on v8

--- a/solution.py
+++ b/solution.py
@@ -189,7 +189,7 @@
     )(place, interaction, *smalls, *made)
 
 
-def step_body(parts, rows, opening, closing, orbitals, scale, *refs):
+def step_body(parts, rows, opening, closing, summing, before, orbitals, *refs):
     place_ref = refs[0]
     refs = list(refs[1:])
     chips = len(parts)
@@ -200,6 +200,7 @@
         greens.append([pieces[:count], pieces[count:]])
     sums = [] if opening else [refs.pop(0) for _ in range(3)]
     olds = [refs.pop(0) for _ in range(2)] if closing else []
+    del refs[:before]
     held = refs.pop()
     totals = [refs.pop() for _ in range(3)][::-1] if closing else refs[:3]
     core = place_ref[0]
@@ -240,17 +241,23 @@
             for first in range(rows // orbitals):
                 part = slice(first * orbitals, (first + 1) * orbitals)
                 shared = totals[2][part, :]
-                both = None
                 for kind in range(2):
                     slope = totals[kind][part, :] + shared
                     old = olds[kind][part, :].astype(jnp.float32)
                     refs[kind][part, :] = slope
                     refs[2 + kind][part, :] = (old + 0.5 * slope).astype(jnp.bfloat16)
-                    both = slope if both is None else both + slope
-                refs[4][first : first + 1, :] = jnp.sum(both, axis=0, keepdims=True) * scale
-
-
-def step(place, low, mats, greens, sums, olds, orbitals):
+
+    if summing:
+
+        @pl.when(now == chips - 1)
+        def _():
+            for first in range(rows // orbitals):
+                part = slice(first * orbitals, (first + 1) * orbitals)
+                both = totals[0][part, :] + totals[1][part, :] + 2.0 * totals[2][part, :]
+                refs[3][first : first + 1, :] = jnp.sum(both, axis=0, keepdims=True)
+
+
+def step(place, low, mats, greens, sums, olds, orbitals, summing=False, at=0, before=()):
     chips = len(greens)
     opening, closing = not sums, bool(olds)
     rows = mats[0].shape[0]
@@ -258,24 +265,26 @@
     parts = tuple(len(pair[0]) for pair in greens)
     wide = 2 * rows
     span = min(width, 256) if closing else width
-    tall = pl.BlockSpec((rows, span), lambda n, g, p: (0, n))
+    tall = pl.BlockSpec((rows, span), lambda n, g, p: (0, n + at))
     mat = pl.BlockSpec((rows, wide), lambda n, g, p: (0, p[1 + low + g]))
     wide_sum = jax.ShapeDtypeStruct((rows, width), jnp.float32)
     scratch = [pltpu.VMEM((wide, 3 * span), jnp.bfloat16)]
     if closing:
-        out_specs = [tall] * 4 + [pl.BlockSpec((rows // orbitals, span), lambda n, g, p: (0, n))]
+        out_specs = [tall] * 4
         out_shape = [wide_sum] * 2 + [jax.ShapeDtypeStruct((rows, width), jnp.bfloat16)] * 2
-        out_shape += [jax.ShapeDtypeStruct((rows // orbitals, width), jnp.float32)]
         scratch = [pltpu.VMEM((rows, span), jnp.float32)] * 3 + scratch
     else:
         out_specs, out_shape = [tall] * 3, [wide_sum] * 3
+        if summing:
+            out_specs = out_specs + [pl.BlockSpec((rows // orbitals, span), lambda n, g, p: (0, n))]
+            out_shape = out_shape + [jax.ShapeDtypeStruct((rows // orbitals, width), jnp.float32)]
     operands = [pltpu.with_memory_space_constraint(mat_, pltpu.HBM) for mat_ in mats]
     blocks = [block for pair in greens for side in pair for block in side]
     operands += blocks
     in_specs = [mat] * 2
     mode = pl.Buffered(1 if span == width else 2)
     in_specs += [
-        pl.BlockSpec((block.shape[0], span), lambda n, g, p: (0, n), pipeline_mode=mode)
+        pl.BlockSpec((block.shape[0], span), lambda n, g, p: (0, n + at), pipeline_mode=mode)
         for block in blocks
     ]
     aliases = {}
@@ -283,17 +292,20 @@
         if not closing:
             aliases = {1 + len(operands) + n: n for n in range(3)}
         operands += list(sums)
-        in_specs += [pl.BlockSpec((rows, span), lambda n, g, p: (0, n), pipeline_mode=mode)] * 3
+        in_specs += [pl.BlockSpec((rows, span), lambda n, g, p: (0, n + at), pipeline_mode=mode)] * 3
     if closing:
         operands += list(olds)
         in_specs += [tall] * 2
+        aliases = {1 + len(operands) + n: n for n in range(len(before))}
+        operands += list(before)
+        in_specs += [pl.BlockSpec(memory_space=pl.ANY)] * len(before)
     return pl.pallas_call(
         functools.partial(
-            step_body, parts, rows, opening, closing, orbitals, 1.0 / math.sqrt(orbitals)
+            step_body, parts, rows, opening, closing, summing, len(before), orbitals
         ),
         grid_spec=pltpu.PrefetchScalarGridSpec(
             num_scalar_prefetch=1,
-            grid=(width // span, chips),
+            grid=(1, chips),
             in_specs=in_specs,
             out_specs=out_specs,
             scratch_shapes=scratch,
@@ -303,6 +315,88 @@
         compiler_params=pltpu.CompilerParams(vmem_limit_bytes=36 * MIB),
         cost_estimate=pl.CostEstimate(flops=1024, bytes_accessed=1024, transcendentals=0),
         name="add_products",
+    )(place, *operands)
+
+
+def sums_body(orbitals, place_ref, mixed_ref, polar_ref, out_ref):
+    rows, wide = mixed_ref.shape
+    out_ref[...] = jnp.zeros_like(out_ref)
+    for kind, ref in enumerate((mixed_ref, polar_ref)):
+        lines = [
+            jnp.sum(ref[low : low + orbitals, :].astype(jnp.float32), axis=0, keepdims=True)
+            for low in range(0, rows, orbitals)
+        ]
+        lines += [jnp.zeros((8 - len(lines), wide), jnp.float32)] if len(lines) < 8 else []
+        total = jnp.concatenate(lines, axis=0)
+        high = total.astype(jnp.bfloat16).astype(jnp.float32)
+        pair = jnp.concatenate([high, total - high], axis=0)
+        out_ref[16 * kind : 16 * (kind + 1), :] = pair.astype(jnp.bfloat16)
+
+
+def row_sums(place, spot, mats, orbitals):
+    rows, pairs = mats[0].shape
+    mat = pl.BlockSpec((rows, 2 * rows), lambda g, p: (0, p[1 + spot]))
+    return pl.pallas_call(
+        functools.partial(sums_body, orbitals),
+        grid_spec=pltpu.PrefetchScalarGridSpec(
+            num_scalar_prefetch=1,
+            grid=(1,),
+            in_specs=[mat, mat],
+            out_specs=pl.BlockSpec((32, 2 * rows), lambda g, p: (0, 0)),
+        ),
+        out_shape=jax.ShapeDtypeStruct((32, 2 * rows), jnp.bfloat16),
+        compiler_params=pltpu.CompilerParams(vmem_limit_bytes=20 * MIB),
+        cost_estimate=pl.CostEstimate(flops=1024, bytes_accessed=1024, transcendentals=0),
+        name="row_sums",
+    )(place, *[pltpu.with_memory_space_constraint(mat_, pltpu.HBM) for mat_ in mats])
+
+
+def share_body(scale, place_ref, own_ref, other_ref, same_ref, opp_ref, part_ref, out_ref, held):
+    core = place_ref[0]
+    rows, width = same_ref.shape
+    there = pl.ds(pl.multiple_of(core * rows, 64), rows)
+    rest = pl.ds(pl.multiple_of((1 - core) * rows, 64), rows)
+    same, opp = same_ref[...], opp_ref[...]
+    both = same.astype(jnp.float32) + opp.astype(jnp.float32)
+    held[rest, :] = jnp.zeros((rows, 3 * width), jnp.bfloat16)
+    held[there, :width] = same
+    held[there, width : 2 * width] = opp
+    held[there, 2 * width :] = both.astype(jnp.bfloat16)
+    lines = jnp.concatenate([own_ref[...], other_ref[...]], axis=0)
+    all_terms = product(lines, held[...])
+    ends = []
+    for low in (0, 32):
+        terms = all_terms[low : low + 32]
+        mixed = terms[0:8] + terms[8:16]
+        polar = terms[16:24] + terms[24:32]
+        ends.append(
+            mixed[:, :width] + mixed[:, width : 2 * width] + 2.0 * polar[:, 2 * width :]
+        )
+    count = part_ref.shape[0]
+    mine = (ends[0][:count] + part_ref[...]) * scale
+    theirs = ends[1][:count] * scale
+    first = core == 0
+    out_ref[:count, :] = jnp.where(first, mine, theirs)
+    out_ref[count:, :] = jnp.where(first, theirs, mine)
+
+
+def chip_share(place, own_lines, other_lines, far, part, orbitals):
+    rows, width = far[0].shape
+    whole = lambda array: pl.BlockSpec(array.shape, lambda g, p: (0, 0))
+    operands = [own_lines, other_lines, *far, part]
+    return pl.pallas_call(
+        functools.partial(share_body, 1.0 / math.sqrt(orbitals)),
+        grid_spec=pltpu.PrefetchScalarGridSpec(
+            num_scalar_prefetch=1,
+            grid=(1,),
+            in_specs=[whole(array) for array in operands],
+            out_specs=pl.BlockSpec((2 * part.shape[0], width), lambda g, p: (0, 0)),
+            scratch_shapes=[pltpu.VMEM((2 * rows, 3 * width), jnp.bfloat16)],
+        ),
+        out_shape=jax.ShapeDtypeStruct((2 * part.shape[0], width), jnp.float32),
+        compiler_params=pltpu.CompilerParams(vmem_limit_bytes=20 * MIB),
+        cost_estimate=pl.CostEstimate(flops=1024, bytes_accessed=1024, transcendentals=0),
+        name="chip_share",
     )(place, *operands)
 
 
@@ -396,28 +490,45 @@
                 came = [([got[1]], [passed[0]]), ([got[0]], [passed[1]])]
                 split = 0 if far == 1 else 1
                 waiting, later = waiting + came[:split], came[split:]
-            sums = step(after(place, block), low, mats, waiting, sums, (), orbitals)
+            when = after(place, block)
+            if far == 2 and turn == 0:
+                lines = row_sums(when, chips - 1, mats, orbitals)
+                when = after(when, lines)
+            if far == half - 1 and turn == 0:
+                when = after(when, other_lines)
+            sums = step(when, low, mats, waiting, sums, (), orbitals)
             low += len(waiting)
             waiting, done = later, sums[0]
-    sums = step(place, low, mats, waiting, sums, (), orbitals)
+            if far == 2 and turn == 0:
+                other_lines = send(after(lines, done), across)
+    *sums, part = step(place, low, mats, waiting, sums, (), orbitals, summing=True)
     low += len(waiting)
     last = [after(block, sums[0]) for block in moving]
     shared = [send(block, across) for block in last]
-    new_same, new_opp, next_same, next_opp, part = step(
-        place, low, mats, [(last, shared)], sums, (green_same, green_opp), orbitals
-    )
-    if devices == 16:
-        collision = spread_blocks(spread_blocks(part, me, 1, devices), me, 4, devices)
-    else:
-        collision = lax.all_gather(part, "prow", axis=0, tiled=True)
-    return (new_same, new_opp, next_same, next_opp, collision)
+
+    mine = chip_share(place, lines, other_lines, last, part, orbitals)
+    quad = [mine]
+    for other in range(1, 4):
+        quad.append(lax.ppermute(mine, "prow", [(d, d ^ other) for d in range(devices)]))
+    olds = (green_same, green_opp)
+    outs = step(after(place, mine), low, mats, [(last, shared)], sums, olds, orbitals)
+    quad = lax.optimization_barrier((*quad, outs[0]))
+    here, there = quad[0] + quad[1], quad[2] + quad[3]
+    lower = me // 2 % 2 == 0
+    rows_four = jnp.concatenate(
+        [jnp.where(lower, here, there), jnp.where(lower, there, here)], axis=0
+    )
+    collision = spread_blocks(rows_four, me, 4, devices)
+    outs = step(place, low, mats, [(last, shared)], sums, olds, orbitals, at=1, before=outs)
+    return (*outs, collision)
 
 
 def per_device(green_same, green_opp, interaction, pattern, occupation, hopping):
     rows = green_same.shape[0]
     orbitals = hopping.shape[0]
     devices = orbitals * orbitals // rows
-    fits = rows % orbitals == 0 and rows % 576 == 0 and devices % 4 == 0 and devices >= 12
+    fits = rows % orbitals == 0 and rows % 576 == 0 and devices == 16 and rows // orbitals <= 8
+    fits = fits and green_same.shape[1] == 512
     form = ring_form if fits else plain_form
     return form(green_same, green_opp, interaction, pattern, occupation, hopping)
 

time: 123 us -> 129 us (1.049)
  waiting for transfers between devices: 21.2 us -> 5.96 us
  Pallas kernels: 76.5 us -> 86.6 us
  local copies, waits for them, and re-layouts: 2.07 us -> 10.5 us
  other arithmetic: 1.02 us -> 3.3 us
    unnamed x13 -> x35, local copies, waits for them, and re-layouts: 1.26 us -> 9.68 us
    ppermute x6 -> x3, waiting for transfers between devices: 7.69 us -> 0.01 us  [spread_blocks(): blocks.append(lax.ppermute(block, 'prow', pairs_of))]
    ppermute x17 -> x18, waiting for transfers between devices: 13.5 us -> 5.95 us  [send(): return lax.ppermute(block, 'prow', pairs_of)]
    pallas_call x0 -> x2, Pallas kernels: none -> 6.35 us  [the longest x1 3.63 us: chip_share(): pl.pallas_call(functools.partial(share_body, 1.0 / math.sqrt(orbitals)),...]
    pallas_call x7 -> x8, Pallas kernels: 45.9 us -> 49.7 us  [step(): pl.pallas_call(functools.partial(step_body, parts, rows, opening, closing...]
    ppermute x0 -> x3, starting transfers between devices: none -> 2 us  [ring_form(): lax.ppermute(mine, 'prow', [(d, d ^ other) for d in range(devices)])]
    ppermute x6 -> x3, starting transfers between devices: 6.58 us -> 4.89 us  [spread_blocks(): blocks.append(lax.ppermute(block, 'prow', pairs_of))]
    ppermute x17 -> x18, starting transfers between devices: 14.7 us -> 13.8 us  [send(): return lax.ppermute(block, 'prow', pairs_of)]
  transfers between devices with their start and end apart: 23 -> 24, of which waited for: 13 -> 4; matrix products, arithmetic and copies ran while one was open for 1% -> 1% of each run, Pallas kernels for 56% -> 68%
where the time goes in v9:
time: 129 us; the launch traced here: 128 us
  Pallas kernels  86.6 us (67%)
  starting transfers between devices  20.7 us (16%)
  local copies, waits for them, and re-layouts  10.5 us (8%)
  waiting for transfers between devices  5.96 us (5%)
  other arithmetic  3.3 us (3%)
    pallas_call x8, Pallas kernels, step(): pl.pallas_call(functools.partial(step_body, parts, rows, opening, closing...  49.7 us
    pallas_call x3, Pallas kernels, build_rows(): pl.pallas_call(functools.partial(build_body, orbitals, low, high, pairs),...  30.6 us
    ppermute x18, starting transfers between devices, send(): return lax.ppermute(block, 'prow', pairs_of)  13.8 us
    unnamed x35, local copies, waits for them, and re-layouts  9.68 us
    ppermute x18, waiting for transfers between devices, send(): return lax.ppermute(block, 'prow', pairs_of)  5.95 us
    ppermute x3, starting transfers between devices, spread_blocks(): blocks.append(lax.ppermute(block, 'prow', pairs_of))  4.89 us
    pallas_call x1, Pallas kernels, chip_share(): pl.pallas_call(functools.partial(share_body, 1.0 / math.sqrt(orbitals)),...  3.63 us
    pallas_call x1, Pallas kernels, row_sums(): pl.pallas_call(functools.partial(sums_body, orbitals), grid_spec=pltpu.Pr...  2.72 us
  transfers between devices with their start and end apart: 24, of which 4 were waited for; matrix products, arithmetic and copies ran while one was open for 1% of the time, Pallas kernels for 68%

profile of v9, /device:TPU:0, one launch (start us, length us, event | category | flops | bytes accessed | tf_op | source)
XLA Modules:
  0.0 128.0 jit_solution(10743782603341823891)
XLA Ops:
  0.6 0.0 copy-start.7
  0.6 0.0 copy-start.2
  0.7 1.2 constant_dynamic-update-slice_fusion.1
  1.9 0.1 copy-done.2
  2.0 0.0 copy-start.5
  2.0 3.1 %collective-permute-start = (bf16[1152,512]{1,0:T(8,128)(2,1)S(1)}, bf16[1152,512]{1,0:T(8,128)(2,1)}, u32[]{:S(2)}, u32[]{:S(2)}) collective-permute-start(bf16[1152,512]{1,0:T(8,128)(2,1)S(1)} %constant_dynamic-update-slice_fusion.refs_3_), channel_id=1, source_target_pairs={{2,0},{5,1},{6,2},{1,3},{0,4},{9,5},{10,6},{3,7},{4,8},{13,9},{14,... | collective-permute-start | bytes 3538952 | tf_op jit(solution)/shard_map/ppermute | solution.py:447
  5.1 0.1 pad_maximum_fusion.2
  5.2 0.2 maximum_maximum_fusion.refs_5_
  5.4 7.1 %build_rows.3 = (bf16[576,9216]{1,0:T(8,128)(2,1)}, bf16[576,9216]{1,0:T(8,128)(2,1)}) custom-call(s32[1]{0:T(128)} %bitcast.1.refs_0_, bf16[576,9216]{1,0:T(8,128)(2,1)} %refs_1_.5, s32[96,96]{1,0:T(8,128)S(1)} %copy-done.10, f32[96,96]{1,0:T(8,128)S(1)} %copy-done.11, f32[96]{0:T(128)S(1)} %copy-done.12, f32[192,384]{1,0:T(8,128)S(1)} %maximum_maximum_fusion.refs_5_, ...), custom_call_target="tpu_custom_call" | custom-call | flops 1024 | bytes 1024 | tf_op jit(solution)/shard_map/build_rows/pallas_call | solution.py:174
  12.5 0.1 collective-permute-start.3
  12.6 11.7 %build_rows.4 = (bf16[576,9216]{1,0:T(8,128)(2,1)}, bf16[576,9216]{1,0:T(8,128)(2,1)}) custom-call(s32[1]{0:T(128)} %bitcast.1.refs_0_, bf16[576,9216]{1,0:T(8,128)(2,1)} %refs_1_.5, s32[96,96]{1,0:T(8,128)S(1)} %copy-done.10, f32[96,96]{1,0:T(8,128)S(1)} %copy-done.11, f32[96]{0:T(128)S(1)} %copy-done.12, ...), custom_call_target="tpu_custom_call", output_to_operand_aliasing={{0}: (8, {}), {1}: (9, {})} | custom-call | flops 1024 | bytes 1024 | tf_op jit(solution)/shard_map/build_rows/pallas_call | solution.py:174
  24.3 0.7 collective-permute-done.refs_5_
  25.0 2.6 %collective-permute-start.1 = (bf16[1152,512]{1,0:T(8,128)(2,1)}, bf16[1152,512]{1,0:T(8,128)(2,1)}, u32[]{:S(2)}, u32[]{:S(2)}) collective-permute-start(bf16[1152,512]{1,0:T(8,128)(2,1)} %collective-permute-done.refs_5_), channel_id=1, source_target_pairs={{2,0},{5,1},{6,2},{1,3},{0,4},{9,5},{10,6},{3,7},{4,8},{13,9},{14,... | collective-permute-start | bytes 3538952 | tf_op jit(solution)/shard_map/ppermute | solution.py:447
  27.6 11.7 %build_rows.5 = (bf16[576,9216]{1,0:T(8,128)(2,1)}, bf16[576,9216]{1,0:T(8,128)(2,1)}) custom-call(s32[1]{0:T(128)} %bitcast.1.refs_0_, bf16[576,9216]{1,0:T(8,128)(2,1)} %refs_1_.5, s32[96,96]{1,0:T(8,128)S(1)} %copy-done.10, f32[96,96]{1,0:T(8,128)S(1)} %copy-done.11, f32[96]{0:T(128)S(1)} %copy-done.12, ...), custom_call_target="tpu_custom_call", output_to_operand_aliasing={{0}: (8, {}), {1}: (9, {})} | custom-call | flops 1024 | bytes 1024 | tf_op jit(solution)/shard_map/build_rows/pallas_call | solution.py:174
  39.3 0.5 collective-permute-start.6
  39.8 0.7 dynamic-slice_bitcast_fusion.refs_0_.place_ref
  40.5 1.0 copy-done.8
  41.5 1.3 copy-done.6
  42.8 1.3 copy-done.9
  44.1 5.4 %add_products.8 = (f32[576,512]{1,0:T(8,128)S(1)}, f32[576,512]{1,0:T(8,128)S(1)}, f32[576,512]{1,0:T(8,128)S(1)}) custom-call(s32[10]{0:T(128)S(1)} %dynamic-slice_bitcast_fusion.refs_0_.place_ref, bf16[576,9216]{1,0:T(8,128)(2,1)} %get-tuple-element.67.refs_1_.mixed_ref, bf16[576,9216]{1,0:T(8,128)(2,1)} %get-tuple-element.68.refs_2_.polar_ref, ...), custom_call_target="tpu_custom_call" | custom-call | flops 1024 | bytes 1024 | tf_op jit(solution)/shard_map/add_products/pallas_call | solution.py:302
  49.5 1.3 %collective-permute-start.8 = (bf16[1152,512]{1,0:T(8,128)(2,1)}, bf16[1152,512]{1,0:T(8,128)(2,1)S(1)}, u32[]{:S(2)}, u32[]{:S(2)}) collective-permute-start(bf16[1152,512]{1,0:T(8,128)(2,1)} %collective-permute-done.1.refs_3_), channel_id=1, source_target_pairs={{0,1},{1,0},{2,3},{3,2},{4,5},{5,4},{6,7},{7,6},{8,9},{9,8},{10,11... | collective-permute-start | bytes 3538952 | tf_op jit(solution)/shard_map/ppermute | solution.py:447
  50.8 1.6 %collective-permute-start.4 = (bf16[1152,512]{1,0:T(8,128)(2,1)}, bf16[1152,512]{1,0:T(8,128)(2,1)S(1)}, u32[]{:S(2)}, u32[]{:S(2)}) collective-permute-start(bf16[1152,512]{1,0:T(8,128)(2,1)} %collective-permute-done.1.refs_3_), channel_id=1, source_target_pairs={{2,0},{5,1},{6,2},{1,3},{0,4},{9,5},{10,6},{3,7},{4,8},{13,9},{14,... | collective-permute-start | bytes 3538952 | tf_op jit(solution)/shard_map/ppermute | solution.py:447
  52.4 2.7 %row_sums.1.own_ref = bf16[32,1152]{1,0:T(8,128)(2,1)S(1)} custom-call(s32[10]{0:T(128)S(1)} %dynamic-slice_bitcast_fusion.refs_0_.place_ref, bf16[576,9216]{1,0:T(8,128)(2,1)} %get-tuple-element.67.refs_1_.mixed_ref, bf16[576,9216]{1,0:T(8,128)(2,1)} %get-tuple-element.68.refs_2_.polar_ref), custom_call_target="tpu_custom_call" | custom-call | flops 1024 | bytes 1024 | tf_op jit(solution)/shard_map/row_sums/pallas_call | solution.py:339
  55.1 0.0 collective-permute-done.6.refs_4_
  55.1 10.2 %add_products.9 = (f32[576,512]{1,0:T(8,128)S(1)}, f32[576,512]{1,0:T(8,128)S(1)}, f32[576,512]{1,0:T(8,128)S(1)}) custom-call(s32[10]{0:T(128)S(1)} %dynamic-slice_bitcast_fusion.refs_0_.place_ref, bf16[576,9216]{1,0:T(8,128)(2,1)} %get-tuple-element.67.refs_1_.mixed_ref, ...), custom_call_target="tpu_custom_call", output_to_operand_aliasing={{0}: (7, {}), {1}: (8, {}), {2}: (9, {})} | custom-call | flops 1024 | bytes 1024 | tf_op jit(solution)/shard_map/add_products/pallas_call | solution.py:302
  65.3 0.1 collective-permute-start.12
  65.4 0.7 collective-permute-start.10
  66.1 1.0 collective-permute-start.11
  67.1 0.0 collective-permute-done.8.refs_4_
  67.1 5.9 %add_products.10 = (f32[576,512]{1,0:T(8,128)S(1)}, f32[576,512]{1,0:T(8,128)S(1)}, f32[576,512]{1,0:T(8,128)S(1)}) custom-call(s32[10]{0:T(128)S(1)} %dynamic-slice_bitcast_fusion.refs_0_.place_ref, bf16[576,9216]{1,0:T(8,128)(2,1)} %get-tuple-element.67.refs_1_.mixed_ref, ...), custom_call_target="tpu_custom_call", output_to_operand_aliasing={{0}: (5, {}), {1}: (6, {}), {2}: (7, {})} | custom-call | flops 1024 | bytes 1024 | tf_op jit(solution)/shard_map/add_products/pallas_call | solution.py:302
  72.9 0.0 collective-permute-done.4.refs_3_
  72.9 0.1 collective-permute-start.14
  73.0 0.0 collective-permute-done.11.other_ref
  73.0 0.0 collective-permute-done.12.refs_4_
  73.0 5.9 %add_products.11 = (f32[576,512]{1,0:T(8,128)S(1)}, f32[576,512]{1,0:T(8,128)S(1)}, f32[576,512]{1,0:T(8,128)S(1)}) custom-call(s32[10]{0:T(128)S(1)} %dynamic-slice_bitcast_fusion.refs_0_.place_ref, bf16[576,9216]{1,0:T(8,128)(2,1)} %get-tuple-element.67.refs_1_.mixed_ref, ...), custom_call_target="tpu_custom_call", output_to_operand_aliasing={{0}: (5, {}), {1}: (6, {}), {2}: (7, {})} | custom-call | flops 1024 | bytes 1024 | tf_op jit(solution)/shard_map/add_products/pallas_call | solution.py:302
  78.9 3.1 %collective-permute-done.10.refs_3_ = bf16[1152,512]{1,0:T(8,128)(2,1)S(1)} collective-permute-done((bf16[1152,512]{1,0:T(8,128)(2,1)}, bf16[1152,512]{1,0:T(8,128)(2,1)S(1)}, u32[]{:S(2)}, u32[]{:S(2)}) %collective-permute-start.10) | collective-permute-done | bytes 1179680 | tf_op jit(solution)/shard_map/ppermute | solution.py:447
  82.0 0.2 collective-permute-start.13
  82.2 2.1 %collective-permute-start.15 = (bf16[576,512]{1,0:T(8,128)(2,1)S(1)}, bf16[576,512]{1,0:T(8,128)(2,1)}, u32[]{:S(2)}, u32[]{:S(2)}) collective-permute-start(bf16[576,512]{1,0:T(8,128)(2,1)S(1)} %slice.7), channel_id=1, source_target_pairs={{0,2},{1,5},{2,6},{3,1},{4,0},{5,9},{6,10},{7,3},{8,4},{9,13},{10,... | collective-permute-start | bytes 1769480 | tf_op jit(solution)/shard_map/ppermute | solution.py:447
  84.4 0.1 collective-permute-start.9
  84.5 5.5 %add_products.12 = (f32[576,512]{1,0:T(8,128)S(1)}, f32[576,512]{1,0:T(8,128)S(1)}, f32[576,512]{1,0:T(8,128)S(1)}) custom-call(s32[10]{0:T(128)S(1)} %dynamic-slice_bitcast_fusion.refs_0_.place_ref, bf16[576,9216]{1,0:T(8,128)(2,1)} %get-tuple-element.67.refs_1_.mixed_ref, ...), custom_call_target="tpu_custom_call", output_to_operand_aliasing={{0}: (5, {}), {1}: (6, {}), {2}: (7, {})} | custom-call | flops 1024 | bytes 1024 | tf_op jit(solution)/shard_map/add_products/pallas_call | solution.py:302
  90.0 0.0 collective-permute-done.13.refs_4_
  90.0 5.9 %add_products.13 = (f32[576,512]{1,0:T(8,128)S(1)}, f32[576,512]{1,0:T(8,128)S(1)}, f32[576,512]{1,0:T(8,128)S(1)}, f32[6,512]{1,0:T(8,128)S(1)}) custom-call(s32[10]{0:T(128)S(1)} %dynamic-slice_bitcast_fusion.refs_0_.place_ref, bf16[576,9216]{1,0:T(8,128)(2,1)} %get-tuple-element.67.refs_1_.mixed_ref, ...), custom_call_target="tpu_custom_call", output_to_operand_aliasing={{0}: (5, {}), {1}: (6, {}), {2}: (7, {})} | custom-call | flops 1024 | bytes 1024 | tf_op jit(solution)/shard_map/add_products/pallas_call | solution.py:302
  95.9 2.0 %collective-permute-done.15.opp_ref.refs_4_ = bf16[576,512]{1,0:T(8,128)(2,1)} collective-permute-done((bf16[576,512]{1,0:T(8,128)(2,1)S(1)}, bf16[576,512]{1,0:T(8,128)(2,1)}, u32[]{:S(2)}, u32[]{:S(2)}) %collective-permute-start.15) | collective-permute-done | bytes 589856 | tf_op jit(solution)/shard_map/ppermute | solution.py:447
  97.8 0.0 collective-permute-start.17
  97.8 0.2 collective-permute-done.9.same_ref.refs_3_
  98.0 0.5 collective-permute-start.16
  98.5 3.6 %chip_share.1 = f32[12,512]{1,0:T(8,128)} custom-call(s32[10]{0:T(128)S(1)} %dynamic-slice_bitcast_fusion.refs_0_.place_ref, bf16[32,1152]{1,0:T(8,128)(2,1)S(1)} %row_sums.1.own_ref, bf16[32,1152]{1,0:T(8,128)(2,1)S(1)} %collective-permute-done.11.other_ref, bf16[576,512]{1,0:T(8,128)(2,1)} %collective-permute-done.9.same_ref.refs_3_, ...), custom_call_target="tpu_custom_call" | custom-call | flops 1024 | bytes 1024 | tf_op jit(solution)/shard_map/chip_share/pallas_call | solution.py:387
  102.1 0.0 collective-permute-start.18
  102.1 1.8 %collective-permute-start.19 = (f32[12,512]{1,0:T(8,128)}, f32[12,512]{1,0:T(8,128)}, u32[]{:S(2)}, u32[]{:S(2)}) collective-permute-start(f32[12,512]{1,0:T(8,128)} %chip_share.1), channel_id=1, source_target_pairs={{0,2},{1,3},{2,0},{3,1},{4,6},{5,7},{6,4},{7,5},{8,10},{9,11},{10,... | collective-permute-start | bytes 73736 | tf_op jit(solution)/shard_map/ppermute | solution.py:512
  104.0 0.1 collective-permute-start.20
  104.1 0.0 collective-permute-done.17.refs_6_
  104.1 1.1 copy-done
  105.2 1.1 copy-done.3
  106.3 5.5 %add_products.14 = (f32[576,512]{1,0:T(8,128)}, f32[576,512]{1,0:T(8,128)}, bf16[576,512]{1,0:T(8,128)(2,1)}, bf16[576,512]{1,0:T(8,128)(2,1)}) custom-call(s32[10]{0:T(128)S(1)} %dynamic-slice_bitcast_fusion.refs_0_.place_ref, bf16[576,9216]{1,0:T(8,128)(2,1)} %get-tuple-element.67.refs_1_.mixed_ref, bf16[576,9216]{1,0:T(8,128)(2,1)} %get-tuple-element.68.refs_2_.polar_ref, ...), custom_call_target="tpu_custom_call" | custom-call | flops 1024 | bytes 1024 | tf_op jit(solution)/shard_map/add_products/pallas_call | solution.py:302
  111.8 0.8 broadcast_select_fusion.9
  112.6 0.6 copy-done.13
  113.2 0.6 pad_maximum_fusion.1
  113.9 4.3 %collective-permute-start.21 = (f32[24,512]{1,0:T(8,128)}, f32[24,512]{1,0:T(8,128)}, u32[]{:S(2)}, u32[]{:S(2)}) collective-permute-start(f32[24,512]{1,0:T(8,128)} %pad_maximum_fusion.1), channel_id=1, source_target_pairs={{0,12},{1,13},{2,14},{3,15},{4,8},{5,9},{6,10},{7,11},{8,4},{9,5},... | collective-permute-start | bytes 147464 | tf_op jit(solution)/shard_map/ppermute | solution.py:407
  118.2 0.6 collective-permute-start.23
  118.8 1.1 copy-done.1
  119.8 1.1 copy-done.4
  120.9 5.5 %add_products.15 = (f32[576,512]{1,0:T(8,128)}, f32[576,512]{1,0:T(8,128)}, bf16[576,512]{1,0:T(8,128)(2,1)}, bf16[576,512]{1,0:T(8,128)(2,1)}) custom-call(s32[10]{0:T(128)S(1)} %dynamic-slice_bitcast_fusion.refs_0_.place_ref, ...), custom_call_target="tpu_custom_call", output_to_operand_aliasing={{0}: (12, {}), {1}: (13, {}), {2}: (14, {}), {3}: (15, {})} | custom-call | flops 1024 | bytes 1024 | tf_op jit(solution)/shard_map/add_products/pallas_call | solution.py:302
  126.4 0.9 broadcast_select_fusion.7
  127.3 0.7 pad_maximum_fusion
  (44 shorter events, 0.2 us)
Async XLA Ops:
  0.6 4.7 %copy-start.7 = (f32[96,384]{1,0:T(8,128)S(1)}, f32[96,384]{1,0:T(8,128)}, u32[]{:S(2)}) copy-start(f32[96,384]{1,0:T(8,128)} %constant.71.clone.refs_6_) | copy-start | bytes 442372
  0.6 1.3 %copy-start.2 = (bf16[576,512]{1,0:T(8,128)(2,1)S(1)}, bf16[576,512]{1,0:T(8,128)(2,1)}, u32[]{:S(2)}) copy-start(bf16[576,512]{1,0:T(8,128)(2,1)} %refs_11_.3) | copy-start | bytes 1769476
  0.7 4.4 %copy-start.10 = (s32[96,96]{1,0:T(8,128)S(1)}, s32[96,96]{1,0:T(8,128)}, u32[]{:S(2)}) copy-start(s32[96,96]{1,0:T(8,128)} %refs_2_.5) | copy-start | bytes 110596
  0.7 4.4 %copy-start.12 = (f32[96]{0:T(128)S(1)}, f32[96]{0:T(128)}, u32[]{:S(2)}) copy-start(f32[96]{0:T(128)} %refs_4_.5) | copy-start | bytes 1156
  0.7 4.5 %copy-start.11 = (f32[96,96]{1,0:T(8,128)S(1)}, f32[96,96]{1,0:T(8,128)}, u32[]{:S(2)}) copy-start(f32[96,96]{1,0:T(8,128)} %refs_3_.5) | copy-start | bytes 110596
  2.0 10.6 %copy-start.5 = (bf16[1152,512]{1,0:T(8,128)(2,1)}, bf16[1152,512]{1,0:T(8,128)(2,1)S(1)}, u32[]{:S(2)}) copy-start(bf16[1152,512]{1,0:T(8,128)(2,1)S(1)} %constant_dynamic-update-slice_fusion.refs_3_) | copy-start | bytes 3538948
  2.0 23.0 %collective-permute-start = (bf16[1152,512]{1,0:T(8,128)(2,1)S(1)}, bf16[1152,512]{1,0:T(8,128)(2,1)}, u32[]{:S(2)}, u32[]{:S(2)}) collective-permute-start(bf16[1152,512]{1,0:T(8,128)(2,1)S(1)} %constant_dynamic-update-slice_fusion.refs_3_), channel_id=1, source_target_pairs={{2,0},{5,1},{6,2},{1,3},{0,4},{9,5},{10,6},{3,7},{4,8},{13,9},{14,... | collective-permute-start | bytes 3538952 | tf_op jit(solution)/shard_map/ppermute | solution.py:447
  12.5 26.8 %collective-permute-start.2 = (bf16[1152,512]{1,0:T(8,128)(2,1)S(1)}, bf16[1152,512]{1,0:T(8,128)(2,1)}, u32[]{:S(2)}, u32[]{:S(2)}) collective-permute-start(bf16[1152,512]{1,0:T(8,128)(2,1)S(1)} %constant_dynamic-update-slice_fusion.refs_3_), channel_id=1, source_target_pairs={{0,2},{1,5},{2,6},{3,1},{4,0},{5,9},{6,10},{7,3},{8,4},{9,13},{10,... | collective-permute-start | bytes 3538952 | tf_op jit(solution)/shard_map/ppermute | solution.py:447
  12.5 28.0 %collective-permute-start.3 = (bf16[1152,512]{1,0:T(8,128)(2,1)S(1)}, bf16[1152,512]{1,0:T(8,128)(2,1)S(1)}, u32[]{:S(2)}, u32[]{:S(2)}) collective-permute-start(bf16[1152,512]{1,0:T(8,128)(2,1)S(1)} %constant_dynamic-update-slice_fusion.refs_3_), channel_id=1, source_target_pairs={{0,1},{1,0},{2,3},{3,2},{4,5},{5,4},{6,7},{7,6},{8,9},{9,8},{10,11... | collective-permute-start | bytes 3538952 | tf_op jit(solution)/shard_map/ppermute | solution.py:447
  25.0 24.5 %collective-permute-start.1 = (bf16[1152,512]{1,0:T(8,128)(2,1)}, bf16[1152,512]{1,0:T(8,128)(2,1)}, u32[]{:S(2)}, u32[]{:S(2)}) collective-permute-start(bf16[1152,512]{1,0:T(8,128)(2,1)} %collective-permute-done.refs_5_), channel_id=1, source_target_pairs={{2,0},{5,1},{6,2},{1,3},{0,4},{9,5},{10,6},{3,7},{4,8},{13,9},{14,... | collective-permute-start | bytes 3538952 | tf_op jit(solution)/shard_map/ppermute | solution.py:447
  39.3 15.8 %collective-permute-start.7 = (bf16[1152,512]{1,0:T(8,128)(2,1)}, bf16[1152,512]{1,0:T(8,128)(2,1)}, u32[]{:S(2)}, u32[]{:S(2)}) collective-permute-start(bf16[1152,512]{1,0:T(8,128)(2,1)} %collective-permute-done.2.refs_3_), channel_id=1, source_target_pairs={{0,1},{1,0},{2,3},{3,2},{4,5},{5,4},{6,7},{7,6},{8,9},{9,8},{10,11... | collective-permute-start | bytes 3538952 | tf_op jit(solution)/shard_map/ppermute | solution.py:447
  39.3 15.8 %collective-permute-start.6 = (bf16[1152,512]{1,0:T(8,128)(2,1)}, bf16[1152,512]{1,0:T(8,128)(2,1)}, u32[]{:S(2)}, u32[]{:S(2)}) collective-permute-start(bf16[1152,512]{1,0:T(8,128)(2,1)} %collective-permute-done.refs_5_), channel_id=1, source_target_pairs={{0,1},{1,0},{2,3},{3,2},{4,5},{5,4},{6,7},{7,6},{8,9},{9,8},{10,11... | collective-permute-start | bytes 3538952 | tf_op jit(solution)/shard_map/ppermute | solution.py:447
  39.8 25.5 %collective-permute-start.5 = (bf16[1152,512]{1,0:T(8,128)(2,1)}, bf16[1152,512]{1,0:T(8,128)(2,1)}, u32[]{:S(2)}, u32[]{:S(2)}) collective-permute-start(bf16[1152,512]{1,0:T(8,128)(2,1)} %collective-permute-done.2.refs_3_), channel_id=1, source_target_pairs={{0,2},{1,5},{2,6},{3,1},{4,0},{5,9},{6,10},{7,3},{8,4},{9,13},{10,... | collective-permute-start | bytes 3538952 | tf_op jit(solution)/shard_map/ppermute | solution.py:447
  40.5 1.0 copy-start.8
  41.5 1.3 copy-start.6
  42.8 1.3 copy-start.9
  49.5 17.6 %collective-permute-start.8 = (bf16[1152,512]{1,0:T(8,128)(2,1)}, bf16[1152,512]{1,0:T(8,128)(2,1)S(1)}, u32[]{:S(2)}, u32[]{:S(2)}) collective-permute-start(bf16[1152,512]{1,0:T(8,128)(2,1)} %collective-permute-done.1.refs_3_), channel_id=1, source_target_pairs={{0,1},{1,0},{2,3},{3,2},{4,5},{5,4},{6,7},{7,6},{8,9},{9,8},{10,11... | collective-permute-start | bytes 3538952 | tf_op jit(solution)/shard_map/ppermute | solution.py:447
  50.8 22.1 %collective-permute-start.4 = (bf16[1152,512]{1,0:T(8,128)(2,1)}, bf16[1152,512]{1,0:T(8,128)(2,1)S(1)}, u32[]{:S(2)}, u32[]{:S(2)}) collective-permute-start(bf16[1152,512]{1,0:T(8,128)(2,1)} %collective-permute-done.1.refs_3_), channel_id=1, source_target_pairs={{2,0},{5,1},{6,2},{1,3},{0,4},{9,5},{10,6},{3,7},{4,8},{13,9},{14,... | collective-permute-start | bytes 3538952 | tf_op jit(solution)/shard_map/ppermute | solution.py:447
  65.3 7.7 %collective-permute-start.12 = (bf16[1152,512]{1,0:T(8,128)(2,1)}, bf16[1152,512]{1,0:T(8,128)(2,1)S(1)}, u32[]{:S(2)}, u32[]{:S(2)}) collective-permute-start(bf16[1152,512]{1,0:T(8,128)(2,1)} %collective-permute-done.5.refs_3_), channel_id=1, source_target_pairs={{0,1},{1,0},{2,3},{3,2},{4,5},{5,4},{6,7},{7,6},{8,9},{9,8},{10,11... | collective-permute-start | bytes 3538952 | tf_op jit(solution)/shard_map/ppermute | solution.py:447
  65.4 16.6 %collective-permute-start.10 = (bf16[1152,512]{1,0:T(8,128)(2,1)}, bf16[1152,512]{1,0:T(8,128)(2,1)S(1)}, u32[]{:S(2)}, u32[]{:S(2)}) collective-permute-start(bf16[1152,512]{1,0:T(8,128)(2,1)} %collective-permute-done.5.refs_3_), channel_id=1, source_target_pairs={{0,2},{1,5},{2,6},{3,1},{4,0},{5,9},{6,10},{7,3},{8,4},{9,13},{10,... | collective-permute-start | bytes 3538952 | tf_op jit(solution)/shard_map/ppermute | solution.py:447
  66.1 7.0 %collective-permute-start.11 = (bf16[32,1152]{1,0:T(8,128)(2,1)S(1)}, bf16[32,1152]{1,0:T(8,128)(2,1)S(1)}, u32[]{:S(2)}, u32[]{:S(2)}) collective-permute-start(bf16[32,1152]{1,0:T(8,128)(2,1)S(1)} %row_sums.1.own_ref), channel_id=1, source_target_pairs={{0,1},{1,0},{2,3},{3,2},{4,5},{5,4},{6,7},{7,6},{8,9},{9,8},{10,11... | collective-permute-start | bytes 221192 | tf_op jit(solution)/shard_map/ppermute | solution.py:447
  72.9 11.5 %collective-permute-start.14 = (bf16[1152,512]{1,0:T(8,128)(2,1)S(1)}, bf16[1152,512]{1,0:T(8,128)(2,1)S(1)}, u32[]{:S(2)}, u32[]{:S(2)}) collective-permute-start(bf16[1152,512]{1,0:T(8,128)(2,1)S(1)} %collective-permute-done.4.refs_3_), channel_id=1, source_target_pairs={{0,1},{1,0},{2,3},{3,2},{4,5},{5,4},{6,7},{7,6},{8,9},{9,8},{10,11... | collective-permute-start | bytes 3538952 | tf_op jit(solution)/shard_map/ppermute | solution.py:447
  82.0 8.0 %collective-permute-start.13 = (bf16[1152,512]{1,0:T(8,128)(2,1)S(1)}, bf16[1152,512]{1,0:T(8,128)(2,1)S(1)}, u32[]{:S(2)}, u32[]{:S(2)}) collective-permute-start(bf16[1152,512]{1,0:T(8,128)(2,1)S(1)} %collective-permute-done.10.refs_3_), channel_id=1, source_target_pairs={{0,1},{1,0},{2,3},{3,2},{4,5},{5,4},{6,7},{7,6},{8,9},{9,8},{10,11... | collective-permute-start | bytes 3538952 | tf_op jit(solution)/shard_map/ppermute | solution.py:447
  82.2 15.6 %collective-permute-start.15 = (bf16[576,512]{1,0:T(8,128)(2,1)S(1)}, bf16[576,512]{1,0:T(8,128)(2,1)}, u32[]{:S(2)}, u32[]{:S(2)}) collective-permute-start(bf16[576,512]{1,0:T(8,128)(2,1)S(1)} %slice.7), channel_id=1, source_target_pairs={{0,2},{1,5},{2,6},{3,1},{4,0},{5,9},{6,10},{7,3},{8,4},{9,13},{10,... | collective-permute-start | bytes 1769480 | tf_op jit(solution)/shard_map/ppermute | solution.py:447
  84.4 13.6 %collective-permute-start.9 = (bf16[576,512]{1,0:T(8,128)(2,1)S(1)}, bf16[576,512]{1,0:T(8,128)(2,1)}, u32[]{:S(2)}, u32[]{:S(2)}) collective-permute-start(bf16[576,512]{1,0:T(8,128)(2,1)S(1)} %slice.6), channel_id=1, source_target_pairs={{2,0},{5,1},{6,2},{1,3},{0,4},{9,5},{10,6},{3,7},{4,8},{13,9},{14,... | collective-permute-start | bytes 1769480 | tf_op jit(solution)/shard_map/ppermute | solution.py:447
  97.8 6.3 %collective-permute-start.17 = (bf16[576,512]{1,0:T(8,128)(2,1)}, bf16[576,512]{1,0:T(8,128)(2,1)}, u32[]{:S(2)}, u32[]{:S(2)}) collective-permute-start(bf16[576,512]{1,0:T(8,128)(2,1)} %collective-permute-done.15.opp_ref.refs_4_), channel_id=1, source_target_pairs={{0,1},{1,0},{2,3},{3,2},{4,5},{5,4},{6,7},{7,6},{8,9},{9,8},{10,11... | collective-permute-start | bytes 1769480 | tf_op jit(solution)/shard_map/ppermute | solution.py:447
  98.0 6.1 %collective-permute-start.16 = (bf16[576,512]{1,0:T(8,128)(2,1)}, bf16[576,512]{1,0:T(8,128)(2,1)}, u32[]{:S(2)}, u32[]{:S(2)}) collective-permute-start(bf16[576,512]{1,0:T(8,128)(2,1)} %collective-permute-done.9.same_ref.refs_3_), channel_id=1, source_target_pairs={{0,1},{1,0},{2,3},{3,2},{4,5},{5,4},{6,7},{7,6},{8,9},{9,8},{10,11... | collective-permute-start | bytes 1769480 | tf_op jit(solution)/shard_map/ppermute | solution.py:447
  102.1 9.7 %collective-permute-start.18 = (f32[12,512]{1,0:T(8,128)}, f32[12,512]{1,0:T(8,128)}, u32[]{:S(2)}, u32[]{:S(2)}) collective-permute-start(f32[12,512]{1,0:T(8,128)} %chip_share.1), channel_id=1, source_target_pairs={{0,1},{1,0},{2,3},{3,2},{4,5},{5,4},{6,7},{7,6},{8,9},{9,8},{10,11... | collective-permute-start | bytes 73736 | tf_op jit(solution)/shard_map/ppermute | solution.py:512
  102.1 9.7 %collective-permute-start.19 = (f32[12,512]{1,0:T(8,128)}, f32[12,512]{1,0:T(8,128)}, u32[]{:S(2)}, u32[]{:S(2)}) collective-permute-start(f32[12,512]{1,0:T(8,128)} %chip_share.1), channel_id=1, source_target_pairs={{0,2},{1,3},{2,0},{3,1},{4,6},{5,7},{6,4},{7,5},{8,10},{9,11},{10,... | collective-permute-start | bytes 73736 | tf_op jit(solution)/shard_map/ppermute | solution.py:512
  104.0 7.8 %collective-permute-start.20 = (f32[12,512]{1,0:T(8,128)}, f32[12,512]{1,0:T(8,128)}, u32[]{:S(2)}, u32[]{:S(2)}) collective-permute-start(f32[12,512]{1,0:T(8,128)} %chip_share.1), channel_id=1, source_target_pairs={{0,3},{1,2},{2,1},{3,0},{4,7},{5,6},{6,5},{7,4},{8,11},{9,10},{10,... | collective-permute-start | bytes 73736 | tf_op jit(solution)/shard_map/ppermute | solution.py:512
  104.1 1.1 copy-start
  105.2 1.1 copy-start.3
  112.6 0.6 copy-start.13
  112.6 1.2 copy-start.15
  113.9 12.5 %collective-permute-start.21 = (f32[24,512]{1,0:T(8,128)}, f32[24,512]{1,0:T(8,128)}, u32[]{:S(2)}, u32[]{:S(2)}) collective-permute-start(f32[24,512]{1,0:T(8,128)} %pad_maximum_fusion.1), channel_id=1, source_target_pairs={{0,12},{1,13},{2,14},{3,15},{4,8},{5,9},{6,10},{7,11},{8,4},{9,5},... | collective-permute-start | bytes 147464 | tf_op jit(solution)/shard_map/ppermute | solution.py:407
  118.2 8.2 %collective-permute-start.22 = (f32[24,512]{1,0:T(8,128)}, f32[24,512]{1,0:T(8,128)}, u32[]{:S(2)}, u32[]{:S(2)}) collective-permute-start(f32[24,512]{1,0:T(8,128)} %pad_maximum_fusion.1), channel_id=1, source_target_pairs={{0,8},{1,9},{2,10},{3,11},{4,12},{5,13},{6,14},{7,15},{8,0},{9,1},... | collective-permute-start | bytes 147464 | tf_op jit(solution)/shard_map/ppermute | solution.py:407
  118.2 8.2 %collective-permute-start.23 = (f32[24,512]{1,0:T(8,128)}, f32[24,512]{1,0:T(8,128)}, u32[]{:S(2)}, u32[]{:S(2)}) collective-permute-start(f32[24,512]{1,0:T(8,128)} %pad_maximum_fusion.1), channel_id=1, source_target_pairs={{0,4},{1,5},{2,6},{3,7},{4,0},{5,1},{6,2},{7,3},{8,12},{9,13},{10,... | collective-permute-start | bytes 147464 | tf_op jit(solution)/shard_map/ppermute | solution.py:407
  118.8 1.1 copy-start.1
  119.8 1.1 copy-start.4
  120.9 5.5 %copy-start.14 = (f32[12,512]{1,0:T(8,128)S(1)}, f32[12,512]{1,0:T(8,128)}, u32[]{:S(2)}) copy-start(f32[12,512]{1,0:T(8,128)} %copy-done.13) | copy-start | bytes 73732
  120.9 5.5 %copy-start.16 = (f32[12,512]{1,0:T(8,128)S(1)}, f32[12,512]{1,0:T(8,128)}, u32[]{:S(2)}) copy-start(f32[12,512]{1,0:T(8,128)} %copy-done.15) | copy-start | bytes 73732

commit v10 on v8

--- a/solution.py
+++ b/solution.py
@@ -257,7 +257,7 @@
     width = greens[0][0][0].shape[1]
     parts = tuple(len(pair[0]) for pair in greens)
     wide = 2 * rows
-    span = min(width, 256) if closing else width
+    span = min(width, 128) if closing else width
     tall = pl.BlockSpec((rows, span), lambda n, g, p: (0, n))
     mat = pl.BlockSpec((rows, wide), lambda n, g, p: (0, p[1 + low + g]))
     wide_sum = jax.ShapeDtypeStruct((rows, width), jnp.float32)
@@ -396,7 +396,8 @@
                 came = [([got[1]], [passed[0]]), ([got[0]], [passed[1]])]
                 split = 0 if far == 1 else 1
                 waiting, later = waiting + came[:split], came[split:]
-            sums = step(after(place, block), low, mats, waiting, sums, (), orbitals)
+            when = after(place, block, onward) if turn == 0 else after(place, block)
+            sums = step(when, low, mats, waiting, sums, (), orbitals)
             low += len(waiting)
             waiting, done = later, sums[0]
     sums = step(place, low, mats, waiting, sums, (), orbitals)

time: 123 us -> 125 us (1.016)
  Pallas kernels: 76.5 us -> 78.1 us
    pallas_call x7, Pallas kernels: 45.9 us -> 47.5 us  [step(): pl.pallas_call(functools.partial(step_body, parts, rows, opening, closing...]
  transfers between devices with their start and end apart: 23 -> 23, of which waited for: 13 -> 12; matrix products, arithmetic and copies ran while one was open for 1% -> 1% of each run, Pallas kernels for 56% -> 55%
where the time goes in v10:
time: 125 us; the launch traced here: 124 us
  Pallas kernels  78.1 us (62%)
  waiting for transfers between devices  21.3 us (17%)
  starting transfers between devices  21.2 us (17%)
  local copies, waits for them, and re-layouts  2.07 us (2%)
    pallas_call x7, Pallas kernels, step(): pl.pallas_call(functools.partial(step_body, parts, rows, opening, closing...  47.5 us
    pallas_call x3, Pallas kernels, build_rows(): pl.pallas_call(functools.partial(build_body, orbitals, low, high, pairs),...  30.6 us
    ppermute x17, starting transfers between devices, send(): return lax.ppermute(block, 'prow', pairs_of)  14.8 us
    ppermute x17, waiting for transfers between devices, send(): return lax.ppermute(block, 'prow', pairs_of)  13.6 us
    ppermute x6, waiting for transfers between devices, spread_blocks(): blocks.append(lax.ppermute(block, 'prow', pairs_of))  7.69 us
    ppermute x6, starting transfers between devices, spread_blocks(): blocks.append(lax.ppermute(block, 'prow', pairs_of))  6.38 us
  transfers between devices with their start and end apart: 23, of which 12 were waited for; matrix products, arithmetic and copies ran while one was open for 1% of the time, Pallas kernels for 55%

profile of v10, /device:TPU:0, one launch (start us, length us, event | category | flops | bytes accessed | tf_op | source)
XLA Modules:
  0.0 124.5 jit_solution(9175066261711775904)
XLA Ops:
  0.6 0.0 copy-start.2
  0.7 1.2 constant_dynamic-update-slice_fusion.1
  1.9 0.1 copy-done.1
  2.0 3.1 %collective-permute-start = (bf16[1152,512]{1,0:T(8,128)(2,1)S(1)}, bf16[1152,512]{1,0:T(8,128)(2,1)}, u32[]{:S(2)}, u32[]{:S(2)}) collective-permute-start(bf16[1152,512]{1,0:T(8,128)(2,1)S(1)} %constant_dynamic-update-slice_fusion.refs_3_), channel_id=1, source_target_pairs={{2,0},{5,1},{6,2},{1,3},{0,4},{9,5},{10,6},{3,7},{4,8},{13,9},{14,... | collective-permute-start | bytes 3538952 | tf_op jit(solution)/shard_map/ppermute | solution.py:353
  5.1 0.1 pad_maximum_fusion.2
  5.1 0.2 maximum_maximum_fusion.refs_5_
  5.4 7.1 %build_rows.3 = (bf16[576,9216]{1,0:T(8,128)(2,1)}, bf16[576,9216]{1,0:T(8,128)(2,1)}) custom-call(s32[1]{0:T(128)} %bitcast.1.refs_0_, bf16[576,9216]{1,0:T(8,128)(2,1)} %refs_1_.5, s32[96,96]{1,0:T(8,128)S(1)} %copy-done.3, f32[96,96]{1,0:T(8,128)S(1)} %copy-done.4, f32[96]{0:T(128)S(1)} %copy-done.5, f32[192,384]{1,0:T(8,128)S(1)} %maximum_maximum_fusion.refs_5_, ...), custom_call_target="tpu_custom_call" | custom-call | flops 1024 | bytes 1024 | tf_op jit(solution)/shard_map/build_rows/pallas_call | solution.py:174
  12.5 0.0 collective-permute-start.2
  12.5 0.0 collective-permute-start.3
  12.5 11.7 %build_rows.4 = (bf16[576,9216]{1,0:T(8,128)(2,1)}, bf16[576,9216]{1,0:T(8,128)(2,1)}) custom-call(s32[1]{0:T(128)} %bitcast.1.refs_0_, bf16[576,9216]{1,0:T(8,128)(2,1)} %refs_1_.5, s32[96,96]{1,0:T(8,128)S(1)} %copy-done.3, f32[96,96]{1,0:T(8,128)S(1)} %copy-done.4, f32[96]{0:T(128)S(1)} %copy-done.5, ...), custom_call_target="tpu_custom_call", output_to_operand_aliasing={{0}: (8, {}), {1}: (9, {})} | custom-call | flops 1024 | bytes 1024 | tf_op jit(solution)/shard_map/build_rows/pallas_call | solution.py:174
  24.3 0.7 collective-permute-done.refs_5_
  25.0 2.6 %collective-permute-start.1 = (bf16[1152,512]{1,0:T(8,128)(2,1)}, bf16[1152,512]{1,0:T(8,128)(2,1)S(1)}, u32[]{:S(2)}, u32[]{:S(2)}) collective-permute-start(bf16[1152,512]{1,0:T(8,128)(2,1)} %collective-permute-done.refs_5_), channel_id=1, source_target_pairs={{2,0},{5,1},{6,2},{1,3},{0,4},{9,5},{10,6},{3,7},{4,8},{13,9},{14,... | collective-permute-start | bytes 3538952 | tf_op jit(solution)/shard_map/ppermute | solution.py:353
  27.6 11.7 %build_rows.5 = (bf16[576,9216]{1,0:T(8,128)(2,1)}, bf16[576,9216]{1,0:T(8,128)(2,1)}) custom-call(s32[1]{0:T(128)} %bitcast.1.refs_0_, bf16[576,9216]{1,0:T(8,128)(2,1)} %refs_1_.5, s32[96,96]{1,0:T(8,128)S(1)} %copy-done.3, f32[96,96]{1,0:T(8,128)S(1)} %copy-done.4, f32[96]{0:T(128)S(1)} %copy-done.5, ...), custom_call_target="tpu_custom_call", output_to_operand_aliasing={{0}: (8, {}), {1}: (9, {})} | custom-call | flops 1024 | bytes 1024 | tf_op jit(solution)/shard_map/build_rows/pallas_call | solution.py:174
  39.3 0.0 collective-permute-done.2.refs_3_
  39.3 0.0 collective-permute-start.7
  39.3 0.5 collective-permute-start.6
  39.8 0.0 collective-permute-start.5
  39.8 0.7 dynamic-slice_bitcast_fusion.refs_0_
  40.5 0.0 collective-permute-done.3.refs_4_
  40.5 5.8 %add_products.7 = (f32[576,512]{1,0:T(8,128)S(1)}, f32[576,512]{1,0:T(8,128)S(1)}, f32[576,512]{1,0:T(8,128)S(1)}) custom-call(s32[10]{0:T(128)S(1)} %dynamic-slice_bitcast_fusion.refs_0_, bf16[576,9216]{1,0:T(8,128)(2,1)} %get-tuple-element.55.refs_1_, bf16[576,9216]{1,0:T(8,128)(2,1)} %get-tuple-element.56.refs_2_, ...), custom_call_target="tpu_custom_call" | custom-call | flops 1024 | bytes 1024 | tf_op jit(solution)/shard_map/add_products/pallas_call | solution.py:290
  46.3 0.2 collective-permute-done.1.refs_3_
  46.5 1.1 collective-permute-start.8
  47.6 1.5 %collective-permute-start.4 = (bf16[1152,512]{1,0:T(8,128)(2,1)S(1)}, bf16[1152,512]{1,0:T(8,128)(2,1)S(1)}, u32[]{:S(2)}, u32[]{:S(2)}) collective-permute-start(bf16[1152,512]{1,0:T(8,128)(2,1)S(1)} %collective-permute-done.1.refs_3_), channel_id=1, source_target_pairs={{2,0},{5,1},{6,2},{1,3},{0,4},{9,5},{10,6},{3,7},{4,8},{13,9},{14,... | collective-permute-start | bytes 3538952 | tf_op jit(solution)/shard_map/ppermute | solution.py:353
  49.2 0.0 collective-permute-done.7.refs_6_
  49.2 0.0 collective-permute-done.6.refs_4_
  49.2 10.2 %add_products.8 = (f32[576,512]{1,0:T(8,128)S(1)}, f32[576,512]{1,0:T(8,128)S(1)}, f32[576,512]{1,0:T(8,128)S(1)}) custom-call(s32[10]{0:T(128)S(1)} %dynamic-slice_bitcast_fusion.refs_0_, bf16[576,9216]{1,0:T(8,128)(2,1)} %get-tuple-element.55.refs_1_, ...), custom_call_target="tpu_custom_call", output_to_operand_aliasing={{0}: (7, {}), {1}: (8, {}), {2}: (9, {})} | custom-call | flops 1024 | bytes 1024 | tf_op jit(solution)/shard_map/add_products/pallas_call | solution.py:290
  59.4 2.9 %collective-permute-done.5.refs_3_ = bf16[1152,512]{1,0:T(8,128)(2,1)} collective-permute-done((bf16[1152,512]{1,0:T(8,128)(2,1)}, bf16[1152,512]{1,0:T(8,128)(2,1)}, u32[]{:S(2)}, u32[]{:S(2)}) %collective-permute-start.5) | collective-permute-done | bytes 1179680 | tf_op jit(solution)/shard_map/ppermute | solution.py:353
  62.3 1.0 collective-permute-start.11
  63.3 1.6 %collective-permute-start.10 = (bf16[1152,512]{1,0:T(8,128)(2,1)}, bf16[1152,512]{1,0:T(8,128)(2,1)S(1)}, u32[]{:S(2)}, u32[]{:S(2)}) collective-permute-start(bf16[1152,512]{1,0:T(8,128)(2,1)} %collective-permute-done.5.refs_3_), channel_id=1, source_target_pairs={{0,2},{1,5},{2,6},{3,1},{4,0},{5,9},{6,10},{7,3},{8,4},{9,13},{10,... | collective-permute-start | bytes 3538952 | tf_op jit(solution)/shard_map/ppermute | solution.py:353
  64.8 0.0 collective-permute-done.8.refs_4_
  64.9 5.9 %add_products.9 = (f32[576,512]{1,0:T(8,128)S(1)}, f32[576,512]{1,0:T(8,128)S(1)}, f32[576,512]{1,0:T(8,128)S(1)}) custom-call(s32[10]{0:T(128)S(1)} %dynamic-slice_bitcast_fusion.refs_0_, bf16[576,9216]{1,0:T(8,128)(2,1)} %get-tuple-element.55.refs_1_, ...), custom_call_target="tpu_custom_call", output_to_operand_aliasing={{0}: (5, {}), {1}: (6, {}), {2}: (7, {})} | custom-call | flops 1024 | bytes 1024 | tf_op jit(solution)/shard_map/add_products/pallas_call | solution.py:290
  70.7 2.6 %collective-permute-done.4.refs_3_ = bf16[1152,512]{1,0:T(8,128)(2,1)S(1)} collective-permute-done((bf16[1152,512]{1,0:T(8,128)(2,1)S(1)}, bf16[1152,512]{1,0:T(8,128)(2,1)S(1)}, u32[]{:S(2)}, u32[]{:S(2)}) %collective-permute-start.4) | collective-permute-done | bytes 1179680 | tf_op jit(solution)/shard_map/ppermute | solution.py:353
  73.3 0.1 collective-permute-start.13
  73.4 0.0 collective-permute-done.11.refs_4_
  73.4 5.5 %add_products.10 = (f32[576,512]{1,0:T(8,128)S(1)}, f32[576,512]{1,0:T(8,128)S(1)}, f32[576,512]{1,0:T(8,128)S(1)}) custom-call(s32[10]{0:T(128)S(1)} %dynamic-slice_bitcast_fusion.refs_0_, bf16[576,9216]{1,0:T(8,128)(2,1)} %get-tuple-element.55.refs_1_, ...), custom_call_target="tpu_custom_call", output_to_operand_aliasing={{0}: (5, {}), {1}: (6, {}), {2}: (7, {})} | custom-call | flops 1024 | bytes 1024 | tf_op jit(solution)/shard_map/add_products/pallas_call | solution.py:290
  79.0 2.6 %collective-permute-done.10.refs_3_ = bf16[1152,512]{1,0:T(8,128)(2,1)S(1)} collective-permute-done((bf16[1152,512]{1,0:T(8,128)(2,1)}, bf16[1152,512]{1,0:T(8,128)(2,1)S(1)}, u32[]{:S(2)}, u32[]{:S(2)}) %collective-permute-start.10) | collective-permute-done | bytes 1179680 | tf_op jit(solution)/shard_map/ppermute | solution.py:353
  81.6 0.6 collective-permute-start.12
  82.2 2.1 %collective-permute-start.14 = (bf16[576,512]{1,0:T(8,128)(2,1)S(1)}, bf16[576,512]{1,0:T(8,128)(2,1)S(1)}, u32[]{:S(2)}, u32[]{:S(2)}) collective-permute-start(bf16[576,512]{1,0:T(8,128)(2,1)S(1)} %slice.7), channel_id=1, source_target_pairs={{0,2},{1,5},{2,6},{3,1},{4,0},{5,9},{6,10},{7,3},{8,4},{9,13},{10,... | collective-permute-start | bytes 1769480 | tf_op jit(solution)/shard_map/ppermute | solution.py:353
  84.3 0.1 collective-permute-start.9
  84.4 0.0 collective-permute-done.13.refs_4_
  84.4 5.5 %add_products.11 = (f32[576,512]{1,0:T(8,128)S(1)}, f32[576,512]{1,0:T(8,128)S(1)}, f32[576,512]{1,0:T(8,128)S(1)}) custom-call(s32[10]{0:T(128)S(1)} %dynamic-slice_bitcast_fusion.refs_0_, bf16[576,9216]{1,0:T(8,128)(2,1)} %get-tuple-element.55.refs_1_, ...), custom_call_target="tpu_custom_call", output_to_operand_aliasing={{0}: (5, {}), {1}: (6, {}), {2}: (7, {})} | custom-call | flops 1024 | bytes 1024 | tf_op jit(solution)/shard_map/add_products/pallas_call | solution.py:290
  90.0 0.0 collective-permute-done.12.refs_4_
  90.0 0.0 copy-start
  90.0 5.5 %add_products.12 = (f32[576,512]{1,0:T(8,128)S(1)}, f32[576,512]{1,0:T(8,128)S(1)}, f32[576,512]{1,0:T(8,128)S(1)}) custom-call(s32[10]{0:T(128)S(1)} %dynamic-slice_bitcast_fusion.refs_0_, bf16[576,9216]{1,0:T(8,128)(2,1)} %get-tuple-element.55.refs_1_, ...), custom_call_target="tpu_custom_call", output_to_operand_aliasing={{0}: (5, {}), {1}: (6, {}), {2}: (7, {})} | custom-call | flops 1024 | bytes 1024 | tf_op jit(solution)/shard_map/add_products/pallas_call | solution.py:290
  95.5 2.3 %collective-permute-done.14.refs_4_ = bf16[576,512]{1,0:T(8,128)(2,1)S(1)} collective-permute-done((bf16[576,512]{1,0:T(8,128)(2,1)S(1)}, bf16[576,512]{1,0:T(8,128)(2,1)S(1)}, u32[]{:S(2)}, u32[]{:S(2)}) %collective-permute-start.14) | collective-permute-done | bytes 589856 | tf_op jit(solution)/shard_map/ppermute | solution.py:353
  97.8 0.0 collective-permute-start.16
  97.8 0.0 collective-permute-done.9.refs_3_
  97.8 0.6 collective-permute-start.15
  98.4 1.4 %collective-permute-done.16.refs_6_ = bf16[576,512]{1,0:T(8,128)(2,1)S(1)} collective-permute-done((bf16[576,512]{1,0:T(8,128)(2,1)S(1)}, bf16[576,512]{1,0:T(8,128)(2,1)S(1)}, u32[]{:S(2)}, u32[]{:S(2)}) %collective-permute-start.16) | collective-permute-done | bytes 589856 | tf_op jit(solution)/shard_map/ppermute | solution.py:353
  99.8 0.8 collective-permute-done.15.refs_5_
  100.6 9.0 %add_products.13 = (f32[576,512]{1,0:T(8,128)}, f32[576,512]{1,0:T(8,128)}, bf16[576,512]{1,0:T(8,128)(2,1)}, bf16[576,512]{1,0:T(8,128)(2,1)}, f32[6,512]{1,0:T(8,128)S(1)}) custom-call(s32[10]{0:T(128)S(1)} %dynamic-slice_bitcast_fusion.refs_0_, bf16[576,9216]{1,0:T(8,128)(2,1)} %get-tuple-element.55.refs_1_, bf16[576,9216]{1,0:T(8,128)(2,1)} %get-tuple-element.56.refs_2_, ...), custom_call_target="tpu_custom_call" | custom-call | flops 1024 | bytes 1024 | tf_op jit(solution)/shard_map/add_products/pallas_call | solution.py:290
  109.7 1.5 %collective-permute-start.17 = (f32[6,512]{1,0:T(8,128)S(1)}, f32[6,512]{1,0:T(8,128)S(1)}, u32[]{:S(2)}, u32[]{:S(2)}) collective-permute-start(f32[6,512]{1,0:T(8,128)S(1)} %get-tuple-element.92), channel_id=1, source_target_pairs={{0,3},{1,2},{2,1},{3,0},{4,7},{5,6},{6,5},{7,4},{8,11},{9,10},{10,... | collective-permute-start | bytes 36872 | tf_op jit(solution)/shard_map/ppermute | solution.py:313
  111.2 0.3 collective-permute-start.18
  111.5 0.1 collective-permute-start.19
  111.6 1.2 collective-permute-done.17
  112.8 2.1 %collective-permute-done.18 = f32[6,512]{1,0:T(8,128)S(1)} collective-permute-done((f32[6,512]{1,0:T(8,128)S(1)}, f32[6,512]{1,0:T(8,128)S(1)}, u32[]{:S(2)}, u32[]{:S(2)}) %collective-permute-start.18) | collective-permute-done | bytes 12320 | tf_op jit(solution)/shard_map/ppermute | solution.py:313
  115.0 0.0 collective-permute-done.19
  115.0 3.8 %collective-permute-start.20 = (f32[24,512]{1,0:T(8,128)S(1)}, f32[24,512]{1,0:T(8,128)S(1)}, u32[]{:S(2)}, u32[]{:S(2)}) collective-permute-start(f32[24,512]{1,0:T(8,128)S(1)} %pad_maximum_fusion.1), channel_id=1, source_target_pairs={{0,12},{1,13},{2,14},{3,15},{4,8},{5,9},{6,10},{7,11},{8,4},{9,5},... | collective-permute-start | bytes 147464 | tf_op jit(solution)/shard_map/ppermute | solution.py:313
  118.8 0.0 collective-permute-start.21
  118.8 0.7 collective-permute-start.22
  119.5 1.9 %collective-permute-done.20 = f32[24,512]{1,0:T(8,128)S(1)} collective-permute-done((f32[24,512]{1,0:T(8,128)S(1)}, f32[24,512]{1,0:T(8,128)S(1)}, u32[]{:S(2)}, u32[]{:S(2)}) %collective-permute-start.20) | collective-permute-done | bytes 49184 | tf_op jit(solution)/shard_map/ppermute | solution.py:313
  121.4 2.4 %collective-permute-done.21 = f32[24,512]{1,0:T(8,128)S(1)} collective-permute-done((f32[24,512]{1,0:T(8,128)S(1)}, f32[24,512]{1,0:T(8,128)S(1)}, u32[]{:S(2)}, u32[]{:S(2)}) %collective-permute-start.21) | collective-permute-done | bytes 49184 | tf_op jit(solution)/shard_map/ppermute | solution.py:313
  123.8 0.0 collective-permute-done.22
  123.8 0.7 pad_maximum_fusion
  (17 shorter events, 0.2 us)
Async XLA Ops:
  0.6 4.7 %copy-start.2 = (f32[96,384]{1,0:T(8,128)S(1)}, f32[96,384]{1,0:T(8,128)}, u32[]{:S(2)}) copy-start(f32[96,384]{1,0:T(8,128)} %constant.82.clone.refs_6_) | copy-start | bytes 442372
  0.6 1.3 %copy-start.1 = (bf16[576,512]{1,0:T(8,128)(2,1)S(1)}, bf16[576,512]{1,0:T(8,128)(2,1)}, u32[]{:S(2)}) copy-start(bf16[576,512]{1,0:T(8,128)(2,1)} %refs_11_.1) | copy-start | bytes 1769476
  0.7 4.4 %copy-start.3 = (s32[96,96]{1,0:T(8,128)S(1)}, s32[96,96]{1,0:T(8,128)}, u32[]{:S(2)}) copy-start(s32[96,96]{1,0:T(8,128)} %refs_2_.5) | copy-start | bytes 110596
  0.7 4.4 %copy-start.5 = (f32[96]{0:T(128)S(1)}, f32[96]{0:T(128)}, u32[]{:S(2)}) copy-start(f32[96]{0:T(128)} %refs_4_.5) | copy-start | bytes 1156
  0.7 4.5 %copy-start.4 = (f32[96,96]{1,0:T(8,128)S(1)}, f32[96,96]{1,0:T(8,128)}, u32[]{:S(2)}) copy-start(f32[96,96]{1,0:T(8,128)} %refs_3_.5) | copy-start | bytes 110596
  2.0 23.0 %collective-permute-start = (bf16[1152,512]{1,0:T(8,128)(2,1)S(1)}, bf16[1152,512]{1,0:T(8,128)(2,1)}, u32[]{:S(2)}, u32[]{:S(2)}) collective-permute-start(bf16[1152,512]{1,0:T(8,128)(2,1)S(1)} %constant_dynamic-update-slice_fusion.refs_3_), channel_id=1, source_target_pairs={{2,0},{5,1},{6,2},{1,3},{0,4},{9,5},{10,6},{3,7},{4,8},{13,9},{14,... | collective-permute-start | bytes 3538952 | tf_op jit(solution)/shard_map/ppermute | solution.py:353
  12.5 26.7 %collective-permute-start.2 = (bf16[1152,512]{1,0:T(8,128)(2,1)S(1)}, bf16[1152,512]{1,0:T(8,128)(2,1)}, u32[]{:S(2)}, u32[]{:S(2)}) collective-permute-start(bf16[1152,512]{1,0:T(8,128)(2,1)S(1)} %constant_dynamic-update-slice_fusion.refs_3_), channel_id=1, source_target_pairs={{0,2},{1,5},{2,6},{3,1},{4,0},{5,9},{6,10},{7,3},{8,4},{9,13},{10,... | collective-permute-start | bytes 3538952 | tf_op jit(solution)/shard_map/ppermute | solution.py:353
  12.5 28.0 %collective-permute-start.3 = (bf16[1152,512]{1,0:T(8,128)(2,1)S(1)}, bf16[1152,512]{1,0:T(8,128)(2,1)}, u32[]{:S(2)}, u32[]{:S(2)}) collective-permute-start(bf16[1152,512]{1,0:T(8,128)(2,1)S(1)} %constant_dynamic-update-slice_fusion.refs_3_), channel_id=1, source_target_pairs={{0,1},{1,0},{2,3},{3,2},{4,5},{5,4},{6,7},{7,6},{8,9},{9,8},{10,11... | collective-permute-start | bytes 3538952 | tf_op jit(solution)/shard_map/ppermute | solution.py:353
  25.0 21.5 %collective-permute-start.1 = (bf16[1152,512]{1,0:T(8,128)(2,1)}, bf16[1152,512]{1,0:T(8,128)(2,1)S(1)}, u32[]{:S(2)}, u32[]{:S(2)}) collective-permute-start(bf16[1152,512]{1,0:T(8,128)(2,1)} %collective-permute-done.refs_5_), channel_id=1, source_target_pairs={{2,0},{5,1},{6,2},{1,3},{0,4},{9,5},{10,6},{3,7},{4,8},{13,9},{14,... | collective-permute-start | bytes 3538952 | tf_op jit(solution)/shard_map/ppermute | solution.py:353
  39.3 9.9 %collective-permute-start.7 = (bf16[1152,512]{1,0:T(8,128)(2,1)}, bf16[1152,512]{1,0:T(8,128)(2,1)}, u32[]{:S(2)}, u32[]{:S(2)}) collective-permute-start(bf16[1152,512]{1,0:T(8,128)(2,1)} %collective-permute-done.2.refs_3_), channel_id=1, source_target_pairs={{0,1},{1,0},{2,3},{3,2},{4,5},{5,4},{6,7},{7,6},{8,9},{9,8},{10,11... | collective-permute-start | bytes 3538952 | tf_op jit(solution)/shard_map/ppermute | solution.py:353
  39.3 9.9 %collective-permute-start.6 = (bf16[1152,512]{1,0:T(8,128)(2,1)}, bf16[1152,512]{1,0:T(8,128)(2,1)}, u32[]{:S(2)}, u32[]{:S(2)}) collective-permute-start(bf16[1152,512]{1,0:T(8,128)(2,1)} %collective-permute-done.refs_5_), channel_id=1, source_target_pairs={{0,1},{1,0},{2,3},{3,2},{4,5},{5,4},{6,7},{7,6},{8,9},{9,8},{10,11... | collective-permute-start | bytes 3538952 | tf_op jit(solution)/shard_map/ppermute | solution.py:353
  39.8 22.5 %collective-permute-start.5 = (bf16[1152,512]{1,0:T(8,128)(2,1)}, bf16[1152,512]{1,0:T(8,128)(2,1)}, u32[]{:S(2)}, u32[]{:S(2)}) collective-permute-start(bf16[1152,512]{1,0:T(8,128)(2,1)} %collective-permute-done.2.refs_3_), channel_id=1, source_target_pairs={{0,2},{1,5},{2,6},{3,1},{4,0},{5,9},{6,10},{7,3},{8,4},{9,13},{10,... | collective-permute-start | bytes 3538952 | tf_op jit(solution)/shard_map/ppermute | solution.py:353
  46.5 18.3 %collective-permute-start.8 = (bf16[1152,512]{1,0:T(8,128)(2,1)S(1)}, bf16[1152,512]{1,0:T(8,128)(2,1)S(1)}, u32[]{:S(2)}, u32[]{:S(2)}) collective-permute-start(bf16[1152,512]{1,0:T(8,128)(2,1)S(1)} %collective-permute-done.1.refs_3_), channel_id=1, source_target_pairs={{0,1},{1,0},{2,3},{3,2},{4,5},{5,4},{6,7},{7,6},{8,9},{9,8},{10,11... | collective-permute-start | bytes 3538952 | tf_op jit(solution)/shard_map/ppermute | solution.py:353
  47.6 25.7 %collective-permute-start.4 = (bf16[1152,512]{1,0:T(8,128)(2,1)S(1)}, bf16[1152,512]{1,0:T(8,128)(2,1)S(1)}, u32[]{:S(2)}, u32[]{:S(2)}) collective-permute-start(bf16[1152,512]{1,0:T(8,128)(2,1)S(1)} %collective-permute-done.1.refs_3_), channel_id=1, source_target_pairs={{2,0},{5,1},{6,2},{1,3},{0,4},{9,5},{10,6},{3,7},{4,8},{13,9},{14,... | collective-permute-start | bytes 3538952 | tf_op jit(solution)/shard_map/ppermute | solution.py:353
  62.3 11.1 %collective-permute-start.11 = (bf16[1152,512]{1,0:T(8,128)(2,1)}, bf16[1152,512]{1,0:T(8,128)(2,1)S(1)}, u32[]{:S(2)}, u32[]{:S(2)}) collective-permute-start(bf16[1152,512]{1,0:T(8,128)(2,1)} %collective-permute-done.5.refs_3_), channel_id=1, source_target_pairs={{0,1},{1,0},{2,3},{3,2},{4,5},{5,4},{6,7},{7,6},{8,9},{9,8},{10,11... | collective-permute-start | bytes 3538952 | tf_op jit(solution)/shard_map/ppermute | solution.py:353
  63.3 18.3 %collective-permute-start.10 = (bf16[1152,512]{1,0:T(8,128)(2,1)}, bf16[1152,512]{1,0:T(8,128)(2,1)S(1)}, u32[]{:S(2)}, u32[]{:S(2)}) collective-permute-start(bf16[1152,512]{1,0:T(8,128)(2,1)} %collective-permute-done.5.refs_3_), channel_id=1, source_target_pairs={{0,2},{1,5},{2,6},{3,1},{4,0},{5,9},{6,10},{7,3},{8,4},{9,13},{10,... | collective-permute-start | bytes 3538952 | tf_op jit(solution)/shard_map/ppermute | solution.py:353
  73.3 11.1 %collective-permute-start.13 = (bf16[1152,512]{1,0:T(8,128)(2,1)S(1)}, bf16[1152,512]{1,0:T(8,128)(2,1)S(1)}, u32[]{:S(2)}, u32[]{:S(2)}) collective-permute-start(bf16[1152,512]{1,0:T(8,128)(2,1)S(1)} %collective-permute-done.4.refs_3_), channel_id=1, source_target_pairs={{0,1},{1,0},{2,3},{3,2},{4,5},{5,4},{6,7},{7,6},{8,9},{9,8},{10,11... | collective-permute-start | bytes 3538952 | tf_op jit(solution)/shard_map/ppermute | solution.py:353
  81.6 8.4 %collective-permute-start.12 = (bf16[1152,512]{1,0:T(8,128)(2,1)S(1)}, bf16[1152,512]{1,0:T(8,128)(2,1)S(1)}, u32[]{:S(2)}, u32[]{:S(2)}) collective-permute-start(bf16[1152,512]{1,0:T(8,128)(2,1)S(1)} %collective-permute-done.10.refs_3_), channel_id=1, source_target_pairs={{0,1},{1,0},{2,3},{3,2},{4,5},{5,4},{6,7},{7,6},{8,9},{9,8},{10,11... | collective-permute-start | bytes 3538952 | tf_op jit(solution)/shard_map/ppermute | solution.py:353
  82.2 15.6 %collective-permute-start.14 = (bf16[576,512]{1,0:T(8,128)(2,1)S(1)}, bf16[576,512]{1,0:T(8,128)(2,1)S(1)}, u32[]{:S(2)}, u32[]{:S(2)}) collective-permute-start(bf16[576,512]{1,0:T(8,128)(2,1)S(1)} %slice.7), channel_id=1, source_target_pairs={{0,2},{1,5},{2,6},{3,1},{4,0},{5,9},{6,10},{7,3},{8,4},{9,13},{10,... | collective-permute-start | bytes 1769480 | tf_op jit(solution)/shard_map/ppermute | solution.py:353
  84.3 13.5 %collective-permute-start.9 = (bf16[576,512]{1,0:T(8,128)(2,1)S(1)}, bf16[576,512]{1,0:T(8,128)(2,1)S(1)}, u32[]{:S(2)}, u32[]{:S(2)}) collective-permute-start(bf16[576,512]{1,0:T(8,128)(2,1)S(1)} %slice.6), channel_id=1, source_target_pairs={{2,0},{5,1},{6,2},{1,3},{0,4},{9,5},{10,6},{3,7},{4,8},{13,9},{14,... | collective-permute-start | bytes 1769480 | tf_op jit(solution)/shard_map/ppermute | solution.py:353
  90.0 10.7 %copy-start = (bf16[576,512]{1,0:T(8,128)(2,1)S(1)}, bf16[576,512]{1,0:T(8,128)(2,1)}, u32[]{:S(2)}) copy-start(bf16[576,512]{1,0:T(8,128)(2,1)} %refs_10_.1) | copy-start | bytes 1769476
  97.8 2.0 %collective-permute-start.16 = (bf16[576,512]{1,0:T(8,128)(2,1)S(1)}, bf16[576,512]{1,0:T(8,128)(2,1)S(1)}, u32[]{:S(2)}, u32[]{:S(2)}) collective-permute-start(bf16[576,512]{1,0:T(8,128)(2,1)S(1)} %collective-permute-done.14.refs_4_), channel_id=1, source_target_pairs={{0,1},{1,0},{2,3},{3,2},{4,5},{5,4},{6,7},{7,6},{8,9},{9,8},{10,11... | collective-permute-start | bytes 1769480 | tf_op jit(solution)/shard_map/ppermute | solution.py:353
  97.8 2.8 %collective-permute-start.15 = (bf16[576,512]{1,0:T(8,128)(2,1)S(1)}, bf16[576,512]{1,0:T(8,128)(2,1)S(1)}, u32[]{:S(2)}, u32[]{:S(2)}) collective-permute-start(bf16[576,512]{1,0:T(8,128)(2,1)S(1)} %collective-permute-done.9.refs_3_), channel_id=1, source_target_pairs={{0,1},{1,0},{2,3},{3,2},{4,5},{5,4},{6,7},{7,6},{8,9},{9,8},{10,11... | collective-permute-start | bytes 1769480 | tf_op jit(solution)/shard_map/ppermute | solution.py:353
  109.7 3.2 %collective-permute-start.17 = (f32[6,512]{1,0:T(8,128)S(1)}, f32[6,512]{1,0:T(8,128)S(1)}, u32[]{:S(2)}, u32[]{:S(2)}) collective-permute-start(f32[6,512]{1,0:T(8,128)S(1)} %get-tuple-element.92), channel_id=1, source_target_pairs={{0,3},{1,2},{2,1},{3,0},{4,7},{5,6},{6,5},{7,4},{8,11},{9,10},{10,... | collective-permute-start | bytes 36872 | tf_op jit(solution)/shard_map/ppermute | solution.py:313
  111.2 3.8 %collective-permute-start.18 = (f32[6,512]{1,0:T(8,128)S(1)}, f32[6,512]{1,0:T(8,128)S(1)}, u32[]{:S(2)}, u32[]{:S(2)}) collective-permute-start(f32[6,512]{1,0:T(8,128)S(1)} %get-tuple-element.92), channel_id=1, source_target_pairs={{0,2},{1,3},{2,0},{3,1},{4,6},{5,7},{6,4},{7,5},{8,10},{9,11},{10,... | collective-permute-start | bytes 36872 | tf_op jit(solution)/shard_map/ppermute | solution.py:313
  111.5 3.4 %collective-permute-start.19 = (f32[6,512]{1,0:T(8,128)S(1)}, f32[6,512]{1,0:T(8,128)S(1)}, u32[]{:S(2)}, u32[]{:S(2)}) collective-permute-start(f32[6,512]{1,0:T(8,128)S(1)} %get-tuple-element.92), channel_id=1, source_target_pairs={{0,1},{1,0},{2,3},{3,2},{4,5},{5,4},{6,7},{7,6},{8,9},{9,8},{10,11... | collective-permute-start | bytes 36872 | tf_op jit(solution)/shard_map/ppermute | solution.py:313
  115.0 6.4 %collective-permute-start.20 = (f32[24,512]{1,0:T(8,128)S(1)}, f32[24,512]{1,0:T(8,128)S(1)}, u32[]{:S(2)}, u32[]{:S(2)}) collective-permute-start(f32[24,512]{1,0:T(8,128)S(1)} %pad_maximum_fusion.1), channel_id=1, source_target_pairs={{0,12},{1,13},{2,14},{3,15},{4,8},{5,9},{6,10},{7,11},{8,4},{9,5},... | collective-permute-start | bytes 147464 | tf_op jit(solution)/shard_map/ppermute | solution.py:313
  118.8 5.0 %collective-permute-start.21 = (f32[24,512]{1,0:T(8,128)S(1)}, f32[24,512]{1,0:T(8,128)S(1)}, u32[]{:S(2)}, u32[]{:S(2)}) collective-permute-start(f32[24,512]{1,0:T(8,128)S(1)} %pad_maximum_fusion.1), channel_id=1, source_target_pairs={{0,8},{1,9},{2,10},{3,11},{4,12},{5,13},{6,14},{7,15},{8,0},{9,1},... | collective-permute-start | bytes 147464 | tf_op jit(solution)/shard_map/ppermute | solution.py:313
  118.8 5.0 %collective-permute-start.22 = (f32[24,512]{1,0:T(8,128)S(1)}, f32[24,512]{1,0:T(8,128)S(1)}, u32[]{:S(2)}, u32[]{:S(2)}) collective-permute-start(f32[24,512]{1,0:T(8,128)S(1)} %pad_maximum_fusion.1), channel_id=1, source_target_pairs={{0,4},{1,5},{2,6},{3,7},{4,0},{5,1},{6,2},{7,3},{8,12},{9,13},{10,... | collective-permute-start | bytes 147464 | tf_op jit(solution)/shard_map/ppermute | solution.py:313

commit v11 on v8

--- a/solution.py
+++ b/solution.py
@@ -257,7 +257,7 @@
     width = greens[0][0][0].shape[1]
     parts = tuple(len(pair[0]) for pair in greens)
     wide = 2 * rows
-    span = min(width, 256) if closing else width
+    span = width
     tall = pl.BlockSpec((rows, span), lambda n, g, p: (0, n))
     mat = pl.BlockSpec((rows, wide), lambda n, g, p: (0, p[1 + low + g]))
     wide_sum = jax.ShapeDtypeStruct((rows, width), jnp.float32)

time: 123 us -> 124 us (level)
  no operation moved by 1% of the time
where the time goes in v11:
time: 124 us; the launch traced here: 123 us
  Pallas kernels  76.9 us (62%)
  starting transfers between devices  21.3 us (17%)
  waiting for transfers between devices  21.2 us (17%)
  local copies, waits for them, and re-layouts  2.07 us (2%)
    pallas_call x7, Pallas kernels, step(): pl.pallas_call(functools.partial(step_body, parts, rows, opening, closing...  46.3 us
    pallas_call x3, Pallas kernels, build_rows(): pl.pallas_call(functools.partial(build_body, orbitals, low, high, pairs),...  30.6 us
    ppermute x17, starting transfers between devices, send(): return lax.ppermute(block, 'prow', pairs_of)  14.7 us
    ppermute x17, waiting for transfers between devices, send(): return lax.ppermute(block, 'prow', pairs_of)  13.5 us
    ppermute x6, waiting for transfers between devices, spread_blocks(): blocks.append(lax.ppermute(block, 'prow', pairs_of))  7.69 us
    ppermute x6, starting transfers between devices, spread_blocks(): blocks.append(lax.ppermute(block, 'prow', pairs_of))  6.58 us
  transfers between devices with their start and end apart: 23, of which 13 were waited for; matrix products, arithmetic and copies ran while one was open for 1% of the time, Pallas kernels for 56%

profile of v11, /device:TPU:0, one launch (start us, length us, event | category | flops | bytes accessed | tf_op | source)
XLA Modules:
  0.0 123.4 jit_solution(5285875207019822348)
XLA Ops:
  0.6 0.0 copy-start.2
  0.7 1.2 constant_dynamic-update-slice_fusion.1
  1.9 0.1 copy-done.1
  2.0 3.1 %collective-permute-start = (bf16[1152,512]{1,0:T(8,128)(2,1)S(1)}, bf16[1152,512]{1,0:T(8,128)(2,1)}, u32[]{:S(2)}, u32[]{:S(2)}) collective-permute-start(bf16[1152,512]{1,0:T(8,128)(2,1)S(1)} %constant_dynamic-update-slice_fusion.refs_3_), channel_id=1, source_target_pairs={{2,0},{5,1},{6,2},{1,3},{0,4},{9,5},{10,6},{3,7},{4,8},{13,9},{14,... | collective-permute-start | bytes 3538952 | tf_op jit(solution)/shard_map/ppermute | solution.py:353
  5.1 0.1 pad_maximum_fusion.2
  5.1 0.2 maximum_maximum_fusion.refs_5_
  5.4 7.1 %build_rows.3 = (bf16[576,9216]{1,0:T(8,128)(2,1)}, bf16[576,9216]{1,0:T(8,128)(2,1)}) custom-call(s32[1]{0:T(128)} %bitcast.1.refs_0_, bf16[576,9216]{1,0:T(8,128)(2,1)} %refs_1_.5, s32[96,96]{1,0:T(8,128)S(1)} %copy-done.3, f32[96,96]{1,0:T(8,128)S(1)} %copy-done.4, f32[96]{0:T(128)S(1)} %copy-done.5, f32[192,384]{1,0:T(8,128)S(1)} %maximum_maximum_fusion.refs_5_, ...), custom_call_target="tpu_custom_call" | custom-call | flops 1024 | bytes 1024 | tf_op jit(solution)/shard_map/build_rows/pallas_call | solution.py:174
  12.5 0.0 collective-permute-start.2
  12.5 0.0 collective-permute-start.3
  12.5 11.7 %build_rows.4 = (bf16[576,9216]{1,0:T(8,128)(2,1)}, bf16[576,9216]{1,0:T(8,128)(2,1)}) custom-call(s32[1]{0:T(128)} %bitcast.1.refs_0_, bf16[576,9216]{1,0:T(8,128)(2,1)} %refs_1_.5, s32[96,96]{1,0:T(8,128)S(1)} %copy-done.3, f32[96,96]{1,0:T(8,128)S(1)} %copy-done.4, f32[96]{0:T(128)S(1)} %copy-done.5, ...), custom_call_target="tpu_custom_call", output_to_operand_aliasing={{0}: (8, {}), {1}: (9, {})} | custom-call | flops 1024 | bytes 1024 | tf_op jit(solution)/shard_map/build_rows/pallas_call | solution.py:174
  24.3 0.7 collective-permute-done.refs_5_
  25.0 2.6 %collective-permute-start.1 = (bf16[1152,512]{1,0:T(8,128)(2,1)}, bf16[1152,512]{1,0:T(8,128)(2,1)S(1)}, u32[]{:S(2)}, u32[]{:S(2)}) collective-permute-start(bf16[1152,512]{1,0:T(8,128)(2,1)} %collective-permute-done.refs_5_), channel_id=1, source_target_pairs={{2,0},{5,1},{6,2},{1,3},{0,4},{9,5},{10,6},{3,7},{4,8},{13,9},{14,... | collective-permute-start | bytes 3538952 | tf_op jit(solution)/shard_map/ppermute | solution.py:353
  27.6 11.7 %build_rows.5 = (bf16[576,9216]{1,0:T(8,128)(2,1)}, bf16[576,9216]{1,0:T(8,128)(2,1)}) custom-call(s32[1]{0:T(128)} %bitcast.1.refs_0_, bf16[576,9216]{1,0:T(8,128)(2,1)} %refs_1_.5, s32[96,96]{1,0:T(8,128)S(1)} %copy-done.3, f32[96,96]{1,0:T(8,128)S(1)} %copy-done.4, f32[96]{0:T(128)S(1)} %copy-done.5, ...), custom_call_target="tpu_custom_call", output_to_operand_aliasing={{0}: (8, {}), {1}: (9, {})} | custom-call | flops 1024 | bytes 1024 | tf_op jit(solution)/shard_map/build_rows/pallas_call | solution.py:174
  39.3 0.0 collective-permute-done.2.refs_3_
  39.3 0.0 collective-permute-start.7
  39.3 0.5 collective-permute-start.6
  39.8 0.0 collective-permute-start.5
  39.8 0.7 dynamic-slice_bitcast_fusion.refs_0_
  40.5 0.0 collective-permute-done.3.refs_4_
  40.5 5.8 %add_products.7 = (f32[576,512]{1,0:T(8,128)S(1)}, f32[576,512]{1,0:T(8,128)S(1)}, f32[576,512]{1,0:T(8,128)S(1)}) custom-call(s32[10]{0:T(128)S(1)} %dynamic-slice_bitcast_fusion.refs_0_, bf16[576,9216]{1,0:T(8,128)(2,1)} %get-tuple-element.55.refs_1_, bf16[576,9216]{1,0:T(8,128)(2,1)} %get-tuple-element.56.refs_2_, ...), custom_call_target="tpu_custom_call" | custom-call | flops 1024 | bytes 1024 | tf_op jit(solution)/shard_map/add_products/pallas_call | solution.py:290
  46.3 0.2 collective-permute-done.1.refs_3_
  46.5 1.1 collective-permute-start.8
  47.6 1.5 %collective-permute-start.4 = (bf16[1152,512]{1,0:T(8,128)(2,1)S(1)}, bf16[1152,512]{1,0:T(8,128)(2,1)S(1)}, u32[]{:S(2)}, u32[]{:S(2)}) collective-permute-start(bf16[1152,512]{1,0:T(8,128)(2,1)S(1)} %collective-permute-done.1.refs_3_), channel_id=1, source_target_pairs={{2,0},{5,1},{6,2},{1,3},{0,4},{9,5},{10,6},{3,7},{4,8},{13,9},{14,... | collective-permute-start | bytes 3538952 | tf_op jit(solution)/shard_map/ppermute | solution.py:353
  49.2 0.0 collective-permute-done.7.refs_6_
  49.2 0.0 collective-permute-done.6.refs_4_
  49.2 10.2 %add_products.8 = (f32[576,512]{1,0:T(8,128)S(1)}, f32[576,512]{1,0:T(8,128)S(1)}, f32[576,512]{1,0:T(8,128)S(1)}) custom-call(s32[10]{0:T(128)S(1)} %dynamic-slice_bitcast_fusion.refs_0_, bf16[576,9216]{1,0:T(8,128)(2,1)} %get-tuple-element.55.refs_1_, ...), custom_call_target="tpu_custom_call", output_to_operand_aliasing={{0}: (7, {}), {1}: (8, {}), {2}: (9, {})} | custom-call | flops 1024 | bytes 1024 | tf_op jit(solution)/shard_map/add_products/pallas_call | solution.py:290
  59.4 2.9 %collective-permute-done.5.refs_3_ = bf16[1152,512]{1,0:T(8,128)(2,1)} collective-permute-done((bf16[1152,512]{1,0:T(8,128)(2,1)}, bf16[1152,512]{1,0:T(8,128)(2,1)}, u32[]{:S(2)}, u32[]{:S(2)}) %collective-permute-start.5) | collective-permute-done | bytes 1179680 | tf_op jit(solution)/shard_map/ppermute | solution.py:353
  62.3 1.0 collective-permute-start.11
  63.3 1.6 %collective-permute-start.10 = (bf16[1152,512]{1,0:T(8,128)(2,1)}, bf16[1152,512]{1,0:T(8,128)(2,1)S(1)}, u32[]{:S(2)}, u32[]{:S(2)}) collective-permute-start(bf16[1152,512]{1,0:T(8,128)(2,1)} %collective-permute-done.5.refs_3_), channel_id=1, source_target_pairs={{0,2},{1,5},{2,6},{3,1},{4,0},{5,9},{6,10},{7,3},{8,4},{9,13},{10,... | collective-permute-start | bytes 3538952 | tf_op jit(solution)/shard_map/ppermute | solution.py:353
  64.8 0.0 collective-permute-done.8.refs_4_
  64.9 5.9 %add_products.9 = (f32[576,512]{1,0:T(8,128)S(1)}, f32[576,512]{1,0:T(8,128)S(1)}, f32[576,512]{1,0:T(8,128)S(1)}) custom-call(s32[10]{0:T(128)S(1)} %dynamic-slice_bitcast_fusion.refs_0_, bf16[576,9216]{1,0:T(8,128)(2,1)} %get-tuple-element.55.refs_1_, ...), custom_call_target="tpu_custom_call", output_to_operand_aliasing={{0}: (5, {}), {1}: (6, {}), {2}: (7, {})} | custom-call | flops 1024 | bytes 1024 | tf_op jit(solution)/shard_map/add_products/pallas_call | solution.py:290
  70.7 2.6 %collective-permute-done.4.refs_3_ = bf16[1152,512]{1,0:T(8,128)(2,1)S(1)} collective-permute-done((bf16[1152,512]{1,0:T(8,128)(2,1)S(1)}, bf16[1152,512]{1,0:T(8,128)(2,1)S(1)}, u32[]{:S(2)}, u32[]{:S(2)}) %collective-permute-start.4) | collective-permute-done | bytes 1179680 | tf_op jit(solution)/shard_map/ppermute | solution.py:353
  73.3 0.0 collective-permute-start.13
  73.3 0.0 collective-permute-done.11.refs_4_
  73.3 5.5 %add_products.10 = (f32[576,512]{1,0:T(8,128)S(1)}, f32[576,512]{1,0:T(8,128)S(1)}, f32[576,512]{1,0:T(8,128)S(1)}) custom-call(s32[10]{0:T(128)S(1)} %dynamic-slice_bitcast_fusion.refs_0_, bf16[576,9216]{1,0:T(8,128)(2,1)} %get-tuple-element.55.refs_1_, ...), custom_call_target="tpu_custom_call", output_to_operand_aliasing={{0}: (5, {}), {1}: (6, {}), {2}: (7, {})} | custom-call | flops 1024 | bytes 1024 | tf_op jit(solution)/shard_map/add_products/pallas_call | solution.py:290
  78.8 2.7 %collective-permute-done.10.refs_3_ = bf16[1152,512]{1,0:T(8,128)(2,1)S(1)} collective-permute-done((bf16[1152,512]{1,0:T(8,128)(2,1)}, bf16[1152,512]{1,0:T(8,128)(2,1)S(1)}, u32[]{:S(2)}, u32[]{:S(2)}) %collective-permute-start.10) | collective-permute-done | bytes 1179680 | tf_op jit(solution)/shard_map/ppermute | solution.py:353
  81.6 0.6 collective-permute-start.12
  82.2 2.1 %collective-permute-start.14 = (bf16[576,512]{1,0:T(8,128)(2,1)S(1)}, bf16[576,512]{1,0:T(8,128)(2,1)S(1)}, u32[]{:S(2)}, u32[]{:S(2)}) collective-permute-start(bf16[576,512]{1,0:T(8,128)(2,1)S(1)} %slice.7), channel_id=1, source_target_pairs={{0,2},{1,5},{2,6},{3,1},{4,0},{5,9},{6,10},{7,3},{8,4},{9,13},{10,... | collective-permute-start | bytes 1769480 | tf_op jit(solution)/shard_map/ppermute | solution.py:353
  84.3 0.1 collective-permute-start.9
  84.5 0.0 collective-permute-done.13.refs_4_
  84.5 5.5 %add_products.11 = (f32[576,512]{1,0:T(8,128)S(1)}, f32[576,512]{1,0:T(8,128)S(1)}, f32[576,512]{1,0:T(8,128)S(1)}) custom-call(s32[10]{0:T(128)S(1)} %dynamic-slice_bitcast_fusion.refs_0_, bf16[576,9216]{1,0:T(8,128)(2,1)} %get-tuple-element.55.refs_1_, ...), custom_call_target="tpu_custom_call", output_to_operand_aliasing={{0}: (5, {}), {1}: (6, {}), {2}: (7, {})} | custom-call | flops 1024 | bytes 1024 | tf_op jit(solution)/shard_map/add_products/pallas_call | solution.py:290
  90.0 0.0 collective-permute-done.12.refs_4_
  90.0 0.0 copy-start
  90.0 5.5 %add_products.12 = (f32[576,512]{1,0:T(8,128)S(1)}, f32[576,512]{1,0:T(8,128)S(1)}, f32[576,512]{1,0:T(8,128)S(1)}) custom-call(s32[10]{0:T(128)S(1)} %dynamic-slice_bitcast_fusion.refs_0_, bf16[576,9216]{1,0:T(8,128)(2,1)} %get-tuple-element.55.refs_1_, ...), custom_call_target="tpu_custom_call", output_to_operand_aliasing={{0}: (5, {}), {1}: (6, {}), {2}: (7, {})} | custom-call | flops 1024 | bytes 1024 | tf_op jit(solution)/shard_map/add_products/pallas_call | solution.py:290
  95.6 2.1 %collective-permute-done.14.refs_4_ = bf16[576,512]{1,0:T(8,128)(2,1)S(1)} collective-permute-done((bf16[576,512]{1,0:T(8,128)(2,1)S(1)}, bf16[576,512]{1,0:T(8,128)(2,1)S(1)}, u32[]{:S(2)}, u32[]{:S(2)}) %collective-permute-start.14) | collective-permute-done | bytes 589856 | tf_op jit(solution)/shard_map/ppermute | solution.py:353
  97.7 0.0 collective-permute-start.16
  97.7 0.1 collective-permute-done.9.refs_3_
  97.8 0.6 collective-permute-start.15
  98.4 1.3 %collective-permute-done.16.refs_6_ = bf16[576,512]{1,0:T(8,128)(2,1)S(1)} collective-permute-done((bf16[576,512]{1,0:T(8,128)(2,1)S(1)}, bf16[576,512]{1,0:T(8,128)(2,1)S(1)}, u32[]{:S(2)}, u32[]{:S(2)}) %collective-permute-start.16) | collective-permute-done | bytes 589856 | tf_op jit(solution)/shard_map/ppermute | solution.py:353
  99.7 0.8 collective-permute-done.15.refs_5_
  100.5 7.8 %add_products.13 = (f32[576,512]{1,0:T(8,128)}, f32[576,512]{1,0:T(8,128)}, bf16[576,512]{1,0:T(8,128)(2,1)}, bf16[576,512]{1,0:T(8,128)(2,1)}, f32[6,512]{1,0:T(8,128)S(1)}) custom-call(s32[10]{0:T(128)S(1)} %dynamic-slice_bitcast_fusion.refs_0_, bf16[576,9216]{1,0:T(8,128)(2,1)} %get-tuple-element.55.refs_1_, bf16[576,9216]{1,0:T(8,128)(2,1)} %get-tuple-element.56.refs_2_, ...), custom_call_target="tpu_custom_call" | custom-call | flops 1024 | bytes 1024 | tf_op jit(solution)/shard_map/add_products/pallas_call | solution.py:290
  108.4 1.7 %collective-permute-start.17 = (f32[6,512]{1,0:T(8,128)S(1)}, f32[6,512]{1,0:T(8,128)S(1)}, u32[]{:S(2)}, u32[]{:S(2)}) collective-permute-start(f32[6,512]{1,0:T(8,128)S(1)} %get-tuple-element.92), channel_id=1, source_target_pairs={{0,3},{1,2},{2,1},{3,0},{4,7},{5,6},{6,5},{7,4},{8,11},{9,10},{10,... | collective-permute-start | bytes 36872 | tf_op jit(solution)/shard_map/ppermute | solution.py:313
  110.1 0.3 collective-permute-start.18
  110.4 0.1 collective-permute-start.19
  110.5 1.1 collective-permute-done.17
  111.6 2.3 %collective-permute-done.18 = f32[6,512]{1,0:T(8,128)S(1)} collective-permute-done((f32[6,512]{1,0:T(8,128)S(1)}, f32[6,512]{1,0:T(8,128)S(1)}, u32[]{:S(2)}, u32[]{:S(2)}) %collective-permute-start.18) | collective-permute-done | bytes 12320 | tf_op jit(solution)/shard_map/ppermute | solution.py:313
  113.9 0.0 collective-permute-done.19
  113.9 3.8 %collective-permute-start.20 = (f32[24,512]{1,0:T(8,128)S(1)}, f32[24,512]{1,0:T(8,128)S(1)}, u32[]{:S(2)}, u32[]{:S(2)}) collective-permute-start(f32[24,512]{1,0:T(8,128)S(1)} %pad_maximum_fusion.1), channel_id=1, source_target_pairs={{0,12},{1,13},{2,14},{3,15},{4,8},{5,9},{6,10},{7,11},{8,4},{9,5},... | collective-permute-start | bytes 147464 | tf_op jit(solution)/shard_map/ppermute | solution.py:313
  117.7 0.0 collective-permute-start.21
  117.7 0.7 collective-permute-start.22
  118.4 1.9 %collective-permute-done.20 = f32[24,512]{1,0:T(8,128)S(1)} collective-permute-done((f32[24,512]{1,0:T(8,128)S(1)}, f32[24,512]{1,0:T(8,128)S(1)}, u32[]{:S(2)}, u32[]{:S(2)}) %collective-permute-start.20) | collective-permute-done | bytes 49184 | tf_op jit(solution)/shard_map/ppermute | solution.py:313
  120.3 2.4 %collective-permute-done.21 = f32[24,512]{1,0:T(8,128)S(1)} collective-permute-done((f32[24,512]{1,0:T(8,128)S(1)}, f32[24,512]{1,0:T(8,128)S(1)}, u32[]{:S(2)}, u32[]{:S(2)}) %collective-permute-start.21) | collective-permute-done | bytes 49184 | tf_op jit(solution)/shard_map/ppermute | solution.py:313
  122.7 0.0 collective-permute-done.22
  122.7 0.7 pad_maximum_fusion
  (17 shorter events, 0.2 us)
Async XLA Ops:
  0.6 4.7 %copy-start.2 = (f32[96,384]{1,0:T(8,128)S(1)}, f32[96,384]{1,0:T(8,128)}, u32[]{:S(2)}) copy-start(f32[96,384]{1,0:T(8,128)} %constant.82.clone.refs_6_) | copy-start | bytes 442372
  0.6 1.3 %copy-start.1 = (bf16[576,512]{1,0:T(8,128)(2,1)S(1)}, bf16[576,512]{1,0:T(8,128)(2,1)}, u32[]{:S(2)}) copy-start(bf16[576,512]{1,0:T(8,128)(2,1)} %refs_11_.1) | copy-start | bytes 1769476
  0.7 4.4 %copy-start.3 = (s32[96,96]{1,0:T(8,128)S(1)}, s32[96,96]{1,0:T(8,128)}, u32[]{:S(2)}) copy-start(s32[96,96]{1,0:T(8,128)} %refs_2_.5) | copy-start | bytes 110596
  0.7 4.4 %copy-start.5 = (f32[96]{0:T(128)S(1)}, f32[96]{0:T(128)}, u32[]{:S(2)}) copy-start(f32[96]{0:T(128)} %refs_4_.5) | copy-start | bytes 1156
  0.7 4.5 %copy-start.4 = (f32[96,96]{1,0:T(8,128)S(1)}, f32[96,96]{1,0:T(8,128)}, u32[]{:S(2)}) copy-start(f32[96,96]{1,0:T(8,128)} %refs_3_.5) | copy-start | bytes 110596
  2.0 23.0 %collective-permute-start = (bf16[1152,512]{1,0:T(8,128)(2,1)S(1)}, bf16[1152,512]{1,0:T(8,128)(2,1)}, u32[]{:S(2)}, u32[]{:S(2)}) collective-permute-start(bf16[1152,512]{1,0:T(8,128)(2,1)S(1)} %constant_dynamic-update-slice_fusion.refs_3_), channel_id=1, source_target_pairs={{2,0},{5,1},{6,2},{1,3},{0,4},{9,5},{10,6},{3,7},{4,8},{13,9},{14,... | collective-permute-start | bytes 3538952 | tf_op jit(solution)/shard_map/ppermute | solution.py:353
  12.5 26.7 %collective-permute-start.2 = (bf16[1152,512]{1,0:T(8,128)(2,1)S(1)}, bf16[1152,512]{1,0:T(8,128)(2,1)}, u32[]{:S(2)}, u32[]{:S(2)}) collective-permute-start(bf16[1152,512]{1,0:T(8,128)(2,1)S(1)} %constant_dynamic-update-slice_fusion.refs_3_), channel_id=1, source_target_pairs={{0,2},{1,5},{2,6},{3,1},{4,0},{5,9},{6,10},{7,3},{8,4},{9,13},{10,... | collective-permute-start | bytes 3538952 | tf_op jit(solution)/shard_map/ppermute | solution.py:353
  12.5 28.0 %collective-permute-start.3 = (bf16[1152,512]{1,0:T(8,128)(2,1)S(1)}, bf16[1152,512]{1,0:T(8,128)(2,1)}, u32[]{:S(2)}, u32[]{:S(2)}) collective-permute-start(bf16[1152,512]{1,0:T(8,128)(2,1)S(1)} %constant_dynamic-update-slice_fusion.refs_3_), channel_id=1, source_target_pairs={{0,1},{1,0},{2,3},{3,2},{4,5},{5,4},{6,7},{7,6},{8,9},{9,8},{10,11... | collective-permute-start | bytes 3538952 | tf_op jit(solution)/shard_map/ppermute | solution.py:353
  25.0 21.5 %collective-permute-start.1 = (bf16[1152,512]{1,0:T(8,128)(2,1)}, bf16[1152,512]{1,0:T(8,128)(2,1)S(1)}, u32[]{:S(2)}, u32[]{:S(2)}) collective-permute-start(bf16[1152,512]{1,0:T(8,128)(2,1)} %collective-permute-done.refs_5_), channel_id=1, source_target_pairs={{2,0},{5,1},{6,2},{1,3},{0,4},{9,5},{10,6},{3,7},{4,8},{13,9},{14,... | collective-permute-start | bytes 3538952 | tf_op jit(solution)/shard_map/ppermute | solution.py:353
  39.3 9.9 %collective-permute-start.7 = (bf16[1152,512]{1,0:T(8,128)(2,1)}, bf16[1152,512]{1,0:T(8,128)(2,1)}, u32[]{:S(2)}, u32[]{:S(2)}) collective-permute-start(bf16[1152,512]{1,0:T(8,128)(2,1)} %collective-permute-done.2.refs_3_), channel_id=1, source_target_pairs={{0,1},{1,0},{2,3},{3,2},{4,5},{5,4},{6,7},{7,6},{8,9},{9,8},{10,11... | collective-permute-start | bytes 3538952 | tf_op jit(solution)/shard_map/ppermute | solution.py:353
  39.3 9.9 %collective-permute-start.6 = (bf16[1152,512]{1,0:T(8,128)(2,1)}, bf16[1152,512]{1,0:T(8,128)(2,1)}, u32[]{:S(2)}, u32[]{:S(2)}) collective-permute-start(bf16[1152,512]{1,0:T(8,128)(2,1)} %collective-permute-done.refs_5_), channel_id=1, source_target_pairs={{0,1},{1,0},{2,3},{3,2},{4,5},{5,4},{6,7},{7,6},{8,9},{9,8},{10,11... | collective-permute-start | bytes 3538952 | tf_op jit(solution)/shard_map/ppermute | solution.py:353
  39.8 22.5 %collective-permute-start.5 = (bf16[1152,512]{1,0:T(8,128)(2,1)}, bf16[1152,512]{1,0:T(8,128)(2,1)}, u32[]{:S(2)}, u32[]{:S(2)}) collective-permute-start(bf16[1152,512]{1,0:T(8,128)(2,1)} %collective-permute-done.2.refs_3_), channel_id=1, source_target_pairs={{0,2},{1,5},{2,6},{3,1},{4,0},{5,9},{6,10},{7,3},{8,4},{9,13},{10,... | collective-permute-start | bytes 3538952 | tf_op jit(solution)/shard_map/ppermute | solution.py:353
  46.5 18.3 %collective-permute-start.8 = (bf16[1152,512]{1,0:T(8,128)(2,1)S(1)}, bf16[1152,512]{1,0:T(8,128)(2,1)S(1)}, u32[]{:S(2)}, u32[]{:S(2)}) collective-permute-start(bf16[1152,512]{1,0:T(8,128)(2,1)S(1)} %collective-permute-done.1.refs_3_), channel_id=1, source_target_pairs={{0,1},{1,0},{2,3},{3,2},{4,5},{5,4},{6,7},{7,6},{8,9},{9,8},{10,11... | collective-permute-start | bytes 3538952 | tf_op jit(solution)/shard_map/ppermute | solution.py:353
  47.6 25.7 %collective-permute-start.4 = (bf16[1152,512]{1,0:T(8,128)(2,1)S(1)}, bf16[1152,512]{1,0:T(8,128)(2,1)S(1)}, u32[]{:S(2)}, u32[]{:S(2)}) collective-permute-start(bf16[1152,512]{1,0:T(8,128)(2,1)S(1)} %collective-permute-done.1.refs_3_), channel_id=1, source_target_pairs={{2,0},{5,1},{6,2},{1,3},{0,4},{9,5},{10,6},{3,7},{4,8},{13,9},{14,... | collective-permute-start | bytes 3538952 | tf_op jit(solution)/shard_map/ppermute | solution.py:353
  62.3 11.0 %collective-permute-start.11 = (bf16[1152,512]{1,0:T(8,128)(2,1)}, bf16[1152,512]{1,0:T(8,128)(2,1)S(1)}, u32[]{:S(2)}, u32[]{:S(2)}) collective-permute-start(bf16[1152,512]{1,0:T(8,128)(2,1)} %collective-permute-done.5.refs_3_), channel_id=1, source_target_pairs={{0,1},{1,0},{2,3},{3,2},{4,5},{5,4},{6,7},{7,6},{8,9},{9,8},{10,11... | collective-permute-start | bytes 3538952 | tf_op jit(solution)/shard_map/ppermute | solution.py:353
  63.3 18.3 %collective-permute-start.10 = (bf16[1152,512]{1,0:T(8,128)(2,1)}, bf16[1152,512]{1,0:T(8,128)(2,1)S(1)}, u32[]{:S(2)}, u32[]{:S(2)}) collective-permute-start(bf16[1152,512]{1,0:T(8,128)(2,1)} %collective-permute-done.5.refs_3_), channel_id=1, source_target_pairs={{0,2},{1,5},{2,6},{3,1},{4,0},{5,9},{6,10},{7,3},{8,4},{9,13},{10,... | collective-permute-start | bytes 3538952 | tf_op jit(solution)/shard_map/ppermute | solution.py:353
  73.3 11.2 %collective-permute-start.13 = (bf16[1152,512]{1,0:T(8,128)(2,1)S(1)}, bf16[1152,512]{1,0:T(8,128)(2,1)S(1)}, u32[]{:S(2)}, u32[]{:S(2)}) collective-permute-start(bf16[1152,512]{1,0:T(8,128)(2,1)S(1)} %collective-permute-done.4.refs_3_), channel_id=1, source_target_pairs={{0,1},{1,0},{2,3},{3,2},{4,5},{5,4},{6,7},{7,6},{8,9},{9,8},{10,11... | collective-permute-start | bytes 3538952 | tf_op jit(solution)/shard_map/ppermute | solution.py:353
  81.6 8.4 %collective-permute-start.12 = (bf16[1152,512]{1,0:T(8,128)(2,1)S(1)}, bf16[1152,512]{1,0:T(8,128)(2,1)S(1)}, u32[]{:S(2)}, u32[]{:S(2)}) collective-permute-start(bf16[1152,512]{1,0:T(8,128)(2,1)S(1)} %collective-permute-done.10.refs_3_), channel_id=1, source_target_pairs={{0,1},{1,0},{2,3},{3,2},{4,5},{5,4},{6,7},{7,6},{8,9},{9,8},{10,11... | collective-permute-start | bytes 3538952 | tf_op jit(solution)/shard_map/ppermute | solution.py:353
  82.2 15.5 %collective-permute-start.14 = (bf16[576,512]{1,0:T(8,128)(2,1)S(1)}, bf16[576,512]{1,0:T(8,128)(2,1)S(1)}, u32[]{:S(2)}, u32[]{:S(2)}) collective-permute-start(bf16[576,512]{1,0:T(8,128)(2,1)S(1)} %slice.7), channel_id=1, source_target_pairs={{0,2},{1,5},{2,6},{3,1},{4,0},{5,9},{6,10},{7,3},{8,4},{9,13},{10,... | collective-permute-start | bytes 1769480 | tf_op jit(solution)/shard_map/ppermute | solution.py:353
  84.3 13.5 %collective-permute-start.9 = (bf16[576,512]{1,0:T(8,128)(2,1)S(1)}, bf16[576,512]{1,0:T(8,128)(2,1)S(1)}, u32[]{:S(2)}, u32[]{:S(2)}) collective-permute-start(bf16[576,512]{1,0:T(8,128)(2,1)S(1)} %slice.6), channel_id=1, source_target_pairs={{2,0},{5,1},{6,2},{1,3},{0,4},{9,5},{10,6},{3,7},{4,8},{13,9},{14,... | collective-permute-start | bytes 1769480 | tf_op jit(solution)/shard_map/ppermute | solution.py:353
  90.0 10.5 %copy-start = (bf16[576,512]{1,0:T(8,128)(2,1)S(1)}, bf16[576,512]{1,0:T(8,128)(2,1)}, u32[]{:S(2)}) copy-start(bf16[576,512]{1,0:T(8,128)(2,1)} %refs_10_.1) | copy-start | bytes 1769476
  97.7 2.0 %collective-permute-start.16 = (bf16[576,512]{1,0:T(8,128)(2,1)S(1)}, bf16[576,512]{1,0:T(8,128)(2,1)S(1)}, u32[]{:S(2)}, u32[]{:S(2)}) collective-permute-start(bf16[576,512]{1,0:T(8,128)(2,1)S(1)} %collective-permute-done.14.refs_4_), channel_id=1, source_target_pairs={{0,1},{1,0},{2,3},{3,2},{4,5},{5,4},{6,7},{7,6},{8,9},{9,8},{10,11... | collective-permute-start | bytes 1769480 | tf_op jit(solution)/shard_map/ppermute | solution.py:353
  97.8 2.7 %collective-permute-start.15 = (bf16[576,512]{1,0:T(8,128)(2,1)S(1)}, bf16[576,512]{1,0:T(8,128)(2,1)S(1)}, u32[]{:S(2)}, u32[]{:S(2)}) collective-permute-start(bf16[576,512]{1,0:T(8,128)(2,1)S(1)} %collective-permute-done.9.refs_3_), channel_id=1, source_target_pairs={{0,1},{1,0},{2,3},{3,2},{4,5},{5,4},{6,7},{7,6},{8,9},{9,8},{10,11... | collective-permute-start | bytes 1769480 | tf_op jit(solution)/shard_map/ppermute | solution.py:353
  108.4 3.2 %collective-permute-start.17 = (f32[6,512]{1,0:T(8,128)S(1)}, f32[6,512]{1,0:T(8,128)S(1)}, u32[]{:S(2)}, u32[]{:S(2)}) collective-permute-start(f32[6,512]{1,0:T(8,128)S(1)} %get-tuple-element.92), channel_id=1, source_target_pairs={{0,3},{1,2},{2,1},{3,0},{4,7},{5,6},{6,5},{7,4},{8,11},{9,10},{10,... | collective-permute-start | bytes 36872 | tf_op jit(solution)/shard_map/ppermute | solution.py:313
  110.1 3.8 %collective-permute-start.18 = (f32[6,512]{1,0:T(8,128)S(1)}, f32[6,512]{1,0:T(8,128)S(1)}, u32[]{:S(2)}, u32[]{:S(2)}) collective-permute-start(f32[6,512]{1,0:T(8,128)S(1)} %get-tuple-element.92), channel_id=1, source_target_pairs={{0,2},{1,3},{2,0},{3,1},{4,6},{5,7},{6,4},{7,5},{8,10},{9,11},{10,... | collective-permute-start | bytes 36872 | tf_op jit(solution)/shard_map/ppermute | solution.py:313
  110.4 3.5 %collective-permute-start.19 = (f32[6,512]{1,0:T(8,128)S(1)}, f32[6,512]{1,0:T(8,128)S(1)}, u32[]{:S(2)}, u32[]{:S(2)}) collective-permute-start(f32[6,512]{1,0:T(8,128)S(1)} %get-tuple-element.92), channel_id=1, source_target_pairs={{0,1},{1,0},{2,3},{3,2},{4,5},{5,4},{6,7},{7,6},{8,9},{9,8},{10,11... | collective-permute-start | bytes 36872 | tf_op jit(solution)/shard_map/ppermute | solution.py:313
  113.9 6.4 %collective-permute-start.20 = (f32[24,512]{1,0:T(8,128)S(1)}, f32[24,512]{1,0:T(8,128)S(1)}, u32[]{:S(2)}, u32[]{:S(2)}) collective-permute-start(f32[24,512]{1,0:T(8,128)S(1)} %pad_maximum_fusion.1), channel_id=1, source_target_pairs={{0,12},{1,13},{2,14},{3,15},{4,8},{5,9},{6,10},{7,11},{8,4},{9,5},... | collective-permute-start | bytes 147464 | tf_op jit(solution)/shard_map/ppermute | solution.py:313
  117.7 5.0 %collective-permute-start.21 = (f32[24,512]{1,0:T(8,128)S(1)}, f32[24,512]{1,0:T(8,128)S(1)}, u32[]{:S(2)}, u32[]{:S(2)}) collective-permute-start(f32[24,512]{1,0:T(8,128)S(1)} %pad_maximum_fusion.1), channel_id=1, source_target_pairs={{0,8},{1,9},{2,10},{3,11},{4,12},{5,13},{6,14},{7,15},{8,0},{9,1},... | collective-permute-start | bytes 147464 | tf_op jit(solution)/shard_map/ppermute | solution.py:313
  117.7 5.0 %collective-permute-start.22 = (f32[24,512]{1,0:T(8,128)S(1)}, f32[24,512]{1,0:T(8,128)S(1)}, u32[]{:S(2)}, u32[]{:S(2)}) collective-permute-start(f32[24,512]{1,0:T(8,128)S(1)} %pad_maximum_fusion.1), channel_id=1, source_target_pairs={{0,4},{1,5},{2,6},{3,7},{4,0},{5,1},{6,2},{7,3},{8,12},{9,13},{10,... | collective-permute-start | bytes 147464 | tf_op jit(solution)/shard_map/ppermute | solution.py:313

commit v12 on v8

--- a/solution.py
+++ b/solution.py
@@ -189,7 +189,7 @@
     )(place, interaction, *smalls, *made)
 
 
-def step_body(parts, rows, opening, closing, orbitals, scale, *refs):
+def step_body(parts, rows, opening, closing, folding, orbitals, scale, *refs):
     place_ref = refs[0]
     refs = list(refs[1:])
     chips = len(parts)
@@ -198,10 +198,13 @@
     for count in parts:
         pieces = [refs.pop(0) for _ in range(2 * count)]
         greens.append([pieces[:count], pieces[count:]])
-    sums = [] if opening else [refs.pop(0) for _ in range(3)]
+    sums = [] if opening else [refs.pop(0) for _ in range(2 if closing else 3)]
     olds = [refs.pop(0) for _ in range(2)] if closing else []
     held = refs.pop()
-    totals = [refs.pop() for _ in range(3)][::-1] if closing else refs[:3]
+    if closing:
+        totals = [refs.pop() for _ in range(3)][::-1]
+    else:
+        totals = refs[:2] + [refs.pop()] if folding else refs[:3]
     core = place_ref[0]
     span = greens[0][0][0].shape[1]
     now = pl.program_id(1)
@@ -224,7 +227,7 @@
     @pl.when(now == 0)
     def _():
         for n in range(3):
-            if opening:
+            if n >= len(sums):
                 totals[n][...] = jnp.zeros_like(totals[n])
             else:
                 totals[n][...] = sums[n][...]
@@ -233,6 +236,13 @@
     totals[0][...] += mixed[:, :span]
     totals[1][...] += mixed[:, span:]
     totals[2][...] += product(polar_ref[...], held[:, 2 * span :])
+    if folding:
+
+        @pl.when(now == chips - 1)
+        def _():
+            for n in range(2):
+                totals[n][...] += totals[2][...]
+
     if closing:
 
         @pl.when(now == chips - 1)
@@ -250,7 +260,7 @@
                 refs[4][first : first + 1, :] = jnp.sum(both, axis=0, keepdims=True) * scale
 
 
-def step(place, low, mats, greens, sums, olds, orbitals):
+def step(place, low, mats, greens, sums, olds, orbitals, folding=False):
     chips = len(greens)
     opening, closing = not sums, bool(olds)
     rows = mats[0].shape[0]
@@ -268,7 +278,9 @@
         out_shape += [jax.ShapeDtypeStruct((rows // orbitals, width), jnp.float32)]
         scratch = [pltpu.VMEM((rows, span), jnp.float32)] * 3 + scratch
     else:
-        out_specs, out_shape = [tall] * 3, [wide_sum] * 3
+        kept = 2 if folding else 3
+        out_specs, out_shape = [tall] * kept, [wide_sum] * kept
+        scratch = [pltpu.VMEM((rows, span), jnp.float32)] * (3 - kept) + scratch
     operands = [pltpu.with_memory_space_constraint(mat_, pltpu.HBM) for mat_ in mats]
     blocks = [block for pair in greens for side in pair for block in side]
     operands += blocks
@@ -281,15 +293,15 @@
     aliases = {}
     if not opening:
         if not closing:
-            aliases = {1 + len(operands) + n: n for n in range(3)}
+            aliases = {1 + len(operands) + n: n for n in range(kept)}
         operands += list(sums)
-        in_specs += [pl.BlockSpec((rows, span), lambda n, g, p: (0, n), pipeline_mode=mode)] * 3
+        in_specs += [pl.BlockSpec((rows, span), lambda n, g, p: (0, n), pipeline_mode=mode)] * len(sums)
     if closing:
         operands += list(olds)
         in_specs += [tall] * 2
     return pl.pallas_call(
         functools.partial(
-            step_body, parts, rows, opening, closing, orbitals, 1.0 / math.sqrt(orbitals)
+            step_body, parts, rows, opening, closing, folding, orbitals, 1.0 / math.sqrt(orbitals)
         ),
         grid_spec=pltpu.PrefetchScalarGridSpec(
             num_scalar_prefetch=1,
@@ -399,7 +411,7 @@
             sums = step(after(place, block), low, mats, waiting, sums, (), orbitals)
             low += len(waiting)
             waiting, done = later, sums[0]
-    sums = step(place, low, mats, waiting, sums, (), orbitals)
+    sums = step(place, low, mats, waiting, sums, (), orbitals, folding=True)
     low += len(waiting)
     last = [after(block, sums[0]) for block in moving]
     shared = [send(block, across) for block in last]

time: 123 us -> 123 us (level)
  no operation moved by 1% of the time
where the time goes in v12:
time: 123 us
  Pallas kernels  76.4 us (62%)
  starting transfers between devices  21.3 us (17%)
  waiting for transfers between devices  21.2 us (17%)
  local copies, waits for them, and re-layouts  2.07 us (2%)
    pallas_call x7, Pallas kernels, step(): pl.pallas_call(functools.partial(step_body, parts, rows, opening, closing...  45.8 us
    pallas_call x3, Pallas kernels, build_rows(): pl.pallas_call(functools.partial(build_body, orbitals, low, high, pairs),...  30.6 us
    ppermute x17, starting transfers between devices, send(): return lax.ppermute(block, 'prow', pairs_of)  14.7 us
    ppermute x17, waiting for transfers between devices, send(): return lax.ppermute(block, 'prow', pairs_of)  13.5 us
    ppermute x6, waiting for transfers between devices, spread_blocks(): blocks.append(lax.ppermute(block, 'prow', pairs_of))  7.69 us
    ppermute x6, starting transfers between devices, spread_blocks(): blocks.append(lax.ppermute(block, 'prow', pairs_of))  6.57 us
  transfers between devices with their start and end apart: 23, of which 13 were waited for; matrix products, arithmetic and copies ran while one was open for 1% of the time, Pallas kernels for 56%

profile of v12, /device:TPU:0, one launch (start us, length us, event | category | flops | bytes accessed | tf_op | source)
XLA Modules:
  0.0 122.9 jit_solution(11475786216764804579)
XLA Ops:
  0.6 0.0 copy-start.2
  0.7 1.2 constant_dynamic-update-slice_fusion.1
  1.9 0.1 copy-done.1
  2.0 3.1 %collective-permute-start = (bf16[1152,512]{1,0:T(8,128)(2,1)S(1)}, bf16[1152,512]{1,0:T(8,128)(2,1)}, u32[]{:S(2)}, u32[]{:S(2)}) collective-permute-start(bf16[1152,512]{1,0:T(8,128)(2,1)S(1)} %constant_dynamic-update-slice_fusion.refs_3_), channel_id=1, source_target_pairs={{2,0},{5,1},{6,2},{1,3},{0,4},{9,5},{10,6},{3,7},{4,8},{13,9},{14,... | collective-permute-start | bytes 3538952 | tf_op jit(solution)/shard_map/ppermute | solution.py:365
  5.1 0.1 pad_maximum_fusion.2
  5.1 0.2 maximum_maximum_fusion.refs_5_
  5.4 7.1 %build_rows.3 = (bf16[576,9216]{1,0:T(8,128)(2,1)}, bf16[576,9216]{1,0:T(8,128)(2,1)}) custom-call(s32[1]{0:T(128)} %bitcast.1.refs_0_, bf16[576,9216]{1,0:T(8,128)(2,1)} %refs_1_.5, s32[96,96]{1,0:T(8,128)S(1)} %copy-done.3, f32[96,96]{1,0:T(8,128)S(1)} %copy-done.4, f32[96]{0:T(128)S(1)} %copy-done.5, f32[192,384]{1,0:T(8,128)S(1)} %maximum_maximum_fusion.refs_5_, ...), custom_call_target="tpu_custom_call" | custom-call | flops 1024 | bytes 1024 | tf_op jit(solution)/shard_map/build_rows/pallas_call | solution.py:174
  12.5 0.0 collective-permute-start.2
  12.5 0.0 collective-permute-start.3
  12.5 11.7 %build_rows.4 = (bf16[576,9216]{1,0:T(8,128)(2,1)}, bf16[576,9216]{1,0:T(8,128)(2,1)}) custom-call(s32[1]{0:T(128)} %bitcast.1.refs_0_, bf16[576,9216]{1,0:T(8,128)(2,1)} %refs_1_.5, s32[96,96]{1,0:T(8,128)S(1)} %copy-done.3, f32[96,96]{1,0:T(8,128)S(1)} %copy-done.4, f32[96]{0:T(128)S(1)} %copy-done.5, ...), custom_call_target="tpu_custom_call", output_to_operand_aliasing={{0}: (8, {}), {1}: (9, {})} | custom-call | flops 1024 | bytes 1024 | tf_op jit(solution)/shard_map/build_rows/pallas_call | solution.py:174
  24.3 0.7 collective-permute-done.refs_5_
  25.0 2.6 %collective-permute-start.1 = (bf16[1152,512]{1,0:T(8,128)(2,1)}, bf16[1152,512]{1,0:T(8,128)(2,1)S(1)}, u32[]{:S(2)}, u32[]{:S(2)}) collective-permute-start(bf16[1152,512]{1,0:T(8,128)(2,1)} %collective-permute-done.refs_5_), channel_id=1, source_target_pairs={{2,0},{5,1},{6,2},{1,3},{0,4},{9,5},{10,6},{3,7},{4,8},{13,9},{14,... | collective-permute-start | bytes 3538952 | tf_op jit(solution)/shard_map/ppermute | solution.py:365
  27.6 11.7 %build_rows.5 = (bf16[576,9216]{1,0:T(8,128)(2,1)}, bf16[576,9216]{1,0:T(8,128)(2,1)}) custom-call(s32[1]{0:T(128)} %bitcast.1.refs_0_, bf16[576,9216]{1,0:T(8,128)(2,1)} %refs_1_.5, s32[96,96]{1,0:T(8,128)S(1)} %copy-done.3, f32[96,96]{1,0:T(8,128)S(1)} %copy-done.4, f32[96]{0:T(128)S(1)} %copy-done.5, ...), custom_call_target="tpu_custom_call", output_to_operand_aliasing={{0}: (8, {}), {1}: (9, {})} | custom-call | flops 1024 | bytes 1024 | tf_op jit(solution)/shard_map/build_rows/pallas_call | solution.py:174
  39.3 0.0 collective-permute-done.2.refs_3_
  39.3 0.0 collective-permute-start.7
  39.3 0.5 collective-permute-start.6
  39.8 0.0 collective-permute-start.5
  39.8 0.7 dynamic-slice_bitcast_fusion.refs_0_
  40.5 0.0 collective-permute-done.3.refs_4_
  40.5 5.8 %add_products.7 = (f32[576,512]{1,0:T(8,128)S(1)}, f32[576,512]{1,0:T(8,128)S(1)}, f32[576,512]{1,0:T(8,128)S(1)}) custom-call(s32[10]{0:T(128)S(1)} %dynamic-slice_bitcast_fusion.refs_0_, bf16[576,9216]{1,0:T(8,128)(2,1)} %get-tuple-element.54.refs_1_, bf16[576,9216]{1,0:T(8,128)(2,1)} %get-tuple-element.55.refs_2_, ...), custom_call_target="tpu_custom_call" | custom-call | flops 1024 | bytes 1024 | tf_op jit(solution)/shard_map/add_products/pallas_call | solution.py:302
  46.3 0.2 collective-permute-done.1.refs_3_
  46.5 1.1 collective-permute-start.8
  47.6 1.5 %collective-permute-start.4 = (bf16[1152,512]{1,0:T(8,128)(2,1)S(1)}, bf16[1152,512]{1,0:T(8,128)(2,1)S(1)}, u32[]{:S(2)}, u32[]{:S(2)}) collective-permute-start(bf16[1152,512]{1,0:T(8,128)(2,1)S(1)} %collective-permute-done.1.refs_3_), channel_id=1, source_target_pairs={{2,0},{5,1},{6,2},{1,3},{0,4},{9,5},{10,6},{3,7},{4,8},{13,9},{14,... | collective-permute-start | bytes 3538952 | tf_op jit(solution)/shard_map/ppermute | solution.py:365
  49.2 0.0 collective-permute-done.7.refs_6_
  49.2 0.0 collective-permute-done.6.refs_4_
  49.2 10.2 %add_products.8 = (f32[576,512]{1,0:T(8,128)S(1)}, f32[576,512]{1,0:T(8,128)S(1)}, f32[576,512]{1,0:T(8,128)S(1)}) custom-call(s32[10]{0:T(128)S(1)} %dynamic-slice_bitcast_fusion.refs_0_, bf16[576,9216]{1,0:T(8,128)(2,1)} %get-tuple-element.54.refs_1_, ...), custom_call_target="tpu_custom_call", output_to_operand_aliasing={{0}: (7, {}), {1}: (8, {}), {2}: (9, {})} | custom-call | flops 1024 | bytes 1024 | tf_op jit(solution)/shard_map/add_products/pallas_call | solution.py:302
  59.4 2.9 %collective-permute-done.5.refs_3_ = bf16[1152,512]{1,0:T(8,128)(2,1)} collective-permute-done((bf16[1152,512]{1,0:T(8,128)(2,1)}, bf16[1152,512]{1,0:T(8,128)(2,1)}, u32[]{:S(2)}, u32[]{:S(2)}) %collective-permute-start.5) | collective-permute-done | bytes 1179680 | tf_op jit(solution)/shard_map/ppermute | solution.py:365
  62.3 1.0 collective-permute-start.11
  63.3 1.6 %collective-permute-start.10 = (bf16[1152,512]{1,0:T(8,128)(2,1)}, bf16[1152,512]{1,0:T(8,128)(2,1)S(1)}, u32[]{:S(2)}, u32[]{:S(2)}) collective-permute-start(bf16[1152,512]{1,0:T(8,128)(2,1)} %collective-permute-done.5.refs_3_), channel_id=1, source_target_pairs={{0,2},{1,5},{2,6},{3,1},{4,0},{5,9},{6,10},{7,3},{8,4},{9,13},{10,... | collective-permute-start | bytes 3538952 | tf_op jit(solution)/shard_map/ppermute | solution.py:365
  64.8 0.0 collective-permute-done.8.refs_4_
  64.9 5.9 %add_products.9 = (f32[576,512]{1,0:T(8,128)S(1)}, f32[576,512]{1,0:T(8,128)S(1)}, f32[576,512]{1,0:T(8,128)S(1)}) custom-call(s32[10]{0:T(128)S(1)} %dynamic-slice_bitcast_fusion.refs_0_, bf16[576,9216]{1,0:T(8,128)(2,1)} %get-tuple-element.54.refs_1_, ...), custom_call_target="tpu_custom_call", output_to_operand_aliasing={{0}: (5, {}), {1}: (6, {}), {2}: (7, {})} | custom-call | flops 1024 | bytes 1024 | tf_op jit(solution)/shard_map/add_products/pallas_call | solution.py:302
  70.7 2.6 %collective-permute-done.4.refs_3_ = bf16[1152,512]{1,0:T(8,128)(2,1)S(1)} collective-permute-done((bf16[1152,512]{1,0:T(8,128)(2,1)S(1)}, bf16[1152,512]{1,0:T(8,128)(2,1)S(1)}, u32[]{:S(2)}, u32[]{:S(2)}) %collective-permute-start.4) | collective-permute-done | bytes 1179680 | tf_op jit(solution)/shard_map/ppermute | solution.py:365
  73.3 0.0 collective-permute-start.13
  73.3 0.0 collective-permute-done.11.refs_4_
  73.3 5.5 %add_products.10 = (f32[576,512]{1,0:T(8,128)S(1)}, f32[576,512]{1,0:T(8,128)S(1)}, f32[576,512]{1,0:T(8,128)S(1)}) custom-call(s32[10]{0:T(128)S(1)} %dynamic-slice_bitcast_fusion.refs_0_, bf16[576,9216]{1,0:T(8,128)(2,1)} %get-tuple-element.54.refs_1_, ...), custom_call_target="tpu_custom_call", output_to_operand_aliasing={{0}: (5, {}), {1}: (6, {}), {2}: (7, {})} | custom-call | flops 1024 | bytes 1024 | tf_op jit(solution)/shard_map/add_products/pallas_call | solution.py:302
  78.8 2.7 %collective-permute-done.10.refs_3_ = bf16[1152,512]{1,0:T(8,128)(2,1)S(1)} collective-permute-done((bf16[1152,512]{1,0:T(8,128)(2,1)}, bf16[1152,512]{1,0:T(8,128)(2,1)S(1)}, u32[]{:S(2)}, u32[]{:S(2)}) %collective-permute-start.10) | collective-permute-done | bytes 1179680 | tf_op jit(solution)/shard_map/ppermute | solution.py:365
  81.6 0.6 collective-permute-start.12
  82.2 2.1 %collective-permute-start.14 = (bf16[576,512]{1,0:T(8,128)(2,1)S(1)}, bf16[576,512]{1,0:T(8,128)(2,1)S(1)}, u32[]{:S(2)}, u32[]{:S(2)}) collective-permute-start(bf16[576,512]{1,0:T(8,128)(2,1)S(1)} %slice.7), channel_id=1, source_target_pairs={{0,2},{1,5},{2,6},{3,1},{4,0},{5,9},{6,10},{7,3},{8,4},{9,13},{10,... | collective-permute-start | bytes 1769480 | tf_op jit(solution)/shard_map/ppermute | solution.py:365
  84.3 0.1 collective-permute-start.9
  84.5 0.0 collective-permute-done.13.refs_4_
  84.5 5.5 %add_products.11 = (f32[576,512]{1,0:T(8,128)S(1)}, f32[576,512]{1,0:T(8,128)S(1)}, f32[576,512]{1,0:T(8,128)S(1)}) custom-call(s32[10]{0:T(128)S(1)} %dynamic-slice_bitcast_fusion.refs_0_, bf16[576,9216]{1,0:T(8,128)(2,1)} %get-tuple-element.54.refs_1_, ...), custom_call_target="tpu_custom_call", output_to_operand_aliasing={{0}: (5, {}), {1}: (6, {}), {2}: (7, {})} | custom-call | flops 1024 | bytes 1024 | tf_op jit(solution)/shard_map/add_products/pallas_call | solution.py:302
  90.0 0.0 collective-permute-done.12.refs_4_
  90.0 0.0 copy-start
  90.0 5.6 %add_products.12 = (f32[576,512]{1,0:T(8,128)S(1)}, f32[576,512]{1,0:T(8,128)S(1)}) custom-call(s32[10]{0:T(128)S(1)} %dynamic-slice_bitcast_fusion.refs_0_, bf16[576,9216]{1,0:T(8,128)(2,1)} %get-tuple-element.54.refs_1_, bf16[576,9216]{1,0:T(8,128)(2,1)} %get-tuple-element.55.refs_2_, ...), custom_call_target="tpu_custom_call", output_to_operand_aliasing={{0}: (5, {}), {1}: (6, {})} | custom-call | flops 1024 | bytes 1024 | tf_op jit(solution)/shard_map/add_products/pallas_call | solution.py:302
  95.6 2.1 %collective-permute-done.14.refs_4_ = bf16[576,512]{1,0:T(8,128)(2,1)S(1)} collective-permute-done((bf16[576,512]{1,0:T(8,128)(2,1)S(1)}, bf16[576,512]{1,0:T(8,128)(2,1)S(1)}, u32[]{:S(2)}, u32[]{:S(2)}) %collective-permute-start.14) | collective-permute-done | bytes 589856 | tf_op jit(solution)/shard_map/ppermute | solution.py:365
  97.7 0.0 collective-permute-start.16
  97.7 0.1 collective-permute-done.9.refs_3_
  97.8 0.6 collective-permute-start.15
  98.4 1.3 %collective-permute-done.16.refs_6_ = bf16[576,512]{1,0:T(8,128)(2,1)S(1)} collective-permute-done((bf16[576,512]{1,0:T(8,128)(2,1)S(1)}, bf16[576,512]{1,0:T(8,128)(2,1)S(1)}, u32[]{:S(2)}, u32[]{:S(2)}) %collective-permute-start.16) | collective-permute-done | bytes 589856 | tf_op jit(solution)/shard_map/ppermute | solution.py:365
  99.7 0.8 collective-permute-done.15.refs_5_
  100.5 7.3 %add_products.13 = (f32[576,512]{1,0:T(8,128)}, f32[576,512]{1,0:T(8,128)}, bf16[576,512]{1,0:T(8,128)(2,1)}, bf16[576,512]{1,0:T(8,128)(2,1)}, f32[6,512]{1,0:T(8,128)S(1)}) custom-call(s32[10]{0:T(128)S(1)} %dynamic-slice_bitcast_fusion.refs_0_, bf16[576,9216]{1,0:T(8,128)(2,1)} %get-tuple-element.54.refs_1_, bf16[576,9216]{1,0:T(8,128)(2,1)} %get-tuple-element.55.refs_2_, ...), custom_call_target="tpu_custom_call" | custom-call | flops 1024 | bytes 1024 | tf_op jit(solution)/shard_map/add_products/pallas_call | solution.py:302
  107.8 1.7 %collective-permute-start.17 = (f32[6,512]{1,0:T(8,128)S(1)}, f32[6,512]{1,0:T(8,128)S(1)}, u32[]{:S(2)}, u32[]{:S(2)}) collective-permute-start(f32[6,512]{1,0:T(8,128)S(1)} %get-tuple-element.90), channel_id=1, source_target_pairs={{0,3},{1,2},{2,1},{3,0},{4,7},{5,6},{6,5},{7,4},{8,11},{9,10},{10,... | collective-permute-start | bytes 36872 | tf_op jit(solution)/shard_map/ppermute | solution.py:325
  109.6 0.3 collective-permute-start.18
  109.9 0.1 collective-permute-start.19
  110.0 1.1 collective-permute-done.17
  111.0 2.3 %collective-permute-done.18 = f32[6,512]{1,0:T(8,128)S(1)} collective-permute-done((f32[6,512]{1,0:T(8,128)S(1)}, f32[6,512]{1,0:T(8,128)S(1)}, u32[]{:S(2)}, u32[]{:S(2)}) %collective-permute-start.18) | collective-permute-done | bytes 12320 | tf_op jit(solution)/shard_map/ppermute | solution.py:325
  113.3 0.0 collective-permute-done.19
  113.4 3.8 %collective-permute-start.20 = (f32[24,512]{1,0:T(8,128)S(1)}, f32[24,512]{1,0:T(8,128)S(1)}, u32[]{:S(2)}, u32[]{:S(2)}) collective-permute-start(f32[24,512]{1,0:T(8,128)S(1)} %pad_maximum_fusion.1), channel_id=1, source_target_pairs={{0,12},{1,13},{2,14},{3,15},{4,8},{5,9},{6,10},{7,11},{8,4},{9,5},... | collective-permute-start | bytes 147464 | tf_op jit(solution)/shard_map/ppermute | solution.py:325
  117.2 0.0 collective-permute-start.21
  117.2 0.7 collective-permute-start.22
  117.8 1.9 %collective-permute-done.20 = f32[24,512]{1,0:T(8,128)S(1)} collective-permute-done((f32[24,512]{1,0:T(8,128)S(1)}, f32[24,512]{1,0:T(8,128)S(1)}, u32[]{:S(2)}, u32[]{:S(2)}) %collective-permute-start.20) | collective-permute-done | bytes 49184 | tf_op jit(solution)/shard_map/ppermute | solution.py:325
  119.7 2.4 %collective-permute-done.21 = f32[24,512]{1,0:T(8,128)S(1)} collective-permute-done((f32[24,512]{1,0:T(8,128)S(1)}, f32[24,512]{1,0:T(8,128)S(1)}, u32[]{:S(2)}, u32[]{:S(2)}) %collective-permute-start.21) | collective-permute-done | bytes 49184 | tf_op jit(solution)/shard_map/ppermute | solution.py:325
  122.1 0.0 collective-permute-done.22
  122.2 0.7 pad_maximum_fusion
  (17 shorter events, 0.2 us)
Async XLA Ops:
  0.6 4.7 %copy-start.2 = (f32[96,384]{1,0:T(8,128)S(1)}, f32[96,384]{1,0:T(8,128)}, u32[]{:S(2)}) copy-start(f32[96,384]{1,0:T(8,128)} %constant.82.clone.refs_6_) | copy-start | bytes 442372
  0.6 1.3 %copy-start.1 = (bf16[576,512]{1,0:T(8,128)(2,1)S(1)}, bf16[576,512]{1,0:T(8,128)(2,1)}, u32[]{:S(2)}) copy-start(bf16[576,512]{1,0:T(8,128)(2,1)} %refs_10_.1) | copy-start | bytes 1769476
  0.7 4.4 %copy-start.3 = (s32[96,96]{1,0:T(8,128)S(1)}, s32[96,96]{1,0:T(8,128)}, u32[]{:S(2)}) copy-start(s32[96,96]{1,0:T(8,128)} %refs_2_.5) | copy-start | bytes 110596
  0.7 4.4 %copy-start.5 = (f32[96]{0:T(128)S(1)}, f32[96]{0:T(128)}, u32[]{:S(2)}) copy-start(f32[96]{0:T(128)} %refs_4_.5) | copy-start | bytes 1156
  0.7 4.5 %copy-start.4 = (f32[96,96]{1,0:T(8,128)S(1)}, f32[96,96]{1,0:T(8,128)}, u32[]{:S(2)}) copy-start(f32[96,96]{1,0:T(8,128)} %refs_3_.5) | copy-start | bytes 110596
  2.0 23.0 %collective-permute-start = (bf16[1152,512]{1,0:T(8,128)(2,1)S(1)}, bf16[1152,512]{1,0:T(8,128)(2,1)}, u32[]{:S(2)}, u32[]{:S(2)}) collective-permute-start(bf16[1152,512]{1,0:T(8,128)(2,1)S(1)} %constant_dynamic-update-slice_fusion.refs_3_), channel_id=1, source_target_pairs={{2,0},{5,1},{6,2},{1,3},{0,4},{9,5},{10,6},{3,7},{4,8},{13,9},{14,... | collective-permute-start | bytes 3538952 | tf_op jit(solution)/shard_map/ppermute | solution.py:365
  12.5 26.7 %collective-permute-start.2 = (bf16[1152,512]{1,0:T(8,128)(2,1)S(1)}, bf16[1152,512]{1,0:T(8,128)(2,1)}, u32[]{:S(2)}, u32[]{:S(2)}) collective-permute-start(bf16[1152,512]{1,0:T(8,128)(2,1)S(1)} %constant_dynamic-update-slice_fusion.refs_3_), channel_id=1, source_target_pairs={{0,2},{1,5},{2,6},{3,1},{4,0},{5,9},{6,10},{7,3},{8,4},{9,13},{10,... | collective-permute-start | bytes 3538952 | tf_op jit(solution)/shard_map/ppermute | solution.py:365
  12.5 28.0 %collective-permute-start.3 = (bf16[1152,512]{1,0:T(8,128)(2,1)S(1)}, bf16[1152,512]{1,0:T(8,128)(2,1)}, u32[]{:S(2)}, u32[]{:S(2)}) collective-permute-start(bf16[1152,512]{1,0:T(8,128)(2,1)S(1)} %constant_dynamic-update-slice_fusion.refs_3_), channel_id=1, source_target_pairs={{0,1},{1,0},{2,3},{3,2},{4,5},{5,4},{6,7},{7,6},{8,9},{9,8},{10,11... | collective-permute-start | bytes 3538952 | tf_op jit(solution)/shard_map/ppermute | solution.py:365
  25.0 21.5 %collective-permute-start.1 = (bf16[1152,512]{1,0:T(8,128)(2,1)}, bf16[1152,512]{1,0:T(8,128)(2,1)S(1)}, u32[]{:S(2)}, u32[]{:S(2)}) collective-permute-start(bf16[1152,512]{1,0:T(8,128)(2,1)} %collective-permute-done.refs_5_), channel_id=1, source_target_pairs={{2,0},{5,1},{6,2},{1,3},{0,4},{9,5},{10,6},{3,7},{4,8},{13,9},{14,... | collective-permute-start | bytes 3538952 | tf_op jit(solution)/shard_map/ppermute | solution.py:365
  39.3 9.9 %collective-permute-start.7 = (bf16[1152,512]{1,0:T(8,128)(2,1)}, bf16[1152,512]{1,0:T(8,128)(2,1)}, u32[]{:S(2)}, u32[]{:S(2)}) collective-permute-start(bf16[1152,512]{1,0:T(8,128)(2,1)} %collective-permute-done.2.refs_3_), channel_id=1, source_target_pairs={{0,1},{1,0},{2,3},{3,2},{4,5},{5,4},{6,7},{7,6},{8,9},{9,8},{10,11... | collective-permute-start | bytes 3538952 | tf_op jit(solution)/shard_map/ppermute | solution.py:365
  39.3 9.9 %collective-permute-start.6 = (bf16[1152,512]{1,0:T(8,128)(2,1)}, bf16[1152,512]{1,0:T(8,128)(2,1)}, u32[]{:S(2)}, u32[]{:S(2)}) collective-permute-start(bf16[1152,512]{1,0:T(8,128)(2,1)} %collective-permute-done.refs_5_), channel_id=1, source_target_pairs={{0,1},{1,0},{2,3},{3,2},{4,5},{5,4},{6,7},{7,6},{8,9},{9,8},{10,11... | collective-permute-start | bytes 3538952 | tf_op jit(solution)/shard_map/ppermute | solution.py:365
  39.8 22.5 %collective-permute-start.5 = (bf16[1152,512]{1,0:T(8,128)(2,1)}, bf16[1152,512]{1,0:T(8,128)(2,1)}, u32[]{:S(2)}, u32[]{:S(2)}) collective-permute-start(bf16[1152,512]{1,0:T(8,128)(2,1)} %collective-permute-done.2.refs_3_), channel_id=1, source_target_pairs={{0,2},{1,5},{2,6},{3,1},{4,0},{5,9},{6,10},{7,3},{8,4},{9,13},{10,... | collective-permute-start | bytes 3538952 | tf_op jit(solution)/shard_map/ppermute | solution.py:365
  46.5 18.3 %collective-permute-start.8 = (bf16[1152,512]{1,0:T(8,128)(2,1)S(1)}, bf16[1152,512]{1,0:T(8,128)(2,1)S(1)}, u32[]{:S(2)}, u32[]{:S(2)}) collective-permute-start(bf16[1152,512]{1,0:T(8,128)(2,1)S(1)} %collective-permute-done.1.refs_3_), channel_id=1, source_target_pairs={{0,1},{1,0},{2,3},{3,2},{4,5},{5,4},{6,7},{7,6},{8,9},{9,8},{10,11... | collective-permute-start | bytes 3538952 | tf_op jit(solution)/shard_map/ppermute | solution.py:365
  47.6 25.7 %collective-permute-start.4 = (bf16[1152,512]{1,0:T(8,128)(2,1)S(1)}, bf16[1152,512]{1,0:T(8,128)(2,1)S(1)}, u32[]{:S(2)}, u32[]{:S(2)}) collective-permute-start(bf16[1152,512]{1,0:T(8,128)(2,1)S(1)} %collective-permute-done.1.refs_3_), channel_id=1, source_target_pairs={{2,0},{5,1},{6,2},{1,3},{0,4},{9,5},{10,6},{3,7},{4,8},{13,9},{14,... | collective-permute-start | bytes 3538952 | tf_op jit(solution)/shard_map/ppermute | solution.py:365
  62.3 11.0 %collective-permute-start.11 = (bf16[1152,512]{1,0:T(8,128)(2,1)}, bf16[1152,512]{1,0:T(8,128)(2,1)S(1)}, u32[]{:S(2)}, u32[]{:S(2)}) collective-permute-start(bf16[1152,512]{1,0:T(8,128)(2,1)} %collective-permute-done.5.refs_3_), channel_id=1, source_target_pairs={{0,1},{1,0},{2,3},{3,2},{4,5},{5,4},{6,7},{7,6},{8,9},{9,8},{10,11... | collective-permute-start | bytes 3538952 | tf_op jit(solution)/shard_map/ppermute | solution.py:365
  63.3 18.3 %collective-permute-start.10 = (bf16[1152,512]{1,0:T(8,128)(2,1)}, bf16[1152,512]{1,0:T(8,128)(2,1)S(1)}, u32[]{:S(2)}, u32[]{:S(2)}) collective-permute-start(bf16[1152,512]{1,0:T(8,128)(2,1)} %collective-permute-done.5.refs_3_), channel_id=1, source_target_pairs={{0,2},{1,5},{2,6},{3,1},{4,0},{5,9},{6,10},{7,3},{8,4},{9,13},{10,... | collective-permute-start | bytes 3538952 | tf_op jit(solution)/shard_map/ppermute | solution.py:365
  73.3 11.2 %collective-permute-start.13 = (bf16[1152,512]{1,0:T(8,128)(2,1)S(1)}, bf16[1152,512]{1,0:T(8,128)(2,1)S(1)}, u32[]{:S(2)}, u32[]{:S(2)}) collective-permute-start(bf16[1152,512]{1,0:T(8,128)(2,1)S(1)} %collective-permute-done.4.refs_3_), channel_id=1, source_target_pairs={{0,1},{1,0},{2,3},{3,2},{4,5},{5,4},{6,7},{7,6},{8,9},{9,8},{10,11... | collective-permute-start | bytes 3538952 | tf_op jit(solution)/shard_map/ppermute | solution.py:365
  81.6 8.4 %collective-permute-start.12 = (bf16[1152,512]{1,0:T(8,128)(2,1)S(1)}, bf16[1152,512]{1,0:T(8,128)(2,1)S(1)}, u32[]{:S(2)}, u32[]{:S(2)}) collective-permute-start(bf16[1152,512]{1,0:T(8,128)(2,1)S(1)} %collective-permute-done.10.refs_3_), channel_id=1, source_target_pairs={{0,1},{1,0},{2,3},{3,2},{4,5},{5,4},{6,7},{7,6},{8,9},{9,8},{10,11... | collective-permute-start | bytes 3538952 | tf_op jit(solution)/shard_map/ppermute | solution.py:365
  82.2 15.5 %collective-permute-start.14 = (bf16[576,512]{1,0:T(8,128)(2,1)S(1)}, bf16[576,512]{1,0:T(8,128)(2,1)S(1)}, u32[]{:S(2)}, u32[]{:S(2)}) collective-permute-start(bf16[576,512]{1,0:T(8,128)(2,1)S(1)} %slice.7), channel_id=1, source_target_pairs={{0,2},{1,5},{2,6},{3,1},{4,0},{5,9},{6,10},{7,3},{8,4},{9,13},{10,... | collective-permute-start | bytes 1769480 | tf_op jit(solution)/shard_map/ppermute | solution.py:365
  84.3 13.5 %collective-permute-start.9 = (bf16[576,512]{1,0:T(8,128)(2,1)S(1)}, bf16[576,512]{1,0:T(8,128)(2,1)S(1)}, u32[]{:S(2)}, u32[]{:S(2)}) collective-permute-start(bf16[576,512]{1,0:T(8,128)(2,1)S(1)} %slice.6), channel_id=1, source_target_pairs={{2,0},{5,1},{6,2},{1,3},{0,4},{9,5},{10,6},{3,7},{4,8},{13,9},{14,... | collective-permute-start | bytes 1769480 | tf_op jit(solution)/shard_map/ppermute | solution.py:365
  90.0 10.5 %copy-start = (bf16[576,512]{1,0:T(8,128)(2,1)S(1)}, bf16[576,512]{1,0:T(8,128)(2,1)}, u32[]{:S(2)}) copy-start(bf16[576,512]{1,0:T(8,128)(2,1)} %refs_9_.1) | copy-start | bytes 1769476
  97.7 2.0 %collective-permute-start.16 = (bf16[576,512]{1,0:T(8,128)(2,1)S(1)}, bf16[576,512]{1,0:T(8,128)(2,1)S(1)}, u32[]{:S(2)}, u32[]{:S(2)}) collective-permute-start(bf16[576,512]{1,0:T(8,128)(2,1)S(1)} %collective-permute-done.14.refs_4_), channel_id=1, source_target_pairs={{0,1},{1,0},{2,3},{3,2},{4,5},{5,4},{6,7},{7,6},{8,9},{9,8},{10,11... | collective-permute-start | bytes 1769480 | tf_op jit(solution)/shard_map/ppermute | solution.py:365
  97.8 2.7 %collective-permute-start.15 = (bf16[576,512]{1,0:T(8,128)(2,1)S(1)}, bf16[576,512]{1,0:T(8,128)(2,1)S(1)}, u32[]{:S(2)}, u32[]{:S(2)}) collective-permute-start(bf16[576,512]{1,0:T(8,128)(2,1)S(1)} %collective-permute-done.9.refs_3_), channel_id=1, source_target_pairs={{0,1},{1,0},{2,3},{3,2},{4,5},{5,4},{6,7},{7,6},{8,9},{9,8},{10,11... | collective-permute-start | bytes 1769480 | tf_op jit(solution)/shard_map/ppermute | solution.py:365
  107.8 3.2 %collective-permute-start.17 = (f32[6,512]{1,0:T(8,128)S(1)}, f32[6,512]{1,0:T(8,128)S(1)}, u32[]{:S(2)}, u32[]{:S(2)}) collective-permute-start(f32[6,512]{1,0:T(8,128)S(1)} %get-tuple-element.90), channel_id=1, source_target_pairs={{0,3},{1,2},{2,1},{3,0},{4,7},{5,6},{6,5},{7,4},{8,11},{9,10},{10,... | collective-permute-start | bytes 36872 | tf_op jit(solution)/shard_map/ppermute | solution.py:325
  109.6 3.8 %collective-permute-start.18 = (f32[6,512]{1,0:T(8,128)S(1)}, f32[6,512]{1,0:T(8,128)S(1)}, u32[]{:S(2)}, u32[]{:S(2)}) collective-permute-start(f32[6,512]{1,0:T(8,128)S(1)} %get-tuple-element.90), channel_id=1, source_target_pairs={{0,2},{1,3},{2,0},{3,1},{4,6},{5,7},{6,4},{7,5},{8,10},{9,11},{10,... | collective-permute-start | bytes 36872 | tf_op jit(solution)/shard_map/ppermute | solution.py:325
  109.9 3.5 %collective-permute-start.19 = (f32[6,512]{1,0:T(8,128)S(1)}, f32[6,512]{1,0:T(8,128)S(1)}, u32[]{:S(2)}, u32[]{:S(2)}) collective-permute-start(f32[6,512]{1,0:T(8,128)S(1)} %get-tuple-element.90), channel_id=1, source_target_pairs={{0,1},{1,0},{2,3},{3,2},{4,5},{5,4},{6,7},{7,6},{8,9},{9,8},{10,11... | collective-permute-start | bytes 36872 | tf_op jit(solution)/shard_map/ppermute | solution.py:325
  113.4 6.4 %collective-permute-start.20 = (f32[24,512]{1,0:T(8,128)S(1)}, f32[24,512]{1,0:T(8,128)S(1)}, u32[]{:S(2)}, u32[]{:S(2)}) collective-permute-start(f32[24,512]{1,0:T(8,128)S(1)} %pad_maximum_fusion.1), channel_id=1, source_target_pairs={{0,12},{1,13},{2,14},{3,15},{4,8},{5,9},{6,10},{7,11},{8,4},{9,5},... | collective-permute-start | bytes 147464 | tf_op jit(solution)/shard_map/ppermute | solution.py:325
  117.2 5.0 %collective-permute-start.21 = (f32[24,512]{1,0:T(8,128)S(1)}, f32[24,512]{1,0:T(8,128)S(1)}, u32[]{:S(2)}, u32[]{:S(2)}) collective-permute-start(f32[24,512]{1,0:T(8,128)S(1)} %pad_maximum_fusion.1), channel_id=1, source_target_pairs={{0,8},{1,9},{2,10},{3,11},{4,12},{5,13},{6,14},{7,15},{8,0},{9,1},... | collective-permute-start | bytes 147464 | tf_op jit(solution)/shard_map/ppermute | solution.py:325
  117.2 5.0 %collective-permute-start.22 = (f32[24,512]{1,0:T(8,128)S(1)}, f32[24,512]{1,0:T(8,128)S(1)}, u32[]{:S(2)}, u32[]{:S(2)}) collective-permute-start(f32[24,512]{1,0:T(8,128)S(1)} %pad_maximum_fusion.1), channel_id=1, source_target_pairs={{0,4},{1,5},{2,6},{3,7},{4,0},{5,1},{6,2},{7,3},{8,12},{9,13},{10,... | collective-permute-start | bytes 147464 | tf_op jit(solution)/shard_map/ppermute | solution.py:325
